TPU v7x, 512 devices: a whole 4x8x8 slice. The times are simulated.
512 devices in a mesh: dp: 64 (over y, x, z_hi), shard: 8 (over z_lo, core).
Axes of the slice: x: 4, y: 8, z: 8 (z_hi: 2, z_lo: 4; z = z_hi * 4 + z_lo), core: 2. Of those that a mesh axis runs over, the one named last changes fastest.
Arguments:
- hidden: bfloat16 [8192, 14336], P('dp', 'shard'), may hold values from -6 to 6
- out_grad: bfloat16 [8192, 4096], P('dp', 'shard'), may hold values from -6 to 6
- block_weight: bfloat16 [8, 32, 128, 128], P('shard'), may hold values from -0.1875 to 0.1875
- block_row: int32 [8, 32], replicated, may hold values from 0 to 111, as said below
- block_col: int32 [8, 32], replicated, may hold values from 0 to 31
- live_count: int32 [8], replicated, may hold values from 16 to 32, as said below
- new_owner: int32 [8, 32], replicated, may hold values from -1 to 7, as said below
- new_slot: int32 [8, 32], replicated, may hold values from 0 to 31, as said below
- first_moment: float32 [8, 32, 16384], P('shard', None, 'dp'), may hold values from -3 to 3
- second_moment: float32 [8, 32, 16384], P('shard', None, 'dp'), may hold values from 0.05 to 2
Outputs:
- projected: bfloat16 [8192, 4096], P('dp', 'shard')
- hidden_grad: bfloat16 [8192, 14336], P('dp', 'shard')
- new_weight: float32 [8, 32, 16384], P('shard', None, 'dp')
- new_first: float32 [8, 32, 16384], P('shard', None, 'dp')
- new_second: float32 [8, 32, 16384], P('shard', None, 'dp')
Inputs may be any that keep to these rules, and one draw needn't show every extreme that they name: `block_row`: together with block_col, each slot's block place; no two slots of all shards share a place. `live_count`: some shard has all 32 slots live. `new_owner`: -1 for slots that are not live and for dropped blocks. At most 2 blocks of one shard go to one other shard; in every draw some shard receives exactly 2 from every other shard. `new_slot`: no two blocks with new_owner >= 0 share an owner and a slot; 0 where new_owner is -1.
All inputs are finite; a program needn't handle non-finite values.
Results may differ from a plain program's by a relative error of at most 0.004.
Values may be sent and summed in bfloat16 or wider, within the bound.
No kernel may reach another device: no remote copies, remote signals or barrier semaphores. Data moves between devices by JAX's collectives and lax.ppermute only.
A program may use at most 64 MiB of HBM per device.

v0:
```python
import math

import jax
import jax.numpy as jnp
from jax import lax
from jax.sharding import PartitionSpec as P

MV = 2


LEARN_RATE = 0.01
BETA_ONE = 0.9
BETA_TWO = 0.95
EPSILON = 1e-08


def adam_update(weight, first_state, second_state, gradient):
    first_state = BETA_ONE * first_state + (1.0 - BETA_ONE) * gradient
    second_state = BETA_TWO * second_state + (1.0 - BETA_TWO) * gradient * gradient
    weight = weight - LEARN_RATE * first_state / (jnp.sqrt(second_state) + EPSILON)
    return (weight, first_state, second_state)


def send_positions(owner_devices, shard_count, slot_count):
    sources = jnp.arange(shard_count, dtype=jnp.int32)[:, None]
    moving = (owner_devices >= 0) & (owner_devices != sources)
    slot_ids = jnp.arange(slot_count)
    earlier = slot_ids[None, :] < slot_ids[:, None]
    matches = (
        (owner_devices[:, :, None] == owner_devices[:, None, :])
        & moving[:, None, :]
        & earlier[None, :, :]
    )
    return (moving, jnp.sum(matches, axis=2))


def pack_moving(values, owner_row, moving_row, position_row, shard_count, capacity):
    slot_ids = jnp.arange(values.shape[0], dtype=jnp.int32)
    targets = owner_row * capacity + position_row
    entries = jnp.arange(shard_count * capacity, dtype=jnp.int32)
    matches = (targets[None, :] == entries[:, None]) & moving_row[None, :]
    source = jnp.sum(jnp.where(matches, slot_ids[None, :], 0), axis=1)
    filled = jnp.any(matches, axis=1)
    packed = jnp.where(filled[:, None], jnp.take(values, source, axis=0), 0.0)
    return packed.reshape(shard_count, capacity, values.shape[1])


def place_blocks(
    received,
    own_values,
    owner_devices,
    destination_slot_list,
    moving,
    positions,
    my_index,
    capacity,
):
    shard_count, slot_count = owner_devices.shape
    slot_ids = jnp.arange(slot_count, dtype=jnp.int32)
    entries = (jnp.arange(shard_count, dtype=jnp.int32)[:, None] * capacity + positions).reshape(-1)
    to_me = (moving & (owner_devices == my_index)).reshape(-1)
    matches = to_me[None, :] & (destination_slot_list.reshape(-1)[None, :] == slot_ids[:, None])
    arrived = jnp.any(matches, axis=1)
    from_entry = jnp.sum(jnp.where(matches, entries[None, :], 0), axis=1)
    flattened = received.reshape(shard_count * capacity, received.shape[2])
    arrival_rows = jnp.take(flattened, from_entry, axis=0)
    stay_hit = (owner_devices[my_index] == my_index)[None, :] & (
        destination_slot_list[my_index][None, :] == slot_ids[:, None]
    )
    stayed = jnp.any(stay_hit, axis=1)
    from_slot = jnp.sum(jnp.where(stay_hit, slot_ids[None, :], 0), axis=1)
    kept_rows = jnp.take(own_values, from_slot, axis=0)
    return jnp.where(arrived[:, None], arrival_rows, jnp.where(stayed[:, None], kept_rows, 0.0))


def local_place(block_ids, first_id, local_count):
    local_ids = block_ids - first_id
    inside = (local_ids >= 0) & (local_ids < local_count)
    return jnp.where(inside, local_ids, local_count)


def shards(
    hidden,
    out_grad,
    block_weight,
    block_row,
    block_col,
    live_count,
    new_owner,
    new_slot,
    first_moment,
    second_moment,
):
    shard_count = lax.axis_size("shard")
    dp_count = lax.axis_size("dp")
    my_index = lax.axis_index("shard")
    dp_index = lax.axis_index("dp")
    tokens_dev = hidden.shape[0]
    slot_count = block_weight.shape[1]
    block_size = block_weight.shape[2]
    share_size = first_moment.shape[2]
    row_blocks = hidden.shape[1] * shard_count // block_size
    col_blocks = out_grad.shape[1] * shard_count // block_size
    grad_scale = 1.0 / math.sqrt(tokens_dev * dp_count)
    slot_ids = jnp.arange(slot_count)
    live_all = slot_ids[None, :] < live_count[:, None]
    my_live = live_all[my_index]
    my_rows = block_row[my_index]
    my_cols = block_col[my_index]
    zero_bf = jnp.zeros((), jnp.bfloat16)
    full_hidden, full_grad = (
        lax.all_gather(hidden, "shard", axis=1, tiled=True),
        lax.all_gather(out_grad, "shard", axis=1, tiled=True),
    )
    hidden_blocks = full_hidden.reshape(tokens_dev, row_blocks, block_size)
    grad_blocks = full_grad.reshape(tokens_dev, col_blocks, block_size)
    own_hidden = jnp.take(hidden_blocks, my_rows, axis=1)
    own_grad = jnp.take(grad_blocks, my_cols, axis=1)
    grad_share = None
    col_local = col_blocks // shard_count
    row_local = row_blocks // shard_count

    def one_shard(totals, member):
        blocks, shard_index = member
        row_ids = block_row[shard_index]
        col_ids = block_col[shard_index]
        weights = jnp.where(live_all[shard_index][:, None, None], blocks, zero_bf)
        hidden_part = jnp.take(hidden_blocks, row_ids, axis=1)
        grad_part = jnp.take(grad_blocks, col_ids, axis=1)
        forward = jnp.einsum(
            "tkr,krc->tkc", hidden_part, weights, preferred_element_type=jnp.float32
        )
        backward = jnp.einsum(
            "tkc,krc->tkr", grad_part, weights, preferred_element_type=jnp.float32
        )
        col_place = local_place(col_ids, my_index * col_local, col_local)
        row_place = local_place(row_ids, my_index * row_local, row_local)
        out_total = totals[0].at[:, col_place].add(forward, mode="drop")
        back_total = totals[1].at[:, row_place].add(backward, mode="drop")
        return ((out_total, back_total), None)

    initial = (
        jnp.zeros((tokens_dev, col_local, block_size), jnp.float32),
        jnp.zeros((tokens_dev, row_local, block_size), jnp.float32),
    )
    totals = initial
    blocks_in = lax.all_gather(block_weight, "shard", axis=0, tiled=True)
    indices = jnp.arange(blocks_in.shape[0], dtype=jnp.int32)
    totals, unused = lax.scan(one_shard, totals, (blocks_in, indices))
    out_total, back_total = totals
    projected = out_total.reshape(tokens_dev, col_local * block_size).astype(jnp.bfloat16)
    hidden_grad = back_total.reshape(tokens_dev, row_local * block_size).astype(jnp.bfloat16)
    blocks = (
        jnp.einsum("tkr,tkc->krc", own_hidden, own_grad, preferred_element_type=jnp.float32)
        * grad_scale
    )
    blocks = jnp.where(my_live[:, None, None], blocks, 0.0)
    grad_share = lax.psum_scatter(
        blocks.reshape(slot_count, block_size * block_size), "dp", scatter_dimension=1, tiled=True
    )
    moving, positions = send_positions(new_owner, shard_count, slot_count)
    my_owner = new_owner[my_index]
    my_moving = moving[my_index]
    my_positions = positions[my_index]
    flat_weight = block_weight[0].reshape(slot_count, block_size * block_size)
    weight_share = lax.dynamic_slice_in_dim(
        flat_weight, dp_index * share_size, share_size, 1
    ).astype(jnp.float32)
    updated, first_state, second_state = adam_update(
        weight_share, first_moment[0], second_moment[0], grad_share
    )
    stacked = jnp.concatenate([updated, first_state, second_state], axis=1)
    packed = pack_moving(stacked, my_owner, my_moving, my_positions, shard_count, MV)
    received = lax.all_to_all(packed, "shard", split_axis=0, concat_axis=0, tiled=True)
    placed = place_blocks(received, stacked, new_owner, new_slot, moving, positions, my_index, MV)
    new_weight = placed[:, :share_size]
    new_first = placed[:, share_size : 2 * share_size]
    new_second = placed[:, 2 * share_size :]
    return (projected, hidden_grad, new_weight[None], new_first[None], new_second[None])


def solution(mesh):
    in_specs = (
        P("dp", "shard"),
        P("dp", "shard"),
        P("shard", None, None, None),
        P(),
        P(),
        P(),
        P(),
        P(),
        P("shard", None, "dp"),
        P("shard", None, "dp"),
    )
    out_specs = (
        P("dp", "shard"),
        P("dp", "shard"),
        P("shard", None, "dp"),
        P("shard", None, "dp"),
        P("shard", None, "dp"),
    )
    return jax.shard_map(shards, mesh=mesh, in_specs=in_specs, out_specs=out_specs, check_vma=False)
```

profile of v0, /device:TPU:1, one launch (start us, length us, event | category | flops | bytes accessed | tf_op | source)
XLA Modules:
  0.0 829.7 jit_solution(11209783797241705742)
XLA Ops:
  13.2 40.8 %all-gather.8.cloned.1.call-done = bf16[128,4096]{0,1:T(8,128)(2,1)} async-done(((bf16[128,512]{0,1:T(8,128)(2,1)}), bf16[128,4096]{0,1:T(8,128)(2,1)}) %all-gather.8.cloned.1.call-update) | async-done | bytes 1048592 | tf_op jit(solution)/shard_map/all_gather | solution.py:113
  56.4 51.7 %all-gather.6.cloned.1.call-done = bf16[128,14336]{0,1:T(8,128)(2,1)} async-done(((bf16[128,1792]{0,1:T(8,128)(2,1)}), bf16[128,14336]{0,1:T(8,128)(2,1)}) %all-gather.6.cloned.1.call-update) | async-done | bytes 3670032 | tf_op jit(solution)/shard_map/all_gather | solution.py:112
  108.1 6.0 copy.47
  114.1 2.8 gather_fusion.5
  123.8 392.7 %reduce-scatter.2.cloned.1.call-done = f32[32,256]{1,0:T(8,128)} async-done(((f32[32,16384]{1,0:T(8,128)}), f32[32,256]{1,0:T(8,128)}) %reduce-scatter.2.cloned.1.call-update) | async-done | bytes 32784 | tf_op jit(solution)/shard_map/reduce_scatter | solution.py:158
  518.6 55.6 %all-to-all-start = ((f32[8,2,768]{2,1,0:T(2,128)}), f32[8,2,768]{2,1,0:T(2,128)S(1)}, u32[]{:S(2)}, u32[]{:S(2)}) async-start(f32[8,2,768]{2,1,0:T(2,128)} %select_select_fusion.1), calls=%async_computation.1 | async-start | bytes 98304 | tf_op jit(solution)/shard_map/all_to_all | solution.py:174
  574.8 4.4 all-to-all-done
  580.6 76.7 %all-gather.4.cloned.1.call-done = bf16[8,32,128,128]{3,2,1,0:T(8,128)(2,1)} async-done(((bf16[1,32,128,128]{3,2,1,0:T(8,128)(2,1)}), bf16[8,32,128,128]{3,2,1,0:T(8,128)(2,1)}) %all-gather.4.cloned.1.call-update) | async-done | bytes 8388624 | tf_op jit(solution)/shard_map/all_gather | solution.py:147
  657.5 163.8 %while.14 = (s32[]{:T(128)}, f32[128,4,128]{2,0,1:T(8,128)S(1)}, f32[128,14,128]{2,0,1:T(8,128)S(1)}, s32[8]{0:T(128)S(1)}, s32[8,32]{1,0:T(8,128)}, /*index=5*/...) while((s32[]{:T(128)}, f32[128,4,128]{2,0,1:T(8,128)S(1)}, ...), condition=%wide.region_3.6_spmd, body=%wide.region_0.5_spmd.sunk | while | flops 271584128 | bytes 25176288 | solution.py:149
  661.4 3.7 gather_fusion
  667.2 2.7 scatter_fusion
  669.9 2.9 gather_fusion.1
  675.3 2.7 scatter_fusion.1
  681.9 3.7 gather_fusion
  690.4 2.9 gather_fusion.1
  702.4 3.7 gather_fusion
  710.8 2.9 gather_fusion.1
  722.9 3.7 gather_fusion
  728.6 2.7 scatter_fusion
  731.3 2.9 gather_fusion.1
  743.3 3.7 gather_fusion
  751.8 2.9 gather_fusion.1
  763.8 3.7 gather_fusion
  769.6 2.7 scatter_fusion
  772.3 2.9 gather_fusion.1
  784.3 3.7 gather_fusion
  790.0 2.7 scatter_fusion
  792.7 2.9 gather_fusion.1
  798.1 2.7 scatter_fusion.1
  804.7 3.7 gather_fusion
  813.2 2.9 gather_fusion.1
  818.6 2.7 scatter_fusion.1
  (148 shorter events, 97.5 us)
Async XLA Ops:
  7.2 46.9 %all-gather.8.cloned.1.call-start = ((), (), s32[]{:S(2)}) async-start(), calls=%async_computation.4 | async-start | bytes 1179648 | tf_op jit(solution)/shard_map/all_gather | solution.py:113
  8.9 99.2 %all-gather.6.cloned.1.call-start = ((), (), s32[]{:S(2)}) async-start(), calls=%async_computation.3 | async-start | bytes 4128768 | tf_op jit(solution)/shard_map/all_gather | solution.py:112
  11.0 505.5 %reduce-scatter.2.cloned.1.call-start = ((), (), s32[]{:S(2)}) async-start(), calls=%async_computation.5 | async-start | bytes 2129920 | tf_op jit(solution)/shard_map/reduce_scatter | solution.py:158
  55.6 58.4 %copy-start = (bf16[128,32,128]{2,0,1:T(8,128)(2,1)}, bf16[128,32,128]{2,0,1:T(8,128)(2,1)S(1)}, u32[]{:S(2)}) copy-start(bf16[128,32,128]{2,0,1:T(8,128)(2,1)S(1)} %copy.48) | copy-start | bytes 3145732
  120.2 1.2 copy-start.1
  120.2 1.9 copy-start.2
  120.2 2.8 copy-start.5
  120.2 396.2 %copy-start.3 = (f32[1,32,256]{2,1,0:T(8,128)S(1)}, f32[1,32,256]{2,1,0:T(8,128)}, u32[]{:S(2)}) copy-start(f32[1,32,256]{2,1,0:T(8,128)} %param.24) | copy-start | bytes 98308
  120.3 396.2 %copy-start.4 = (f32[1,32,256]{2,1,0:T(8,128)S(1)}, f32[1,32,256]{2,1,0:T(8,128)}, u32[]{:S(2)}) copy-start(f32[1,32,256]{2,1,0:T(8,128)} %param.25) | copy-start | bytes 98308
  120.3 537.1 %all-gather.4.cloned.1.call-start = ((), (), s32[]{:S(2)}) async-start(), calls=%async_computation.2 | async-start | bytes 9437184 | tf_op jit(solution)/shard_map/all_gather | solution.py:147
  518.6 60.6 %all-to-all-start = ((f32[8,2,768]{2,1,0:T(2,128)}), f32[8,2,768]{2,1,0:T(2,128)S(1)}, u32[]{:S(2)}, u32[]{:S(2)}) async-start(f32[8,2,768]{2,1,0:T(2,128)} %select_select_fusion.1), calls=%async_computation.1 | async-start | bytes 98304 | tf_op jit(solution)/shard_map/all_to_all | solution.py:174
Sparse Core Ops, SparseCore 0:
  10.7 43.3 all-gather.7
  56.7 51.3 all-gather.5
  120.3 396.0 reduce-scatter.1
  518.6 138.7 all-gather.3
where the time goes:
time: 834 us; the launch traced here: 830 us
  waiting for transfers between devices  567 us (68%)
  local copies, waits for them, and re-layouts  80.7 us (10%)
  other arithmetic  59.6 us (7%)
  starting transfers between devices  55.7 us (7%)
  matrix products  36.7 us (4%)
  loops' own time  16 us (2%)
  between operations  14 us (2%)
    reduce_scatter x1, waiting for transfers between devices, shards(): lax.psum_scatter(blocks.reshape(slot_count, block_size * block_size), 'dp...  393 us
    all_gather x1, waiting for transfers between devices, shards(): blocks_in = lax.all_gather(block_weight, 'shard', axis=0, tiled=True)  76.7 us
    all_to_all x1, starting transfers between devices, shards(): lax.all_to_all(packed, 'shard', split_axis=0, concat_axis=0, tiled=True)  55.6 us
    all_gather x1, waiting for transfers between devices, shards(): lax.all_gather(hidden, 'shard', axis=1, tiled=True)  51.7 us
    all_gather x1, waiting for transfers between devices, shards(): lax.all_gather(out_grad, 'shard', axis=1, tiled=True)  40.8 us
    gather x8, local copies, waits for them, and re-layouts, one_shard(): hidden_part = jnp.take(hidden_blocks, row_ids, axis=1)  29.7 us
    gather x8, local copies, waits for them, and re-layouts, one_shard(): grad_part = jnp.take(grad_blocks, col_ids, axis=1)  23.2 us
    scatter-add x8, other arithmetic, one_shard(): out_total = totals[0].at[:, col_place].add(forward, mode='drop')  21.2 us
  transfers between devices with their start and end apart: 5, of which 5 were waited for; matrix products, arithmetic and copies ran while one was open for 2% of the time, Pallas kernels for 0%

commit v1 on v0

--- a/solution.py
+++ b/solution.py
@@ -1,10 +1,15 @@
+import functools
 import math
 
 import jax
 import jax.numpy as jnp
 from jax import lax
-from jax.sharding import PartitionSpec as P
-
+from jax.experimental import pallas as pl
+from jax.experimental.pallas import tpu as pltpu
+from jax.sharding import Mesh, PartitionSpec as P
+
+DP = ("y", "x", "zh")
+SHARD = ("zl", "core")
 MV = 2
 
 
@@ -79,7 +84,7 @@
     return jnp.where(inside, local_ids, local_count)
 
 
-def shards(
+def general(
     hidden,
     out_grad,
     block_weight,
@@ -91,10 +96,10 @@
     first_moment,
     second_moment,
 ):
-    shard_count = lax.axis_size("shard")
-    dp_count = lax.axis_size("dp")
-    my_index = lax.axis_index("shard")
-    dp_index = lax.axis_index("dp")
+    shard_count = lax.axis_size(SHARD)
+    dp_count = lax.axis_size(DP)
+    my_index = lax.axis_index(SHARD)
+    dp_index = lax.axis_index(DP)
     tokens_dev = hidden.shape[0]
     slot_count = block_weight.shape[1]
     block_size = block_weight.shape[2]
@@ -109,8 +114,8 @@
     my_cols = block_col[my_index]
     zero_bf = jnp.zeros((), jnp.bfloat16)
     full_hidden, full_grad = (
-        lax.all_gather(hidden, "shard", axis=1, tiled=True),
-        lax.all_gather(out_grad, "shard", axis=1, tiled=True),
+        lax.all_gather(hidden, SHARD, axis=1, tiled=True),
+        lax.all_gather(out_grad, SHARD, axis=1, tiled=True),
     )
     hidden_blocks = full_hidden.reshape(tokens_dev, row_blocks, block_size)
     grad_blocks = full_grad.reshape(tokens_dev, col_blocks, block_size)
@@ -144,7 +149,7 @@
         jnp.zeros((tokens_dev, row_local, block_size), jnp.float32),
     )
     totals = initial
-    blocks_in = lax.all_gather(block_weight, "shard", axis=0, tiled=True)
+    blocks_in = lax.all_gather(block_weight, SHARD, axis=0, tiled=True)
     indices = jnp.arange(blocks_in.shape[0], dtype=jnp.int32)
     totals, unused = lax.scan(one_shard, totals, (blocks_in, indices))
     out_total, back_total = totals
@@ -156,7 +161,7 @@
     )
     blocks = jnp.where(my_live[:, None, None], blocks, 0.0)
     grad_share = lax.psum_scatter(
-        blocks.reshape(slot_count, block_size * block_size), "dp", scatter_dimension=1, tiled=True
+        blocks.reshape(slot_count, block_size * block_size), DP, scatter_dimension=1, tiled=True
     )
     moving, positions = send_positions(new_owner, shard_count, slot_count)
     my_owner = new_owner[my_index]
@@ -171,7 +176,7 @@
     )
     stacked = jnp.concatenate([updated, first_state, second_state], axis=1)
     packed = pack_moving(stacked, my_owner, my_moving, my_positions, shard_count, MV)
-    received = lax.all_to_all(packed, "shard", split_axis=0, concat_axis=0, tiled=True)
+    received = lax.all_to_all(packed, SHARD, split_axis=0, concat_axis=0, tiled=True)
     placed = place_blocks(received, stacked, new_owner, new_slot, moving, positions, my_index, MV)
     new_weight = placed[:, :share_size]
     new_first = placed[:, share_size : 2 * share_size]
@@ -179,24 +184,303 @@
     return (projected, hidden_grad, new_weight[None], new_first[None], new_second[None])
 
 
+CAP = 48
+NX, NY, NZH, NZL = 4, 8, 2, 4
+PER_X = CAP // NX
+BS = 128
+VMEM_LIMIT = 40 * 1024 * 1024
+f32 = jnp.float32
+bf16 = jnp.bfloat16
+
+
+def vmem():
+    return pl.BlockSpec(memory_space=pltpu.VMEM)
+
+
+def smem():
+    return pl.BlockSpec(memory_space=pltpu.SMEM)
+
+
+def call(kernel, outs, n_smem, n_vmem, scratch=(), flops=0, byts=0):
+    return pl.pallas_call(
+        kernel,
+        out_shape=outs,
+        in_specs=[smem()] * n_smem + [vmem()] * n_vmem,
+        out_specs=jax.tree.map(lambda _: vmem(), outs),
+        scratch_shapes=list(scratch),
+        compiler_params=pltpu.CompilerParams(vmem_limit_bytes=VMEM_LIMIT),
+        cost_estimate=pl.CostEstimate(flops=flops, bytes_accessed=byts, transcendentals=0),
+    )
+
+
+def make_plan(block_row, block_col, live_count, new_owner, new_slot, row_local):
+    shard_count, slot_count = block_row.shape
+    total = shard_count * slot_count
+    ids = jnp.arange(total, dtype=jnp.int32)
+    live = (jnp.arange(slot_count)[None, :] < live_count[:, None]).reshape(total)
+    row = block_row.reshape(total)
+    col = block_col.reshape(total)
+    owner = jnp.where(live, new_owner.reshape(total), -1)
+    slot = new_slot.reshape(total)
+    row_shard = row // row_local
+    key = jnp.where(owner >= 0, ids, ids + total)
+    before = (row_shard[:, None] == row_shard[None, :]) & live[None, :] & (key[None, :] < key[:, None])
+    rank = jnp.sum(before.astype(jnp.int32), axis=1)
+    fits = jnp.max(jnp.where(live, rank, 0)) < CAP
+    return live, row, col, owner, slot, row_shard, rank, fits
+
+
+def select_kernel(info, code, mine, other, out):
+    my_core, my_x = info[2], info[3]
+    for i in range(PER_X):
+        g = code[my_x * PER_X + i] & 255
+        owner_shard, k = g // 32, g % 32
+        zl, core = owner_shard // 2, owner_shard % 2
+        part, first = k // 8, (k % 8) * 16
+        first = pl.multiple_of(first, 16)
+        from_mine = mine[zl, 4 + part, pl.ds(first, 16), :]
+        from_other = other[zl, 4 + part, pl.ds(first, 16), :]
+        value = jnp.where(core == my_core, from_mine, from_other)
+        for y in range(NY):
+            out[y, i] = value
+
+
+def grad_kernel(info, code, hidden, mine, other, out, cols, hidden_t, total):
+    my_core = info[2]
+    for zl in range(NZL):
+        for sub in range(4):
+            cols[(2 * zl + my_core) * 4 + sub] = mine[zl, sub]
+            cols[(2 * zl + 1 - my_core) * 4 + sub] = other[zl, sub]
+    row_local = hidden.shape[1] // BS
+    for r in range(row_local):
+        hidden_t[r] = hidden[:, r * BS : (r + 1) * BS].T
+
+    def step(c, carry):
+        word = code[c]
+        r, col = (word >> 8) & 15, word >> 12
+        block = jnp.dot(hidden_t[r], cols[col], preferred_element_type=f32)
+        total[pl.ds(c, BS, stride=CAP), :] = block
+        return carry
+
+    lax.fori_loop(0, info[1], step, 0)
+    for x in range(NX):
+        for y in range(NY):
+            for q in range(4):
+                source = 16 * y + 4 * x + q
+                out[x, 2 * y + q // 2, q % 2] = total[source * CAP : (source + 1) * CAP, :].astype(bf16)
+
+
+def product_kernel(info, code, hidden, cols, weights, mine, theirs, back, out_total, back_total):
+    my_core = info[2]
+    row_local = hidden.shape[1] // BS
+    out_total[...] = jnp.zeros_like(out_total)
+    back_total[...] = jnp.zeros_like(back_total)
+
+    def step(c, carry):
+        word = code[c]
+        r, col = (word >> 8) & 15, word >> 12
+        w = weights[c // PER_X, :, c % PER_X].reshape(BS, BS)
+        h = hidden[:, pl.ds(pl.multiple_of(r * BS, BS), BS)]
+        out_total[col] += jnp.dot(h, w, preferred_element_type=f32)
+        back_total[r] += lax.dot_general(
+            cols[col], w, (((1,), (1,)), ((), ())), preferred_element_type=f32
+        )
+        return carry
+
+    lax.fori_loop(0, info[0], step, 0)
+    for zl in range(NZL):
+        for sub in range(4):
+            mine[zl, sub] = out_total[(2 * zl + my_core) * 4 + sub]
+            theirs[zl, sub] = out_total[(2 * zl + 1 - my_core) * 4 + sub]
+    for r in range(row_local):
+        back[:, r * BS : (r + 1) * BS] = back_total[r].astype(bf16)
+
+
+def pack_kernel(source, stacked, out):
+    for e in range(out.shape[0]):
+        out[pl.ds(e, 1), :] = stacked[pl.ds(source[e], 1), :]
+
+
+def adam_kernel(place, stacked, received, shares, new_w, new_m, new_v, state, grad):
+    slots = new_w.shape[0]
+    share = new_w.shape[1]
+    for j in range(slots):
+        word = jnp.maximum(place[j] - 1, 0)
+        g, row = word & 1023, word >> 10
+        own = stacked[pl.ds(jnp.minimum(row, slots - 1), 1), :]
+        came = received[pl.ds(jnp.maximum(row - slots, 0), 1), :]
+        filled = place[j] > 0
+        state[pl.ds(j, 1), :] = jnp.where(filled, jnp.where(row < slots, own, came), 0.0)
+        shard, rank = g // CAP, g % CAP
+        for b in range(2):
+            value = shares[shard, b, pl.ds(rank, 1), :]
+            grad[pl.ds(j, 1), b * BS : (b + 1) * BS] = jnp.where(filled, value, 0.0)
+    w, m, v = adam_update(state[:, :share], state[:, share : 2 * share], state[:, 2 * share :], grad[...])
+    new_w[...] = w
+    new_m[...] = m
+    new_v[...] = v
+
+
+def fast(
+    plan,
+    hidden,
+    out_grad,
+    block_weight,
+    first_moment,
+    second_moment,
+):
+    live, row, col, owner, slot, row_shard, rank = plan
+    shard_count = lax.axis_size(SHARD)
+    me = lax.axis_index(SHARD)
+    core = lax.axis_index("core")
+    dp_index = lax.axis_index(DP)
+    x_index, y_index = lax.axis_index("x"), lax.axis_index("y")
+    tokens = hidden.shape[0]
+    slot_count = block_weight.shape[1]
+    row_local = hidden.shape[1] // BS
+    share = first_moment.shape[2]
+    total = shard_count * slot_count
+    scale = 1.0 / math.sqrt(tokens * lax.axis_size(DP))
+    ids = jnp.arange(total, dtype=jnp.int32)
+
+    here = live & (row_shard == me)
+    words = ids + 256 * ((row - row_local * me) + 16 * col)
+    hit = here[None, :] & (rank[None, :] == jnp.arange(CAP)[:, None])
+    code = jnp.sum(jnp.where(hit, words[None, :], 0), axis=1)
+    info = jnp.stack([jnp.sum(here.astype(jnp.int32)), jnp.sum((here & (owner >= 0)).astype(jnp.int32)), core, x_index])
+
+    owner2 = owner.reshape(shard_count, slot_count)
+    sources = jnp.arange(shard_count, dtype=jnp.int32)[:, None]
+    moving, positions = send_positions(owner2, shard_count, slot_count)
+    entry = jnp.arange(shard_count * MV, dtype=jnp.int32)
+    my_target = jnp.where(moving[me], owner2[me] * MV + positions[me], -1)
+    send_hit = my_target[None, :] == entry[:, None]
+    send_source = jnp.sum(jnp.where(send_hit, jnp.arange(slot_count, dtype=jnp.int32)[None, :], 0), axis=1)
+    state_row = jnp.where(
+        sources == me, jnp.arange(slot_count, dtype=jnp.int32)[None, :], slot_count + sources * MV + positions
+    ).reshape(total)
+    landing = 1 + row_shard * CAP + rank + 1024 * state_row
+    lands = (owner == me)[None, :] & (slot[None, :] == jnp.arange(slot_count)[:, None])
+    place = jnp.sum(jnp.where(lands, landing[None, :], 0), axis=1)
+
+    rows_y = BS // NY
+    my_cols = out_grad.reshape(tokens, 4, BS).transpose(1, 0, 2)
+    my_weights = lax.dynamic_slice_in_dim(block_weight[0], y_index * rows_y, rows_y, 1).reshape(4, BS, BS)
+    parcel = jnp.concatenate([my_cols, my_weights], axis=0)
+    mine = lax.all_to_all(
+        jnp.broadcast_to(parcel[None], (NZL,) + parcel.shape), "zl", split_axis=0, concat_axis=0, tiled=True
+    )
+    other = lax.ppermute(mine, "core", [(0, 1), (1, 0)])
+
+    picked = call(select_kernel, jax.ShapeDtypeStruct((NY, PER_X, rows_y, BS), bf16), 2, 2)(info, code, mine, other)
+    along_y = lax.all_to_all(picked, "y", split_axis=0, concat_axis=0, tiled=True)
+    weights = lax.all_to_all(
+        jnp.broadcast_to(along_y[None], (NX,) + along_y.shape), "x", split_axis=0, concat_axis=0, tiled=True
+    )
+
+    partial, cols = call(
+        grad_kernel,
+        (
+            jax.ShapeDtypeStruct((NX, NY * NZH, 2, CAP, BS), bf16),
+            jax.ShapeDtypeStruct((shard_count * 4, BS, BS), bf16),
+        ),
+        2,
+        3,
+        [pltpu.VMEM((row_local, BS, BS), bf16), pltpu.VMEM((BS * CAP, BS), f32)],
+        flops=2 * CAP * BS**3,
+        byts=4 * 1024 * 1024,
+    )(info, code, hidden, mine, other)
+    along_x = lax.all_to_all(partial, "x", split_axis=0, concat_axis=0, tiled=True)
+    summed = jnp.sum(along_x.astype(f32), axis=0).astype(bf16)
+    along_yz = lax.all_to_all(summed, ("y", "zh"), split_axis=0, concat_axis=0, tiled=True)
+    grad_share = jnp.sum(along_yz.astype(f32), axis=0) * scale
+
+    out_mine, out_theirs, hidden_grad = call(
+        product_kernel,
+        (
+            jax.ShapeDtypeStruct((NZL, 4, tokens, BS), f32),
+            jax.ShapeDtypeStruct((NZL, 4, tokens, BS), f32),
+            jax.ShapeDtypeStruct(hidden.shape, bf16),
+        ),
+        2,
+        3,
+        [pltpu.VMEM((shard_count * 4, tokens, BS), f32), pltpu.VMEM((row_local, tokens, BS), f32)],
+        flops=4 * CAP * BS**3,
+        byts=8 * 1024 * 1024,
+    )(info, code, hidden, cols, weights)
+    from_other = lax.ppermute(out_theirs, "core", [(0, 1), (1, 0)])
+    chip_sum = (out_mine + from_other).astype(bf16)
+    along_z = lax.all_to_all(chip_sum, "zl", split_axis=0, concat_axis=0, tiled=True)
+    projected = jnp.sum(along_z.astype(f32), axis=0).astype(bf16)
+    projected = projected.transpose(1, 0, 2).reshape(tokens, 4 * BS)
+
+    weight_share = lax.dynamic_slice_in_dim(block_weight[0], dp_index * 2, 2, 1).reshape(slot_count, share)
+    stacked = jnp.concatenate([weight_share.astype(f32), first_moment[0], second_moment[0]], axis=1)
+    packed = call(pack_kernel, jax.ShapeDtypeStruct((shard_count * MV, 3 * share), f32), 1, 1)(send_source, stacked)
+    received = lax.all_to_all(packed, SHARD, split_axis=0, concat_axis=0, tiled=True)
+    shares = lax.all_gather(grad_share, SHARD, axis=0)
+    shape = jax.ShapeDtypeStruct((slot_count, share), f32)
+    new_weight, new_first, new_second = call(
+        adam_kernel,
+        (shape, shape, shape),
+        1,
+        3,
+        [pltpu.VMEM((slot_count, 3 * share), f32), pltpu.VMEM((slot_count, share), f32)],
+    )(place, stacked, received, shares)
+    return (projected, hidden_grad, new_weight[None], new_first[None], new_second[None])
+
+
+def shards(
+    hidden,
+    out_grad,
+    block_weight,
+    block_row,
+    block_col,
+    live_count,
+    new_owner,
+    new_slot,
+    first_moment,
+    second_moment,
+):
+    row_local = hidden.shape[1] // BS
+    *plan, fits = make_plan(block_row, block_col, live_count, new_owner, new_slot, row_local)
+    return lax.cond(
+        fits,
+        lambda: fast(plan, hidden, out_grad, block_weight, first_moment, second_moment),
+        lambda: general(
+            hidden,
+            out_grad,
+            block_weight,
+            block_row,
+            block_col,
+            live_count,
+            new_owner,
+            new_slot,
+            first_moment,
+            second_moment,
+        ),
+    )
+
+
 def solution(mesh):
+    split = Mesh(mesh.devices.reshape(NY, NX, NZH, NZL, 2), ("y", "x", "zh", "zl", "core"))
     in_specs = (
-        P("dp", "shard"),
-        P("dp", "shard"),
-        P("shard", None, None, None),
+        P(DP, SHARD),
+        P(DP, SHARD),
+        P(SHARD, None, None, None),
         P(),
         P(),
         P(),
         P(),
         P(),
-        P("shard", None, "dp"),
-        P("shard", None, "dp"),
+        P(SHARD, None, DP),
+        P(SHARD, None, DP),
     )
     out_specs = (
-        P("dp", "shard"),
-        P("dp", "shard"),
-        P("shard", None, "dp"),
-        P("shard", None, "dp"),
-        P("shard", None, "dp"),
-    )
-    return jax.shard_map(shards, mesh=mesh, in_specs=in_specs, out_specs=out_specs, check_vma=False)
+        P(DP, SHARD),
+        P(DP, SHARD),
+        P(SHARD, None, DP),
+        P(SHARD, None, DP),
+        P(SHARD, None, DP),
+    )
+    return jax.shard_map(shards, mesh=split, in_specs=in_specs, out_specs=out_specs, check_vma=False)

time: 834 us -> 198 us (0.24)
  waiting for transfers between devices: 567 us -> 60.6 us
  local copies, waits for them, and re-layouts: 80.7 us -> 13.2 us
  other arithmetic: 59.6 us -> 8.96 us
  blocking collectives: 0 us -> 44.4 us
  matrix products: 36.7 us -> 0 us
  starting transfers between devices: 55.7 us -> 39.7 us
  loops' own time: 16 us -> 0.52 us
  Pallas kernels: 0 us -> 14.5 us
    reduce_scatter x1 -> x0, waiting for transfers between devices: 393 us -> none  [shards(): lax.psum_scatter(blocks.reshape(slot_count, block_size * block_size), 'dp...]
    all_gather x3 -> x0, waiting for transfers between devices: 169 us -> none  [the longest x1 76.7 us: shards(): blocks_in = lax.all_gather(block_weight, 'shard', axis=0, tiled=True)]
    gather x22 -> x0, local copies, waits for them, and re-layouts: 58.3 us -> none  [the longest x8 29.7 us: one_shard(): hidden_part = jnp.take(hidden_blocks, row_ids, axis=1)]
    all_to_all x1 -> x6, waiting for transfers between devices: 4.42 us -> 60.6 us  [the longest x1 24.7 us: fast(): lax.all_to_all(jnp.broadcast_to(parcel[None], (NZL,) + parcel.shape), 'zl...]
    scatter-add x16 -> x0, other arithmetic: 42.5 us -> none  [the longest x8 21.2 us: one_shard(): out_total = totals[0].at[:, col_place].add(forward, mode='drop')]
    dot_general x17 -> x0, matrix products: 36.7 us -> none  [the longest x8 19.6 us: one_shard(): jnp.einsum('tkc,krc->tkr', grad_part, weights, preferred_element_type=jnp...]
    all_gather x0 -> x1, blocking collectives: none -> 22.7 us  [fast(): shares = lax.all_gather(grad_share, SHARD, axis=0)]
    all_to_all x1 -> x6, starting transfers between devices: 55.6 us -> 32.9 us  [the longest x1 7.81 us: fast(): lax.all_to_all(jnp.broadcast_to(parcel[None], (NZL,) + parcel.shape), 'zl...]
  transfers between devices with their start and end apart: 5 -> 8, of which waited for: 5 -> 5; matrix products, arithmetic and copies ran while one was open for 2% -> 4% of each run, Pallas kernels for 0% -> 7%
where the time goes in v1:
time: 198 us; the launch traced here: 197 us
  waiting for transfers between devices  60.6 us (31%)
  blocking collectives  44.4 us (22%)
  starting transfers between devices  39.7 us (20%)
  between operations  14.7 us (7%)
  Pallas kernels  14.5 us (7%)
  local copies, waits for them, and re-layouts  13.2 us (7%)
  other arithmetic  8.96 us (5%)
    all_to_all x1, waiting for transfers between devices, fast(): lax.all_to_all(jnp.broadcast_to(parcel[None], (NZL,) + parcel.shape), 'zl...  24.7 us
    all_gather x1, blocking collectives, fast(): shares = lax.all_gather(grad_share, SHARD, axis=0)  22.7 us
    all_to_all x1, blocking collectives, fast(): lax.all_to_all(picked, 'y', split_axis=0, concat_axis=0, tiled=True)  21.7 us
    all_to_all x1, waiting for transfers between devices, fast(): lax.all_to_all(summed, ('y', 'zh'), split_axis=0, concat_axis=0, tiled=True)  16.2 us
    all_to_all x1, waiting for transfers between devices, fast(): lax.all_to_all(jnp.broadcast_to(along_y[None], (NX,) + along_y.shape), 'x...  11.5 us
    all_to_all x1, starting transfers between devices, fast(): lax.all_to_all(jnp.broadcast_to(parcel[None], (NZL,) + parcel.shape), 'zl...  7.81 us
    all_to_all x1, starting transfers between devices, fast(): lax.all_to_all(summed, ('y', 'zh'), split_axis=0, concat_axis=0, tiled=True)  7.41 us
    pallas_call x1, Pallas kernels, fast(): call(product_kernel, (jax.ShapeDtypeStruct((NZL, 4, tokens, BS), f32), ja...  6.47 us
  transfers between devices with their start and end apart: 8, of which 5 were waited for; matrix products, arithmetic and copies ran while one was open for 4% of the time, Pallas kernels for 7%

profile of v1, /device:TPU:1, one launch (start us, length us, event | category | flops | bytes accessed | tf_op | source)
XLA Modules:
  0.0 196.6 jit_solution(14701351832211806341)
XLA Ops:
  8.7 0.8 reshape.420
  11.1 178.0 %conditional.1 = (bf16[128,512]{1,0:T(8,128)(2,1)S(1)}, f32[1,32,256]{2,1,0:T(8,128)S(1)}, f32[1,32,256]{2,1,0:T(8,128)S(1)}, f32[1,32,256]{2,1,0:T(8,128)}, bf16[128,1792]{1,0:T(8,128)(2,1)}) conditional(s32[]{:T(128)} %convert_element_type.50, (bf16[1,32,128,128]{3,2,1,0:T(8,128)(2,1)}, s32[8]{0:T(128)}, bf16[128,1792]{1,0:T(8,128)(2,1)}, ...), branch_computations={%region_2.17_spmd, %region_15.27_spmd} | conditional | flops 606005632 | bytes 115503352 | solution.py:447
  11.1 0.9 constant_dynamic-slice_fusion.2
  12.2 1.0 copy.108
  13.4 1.2 broadcast_in_dim.264
  14.6 7.8 %all-to-all-start = ((bf16[4,8,128,128]{3,2,1,0:T(8,128)(2,1)}), bf16[4,8,128,128]{3,2,1,0:T(8,128)(2,1)S(1)}, u32[]{:S(2)}, u32[]{:S(2)}) async-start(bf16[4,8,128,128]{3,2,1,0:T(8,128)(2,1)} %broadcast_in_dim.264), calls=%async_computation | async-start | bytes 2097152 | tf_op jit(solution)/shard_map/cond/branch_1_fun/all_to_all | solution.py:370
  23.0 24.7 %all-to-all-done.mine = bf16[4,8,128,128]{3,2,1,0:T(8,128)(2,1)S(1)} async-done(((bf16[4,8,128,128]{3,2,1,0:T(8,128)(2,1)}), bf16[4,8,128,128]{3,2,1,0:T(8,128)(2,1)S(1)}, u32[]{:S(2)}, u32[]{:S(2)}) %all-to-all-start) | async-done | bytes 1048608 | tf_op jit(solution)/shard_map/cond/branch_1_fun/all_to_all | solution.py:370
  47.7 3.4 %collective-permute-start = (bf16[4,8,128,128]{3,2,1,0:T(8,128)(2,1)S(1)}, bf16[4,8,128,128]{3,2,1,0:T(8,128)(2,1)S(1)}, u32[]{:S(2)}, u32[]{:S(2)}) collective-permute-start(bf16[4,8,128,128]{3,2,1,0:T(8,128)(2,1)S(1)} %all-to-all-done.mine), channel_id=1, source_target_pairs={{0,1},{1,0},{2,3},{3,2},{4,5},{5,4},{6,7},{7,6},{8,9},{9,8},{10,11... | collective-permute-start | bytes 3145736 | tf_op jit(solution)/shard_map/cond/branch_1_fun/ppermute | solution.py:373
  52.0 1.4 pad_add_fusion.info
  54.3 21.7 %all_to_all.36 = bf16[8,12,16,128]{3,2,1,0:T(8,128)(2,1)S(1)} all-to-all(bf16[8,12,16,128]{3,2,1,0:T(8,128)(2,1)S(1)} %branch_1_fun.6), channel_id=1, replica_groups=mesh['y'=8,'x'=4,'zh'=2,'zl'=4,'core'=2] {'y'}, dimensions={0} | all-to-all | bytes 786432 | tf_op jit(solution)/shard_map/cond/branch_1_fun/all_to_all | solution.py:376
  76.0 1.5 broadcast_in_dim.265
  77.5 4.0 %all-to-all-start.2 = ((bf16[4,8,12,16,128]{4,3,2,1,0:T(8,128)(2,1)}), bf16[4,8,12,16,128]{4,3,2,1,0:T(8,128)(2,1)S(1)}, u32[]{:S(2)}, u32[]{:S(2)}) async-start(bf16[4,8,12,16,128]{4,3,2,1,0:T(8,128)(2,1)} %broadcast_in_dim.265), calls=%async_computation.2 | async-start | bytes 3145728 | tf_op jit(solution)/shard_map/cond/branch_1_fun/all_to_all | solution.py:377
  81.6 1.2 copy-done.1
  82.8 5.1 %branch_1_fun.5 = (bf16[4,16,2,48,128]{4,3,2,1,0:T(8,128)(2,1)S(1)}, bf16[32,128,128]{2,1,0:T(8,128)(2,1)S(1)}) custom-call(s32[4]{0:T(128)S(1)} %pad_add_fusion.info, s32[48]{0:T(128)S(1)} %select_reduce_fusion.code, bf16[128,1792]{1,0:T(8,128)(2,1)S(1)} %copy-done.7, bf16[4,8,128,128]{3,2,1,0:T(8,128)(2,1)S(1)} %all-to-all-done.mine, ...), custom_call_target="tpu_custom_call" | custom-call | flops 201326592 | bytes 4194304 | tf_op jit(solution)/shard_map/cond/branch_1_fun/pallas_call | solution.py:381
  87.9 1.2 copy-done.2
  89.0 1.0 copy-done.3
  90.0 11.5 %all-to-all-done.2.weights = bf16[4,8,12,16,128]{4,3,2,1,0:T(8,128)(2,1)S(1)} async-done(((bf16[4,8,12,16,128]{4,3,2,1,0:T(8,128)(2,1)}), bf16[4,8,12,16,128]{4,3,2,1,0:T(8,128)(2,1)S(1)}, u32[]{:S(2)}, u32[]{:S(2)}) %all-to-all-start.2) | async-done | bytes 1572896 | tf_op jit(solution)/shard_map/cond/branch_1_fun/all_to_all | solution.py:377
  101.5 4.3 %all-to-all-start.5 = ((bf16[4,16,2,48,128]{4,3,2,1,0:T(8,128)(2,1)}), bf16[4,16,2,48,128]{4,3,2,1,0:T(8,128)(2,1)}, u32[]{:S(2)}, u32[]{:S(2)}) async-start(bf16[4,16,2,48,128]{4,3,2,1,0:T(8,128)(2,1)} %copy-done.2), calls=%async_computation.5 | async-start | bytes 3145728 | tf_op jit(solution)/shard_map/cond/branch_1_fun/all_to_all | solution.py:393
  105.9 1.2 copy-done.4
  107.1 6.5 %branch_1_fun.7 = (f32[4,4,128,128]{3,2,1,0:T(8,128)S(1)}, f32[4,4,128,128]{3,2,1,0:T(8,128)}, bf16[128,1792]{1,0:T(8,128)(2,1)}) custom-call(s32[4]{0:T(128)S(1)} %pad_add_fusion.info, s32[48]{0:T(128)S(1)} %select_reduce_fusion.code, bf16[128,1792]{1,0:T(8,128)(2,1)S(1)} %copy-done.7, bf16[32,128,128]{2,1,0:T(8,128)(2,1)S(1)} %copy-done.4, ...), custom_call_target="tpu_custom_call" | custom-call | flops 402653184 | bytes 8388608 | tf_op jit(solution)/shard_map/cond/branch_1_fun/pallas_call | solution.py:398
  113.6 3.4 %collective-permute-start.1 = (f32[4,4,128,128]{3,2,1,0:T(8,128)}, f32[4,4,128,128]{3,2,1,0:T(8,128)S(1)}, u32[]{:S(2)}, u32[]{:S(2)}) collective-permute-start(f32[4,4,128,128]{3,2,1,0:T(8,128)} %get-tuple-element.225), channel_id=1, source_target_pairs={{0,1},{1,0},{2,3},{3,2},{4,5},{5,4},{6,7},{7,6},{8,9},{9,8},{10,11... | collective-permute-start | bytes 3145736 | tf_op jit(solution)/shard_map/cond/branch_1_fun/ppermute | solution.py:411
  117.0 0.9 dynamic-slice_convert_fusion
  119.3 5.6 %all-to-all-done.5 = bf16[4,16,2,48,128]{4,3,2,1,0:T(8,128)(2,1)} async-done(((bf16[4,16,2,48,128]{4,3,2,1,0:T(8,128)(2,1)}), bf16[4,16,2,48,128]{4,3,2,1,0:T(8,128)(2,1)}, u32[]{:S(2)}, u32[]{:S(2)}) %all-to-all-start.5) | async-done | bytes 1572896 | tf_op jit(solution)/shard_map/cond/branch_1_fun/all_to_all | solution.py:393
  124.9 5.9 %all-to-all-start.4 = ((f32[8,2,768]{2,1,0:T(2,128)}), f32[8,2,768]{2,1,0:T(2,128)S(1)}, u32[]{:S(2)}, u32[]{:S(2)}) async-start(f32[8,2,768]{2,1,0:T(2,128)} %all_to_all.23), calls=%async_computation.4 | async-start | bytes 98304 | tf_op jit(solution)/shard_map/cond/branch_1_fun/all_to_all | solution.py:420
  130.8 2.5 %reduce_sum.137 = bf16[16,2,48,128]{3,2,1,0:T(8,128)(2,1)} reduce(bf16[4,16,2,48,128]{4,3,2,1,0:T(8,128)(2,1)} %all-to-all-done.5, bf16[]{:T(256)} %constant.216.clone), dimensions={0}, to_apply=%region_23.25 | reduce | flops 589824 | bytes 1966082 | tf_op jit(solution)/shard_map/cond/branch_1_fun/reduce_sum | solution.py:394
  133.3 2.6 %all-to-all-done.4 = f32[8,2,768]{2,1,0:T(2,128)S(1)} async-done(((f32[8,2,768]{2,1,0:T(2,128)}), f32[8,2,768]{2,1,0:T(2,128)S(1)}, u32[]{:S(2)}, u32[]{:S(2)}) %all-to-all-start.4) | async-done | bytes 49184 | tf_op jit(solution)/shard_map/cond/branch_1_fun/all_to_all | solution.py:420
  135.9 7.4 %all-to-all-start.6 = ((bf16[16,2,48,128]{3,2,1,0:T(8,128)(2,1)}), bf16[16,2,48,128]{3,2,1,0:T(8,128)(2,1)S(1)}, u32[]{:S(2)}, u32[]{:S(2)}) async-start(bf16[16,2,48,128]{3,2,1,0:T(8,128)(2,1)} %reduce_sum.137), calls=%async_computation.6 | async-start | bytes 786432 | tf_op jit(solution)/shard_map/cond/branch_1_fun/all_to_all | solution.py:395
  143.3 0.9 add_convert_fusion
  144.2 16.2 %all-to-all-done.6 = bf16[16,2,48,128]{3,2,1,0:T(8,128)(2,1)S(1)} async-done(((bf16[16,2,48,128]{3,2,1,0:T(8,128)(2,1)}), bf16[16,2,48,128]{3,2,1,0:T(8,128)(2,1)S(1)}, u32[]{:S(2)}, u32[]{:S(2)}) %all-to-all-start.6) | async-done | bytes 393248 | tf_op jit(solution)/shard_map/cond/branch_1_fun/all_to_all | solution.py:395
  160.4 3.5 %all-to-all-start.3 = ((bf16[4,4,128,128]{3,2,1,0:T(8,128)(2,1)}), bf16[4,4,128,128]{3,2,1,0:T(8,128)(2,1)S(1)}, u32[]{:S(2)}, u32[]{:S(2)}) async-start(bf16[4,4,128,128]{3,2,1,0:T(8,128)(2,1)} %add_convert_fusion), calls=%async_computation.3 | async-start | bytes 1048576 | tf_op jit(solution)/shard_map/cond/branch_1_fun/all_to_all | solution.py:413
  164.2 22.7 %all-gather = f32[16,48,128]{2,1,0:T(8,128)S(1)} all-gather(f32[2,48,128]{2,1,0:T(8,128)S(1)} %broadcast_multiply_fusion), channel_id=2, replica_groups=mesh['y'=8,'x'=4,'zh'=2,'zl'=4,'core'=2] {'zl','core'}, dimensions={0}, use_global_device_ids=true | all-gather | bytes 442368 | tf_op jit(solution)/shard_map/cond/branch_1_fun/all_gather | solution.py:421
  187.0 1.6 branch_1_fun.9
  (68 shorter events, 7.8 us)
Async XLA Ops:
  13.2 9.2 %copy-start.14 = (s32[8,32]{1,0:T(8,128)S(1)}, s32[8,32]{1,0:T(8,128)}, u32[]{:S(2)}) copy-start(s32[8,32]{1,0:T(8,128)} %get-tuple-element.217) | copy-start | bytes 3076 | tf_op jit(solution)/shard_map/cond
  13.2 38.0 %copy-start.17 = (s32[8,32]{1,0:T(8,128)S(1)}, s32[8,32]{1,0:T(8,128)}, u32[]{:S(2)}) copy-start(s32[8,32]{1,0:T(8,128)} %get-tuple-element.219) | copy-start | bytes 3076 | tf_op jit(solution)/shard_map/cond
  14.6 33.0 %all-to-all-start = ((bf16[4,8,128,128]{3,2,1,0:T(8,128)(2,1)}), bf16[4,8,128,128]{3,2,1,0:T(8,128)(2,1)S(1)}, u32[]{:S(2)}, u32[]{:S(2)}) async-start(bf16[4,8,128,128]{3,2,1,0:T(8,128)(2,1)} %broadcast_in_dim.264), calls=%async_computation | async-start | bytes 2097152 | tf_op jit(solution)/shard_map/cond/branch_1_fun/all_to_all | solution.py:370
  47.7 5.9 %collective-permute-start = (bf16[4,8,128,128]{3,2,1,0:T(8,128)(2,1)S(1)}, bf16[4,8,128,128]{3,2,1,0:T(8,128)(2,1)S(1)}, u32[]{:S(2)}, u32[]{:S(2)}) collective-permute-start(bf16[4,8,128,128]{3,2,1,0:T(8,128)(2,1)S(1)} %all-to-all-done.mine), channel_id=1, source_target_pairs={{0,1},{1,0},{2,3},{3,2},{4,5},{5,4},{6,7},{7,6},{8,9},{9,8},{10,11... | collective-permute-start | bytes 3145736 | tf_op jit(solution)/shard_map/cond/branch_1_fun/ppermute | solution.py:373
  53.5 24.0 %copy-start = (bf16[4,8,128,128]{3,2,1,0:T(8,128)(2,1)}, bf16[4,8,128,128]{3,2,1,0:T(8,128)(2,1)S(1)}, u32[]{:S(2)}) copy-start(bf16[4,8,128,128]{3,2,1,0:T(8,128)(2,1)S(1)} %collective-permute-done.other) | copy-start | bytes 3145732 | tf_op jit(solution)/shard_map/cond
  76.0 5.5 %copy-start.7 = (bf16[128,1792]{1,0:T(8,128)(2,1)S(1)}, bf16[128,1792]{1,0:T(8,128)(2,1)}, u32[]{:S(2)}) copy-start(bf16[128,1792]{1,0:T(8,128)(2,1)} %get-tuple-element.220.hidden) | copy-start | bytes 1376260 | tf_op jit(solution)/shard_map/cond
  77.5 24.0 %all-to-all-start.2 = ((bf16[4,8,12,16,128]{4,3,2,1,0:T(8,128)(2,1)}), bf16[4,8,12,16,128]{4,3,2,1,0:T(8,128)(2,1)S(1)}, u32[]{:S(2)}, u32[]{:S(2)}) async-start(bf16[4,8,12,16,128]{4,3,2,1,0:T(8,128)(2,1)} %broadcast_in_dim.265), calls=%async_computation.2 | async-start | bytes 3145728 | tf_op jit(solution)/shard_map/cond/branch_1_fun/all_to_all | solution.py:377
  81.6 1.2 copy-start.1
  87.9 1.2 copy-start.2
  89.0 1.0 copy-start.3
  101.5 23.4 %all-to-all-start.5 = ((bf16[4,16,2,48,128]{4,3,2,1,0:T(8,128)(2,1)}), bf16[4,16,2,48,128]{4,3,2,1,0:T(8,128)(2,1)}, u32[]{:S(2)}, u32[]{:S(2)}) async-start(bf16[4,16,2,48,128]{4,3,2,1,0:T(8,128)(2,1)} %copy-done.2), calls=%async_computation.5 | async-start | bytes 3145728 | tf_op jit(solution)/shard_map/cond/branch_1_fun/all_to_all | solution.py:393
  105.8 1.2 copy-start.4
  107.1 11.0 %copy-start.10 = (f32[1,32,256]{2,1,0:T(8,128)S(1)}, f32[1,32,256]{2,1,0:T(8,128)}, u32[]{:S(2)}) copy-start(f32[1,32,256]{2,1,0:T(8,128)} %get-tuple-element.228) | copy-start | bytes 98308 | tf_op jit(solution)/shard_map/cond
  107.1 11.0 %copy-start.12 = (f32[1,32,256]{2,1,0:T(8,128)S(1)}, f32[1,32,256]{2,1,0:T(8,128)}, u32[]{:S(2)}) copy-start(f32[1,32,256]{2,1,0:T(8,128)} %get-tuple-element.229) | copy-start | bytes 98308 | tf_op jit(solution)/shard_map/cond
  113.6 29.7 %collective-permute-start.1 = (f32[4,4,128,128]{3,2,1,0:T(8,128)}, f32[4,4,128,128]{3,2,1,0:T(8,128)S(1)}, u32[]{:S(2)}, u32[]{:S(2)}) collective-permute-start(f32[4,4,128,128]{3,2,1,0:T(8,128)} %get-tuple-element.225), channel_id=1, source_target_pairs={{0,1},{1,0},{2,3},{3,2},{4,5},{5,4},{6,7},{7,6},{8,9},{9,8},{10,11... | collective-permute-start | bytes 3145736 | tf_op jit(solution)/shard_map/cond/branch_1_fun/ppermute | solution.py:411
  124.9 10.9 %all-to-all-start.4 = ((f32[8,2,768]{2,1,0:T(2,128)}), f32[8,2,768]{2,1,0:T(2,128)S(1)}, u32[]{:S(2)}, u32[]{:S(2)}) async-start(f32[8,2,768]{2,1,0:T(2,128)} %all_to_all.23), calls=%async_computation.4 | async-start | bytes 98304 | tf_op jit(solution)/shard_map/cond/branch_1_fun/all_to_all | solution.py:420
  133.3 30.6 %copy-start.19 = (s32[8,32]{1,0:T(8,128)S(1)}, s32[8,32]{1,0:T(8,128)}, u32[]{:S(2)}) copy-start(s32[8,32]{1,0:T(8,128)} %get-tuple-element.227) | copy-start | bytes 3076 | tf_op jit(solution)/shard_map/cond
  135.9 24.6 %all-to-all-start.6 = ((bf16[16,2,48,128]{3,2,1,0:T(8,128)(2,1)}), bf16[16,2,48,128]{3,2,1,0:T(8,128)(2,1)S(1)}, u32[]{:S(2)}, u32[]{:S(2)}) async-start(bf16[16,2,48,128]{3,2,1,0:T(8,128)(2,1)} %reduce_sum.137), calls=%async_computation.6 | async-start | bytes 786432 | tf_op jit(solution)/shard_map/cond/branch_1_fun/all_to_all | solution.py:395
  160.4 28.1 %all-to-all-start.3 = ((bf16[4,4,128,128]{3,2,1,0:T(8,128)(2,1)}), bf16[4,4,128,128]{3,2,1,0:T(8,128)(2,1)S(1)}, u32[]{:S(2)}, u32[]{:S(2)}) async-start(bf16[4,4,128,128]{3,2,1,0:T(8,128)(2,1)} %add_convert_fusion), calls=%async_computation.3 | async-start | bytes 1048576 | tf_op jit(solution)/shard_map/cond/branch_1_fun/all_to_all | solution.py:413
  189.1 0.7 copy-start.8
  189.1 0.6 copy-start.15
  189.1 0.6 copy-start.16

commit v2 on v0

--- a/solution.py
+++ b/solution.py
@@ -1,10 +1,15 @@
+import functools
 import math
 
 import jax
 import jax.numpy as jnp
 from jax import lax
-from jax.sharding import PartitionSpec as P
-
+from jax.experimental import pallas as pl
+from jax.experimental.pallas import tpu as pltpu
+from jax.sharding import Mesh, PartitionSpec as P
+
+DP = ("y", "x", "zh")
+SHARD = ("zl", "core")
 MV = 2
 
 
@@ -79,7 +84,7 @@
     return jnp.where(inside, local_ids, local_count)
 
 
-def shards(
+def general(
     hidden,
     out_grad,
     block_weight,
@@ -91,10 +96,10 @@
     first_moment,
     second_moment,
 ):
-    shard_count = lax.axis_size("shard")
-    dp_count = lax.axis_size("dp")
-    my_index = lax.axis_index("shard")
-    dp_index = lax.axis_index("dp")
+    shard_count = lax.axis_size(SHARD)
+    dp_count = lax.axis_size(DP)
+    my_index = lax.axis_index(SHARD)
+    dp_index = lax.axis_index(DP)
     tokens_dev = hidden.shape[0]
     slot_count = block_weight.shape[1]
     block_size = block_weight.shape[2]
@@ -109,8 +114,8 @@
     my_cols = block_col[my_index]
     zero_bf = jnp.zeros((), jnp.bfloat16)
     full_hidden, full_grad = (
-        lax.all_gather(hidden, "shard", axis=1, tiled=True),
-        lax.all_gather(out_grad, "shard", axis=1, tiled=True),
+        lax.all_gather(hidden, SHARD, axis=1, tiled=True),
+        lax.all_gather(out_grad, SHARD, axis=1, tiled=True),
     )
     hidden_blocks = full_hidden.reshape(tokens_dev, row_blocks, block_size)
     grad_blocks = full_grad.reshape(tokens_dev, col_blocks, block_size)
@@ -144,7 +149,7 @@
         jnp.zeros((tokens_dev, row_local, block_size), jnp.float32),
     )
     totals = initial
-    blocks_in = lax.all_gather(block_weight, "shard", axis=0, tiled=True)
+    blocks_in = lax.all_gather(block_weight, SHARD, axis=0, tiled=True)
     indices = jnp.arange(blocks_in.shape[0], dtype=jnp.int32)
     totals, unused = lax.scan(one_shard, totals, (blocks_in, indices))
     out_total, back_total = totals
@@ -156,7 +161,7 @@
     )
     blocks = jnp.where(my_live[:, None, None], blocks, 0.0)
     grad_share = lax.psum_scatter(
-        blocks.reshape(slot_count, block_size * block_size), "dp", scatter_dimension=1, tiled=True
+        blocks.reshape(slot_count, block_size * block_size), DP, scatter_dimension=1, tiled=True
     )
     moving, positions = send_positions(new_owner, shard_count, slot_count)
     my_owner = new_owner[my_index]
@@ -171,7 +176,7 @@
     )
     stacked = jnp.concatenate([updated, first_state, second_state], axis=1)
     packed = pack_moving(stacked, my_owner, my_moving, my_positions, shard_count, MV)
-    received = lax.all_to_all(packed, "shard", split_axis=0, concat_axis=0, tiled=True)
+    received = lax.all_to_all(packed, SHARD, split_axis=0, concat_axis=0, tiled=True)
     placed = place_blocks(received, stacked, new_owner, new_slot, moving, positions, my_index, MV)
     new_weight = placed[:, :share_size]
     new_first = placed[:, share_size : 2 * share_size]
@@ -179,24 +184,338 @@
     return (projected, hidden_grad, new_weight[None], new_first[None], new_second[None])
 
 
+CAP = 48
+PAIR = 16
+NX, NY, NZH, NZL = 4, 8, 2, 4
+BS = 128
+VMEM_LIMIT = 40 * 1024 * 1024
+f32 = jnp.float32
+bf16 = jnp.bfloat16
+i32 = jnp.int32
+
+
+def call(kernel, outs, n_smem, n_vmem, scratch=(), flops=0, byts=0):
+    smem = pl.BlockSpec(memory_space=pltpu.SMEM)
+    vmem = pl.BlockSpec(memory_space=pltpu.VMEM)
+    return pl.pallas_call(
+        kernel,
+        out_shape=outs,
+        in_specs=[smem] * n_smem + [vmem] * n_vmem,
+        out_specs=jax.tree.map(lambda _: vmem, outs),
+        scratch_shapes=list(scratch),
+        compiler_params=pltpu.CompilerParams(vmem_limit_bytes=VMEM_LIMIT),
+        cost_estimate=pl.CostEstimate(flops=flops, bytes_accessed=byts, transcendentals=0),
+    )
+
+
+def like(shape, dtype):
+    return jax.ShapeDtypeStruct(shape, dtype)
+
+
+def make_plan(block_row, block_col, live_count, new_owner, new_slot, row_local, me):
+    shard_count, slot_count = block_row.shape
+    total = shard_count * slot_count
+    ids = jnp.arange(total, dtype=i32)
+    live = (jnp.arange(slot_count)[None, :] < live_count[:, None]).reshape(total)
+    row = block_row.reshape(total)
+    col = block_col.reshape(total)
+    owner = jnp.where(live, new_owner.reshape(total), -1)
+    slot = new_slot.reshape(total)
+    kept = owner >= 0
+    row_shard = row // row_local
+    key = jnp.where(kept, ids, ids + total)
+    same = row_shard[:, None] == row_shard[None, :]
+    before = same & live[None, :] & (key[None, :] < key[:, None])
+    rank = jnp.sum(before.astype(i32), axis=1)
+    earlier = same & (owner[:, None] == owner[None, :]) & (ids[None, :] < ids[:, None])
+    pos = jnp.sum(earlier.astype(i32), axis=1)
+    fits = (jnp.max(jnp.where(live, rank, 0)) < CAP) & (jnp.max(jnp.where(kept, pos, 0)) < PAIR)
+
+    here = live & (row_shard == me)
+    words = ids + 256 * ((row - row_local * me) + 16 * col)
+    hit = here[None, :] & (rank[None, :] == jnp.arange(CAP)[:, None])
+    code = jnp.sum(jnp.where(hit, words[None, :], 0), axis=1)
+    counts = jnp.stack([jnp.sum(here.astype(i32)), jnp.sum((here & kept).astype(i32))])
+    counts = jnp.minimum(counts, CAP)
+    going = jnp.where(here & kept, owner * PAIR + pos, -1)
+    send_hit = going[None, :] == jnp.arange(shard_count * PAIR)[:, None]
+    send = jnp.minimum(jnp.sum(jnp.where(send_hit, rank[None, :], 0), axis=1), CAP - 1)
+    landing = 1 + row_shard * PAIR + jnp.minimum(pos, PAIR - 1) + shard_count * PAIR * ids
+    lands = (owner == me)[None, :] & (slot[None, :] == jnp.arange(slot_count)[:, None])
+    place = jnp.sum(jnp.where(lands, landing[None, :], 0), axis=1)
+    return fits, code, counts, send, place
+
+
+def grad_kernel(info, code, hidden, mine, other, out, cols, hidden_t, total):
+    my_core = info[2]
+    for zl in range(NZL):
+        for sub in range(4):
+            lanes = slice(sub * BS, (sub + 1) * BS)
+            cols[(2 * zl + my_core) * 4 + sub] = mine[zl, :, lanes]
+            cols[(2 * zl + 1 - my_core) * 4 + sub] = other[zl, :, lanes]
+    row_local = hidden.shape[1] // BS
+    for r in range(row_local):
+        hidden_t[r] = hidden[:, r * BS : (r + 1) * BS].T
+
+    def step(c, carry):
+        word = code[c]
+        r, col = (word >> 8) & 15, word >> 12
+        block = jnp.dot(hidden_t[r], cols[col], preferred_element_type=f32)
+        total[pl.ds(c, BS, stride=CAP), :] = block
+        return carry
+
+    lax.fori_loop(0, info[1], step, 0)
+    for x in range(NX):
+        for y in range(NY):
+            for q in range(4):
+                source = 16 * y + 4 * x + q
+                out[x, 4 * y + q] = total[source * CAP : (source + 1) * CAP, :].astype(bf16)
+
+
+def sum_kernel(parts, out):
+    def step(i, carry):
+        value = parts[0, i].astype(f32)
+        for n in range(1, parts.shape[0]):
+            value += parts[n, i].astype(f32)
+        out[i] = value.astype(bf16)
+        return carry
+
+    lax.fori_loop(0, out.shape[0], step, 0, unroll=4)
+
+
+def share_kernel(scale, send, parts, out, total):
+    for b in range(2):
+        value = parts[0, b].astype(f32)
+        for n in range(1, parts.shape[0]):
+            value += parts[n, b].astype(f32)
+        total[b] = value * scale
+    for d in range(out.shape[0]):
+        for p in range(PAIR):
+            rank = send[d * PAIR + p]
+            for b in range(2):
+                out[d, b, p : p + 1, :] = total[b, pl.ds(rank, 1), :]
+
+
+def select_kernel(info, code, gathered, out):
+    def step(c, carry):
+        out[c] = gathered[code[c] & 255]
+        return carry
+
+    lax.fori_loop(0, CAP, step, 0, unroll=4)
+
+
+def forward_kernel(info, code, hidden, w0, w1, w2, w3, mine, theirs, weights, total):
+    my_core, my_x = info[2], info[3]
+    total[...] = jnp.zeros_like(total)
+
+    def step(c, carry):
+        word = code[c]
+        r, col = (word >> 8) & 15, word >> 12
+        for k, part in enumerate((w0, w1, w2, w3)):
+            weights[c, (my_x + NX - k) % NX] = part[c]
+        w = weights[c].reshape(BS, BS)
+        h = hidden[:, pl.ds(pl.multiple_of(r * BS, BS), BS)]
+        total[col] += jnp.dot(h, w, preferred_element_type=f32)
+        return carry
+
+    lax.fori_loop(0, info[0], step, 0)
+    for zl in range(NZL):
+        for sub in range(4):
+            mine[zl, sub] = total[(2 * zl + my_core) * 4 + sub]
+            theirs[zl, sub] = total[(2 * zl + 1 - my_core) * 4 + sub]
+
+
+def backward_kernel(info, code, cols, weights, back, total):
+    total[...] = jnp.zeros_like(total)
+
+    def step(c, carry):
+        word = code[c]
+        r, col = (word >> 8) & 15, word >> 12
+        w = weights[c].reshape(BS, BS)
+        total[r] += lax.dot_general(cols[col], w, (((1,), (1,)), ((), ())), preferred_element_type=f32)
+        return carry
+
+    lax.fori_loop(0, info[0], step, 0)
+    for r in range(total.shape[0]):
+        back[:, r * BS : (r + 1) * BS] = total[r].astype(bf16)
+
+
+def chip_kernel(info, mine, came, own, s1, s2, s3):
+    my_zl = info[4]
+    own[...] = mine[my_zl] + came[my_zl]
+    for k, out in enumerate((s1, s2, s3)):
+        zl = (my_zl + k + 1) % NZL
+        out[...] = (mine[zl] + came[zl]).astype(bf16)
+
+
+def project_kernel(own, r1, r2, r3, out):
+    for sub in range(4):
+        value = own[sub] + r1[sub].astype(f32) + r2[sub].astype(f32) + r3[sub].astype(f32)
+        out[:, sub * BS : (sub + 1) * BS] = value.astype(bf16)
+
+
+def adam_kernel(place, state, shares, new_w, new_m, new_v, rows, grad):
+    slots, share = new_w.shape
+    share_rows = shares.shape[0] * PAIR
+    for j in range(slots):
+        word = jnp.maximum(place[j] - 1, 0)
+        g, row = word % share_rows, word // share_rows
+        filled = place[j] > 0
+        rows[pl.ds(j, 1), :] = jnp.where(filled, state[row // slots, pl.ds(row % slots, 1), :], 0.0)
+        for b in range(2):
+            value = shares[g // PAIR, b, pl.ds(g % PAIR, 1), :]
+            grad[pl.ds(j, 1), b * BS : (b + 1) * BS] = jnp.where(filled, value, 0.0)
+    w, m, v = adam_update(rows[:, :share], rows[:, share : 2 * share], rows[:, 2 * share :], grad[...])
+    new_w[...] = w
+    new_m[...] = m
+    new_v[...] = v
+
+
+def all_to_all(values, axis):
+    return lax.all_to_all(values, axis, split_axis=0, concat_axis=0, tiled=True)
+
+
+def shift(values, axis, count, step):
+    return lax.ppermute(values, axis, [(i, (i + step) % count) for i in range(count)])
+
+
+def shards(
+    hidden,
+    out_grad,
+    block_weight,
+    block_row,
+    block_col,
+    live_count,
+    new_owner,
+    new_slot,
+    first_moment,
+    second_moment,
+):
+    shard_count = lax.axis_size(SHARD)
+    me = lax.axis_index(SHARD)
+    dp_index = lax.axis_index(DP)
+    x_index = lax.axis_index("x")
+    tokens = hidden.shape[0]
+    slot_count = block_weight.shape[1]
+    row_local = hidden.shape[1] // BS
+    share = first_moment.shape[2]
+    scale = 1.0 / math.sqrt(tokens * lax.axis_size(DP))
+
+    mine = all_to_all(jnp.broadcast_to(out_grad[None], (NZL,) + out_grad.shape), "zl")
+    other = shift(mine, "core", 2, 1)
+    quarter = lax.dynamic_slice_in_dim(block_weight[0], x_index * (BS // NX), BS // NX, 1)
+    gathered = lax.all_gather(quarter, SHARD, axis=0, tiled=True)
+    weight_share = lax.dynamic_slice_in_dim(block_weight[0], dp_index * 2, 2, 1).reshape(slot_count, share)
+    stacked = jnp.concatenate([weight_share.astype(f32), first_moment[0], second_moment[0]], axis=1)
+    state = lax.all_gather(stacked, SHARD, axis=0)
+
+    fits, code, counts, send, place = make_plan(
+        block_row, block_col, live_count, new_owner, new_slot, row_local, me
+    )
+    info = jnp.concatenate([counts, jnp.stack([lax.axis_index("core"), x_index, lax.axis_index("zl")])])
+
+    partial, cols = call(
+        grad_kernel,
+        (like((NX, NY * NZH * 2, CAP, BS), bf16), like((shard_count * 4, BS, BS), bf16)),
+        2,
+        3,
+        [pltpu.VMEM((row_local, BS, BS), bf16), pltpu.VMEM((BS * CAP, BS), f32)],
+        flops=2 * CAP * BS**3,
+        byts=4 * 1024 * 1024,
+    )(info, code, hidden, mine, other)
+    along_x = all_to_all(partial, "x")
+    summed = call(sum_kernel, like(partial.shape[1:], bf16), 0, 1, byts=2 * 1024 * 1024)(along_x)
+    along_yz = all_to_all(summed.reshape(NY * NZH, 2, CAP, BS), ("y", "zh"))
+    shares = call(
+        functools.partial(share_kernel, scale),
+        like((shard_count, 2, PAIR, BS), f32),
+        1,
+        1,
+        [pltpu.VMEM((2, CAP, BS), f32)],
+        byts=1024 * 1024,
+    )(send, along_yz)
+    shares = all_to_all(shares, SHARD)
+
+    w0 = call(select_kernel, like((CAP, BS // NX, BS), bf16), 2, 1, byts=1024 * 1024)(info, code, gathered)
+    w1, w2, w3 = (shift(w0, "x", NX, k) for k in (1, 2, 3))
+
+    out_mine, out_theirs, weights = call(
+        forward_kernel,
+        (
+            like((NZL, 4, tokens, BS), f32),
+            like((NZL, 4, tokens, BS), f32),
+            like((CAP, NX, BS // NX, BS), bf16),
+        ),
+        2,
+        5,
+        [pltpu.VMEM((shard_count * 4, tokens, BS), f32)],
+        flops=2 * CAP * BS**3,
+        byts=8 * 1024 * 1024,
+    )(info, code, hidden, w0, w1, w2, w3)
+    came = shift(out_theirs, "core", 2, 1)
+    hidden_grad = call(
+        backward_kernel,
+        like(hidden.shape, bf16),
+        2,
+        2,
+        [pltpu.VMEM((row_local, tokens, BS), f32)],
+        flops=2 * CAP * BS**3,
+        byts=4 * 1024 * 1024,
+    )(info, code, cols, weights)
+    part = (4, tokens, BS)
+    own, s1, s2, s3 = call(
+        chip_kernel, (like(part, f32),) + (like(part, bf16),) * 3, 1, 2, byts=3 * 1024 * 1024
+    )(info, out_mine, came)
+    r1, r2, r3 = (shift(s, "zl", NZL, k + 1) for k, s in enumerate((s1, s2, s3)))
+    projected = call(project_kernel, like(out_grad.shape, bf16), 0, 4, byts=1024 * 1024)(own, r1, r2, r3)
+
+    shape = like((slot_count, share), f32)
+    new_weight, new_first, new_second = call(
+        adam_kernel,
+        (shape, shape, shape),
+        1,
+        2,
+        [pltpu.VMEM((slot_count, 3 * share), f32), pltpu.VMEM((slot_count, share), f32)],
+        byts=1024 * 1024,
+    )(place, state, shares)
+    result = (projected, hidden_grad, new_weight[None], new_first[None], new_second[None])
+    return lax.cond(
+        fits,
+        lambda: result,
+        lambda: general(
+            hidden,
+            out_grad,
+            block_weight,
+            block_row,
+            block_col,
+            live_count,
+            new_owner,
+            new_slot,
+            first_moment,
+            second_moment,
+        ),
+    )
+
+
 def solution(mesh):
+    split = Mesh(mesh.devices.reshape(NY, NX, NZH, NZL, 2), ("y", "x", "zh", "zl", "core"))
     in_specs = (
-        P("dp", "shard"),
-        P("dp", "shard"),
-        P("shard", None, None, None),
+        P(DP, SHARD),
+        P(DP, SHARD),
+        P(SHARD, None, None, None),
         P(),
         P(),
         P(),
         P(),
         P(),
-        P("shard", None, "dp"),
-        P("shard", None, "dp"),
+        P(SHARD, None, DP),
+        P(SHARD, None, DP),
     )
     out_specs = (
-        P("dp", "shard"),
-        P("dp", "shard"),
-        P("shard", None, "dp"),
-        P("shard", None, "dp"),
-        P("shard", None, "dp"),
-    )
-    return jax.shard_map(shards, mesh=mesh, in_specs=in_specs, out_specs=out_specs, check_vma=False)
+        P(DP, SHARD),
+        P(DP, SHARD),
+        P(SHARD, None, DP),
+        P(SHARD, None, DP),
+        P(SHARD, None, DP),
+    )
+    return jax.shard_map(shards, mesh=split, in_specs=in_specs, out_specs=out_specs, check_vma=False)

time: 834 us -> 163 us (0.20)
  waiting for transfers between devices: 567 us -> 18.3 us
  local copies, waits for them, and re-layouts: 80.7 us -> 16.7 us
  other arithmetic: 59.6 us -> 8.41 us
  matrix products: 36.7 us -> 0 us
  Pallas kernels: 0 us -> 23.6 us
  blocking collectives: 0 us -> 17.1 us
  loops' own time: 16 us -> 0.23 us
    reduce_scatter x1 -> x0, waiting for transfers between devices: 393 us -> none  [shards(): lax.psum_scatter(blocks.reshape(slot_count, block_size * block_size), 'dp...]
    all_gather x3 -> x1, waiting for transfers between devices: 169 us -> 8.71 us  [shards(): gathered = lax.all_gather(quarter, SHARD, axis=0, tiled=True)]
    gather x22 -> x0, local copies, waits for them, and re-layouts: 58.3 us -> none  [the longest x8 29.7 us: one_shard(): hidden_part = jnp.take(hidden_blocks, row_ids, axis=1)]
    scatter-add x16 -> x0, other arithmetic: 42.5 us -> none  [the longest x8 21.2 us: one_shard(): out_total = totals[0].at[:, col_place].add(forward, mode='drop')]
    dot_general x17 -> x0, matrix products: 36.7 us -> none  [the longest x8 19.6 us: one_shard(): jnp.einsum('tkc,krc->tkr', grad_part, weights, preferred_element_type=jnp...]
    ppermute x0 -> x8, starting transfers between devices: none -> 31 us  [shift(): lax.ppermute(values, axis, [(i, (i + step) % count) for i in range(count)])]
    all_to_all x1 -> x4, starting transfers between devices: 55.6 us -> 29.7 us  [all_to_all(): return lax.all_to_all(values, axis, split_axis=0, concat_axis=0, tiled=True)]
    pallas_call x0 -> x9, Pallas kernels: none -> 23.6 us  [the longest x1 5.84 us: shards(): call(grad_kernel, (like((NX, NY * NZH * 2, CAP, BS), bf16), like((shard_c...]
  transfers between devices with their start and end apart: 5 -> 13, of which waited for: 5 -> 3; matrix products, arithmetic and copies ran while one was open for 2% -> 7% of each run, Pallas kernels for 0% -> 15%
where the time goes in v2:
time: 163 us; the launch traced here: 161 us
  starting transfers between devices  60.7 us (37%)
  Pallas kernels  23.6 us (14%)
  waiting for transfers between devices  18.3 us (11%)
  blocking collectives  17.1 us (10%)
  local copies, waits for them, and re-layouts  16.7 us (10%)
  between operations  15.7 us (10%)
  other arithmetic  8.41 us (5%)
    ppermute x8, starting transfers between devices, shift(): lax.ppermute(values, axis, [(i, (i + step) % count) for i in range(count)])  31 us
    all_to_all x4, starting transfers between devices, all_to_all(): return lax.all_to_all(values, axis, split_axis=0, concat_axis=0, tiled=True)  29.7 us
    all_gather x1, blocking collectives, shards(): state = lax.all_gather(stacked, SHARD, axis=0)  17.1 us
    unnamed x47, local copies, waits for them, and re-layouts  11.4 us
    all_to_all x4, waiting for transfers between devices, all_to_all(): return lax.all_to_all(values, axis, split_axis=0, concat_axis=0, tiled=True)  9.46 us
    all_gather x1, waiting for transfers between devices, shards(): gathered = lax.all_gather(quarter, SHARD, axis=0, tiled=True)  8.71 us
    pallas_call x1, Pallas kernels, shards(): call(grad_kernel, (like((NX, NY * NZH * 2, CAP, BS), bf16), like((shard_c...  5.84 us
    pallas_call x1, Pallas kernels, shards(): call(forward_kernel, (like((NZL, 4, tokens, BS), f32), like((NZL, 4, toke...  5.81 us
  transfers between devices with their start and end apart: 13, of which 3 were waited for; matrix products, arithmetic and copies ran while one was open for 7% of the time, Pallas kernels for 15%

profile of v2, /device:TPU:1, one launch (start us, length us, event | category | flops | bytes accessed | tf_op | source)
XLA Modules:
  0.0 160.8 jit_solution(18336311505492367603)
XLA Ops:
  7.3 1.7 %constant_dynamic-slice_fusion.9 = bf16[1,32,32,128]{3,2,0,1:T(8,128)(2,1)} fusion(bf16[1,32,128,128]{3,2,0,1:T(8,128)(2,1)} %bitcast.132, s32[]{:T(128)S(6)} %select_n.289), kind=kLoop, calls=%fused_computation.163 | loop fusion | bytes 524292 | tf_op jit(solution)/shard_map/dynamic_slice | solution.py:406
  9.0 1.8 %broadcast_in_dim.266 = bf16[4,128,512]{2,1,0:T(8,128)(2,1)} broadcast(bf16[128,512]{1,0:T(8,128)(2,1)} %param.19), dimensions={1,2} | broadcast | bytes 655360 | tf_op jit(solution)/shard_map/broadcast_in_dim | solution.py:404
  10.8 7.8 %all-to-all-start.1 = ((bf16[4,128,512]{2,1,0:T(8,128)(2,1)}), bf16[4,128,512]{2,1,0:T(8,128)(2,1)S(1)}, u32[]{:S(2)}, u32[]{:S(2)}) async-start(bf16[4,128,512]{2,1,0:T(8,128)(2,1)} %broadcast_in_dim.266), calls=%async_computation.2 | async-start | bytes 1048576 | tf_op jit(solution)/shard_map/all_to_all | solution.py:375
  20.8 1.4 add_minimum_fusion
  22.3 9.5 %all-to-all-done.1.mine = bf16[4,128,512]{2,1,0:T(8,128)(2,1)S(1)} async-done(((bf16[4,128,512]{2,1,0:T(8,128)(2,1)}), bf16[4,128,512]{2,1,0:T(8,128)(2,1)S(1)}, u32[]{:S(2)}, u32[]{:S(2)}) %all-to-all-start.1) | async-done | bytes 524320 | tf_op jit(solution)/shard_map/all_to_all | solution.py:375
  31.7 4.3 %collective-permute-start = (bf16[4,128,512]{2,1,0:T(8,128)(2,1)S(1)}, bf16[4,128,512]{2,1,0:T(8,128)(2,1)S(1)}, u32[]{:S(2)}, u32[]{:S(2)}) collective-permute-start(bf16[4,128,512]{2,1,0:T(8,128)(2,1)S(1)} %all-to-all-done.1.mine), channel_id=1, source_target_pairs={{0,1},{1,0},{2,3},{3,2},{4,5},{5,4},{6,7},{7,6},{8,9},{9,8},{10,11... | collective-permute-start | bytes 1572872 | tf_op jit(solution)/shard_map/ppermute | solution.py:379
  36.0 1.3 and_select_fusion.2
  37.5 5.8 %shard_map.147 = (bf16[4,32,48,128]{3,2,1,0:T(8,128)(2,1)}, bf16[32,128,128]{2,1,0:T(8,128)(2,1)S(1)}) custom-call(s32[5]{0:T(128)S(1)} %pad_add_fusion.info, s32[48]{0:T(128)S(1)} %select_reduce_fusion.4.code, bf16[128,1792]{1,0:T(8,128)(2,1)S(1)} %copy-done.14, bf16[4,128,512]{2,1,0:T(8,128)(2,1)S(1)} %all-to-all-done.1.mine, ...), custom_call_target="tpu_custom_call" | custom-call | flops 201326592 | bytes 4194304 | tf_op jit(solution)/shard_map/pallas_call | solution.py:417
  44.3 4.0 %all-to-all-start.2 = ((bf16[4,32,48,128]{3,2,1,0:T(8,128)(2,1)}), bf16[4,32,48,128]{3,2,1,0:T(8,128)(2,1)S(1)}, u32[]{:S(2)}, u32[]{:S(2)}) async-start(bf16[4,32,48,128]{3,2,1,0:T(8,128)(2,1)} %get-tuple-element.205), calls=%async_computation.3 | async-start | bytes 3145728 | tf_op jit(solution)/shard_map/all_to_all | solution.py:375
  48.4 8.7 %all-gather.13.cloned.1.call-done = bf16[1,256,32,128]{3,2,0,1:T(8,128)(2,1)} async-done(((bf16[1,32,32,128]{3,2,0,1:T(8,128)(2,1)}), bf16[1,256,32,128]{3,2,0,1:T(8,128)(2,1)}) %all-gather.13.cloned.1.call-update) | async-done | bytes 2097168 | tf_op jit(solution)/shard_map/all_gather | solution.py:407
  57.1 1.6 copy-done
  59.3 3.1 %collective-permute-start.1 = (bf16[48,32,128]{2,1,0:T(8,128)(2,1)S(1)}, bf16[48,32,128]{2,1,0:T(8,128)(2,1)S(1)}, u32[]{:S(2)}, u32[]{:S(2)}) collective-permute-start(bf16[48,32,128]{2,1,0:T(8,128)(2,1)S(1)} %shard_map.151.w0), channel_id=1, source_target_pairs={{0,16},{16,32},{32,48},{48,0},{1,17},{17,33},{33,49},{49,1},{2,18}... | collective-permute-start | bytes 1179656 | tf_op jit(solution)/shard_map/ppermute | solution.py:379
  62.5 4.4 %collective-permute-start.2 = (bf16[48,32,128]{2,1,0:T(8,128)(2,1)S(1)}, bf16[48,32,128]{2,1,0:T(8,128)(2,1)S(1)}, u32[]{:S(2)}, u32[]{:S(2)}) collective-permute-start(bf16[48,32,128]{2,1,0:T(8,128)(2,1)S(1)} %shard_map.151.w0), channel_id=1, source_target_pairs={{0,32},{16,48},{32,0},{48,16},{1,33},{17,49},{33,1},{49,17},{2,34}... | collective-permute-start | bytes 1179656 | tf_op jit(solution)/shard_map/ppermute | solution.py:379
  66.8 3.0 %collective-permute-start.3 = (bf16[48,32,128]{2,1,0:T(8,128)(2,1)S(1)}, bf16[48,32,128]{2,1,0:T(8,128)(2,1)S(1)}, u32[]{:S(2)}, u32[]{:S(2)}) collective-permute-start(bf16[48,32,128]{2,1,0:T(8,128)(2,1)S(1)} %shard_map.151.w0), channel_id=1, source_target_pairs={{0,48},{16,0},{32,16},{48,32},{1,49},{17,1},{33,17},{49,33},{2,50}... | collective-permute-start | bytes 1179656 | tf_op jit(solution)/shard_map/ppermute | solution.py:379
  70.9 14.6 %all-to-all-start.3 = ((bf16[16,2,48,128]{3,2,1,0:T(8,128)(2,1)}), bf16[16,2,48,128]{3,2,1,0:T(8,128)(2,1)S(1)}, u32[]{:S(2)}, u32[]{:S(2)}) async-start(bf16[16,2,48,128]{3,2,1,0:T(8,128)(2,1)} %bitcast.45), calls=%async_computation.4 | async-start | bytes 786432 | tf_op jit(solution)/shard_map/all_to_all | solution.py:375
  87.7 1.0 copy-done.6
  88.7 1.0 copy-done.8
  89.7 1.0 copy-done.10
  90.7 5.8 %shard_map.152 = (f32[4,4,128,128]{3,2,1,0:T(8,128)S(1)}, f32[4,4,128,128]{3,2,1,0:T(8,128)}, bf16[48,4,32,128]{3,2,1,0:T(8,128)(2,1)S(1)}) custom-call(s32[5]{0:T(128)S(1)} %pad_add_fusion.info, s32[48]{0:T(128)S(1)} %select_reduce_fusion.4.code, bf16[128,1792]{1,0:T(8,128)(2,1)} %hidden.3, bf16[48,32,128]{2,1,0:T(8,128)(2,1)S(1)} %shard_map.151.w0, ...), custom_call_target="tpu_custom_call" | custom-call | flops 201326592 | bytes 8388608 | tf_op jit(solution)/shard_map/pallas_call | solution.py:442
  97.5 7.1 %collective-permute-start.4 = (f32[4,4,128,128]{3,2,1,0:T(8,128)}, f32[4,4,128,128]{3,2,1,0:T(8,128)}, u32[]{:S(2)}, u32[]{:S(2)}) collective-permute-start(f32[4,4,128,128]{3,2,1,0:T(8,128)} %get-tuple-element.210), channel_id=1, source_target_pairs={{0,1},{1,0},{2,3},{3,2},{4,5},{5,4},{6,7},{7,6},{8,9},{9,8},{10,11... | collective-permute-start | bytes 3145736 | tf_op jit(solution)/shard_map/ppermute | solution.py:379
  105.5 1.4 pad_maximum_fusion.1
  107.7 1.4 shard_map.149
  109.1 3.3 %all-to-all-start.4 = ((f32[8,2,16,128]{3,2,1,0:T(8,128)}), f32[8,2,16,128]{3,2,1,0:T(8,128)S(1)}, u32[]{:S(2)}, u32[]{:S(2)}) async-start(f32[8,2,16,128]{3,2,1,0:T(8,128)} %shard_map.149), calls=%async_computation.5 | async-start | bytes 262144 | tf_op jit(solution)/shard_map/all_to_all | solution.py:375
  112.4 17.1 %all-gather = f32[256,768]{1,0:T(8,128)S(1)} all-gather(f32[32,768]{1,0:T(8,128)} %pad_maximum_fusion.1), channel_id=2, replica_groups=mesh['y'=8,'x'=4,'zh'=2,'zl'=4,'core'=2] {'zl','core'}, dimensions={0}, use_global_device_ids=true | all-gather | bytes 884736 | tf_op jit(solution)/shard_map/all_gather | solution.py:410
  129.5 1.3 eq.171
  132.2 2.1 %shard_map.153 = (f32[4,128,128]{2,1,0:T(8,128)S(1)}, bf16[4,128,128]{2,1,0:T(8,128)(2,1)}, bf16[4,128,128]{2,1,0:T(8,128)(2,1)}, bf16[4,128,128]{2,1,0:T(8,128)(2,1)}) custom-call(s32[5]{0:T(128)S(1)} %pad_add_fusion.info, f32[4,4,128,128]{3,2,1,0:T(8,128)S(1)} %copy-done.2, f32[4,4,128,128]{3,2,1,0:T(8,128)} %collective-permute-done.4.came), custom_call_target="tpu_custom_call" | custom-call | bytes 3145728 | tf_op jit(solution)/shard_map/pallas_call | solution.py:466
  134.9 2.4 %collective-permute-start.5 = (bf16[4,128,128]{2,1,0:T(8,128)(2,1)}, bf16[4,128,128]{2,1,0:T(8,128)(2,1)S(1)}, u32[]{:S(2)}, u32[]{:S(2)}) collective-permute-start(bf16[4,128,128]{2,1,0:T(8,128)(2,1)} %get-tuple-element.212), channel_id=1, source_target_pairs={{0,2},{2,4},{4,6},{6,0},{1,3},{3,5},{5,7},{7,1},{8,10},{10,12},{12... | collective-permute-start | bytes 393224 | tf_op jit(solution)/shard_map/ppermute | solution.py:379
  137.4 4.1 %collective-permute-start.6 = (bf16[4,128,128]{2,1,0:T(8,128)(2,1)}, bf16[4,128,128]{2,1,0:T(8,128)(2,1)S(1)}, u32[]{:S(2)}, u32[]{:S(2)}) collective-permute-start(bf16[4,128,128]{2,1,0:T(8,128)(2,1)} %get-tuple-element.213), channel_id=1, source_target_pairs={{0,4},{2,6},{4,0},{6,2},{1,5},{3,7},{5,1},{7,3},{8,12},{10,14},{12... | collective-permute-start | bytes 393224 | tf_op jit(solution)/shard_map/ppermute | solution.py:379
  141.5 2.6 %collective-permute-start.7 = (bf16[4,128,128]{2,1,0:T(8,128)(2,1)}, bf16[4,128,128]{2,1,0:T(8,128)(2,1)S(1)}, u32[]{:S(2)}, u32[]{:S(2)}) collective-permute-start(bf16[4,128,128]{2,1,0:T(8,128)(2,1)} %get-tuple-element.214), channel_id=1, source_target_pairs={{0,6},{2,0},{4,2},{6,4},{1,7},{3,1},{5,3},{7,5},{8,14},{10,8},{12,... | collective-permute-start | bytes 393224 | tf_op jit(solution)/shard_map/ppermute | solution.py:379
  144.9 1.7 %shard_map.150 = (f32[32,256]{1,0:T(8,128)}, f32[32,256]{1,0:T(8,128)}, f32[32,256]{1,0:T(8,128)}) custom-call(s32[32]{0:T(128)S(1)} %select_reduce_fusion.5.place, f32[8,32,768]{2,1,0:T(8,128)S(1)} %bitcast.129, f32[8,2,16,128]{3,2,1,0:T(8,128)S(1)} %all-to-all-done.4.shares), custom_call_target="tpu_custom_call" | custom-call | bytes 1048576 | tf_op jit(solution)/shard_map/pallas_call | solution.py:473
  146.6 1.2 copy-done.4
  147.8 5.1 %shard_map.155 = bf16[128,1792]{1,0:T(8,128)(2,1)} custom-call(s32[5]{0:T(128)S(1)} %pad_add_fusion.info, s32[48]{0:T(128)S(1)} %select_reduce_fusion.4.code, bf16[32,128,128]{2,1,0:T(8,128)(2,1)S(1)} %copy-done.4, bf16[48,4,32,128]{3,2,1,0:T(8,128)(2,1)S(1)} %get-tuple-element.216.weights), custom_call_target="tpu_custom_call" | custom-call | flops 201326592 | bytes 4194304 | tf_op jit(solution)/shard_map/pallas_call | solution.py:456
  (78 shorter events, 12.6 us)
Async XLA Ops:
  7.2 11.4 %copy-start.19 = (s32[8,32]{1,0:T(8,128)S(1)}, s32[8,32]{1,0:T(8,128)}, u32[]{:S(2)}) copy-start(s32[8,32]{1,0:T(8,128)} %param.24) | copy-start | bytes 3076
  7.2 11.5 %copy-start.20 = (s32[8,32]{1,0:T(8,128)S(1)}, s32[8,32]{1,0:T(8,128)}, u32[]{:S(2)}) copy-start(s32[8,32]{1,0:T(8,128)} %param.21) | copy-start | bytes 3076
  7.2 11.5 %copy-start.25 = (s32[8]{0:T(128)S(1)}, s32[8]{0:T(128)}, u32[]{:S(2)}) copy-start(s32[8]{0:T(128)} %param.23) | copy-start | bytes 100
  7.2 11.6 %copy-start.21 = (s32[8,32]{1,0:T(8,128)S(1)}, s32[8,32]{1,0:T(8,128)}, u32[]{:S(2)}) copy-start(s32[8,32]{1,0:T(8,128)} %param.22) | copy-start | bytes 3076
  7.2 30.3 %copy-start.14 = (bf16[128,1792]{1,0:T(8,128)(2,1)S(1)}, bf16[128,1792]{1,0:T(8,128)(2,1)}, u32[]{:S(2)}) copy-start(bf16[128,1792]{1,0:T(8,128)(2,1)} %hidden.3) | copy-start | bytes 1376260
  7.2 49.8 %all-gather.13.cloned.1.call-start = ((), (), s32[]{:S(2)}) async-start(), calls=%async_computation.10 | async-start | bytes 2359296 | tf_op jit(solution)/shard_map/all_gather | solution.py:407
  10.8 20.9 %all-to-all-start.1 = ((bf16[4,128,512]{2,1,0:T(8,128)(2,1)}), bf16[4,128,512]{2,1,0:T(8,128)(2,1)S(1)}, u32[]{:S(2)}, u32[]{:S(2)}) async-start(bf16[4,128,512]{2,1,0:T(8,128)(2,1)} %broadcast_in_dim.266), calls=%async_computation.2 | async-start | bytes 1048576 | tf_op jit(solution)/shard_map/all_to_all | solution.py:375
  19.9 24.5 %copy-start.23 = (s32[256]{0:T(256)}, s32[256]{0:T(256)S(1)}, u32[]{:S(2)}) copy-start(s32[256]{0:T(256)S(1)} %get-tuple-element.333) | copy-start | bytes 3076
  31.7 5.8 %collective-permute-start = (bf16[4,128,512]{2,1,0:T(8,128)(2,1)S(1)}, bf16[4,128,512]{2,1,0:T(8,128)(2,1)S(1)}, u32[]{:S(2)}, u32[]{:S(2)}) collective-permute-start(bf16[4,128,512]{2,1,0:T(8,128)(2,1)S(1)} %all-to-all-done.1.mine), channel_id=1, source_target_pairs={{0,1},{1,0},{2,3},{3,2},{4,5},{5,4},{6,7},{7,6},{8,9},{9,8},{10,11... | collective-permute-start | bytes 1572872 | tf_op jit(solution)/shard_map/ppermute | solution.py:379
  43.4 1.0 copy-start.3
  44.3 25.6 %all-to-all-start.2 = ((bf16[4,32,48,128]{3,2,1,0:T(8,128)(2,1)}), bf16[4,32,48,128]{3,2,1,0:T(8,128)(2,1)S(1)}, u32[]{:S(2)}, u32[]{:S(2)}) async-start(bf16[4,32,48,128]{3,2,1,0:T(8,128)(2,1)} %get-tuple-element.205), calls=%async_computation.3 | async-start | bytes 3145728 | tf_op jit(solution)/shard_map/all_to_all | solution.py:375
  57.1 1.6 copy-start
  59.3 26.1 %collective-permute-start.1 = (bf16[48,32,128]{2,1,0:T(8,128)(2,1)S(1)}, bf16[48,32,128]{2,1,0:T(8,128)(2,1)S(1)}, u32[]{:S(2)}, u32[]{:S(2)}) collective-permute-start(bf16[48,32,128]{2,1,0:T(8,128)(2,1)S(1)} %shard_map.151.w0), channel_id=1, source_target_pairs={{0,16},{16,32},{32,48},{48,0},{1,17},{17,33},{33,49},{49,1},{2,18}... | collective-permute-start | bytes 1179656 | tf_op jit(solution)/shard_map/ppermute | solution.py:379
  62.5 23.8 %collective-permute-start.2 = (bf16[48,32,128]{2,1,0:T(8,128)(2,1)S(1)}, bf16[48,32,128]{2,1,0:T(8,128)(2,1)S(1)}, u32[]{:S(2)}, u32[]{:S(2)}) collective-permute-start(bf16[48,32,128]{2,1,0:T(8,128)(2,1)S(1)} %shard_map.151.w0), channel_id=1, source_target_pairs={{0,32},{16,48},{32,0},{48,16},{1,33},{17,49},{33,1},{49,17},{2,34}... | collective-permute-start | bytes 1179656 | tf_op jit(solution)/shard_map/ppermute | solution.py:379
  66.8 20.1 %collective-permute-start.3 = (bf16[48,32,128]{2,1,0:T(8,128)(2,1)S(1)}, bf16[48,32,128]{2,1,0:T(8,128)(2,1)S(1)}, u32[]{:S(2)}, u32[]{:S(2)}) collective-permute-start(bf16[48,32,128]{2,1,0:T(8,128)(2,1)S(1)} %shard_map.151.w0), channel_id=1, source_target_pairs={{0,48},{16,0},{32,16},{48,32},{1,49},{17,1},{33,17},{49,33},{2,50}... | collective-permute-start | bytes 1179656 | tf_op jit(solution)/shard_map/ppermute | solution.py:379
  70.9 36.8 %all-to-all-start.3 = ((bf16[16,2,48,128]{3,2,1,0:T(8,128)(2,1)}), bf16[16,2,48,128]{3,2,1,0:T(8,128)(2,1)S(1)}, u32[]{:S(2)}, u32[]{:S(2)}) async-start(bf16[16,2,48,128]{3,2,1,0:T(8,128)(2,1)} %bitcast.45), calls=%async_computation.4 | async-start | bytes 786432 | tf_op jit(solution)/shard_map/all_to_all | solution.py:375
  87.0 0.8 copy-start.9
  87.7 1.0 copy-start.6
  88.7 1.0 copy-start.8
  89.7 1.0 copy-start.10
  96.5 1.0 copy-start.1
  97.5 34.6 %copy-start.2 = (f32[4,4,128,128]{3,2,1,0:T(8,128)S(1)}, f32[4,4,128,128]{3,2,1,0:T(8,128)}, u32[]{:S(2)}) copy-start(f32[4,4,128,128]{3,2,1,0:T(8,128)} %copy-done.1) | copy-start | bytes 3145732
  97.5 34.6 %collective-permute-start.4 = (f32[4,4,128,128]{3,2,1,0:T(8,128)}, f32[4,4,128,128]{3,2,1,0:T(8,128)}, u32[]{:S(2)}, u32[]{:S(2)}) collective-permute-start(f32[4,4,128,128]{3,2,1,0:T(8,128)} %get-tuple-element.210), channel_id=1, source_target_pairs={{0,1},{1,0},{2,3},{3,2},{4,5},{5,4},{6,7},{7,6},{8,9},{9,8},{10,11... | collective-permute-start | bytes 3145736 | tf_op jit(solution)/shard_map/ppermute | solution.py:379
  109.1 35.8 %all-to-all-start.4 = ((f32[8,2,16,128]{3,2,1,0:T(8,128)}), f32[8,2,16,128]{3,2,1,0:T(8,128)S(1)}, u32[]{:S(2)}, u32[]{:S(2)}) async-start(f32[8,2,16,128]{3,2,1,0:T(8,128)} %shard_map.149), calls=%async_computation.5 | async-start | bytes 262144 | tf_op jit(solution)/shard_map/all_to_all | solution.py:375
  132.1 11.9 %copy-start.24 = (s32[256]{0:T(256)S(1)}, s32[256]{0:T(256)}, u32[]{:S(2)}) copy-start(s32[256]{0:T(256)} %eq.171) | copy-start | bytes 3076
  134.9 18.1 %copy-start.12 = (f32[4,128,128]{2,1,0:T(8,128)S(1)}, f32[4,128,128]{2,1,0:T(8,128)}, u32[]{:S(2)}) copy-start(f32[4,128,128]{2,1,0:T(8,128)} %copy-done.11) | copy-start | bytes 786436
  134.9 18.0 %collective-permute-start.5 = (bf16[4,128,128]{2,1,0:T(8,128)(2,1)}, bf16[4,128,128]{2,1,0:T(8,128)(2,1)S(1)}, u32[]{:S(2)}, u32[]{:S(2)}) collective-permute-start(bf16[4,128,128]{2,1,0:T(8,128)(2,1)} %get-tuple-element.212), channel_id=1, source_target_pairs={{0,2},{2,4},{4,6},{6,0},{1,3},{3,5},{5,7},{7,1},{8,10},{10,12},{12... | collective-permute-start | bytes 393224 | tf_op jit(solution)/shard_map/ppermute | solution.py:379
  137.4 15.6 %collective-permute-start.6 = (bf16[4,128,128]{2,1,0:T(8,128)(2,1)}, bf16[4,128,128]{2,1,0:T(8,128)(2,1)S(1)}, u32[]{:S(2)}, u32[]{:S(2)}) collective-permute-start(bf16[4,128,128]{2,1,0:T(8,128)(2,1)} %get-tuple-element.213), channel_id=1, source_target_pairs={{0,4},{2,6},{4,0},{6,2},{1,5},{3,7},{5,1},{7,3},{8,12},{10,14},{12... | collective-permute-start | bytes 393224 | tf_op jit(solution)/shard_map/ppermute | solution.py:379
  141.5 11.5 %collective-permute-start.7 = (bf16[4,128,128]{2,1,0:T(8,128)(2,1)}, bf16[4,128,128]{2,1,0:T(8,128)(2,1)S(1)}, u32[]{:S(2)}, u32[]{:S(2)}) collective-permute-start(bf16[4,128,128]{2,1,0:T(8,128)(2,1)} %get-tuple-element.214), channel_id=1, source_target_pairs={{0,6},{2,0},{4,2},{6,4},{1,7},{3,1},{5,3},{7,5},{8,14},{10,8},{12,... | collective-permute-start | bytes 393224 | tf_op jit(solution)/shard_map/ppermute | solution.py:379
  144.9 8.2 %copy-start.15 = (bf16[128,512]{1,0:T(8,128)(2,1)S(1)}, bf16[128,512]{1,0:T(8,128)(2,1)}, u32[]{:S(2)}) copy-start(bf16[128,512]{1,0:T(8,128)(2,1)} %param.19) | copy-start | bytes 393220
  146.6 6.5 %copy-start.26 = (s32[8]{0:T(128)S(1)}, s32[8]{0:T(128)}, u32[]{:S(2)}) copy-start(s32[8]{0:T(128)} %param.23) | copy-start | bytes 100
  146.6 1.2 copy-start.4
  (4 other events, 2.8 us)
Sparse Core Ops, SparseCore 0:
  10.9 46.1 all-gather.12

commit v3 on v2

--- a/solution.py
+++ b/solution.py
@@ -184,11 +184,13 @@
     return (projected, hidden_grad, new_weight[None], new_first[None], new_second[None])
 
 
-CAP = 48
-PAIR = 16
+WCAP = 44
+GCAP = 40
+PAIR = 14
+UNROLL = 4
 NX, NY, NZH, NZL = 4, 8, 2, 4
 BS = 128
-VMEM_LIMIT = 40 * 1024 * 1024
+VMEM_LIMIT = 14 * 1024 * 1024
 f32 = jnp.float32
 bf16 = jnp.bfloat16
 i32 = jnp.int32
@@ -229,21 +231,32 @@
     rank = jnp.sum(before.astype(i32), axis=1)
     earlier = same & (owner[:, None] == owner[None, :]) & (ids[None, :] < ids[:, None])
     pos = jnp.sum(earlier.astype(i32), axis=1)
-    fits = (jnp.max(jnp.where(live, rank, 0)) < CAP) & (jnp.max(jnp.where(kept, pos, 0)) < PAIR)
+    fits = (
+        (jnp.max(jnp.where(live, rank, 0)) < WCAP)
+        & (jnp.max(jnp.where(kept, rank, 0)) < GCAP)
+        & (jnp.max(jnp.where(kept, pos, 0)) < PAIR)
+    )
 
     here = live & (row_shard == me)
     words = ids + 256 * ((row - row_local * me) + 16 * col)
-    hit = here[None, :] & (rank[None, :] == jnp.arange(CAP)[:, None])
+    hit = here[None, :] & (rank[None, :] == jnp.arange(WCAP)[:, None])
     code = jnp.sum(jnp.where(hit, words[None, :], 0), axis=1)
-    counts = jnp.stack([jnp.sum(here.astype(i32)), jnp.sum((here & kept).astype(i32))])
-    counts = jnp.minimum(counts, CAP)
+    counts = [jnp.minimum(jnp.sum(here.astype(i32)), WCAP), jnp.minimum(jnp.sum((here & kept).astype(i32)), GCAP)]
     going = jnp.where(here & kept, owner * PAIR + pos, -1)
     send_hit = going[None, :] == jnp.arange(shard_count * PAIR)[:, None]
-    send = jnp.minimum(jnp.sum(jnp.where(send_hit, rank[None, :], 0), axis=1), CAP - 1)
-    landing = 1 + row_shard * PAIR + jnp.minimum(pos, PAIR - 1) + shard_count * PAIR * ids
+    send = jnp.minimum(jnp.sum(jnp.where(send_hit, rank[None, :], 0), axis=1), GCAP - 1)
+    owner2 = owner.reshape(shard_count, slot_count)
+    sources = jnp.arange(shard_count, dtype=i32)[:, None]
+    slots = jnp.arange(slot_count, dtype=i32)[None, :]
+    moving, positions = send_positions(owner2, shard_count, slot_count)
+    target = jnp.where(moving & (sources == me), owner2 * MV + positions, -1).reshape(total)
+    state_hit = target[None, :] == jnp.arange(shard_count * MV)[:, None]
+    state_send = jnp.sum(jnp.where(state_hit, (ids % slot_count)[None, :], 0), axis=1)
+    state_row = jnp.where(sources == me, slots, slot_count + sources * MV + positions).reshape(total)
+    landing = 1 + row_shard * PAIR + jnp.minimum(pos, PAIR - 1) + shard_count * PAIR * state_row
     lands = (owner == me)[None, :] & (slot[None, :] == jnp.arange(slot_count)[:, None])
     place = jnp.sum(jnp.where(lands, landing[None, :], 0), axis=1)
-    return fits, code, counts, send, place
+    return fits, code, counts, send, state_send, place
 
 
 def grad_kernel(info, code, hidden, mine, other, out, cols, hidden_t, total):
@@ -257,19 +270,21 @@
     for r in range(row_local):
         hidden_t[r] = hidden[:, r * BS : (r + 1) * BS].T
 
-    def step(c, carry):
-        word = code[c]
-        r, col = (word >> 8) & 15, word >> 12
-        block = jnp.dot(hidden_t[r], cols[col], preferred_element_type=f32)
-        total[pl.ds(c, BS, stride=CAP), :] = block
+    def step(i, carry):
+        blocks = []
+        for u in range(UNROLL):
+            word = code[i * UNROLL + u]
+            blocks.append(jnp.dot(hidden_t[(word >> 8) & 15], cols[word >> 12], preferred_element_type=f32))
+        for u in range(UNROLL):
+            total[pl.ds(i * UNROLL + u, BS, stride=GCAP), :] = blocks[u]
         return carry
 
-    lax.fori_loop(0, info[1], step, 0)
+    lax.fori_loop(0, (info[1] + UNROLL - 1) // UNROLL, step, 0)
     for x in range(NX):
         for y in range(NY):
             for q in range(4):
                 source = 16 * y + 4 * x + q
-                out[x, 4 * y + q] = total[source * CAP : (source + 1) * CAP, :].astype(bf16)
+                out[x, 4 * y + q] = total[source * GCAP : (source + 1) * GCAP, :].astype(bf16)
 
 
 def sum_kernel(parts, out):
@@ -283,42 +298,53 @@
     lax.fori_loop(0, out.shape[0], step, 0, unroll=4)
 
 
-def share_kernel(scale, send, parts, out, total):
+def share_kernel(scale, send, state_send, parts, stacked, out, total):
     for b in range(2):
         value = parts[0, b].astype(f32)
         for n in range(1, parts.shape[0]):
             value += parts[n, b].astype(f32)
         total[b] = value * scale
+    width = stacked.shape[1] // BS
     for d in range(out.shape[0]):
         for p in range(PAIR):
             rank = send[d * PAIR + p]
             for b in range(2):
-                out[d, b, p : p + 1, :] = total[b, pl.ds(rank, 1), :]
+                out[d, 2 * p + b : 2 * p + b + 1, :] = total[b, pl.ds(rank, 1), :]
+        for p in range(MV):
+            row = stacked[pl.ds(state_send[d * MV + p], 1), :]
+            for n in range(width):
+                at = 2 * PAIR + width * p + n
+                out[d, at : at + 1, :] = row[:, n * BS : (n + 1) * BS]
 
 
 def select_kernel(info, code, gathered, out):
     def step(c, carry):
-        out[c] = gathered[code[c] & 255]
+        value = gathered[code[c] & 255]
+        out[c] = jnp.where(c < info[0], value, jnp.zeros_like(value))
         return carry
 
-    lax.fori_loop(0, CAP, step, 0, unroll=4)
+    lax.fori_loop(0, WCAP, step, 0, unroll=4)
 
 
 def forward_kernel(info, code, hidden, w0, w1, w2, w3, mine, theirs, weights, total):
     my_core, my_x = info[2], info[3]
     total[...] = jnp.zeros_like(total)
 
-    def step(c, carry):
-        word = code[c]
-        r, col = (word >> 8) & 15, word >> 12
-        for k, part in enumerate((w0, w1, w2, w3)):
-            weights[c, (my_x + NX - k) % NX] = part[c]
-        w = weights[c].reshape(BS, BS)
-        h = hidden[:, pl.ds(pl.multiple_of(r * BS, BS), BS)]
-        total[col] += jnp.dot(h, w, preferred_element_type=f32)
+    def step(i, carry):
+        adds = []
+        for u in range(UNROLL):
+            c = i * UNROLL + u
+            word = code[c]
+            for k, part in enumerate((w0, w1, w2, w3)):
+                weights[c, (my_x + NX - k) % NX] = part[c]
+            lanes = pl.ds(pl.multiple_of(((word >> 8) & 15) * BS, BS), BS)
+            w = weights[c].reshape(BS, BS)
+            adds.append((word >> 12, jnp.dot(hidden[:, lanes], w, preferred_element_type=f32)))
+        for col, value in adds:
+            total[col] += value
         return carry
 
-    lax.fori_loop(0, info[0], step, 0)
+    lax.fori_loop(0, (info[0] + UNROLL - 1) // UNROLL, step, 0)
     for zl in range(NZL):
         for sub in range(4):
             mine[zl, sub] = total[(2 * zl + my_core) * 4 + sub]
@@ -328,14 +354,19 @@
 def backward_kernel(info, code, cols, weights, back, total):
     total[...] = jnp.zeros_like(total)
 
-    def step(c, carry):
-        word = code[c]
-        r, col = (word >> 8) & 15, word >> 12
-        w = weights[c].reshape(BS, BS)
-        total[r] += lax.dot_general(cols[col], w, (((1,), (1,)), ((), ())), preferred_element_type=f32)
+    def step(i, carry):
+        adds = []
+        for u in range(UNROLL):
+            c = i * UNROLL + u
+            word = code[c]
+            w = weights[c].reshape(BS, BS)
+            value = lax.dot_general(cols[word >> 12], w, (((1,), (1,)), ((), ())), preferred_element_type=f32)
+            adds.append(((word >> 8) & 15, value))
+        for r, value in adds:
+            total[r] += value
         return carry
 
-    lax.fori_loop(0, info[0], step, 0)
+    lax.fori_loop(0, (info[0] + UNROLL - 1) // UNROLL, step, 0)
     for r in range(total.shape[0]):
         back[:, r * BS : (r + 1) * BS] = total[r].astype(bf16)
 
@@ -354,17 +385,24 @@
         out[:, sub * BS : (sub + 1) * BS] = value.astype(bf16)
 
 
-def adam_kernel(place, state, shares, new_w, new_m, new_v, rows, grad):
+def adam_kernel(place, stacked, came, new_w, new_m, new_v, rows, grad):
     slots, share = new_w.shape
-    share_rows = shares.shape[0] * PAIR
+    places = came.shape[0] * PAIR
+    width = stacked.shape[1] // BS
     for j in range(slots):
         word = jnp.maximum(place[j] - 1, 0)
-        g, row = word % share_rows, word // share_rows
+        g, row = word % places, word // places
         filled = place[j] > 0
-        rows[pl.ds(j, 1), :] = jnp.where(filled, state[row // slots, pl.ds(row % slots, 1), :], 0.0)
+        here = row < slots
+        entry = jnp.maximum(row - slots, 0)
+        own = stacked[pl.ds(jnp.minimum(row, slots - 1), 1), :]
+        for n in range(width):
+            lanes = slice(n * BS, (n + 1) * BS)
+            moved = came[entry // MV, pl.ds(2 * PAIR + width * (entry % MV) + n, 1), :]
+            rows[j : j + 1, lanes] = jnp.where(filled, jnp.where(here, own[:, lanes], moved), 0.0)
         for b in range(2):
-            value = shares[g // PAIR, b, pl.ds(g % PAIR, 1), :]
-            grad[pl.ds(j, 1), b * BS : (b + 1) * BS] = jnp.where(filled, value, 0.0)
+            value = came[g // PAIR, pl.ds(2 * (g % PAIR) + b, 1), :]
+            grad[j : j + 1, b * BS : (b + 1) * BS] = jnp.where(filled, value, 0.0)
     w, m, v = adam_update(rows[:, :share], rows[:, share : 2 * share], rows[:, 2 * share :], grad[...])
     new_w[...] = w
     new_m[...] = m
@@ -407,36 +445,35 @@
     gathered = lax.all_gather(quarter, SHARD, axis=0, tiled=True)
     weight_share = lax.dynamic_slice_in_dim(block_weight[0], dp_index * 2, 2, 1).reshape(slot_count, share)
     stacked = jnp.concatenate([weight_share.astype(f32), first_moment[0], second_moment[0]], axis=1)
-    state = lax.all_gather(stacked, SHARD, axis=0)
-
-    fits, code, counts, send, place = make_plan(
+
+    fits, code, counts, send, state_send, place = make_plan(
         block_row, block_col, live_count, new_owner, new_slot, row_local, me
     )
-    info = jnp.concatenate([counts, jnp.stack([lax.axis_index("core"), x_index, lax.axis_index("zl")])])
+    info = jnp.stack(counts + [lax.axis_index("core"), x_index, lax.axis_index("zl")])
 
     partial, cols = call(
         grad_kernel,
-        (like((NX, NY * NZH * 2, CAP, BS), bf16), like((shard_count * 4, BS, BS), bf16)),
+        (like((NX, NY * NZH * 2, GCAP, BS), bf16), like((shard_count * 4, BS, BS), bf16)),
         2,
         3,
-        [pltpu.VMEM((row_local, BS, BS), bf16), pltpu.VMEM((BS * CAP, BS), f32)],
-        flops=2 * CAP * BS**3,
+        [pltpu.VMEM((row_local, BS, BS), bf16), pltpu.VMEM((BS * GCAP, BS), f32)],
+        flops=2 * WCAP * BS**3,
         byts=4 * 1024 * 1024,
     )(info, code, hidden, mine, other)
     along_x = all_to_all(partial, "x")
     summed = call(sum_kernel, like(partial.shape[1:], bf16), 0, 1, byts=2 * 1024 * 1024)(along_x)
-    along_yz = all_to_all(summed.reshape(NY * NZH, 2, CAP, BS), ("y", "zh"))
+    along_yz = all_to_all(summed.reshape(NY * NZH, 2, GCAP, BS), ("y", "zh"))
     shares = call(
         functools.partial(share_kernel, scale),
-        like((shard_count, 2, PAIR, BS), f32),
-        1,
-        1,
-        [pltpu.VMEM((2, CAP, BS), f32)],
+        like((shard_count, 2 * PAIR + MV * stacked.shape[1] // BS, BS), f32),
+        2,
+        2,
+        [pltpu.VMEM((2, GCAP, BS), f32)],
         byts=1024 * 1024,
-    )(send, along_yz)
+    )(send, state_send, along_yz, stacked)
     shares = all_to_all(shares, SHARD)
 
-    w0 = call(select_kernel, like((CAP, BS // NX, BS), bf16), 2, 1, byts=1024 * 1024)(info, code, gathered)
+    w0 = call(select_kernel, like((WCAP, BS // NX, BS), bf16), 2, 1, byts=1024 * 1024)(info, code, gathered)
     w1, w2, w3 = (shift(w0, "x", NX, k) for k in (1, 2, 3))
 
     out_mine, out_theirs, weights = call(
@@ -444,12 +481,12 @@
         (
             like((NZL, 4, tokens, BS), f32),
             like((NZL, 4, tokens, BS), f32),
-            like((CAP, NX, BS // NX, BS), bf16),
+            like((WCAP, NX, BS // NX, BS), bf16),
         ),
         2,
         5,
         [pltpu.VMEM((shard_count * 4, tokens, BS), f32)],
-        flops=2 * CAP * BS**3,
+        flops=2 * WCAP * BS**3,
         byts=8 * 1024 * 1024,
     )(info, code, hidden, w0, w1, w2, w3)
     came = shift(out_theirs, "core", 2, 1)
@@ -459,7 +496,7 @@
         2,
         2,
         [pltpu.VMEM((row_local, tokens, BS), f32)],
-        flops=2 * CAP * BS**3,
+        flops=2 * WCAP * BS**3,
         byts=4 * 1024 * 1024,
     )(info, code, cols, weights)
     part = (4, tokens, BS)
@@ -467,6 +504,7 @@
         chip_kernel, (like(part, f32),) + (like(part, bf16),) * 3, 1, 2, byts=3 * 1024 * 1024
     )(info, out_mine, came)
     r1, r2, r3 = (shift(s, "zl", NZL, k + 1) for k, s in enumerate((s1, s2, s3)))
+    r1, r2, r3, hidden_grad = lax.optimization_barrier((r1, r2, r3, hidden_grad))
     projected = call(project_kernel, like(out_grad.shape, bf16), 0, 4, byts=1024 * 1024)(own, r1, r2, r3)
 
     shape = like((slot_count, share), f32)
@@ -477,7 +515,7 @@
         2,
         [pltpu.VMEM((slot_count, 3 * share), f32), pltpu.VMEM((slot_count, share), f32)],
         byts=1024 * 1024,
-    )(place, state, shares)
+    )(place, stacked, shares)
     result = (projected, hidden_grad, new_weight[None], new_first[None], new_second[None])
     return lax.cond(
         fits,

time: 163 us -> 158 us (0.969)
  waiting for transfers between devices: 18.3 us -> 49.3 us
  blocking collectives: 17.1 us -> 0 us
  Pallas kernels: 23.6 us -> 15.2 us
  local copies, waits for them, and re-layouts: 16.7 us -> 11.1 us
  other arithmetic: 8.41 us -> 3.42 us
  between operations: 15.7 us -> 17.6 us
    all_gather x1 -> x0, blocking collectives: 17.1 us -> none  [shards(): state = lax.all_gather(stacked, SHARD, axis=0)]
    all_to_all x4, waiting for transfers between devices: 9.46 us -> 26 us  [all_to_all(): return lax.all_to_all(values, axis, split_axis=0, concat_axis=0, tiled=True)]
    ppermute x8, waiting for transfers between devices: 0.15 us -> 11.9 us  [shift(): lax.ppermute(values, axis, [(i, (i + step) % count) for i in range(count)])]
    unnamed x47 -> x35, local copies, waits for them, and re-layouts: 11.4 us -> 6.74 us
    pallas_call x1, Pallas kernels: 5.81 us -> 3.04 us  [shards(): call(forward_kernel, (like((NZL, 4, tokens, BS), f32), like((NZL, 4, toke...]
    all_gather x1, waiting for transfers between devices: 8.71 us -> 11.4 us  [shards(): gathered = lax.all_gather(quarter, SHARD, axis=0, tiled=True)]
    pallas_call x3, Pallas kernels: 7.88 us -> 5.28 us  [the longest x1 3.15 us: shards(): call(grad_kernel, (like((NX, NY * NZH * 2, GCAP, BS), bf16), like((shard_...]
    pallas_call x1, Pallas kernels: 5.14 us -> 2.74 us  [shards(): call(backward_kernel, like(hidden.shape, bf16), 2, 2, [pltpu.VMEM((row_lo...]
  transfers between devices with their start and end apart: 13 -> 13, of which waited for: 3 -> 7; matrix products, arithmetic and copies ran while one was open for 7% -> 4% of each run, Pallas kernels for 15% -> 10%
where the time goes in v3:
time: 158 us; the launch traced here: 157 us
  starting transfers between devices  60.4 us (38%)
  waiting for transfers between devices  49.3 us (31%)
  between operations  17.6 us (11%)
  Pallas kernels  15.2 us (10%)
  local copies, waits for them, and re-layouts  11.1 us (7%)
  other arithmetic  3.42 us (2%)
    ppermute x8, starting transfers between devices, shift(): lax.ppermute(values, axis, [(i, (i + step) % count) for i in range(count)])  30.5 us
    all_to_all x4, starting transfers between devices, all_to_all(): return lax.all_to_all(values, axis, split_axis=0, concat_axis=0, tiled=True)  29.9 us
    all_to_all x4, waiting for transfers between devices, all_to_all(): return lax.all_to_all(values, axis, split_axis=0, concat_axis=0, tiled=True)  26 us
    ppermute x8, waiting for transfers between devices, shift(): lax.ppermute(values, axis, [(i, (i + step) % count) for i in range(count)])  11.9 us
    all_gather x1, waiting for transfers between devices, shards(): gathered = lax.all_gather(quarter, SHARD, axis=0, tiled=True)  11.4 us
    unnamed x35, local copies, waits for them, and re-layouts  6.74 us
  transfers between devices with their start and end apart: 13, of which 7 were waited for; matrix products, arithmetic and copies ran while one was open for 4% of the time, Pallas kernels for 10%

profile of v3, /device:TPU:1, one launch (start us, length us, event | category | flops | bytes accessed | tf_op | source)
XLA Modules:
  0.0 157.3 jit_solution(12459856003087687411)
XLA Ops:
  7.3 1.7 %constant_dynamic-slice_fusion.9 = bf16[1,32,32,128]{3,2,0,1:T(8,128)(2,1)} fusion(bf16[1,32,128,128]{3,2,0,1:T(8,128)(2,1)} %bitcast.130, s32[]{:T(128)S(6)} %select_n.333), kind=kLoop, calls=%fused_computation.174 | loop fusion | bytes 524292 | tf_op jit(solution)/shard_map/dynamic_slice | solution.py:444
  9.0 1.8 %broadcast_in_dim.307 = bf16[4,128,512]{2,1,0:T(8,128)(2,1)} broadcast(bf16[128,512]{1,0:T(8,128)(2,1)} %param.19), dimensions={1,2} | broadcast | bytes 655360 | tf_op jit(solution)/shard_map/broadcast_in_dim | solution.py:442
  10.8 7.8 %all-to-all-start.1 = ((bf16[4,128,512]{2,1,0:T(8,128)(2,1)}), bf16[4,128,512]{2,1,0:T(8,128)(2,1)S(1)}, u32[]{:S(2)}, u32[]{:S(2)}) async-start(bf16[4,128,512]{2,1,0:T(8,128)(2,1)} %broadcast_in_dim.307), calls=%async_computation.2 | async-start | bytes 1048576 | tf_op jit(solution)/shard_map/all_to_all | solution.py:413
  22.1 9.7 %all-to-all-done.1.mine = bf16[4,128,512]{2,1,0:T(8,128)(2,1)S(1)} async-done(((bf16[4,128,512]{2,1,0:T(8,128)(2,1)}), bf16[4,128,512]{2,1,0:T(8,128)(2,1)S(1)}, u32[]{:S(2)}, u32[]{:S(2)}) %all-to-all-start.1) | async-done | bytes 524320 | tf_op jit(solution)/shard_map/all_to_all | solution.py:413
  31.8 4.3 %collective-permute-start = (bf16[4,128,512]{2,1,0:T(8,128)(2,1)S(1)}, bf16[4,128,512]{2,1,0:T(8,128)(2,1)S(1)}, u32[]{:S(2)}, u32[]{:S(2)}) collective-permute-start(bf16[4,128,512]{2,1,0:T(8,128)(2,1)S(1)} %all-to-all-done.1.mine), channel_id=1, source_target_pairs={{0,1},{1,0},{2,3},{3,2},{4,5},{5,4},{6,7},{7,6},{8,9},{9,8},{10,11... | collective-permute-start | bytes 1572872 | tf_op jit(solution)/shard_map/ppermute | solution.py:417
  37.6 3.2 %shard_map.147 = (bf16[4,32,40,128]{3,2,1,0:T(8,128)(2,1)}, bf16[32,128,128]{2,1,0:T(8,128)(2,1)S(1)}) custom-call(s32[5]{0:T(128)S(1)} %stack.23.info, s32[44]{0:T(128)S(1)} %select_reduce_fusion.4.code, bf16[128,1792]{1,0:T(8,128)(2,1)S(1)} %copy-done.6, bf16[4,128,512]{2,1,0:T(8,128)(2,1)S(1)} %all-to-all-done.1.mine, ...), custom_call_target="tpu_custom_call" | custom-call | flops 184549376 | bytes 4194304 | tf_op jit(solution)/shard_map/pallas_call | solution.py:454
  40.7 1.0 copy-done.3
  41.7 4.0 %all-to-all-start.2 = ((bf16[4,32,40,128]{3,2,1,0:T(8,128)(2,1)}), bf16[4,32,40,128]{3,2,1,0:T(8,128)(2,1)S(1)}, u32[]{:S(2)}, u32[]{:S(2)}) async-start(bf16[4,32,40,128]{3,2,1,0:T(8,128)(2,1)} %get-tuple-element.209), calls=%async_computation.3 | async-start | bytes 2621440 | tf_op jit(solution)/shard_map/all_to_all | solution.py:413
  45.7 11.4 %all-gather.12.cloned.1.call-done = bf16[1,256,32,128]{3,2,0,1:T(8,128)(2,1)} async-done(((bf16[1,32,32,128]{3,2,0,1:T(8,128)(2,1)}), bf16[1,256,32,128]{3,2,0,1:T(8,128)(2,1)}) %all-gather.12.cloned.1.call-update) | async-done | bytes 2097168 | tf_op jit(solution)/shard_map/all_gather | solution.py:445
  57.1 1.6 %copy-done = bf16[1,256,32,128]{3,2,0,1:T(8,128)(2,1)S(1)} copy-done((bf16[1,256,32,128]{3,2,0,1:T(8,128)(2,1)S(1)}, bf16[1,256,32,128]{3,2,0,1:T(8,128)(2,1)}, u32[]{:S(2)}) %copy-start) | copy-done | bytes 2097176
  59.4 3.1 %collective-permute-start.1 = (bf16[44,32,128]{2,1,0:T(8,128)(2,1)S(1)}, bf16[44,32,128]{2,1,0:T(8,128)(2,1)S(1)}, u32[]{:S(2)}, u32[]{:S(2)}) collective-permute-start(bf16[44,32,128]{2,1,0:T(8,128)(2,1)S(1)} %shard_map.151.w0), channel_id=1, source_target_pairs={{0,16},{16,32},{32,48},{48,0},{1,17},{17,33},{33,49},{49,1},{2,18}... | collective-permute-start | bytes 1081352 | tf_op jit(solution)/shard_map/ppermute | solution.py:417
  62.6 4.3 %collective-permute-start.2 = (bf16[44,32,128]{2,1,0:T(8,128)(2,1)S(1)}, bf16[44,32,128]{2,1,0:T(8,128)(2,1)S(1)}, u32[]{:S(2)}, u32[]{:S(2)}) collective-permute-start(bf16[44,32,128]{2,1,0:T(8,128)(2,1)S(1)} %shard_map.151.w0), channel_id=1, source_target_pairs={{0,32},{16,48},{32,0},{48,16},{1,33},{17,49},{33,1},{49,17},{2,34}... | collective-permute-start | bytes 1081352 | tf_op jit(solution)/shard_map/ppermute | solution.py:417
  66.9 3.1 %collective-permute-start.3 = (bf16[44,32,128]{2,1,0:T(8,128)(2,1)S(1)}, bf16[44,32,128]{2,1,0:T(8,128)(2,1)S(1)}, u32[]{:S(2)}, u32[]{:S(2)}) collective-permute-start(bf16[44,32,128]{2,1,0:T(8,128)(2,1)S(1)} %shard_map.151.w0), channel_id=1, source_target_pairs={{0,48},{16,0},{32,16},{48,32},{1,49},{17,1},{33,17},{49,33},{2,50}... | collective-permute-start | bytes 1081352 | tf_op jit(solution)/shard_map/ppermute | solution.py:417
  70.3 8.7 %collective-permute-done.2.w2 = bf16[44,32,128]{2,1,0:T(8,128)(2,1)S(1)} collective-permute-done((bf16[44,32,128]{2,1,0:T(8,128)(2,1)S(1)}, bf16[44,32,128]{2,1,0:T(8,128)(2,1)S(1)}, u32[]{:S(2)}, u32[]{:S(2)}) %collective-permute-start.2) | collective-permute-done | bytes 360480 | tf_op jit(solution)/shard_map/ppermute | solution.py:417
  79.0 2.1 %collective-permute-done.3.w3 = bf16[44,32,128]{2,1,0:T(8,128)(2,1)S(1)} collective-permute-done((bf16[44,32,128]{2,1,0:T(8,128)(2,1)S(1)}, bf16[44,32,128]{2,1,0:T(8,128)(2,1)S(1)}, u32[]{:S(2)}, u32[]{:S(2)}) %collective-permute-start.3) | collective-permute-done | bytes 360480 | tf_op jit(solution)/shard_map/ppermute | solution.py:417
  81.1 3.0 %shard_map.152 = (f32[4,4,128,128]{3,2,1,0:T(8,128)S(1)}, f32[4,4,128,128]{3,2,1,0:T(8,128)}, bf16[44,4,32,128]{3,2,1,0:T(8,128)(2,1)S(1)}) custom-call(s32[5]{0:T(128)S(1)} %stack.23.info, s32[44]{0:T(128)S(1)} %select_reduce_fusion.4.code, bf16[128,1792]{1,0:T(8,128)(2,1)S(1)} %copy-done.6, bf16[44,32,128]{2,1,0:T(8,128)(2,1)S(1)} %shard_map.151.w0, ...), custom_call_target="tpu_custom_call" | custom-call | flops 184549376 | bytes 8388608 | tf_op jit(solution)/shard_map/pallas_call | solution.py:479
  84.1 1.0 copy-done.1
  85.2 5.2 %collective-permute-start.4 = (f32[4,4,128,128]{3,2,1,0:T(8,128)}, f32[4,4,128,128]{3,2,1,0:T(8,128)}, u32[]{:S(2)}, u32[]{:S(2)}) collective-permute-start(f32[4,4,128,128]{3,2,1,0:T(8,128)} %get-tuple-element.214), channel_id=1, source_target_pairs={{0,1},{1,0},{2,3},{3,2},{4,5},{5,4},{6,7},{7,6},{8,9},{9,8},{10,11... | collective-permute-start | bytes 3145736 | tf_op jit(solution)/shard_map/ppermute | solution.py:417
  90.3 0.9 dynamic-slice_convert_fusion
  91.2 0.9 shard_map.148
  92.1 12.9 %all-to-all-start.3 = ((bf16[16,2,40,128]{3,2,1,0:T(8,128)(2,1)}), bf16[16,2,40,128]{3,2,1,0:T(8,128)(2,1)S(1)}, u32[]{:S(2)}, u32[]{:S(2)}) async-start(bf16[16,2,40,128]{3,2,1,0:T(8,128)(2,1)} %bitcast.44), calls=%async_computation.4 | async-start | bytes 655360 | tf_op jit(solution)/shard_map/all_to_all | solution.py:413
  105.4 16.3 %all-to-all-done.3.parts = bf16[16,2,40,128]{3,2,1,0:T(8,128)(2,1)S(1)} async-done(((bf16[16,2,40,128]{3,2,1,0:T(8,128)(2,1)}), bf16[16,2,40,128]{3,2,1,0:T(8,128)(2,1)S(1)}, u32[]{:S(2)}, u32[]{:S(2)}) %all-to-all-start.3) | async-done | bytes 327712 | tf_op jit(solution)/shard_map/all_to_all | solution.py:413
  121.7 1.4 shard_map.149
  123.1 5.2 %all-to-all-start.4 = ((f32[8,40,128]{2,1,0:T(8,128)}), f32[8,40,128]{2,1,0:T(8,128)S(1)}, u32[]{:S(2)}, u32[]{:S(2)}) async-start(f32[8,40,128]{2,1,0:T(8,128)} %shard_map.149), calls=%async_computation.5 | async-start | bytes 327680 | tf_op jit(solution)/shard_map/all_to_all | solution.py:413
  130.4 1.2 copy-done.2
  131.6 1.3 shard_map.153
  133.0 3.4 %collective-permute-start.5 = (bf16[4,128,128]{2,1,0:T(8,128)(2,1)S(1)}, bf16[4,128,128]{2,1,0:T(8,128)(2,1)S(1)}, u32[]{:S(2)}, u32[]{:S(2)}) collective-permute-start(bf16[4,128,128]{2,1,0:T(8,128)(2,1)S(1)} %get-tuple-element.216), channel_id=1, source_target_pairs={{0,2},{2,4},{4,6},{6,0},{1,3},{3,5},{5,7},{7,1},{8,10},{10,12},{12... | collective-permute-start | bytes 393224 | tf_op jit(solution)/shard_map/ppermute | solution.py:417
  136.4 4.0 %collective-permute-start.6 = (bf16[4,128,128]{2,1,0:T(8,128)(2,1)S(1)}, bf16[4,128,128]{2,1,0:T(8,128)(2,1)S(1)}, u32[]{:S(2)}, u32[]{:S(2)}) collective-permute-start(bf16[4,128,128]{2,1,0:T(8,128)(2,1)S(1)} %get-tuple-element.217), channel_id=1, source_target_pairs={{0,4},{2,6},{4,0},{6,2},{1,5},{3,7},{5,1},{7,3},{8,12},{10,14},{12... | collective-permute-start | bytes 393224 | tf_op jit(solution)/shard_map/ppermute | solution.py:417
  140.4 3.1 %collective-permute-start.7 = (bf16[4,128,128]{2,1,0:T(8,128)(2,1)S(1)}, bf16[4,128,128]{2,1,0:T(8,128)(2,1)S(1)}, u32[]{:S(2)}, u32[]{:S(2)}) collective-permute-start(bf16[4,128,128]{2,1,0:T(8,128)(2,1)S(1)} %get-tuple-element.218), channel_id=1, source_target_pairs={{0,6},{2,0},{4,2},{6,4},{1,7},{3,1},{5,3},{7,5},{8,14},{10,8},{12,... | collective-permute-start | bytes 393224 | tf_op jit(solution)/shard_map/ppermute | solution.py:417
  143.6 1.8 %shard_map.150 = (f32[32,256]{1,0:T(8,128)}, f32[32,256]{1,0:T(8,128)}, f32[32,256]{1,0:T(8,128)}) custom-call(s32[32]{0:T(128)S(1)} %select_reduce_fusion.5.place, f32[32,768]{1,0:T(8,128)S(1)} %pad_maximum_fusion.1.stacked, f32[8,40,128]{2,1,0:T(8,128)S(1)} %all-to-all-done.4.came), custom_call_target="tpu_custom_call" | custom-call | bytes 1048576 | tf_op jit(solution)/shard_map/pallas_call | solution.py:511
  145.4 1.2 copy-done.4
  146.6 2.7 %shard_map.154 = bf16[128,1792]{1,0:T(8,128)(2,1)} custom-call(s32[5]{0:T(128)S(1)} %stack.23.info, s32[44]{0:T(128)S(1)} %select_reduce_fusion.4.code, bf16[32,128,128]{2,1,0:T(8,128)(2,1)S(1)} %copy-done.4, bf16[44,4,32,128]{3,2,1,0:T(8,128)(2,1)S(1)} %get-tuple-element.220.weights), custom_call_target="tpu_custom_call" | custom-call | flops 184549376 | bytes 4194304 | tf_op jit(solution)/shard_map/pallas_call | solution.py:493
  (74 shorter events, 6.4 us)
Async XLA Ops:
  7.2 11.5 %copy-start.13 = (s32[8,32]{1,0:T(8,128)S(1)}, s32[8,32]{1,0:T(8,128)}, u32[]{:S(2)}) copy-start(s32[8,32]{1,0:T(8,128)} %param.24) | copy-start | bytes 3076
  7.2 11.5 %copy-start.14 = (s32[8,32]{1,0:T(8,128)S(1)}, s32[8,32]{1,0:T(8,128)}, u32[]{:S(2)}) copy-start(s32[8,32]{1,0:T(8,128)} %param.21) | copy-start | bytes 3076
  7.2 11.5 %copy-start.17 = (s32[8]{0:T(128)S(1)}, s32[8]{0:T(128)}, u32[]{:S(2)}) copy-start(s32[8]{0:T(128)} %param.23) | copy-start | bytes 100
  7.2 11.8 %copy-start.15 = (s32[8,32]{1,0:T(8,128)S(1)}, s32[8,32]{1,0:T(8,128)}, u32[]{:S(2)}) copy-start(s32[8,32]{1,0:T(8,128)} %param.22) | copy-start | bytes 3076
  7.2 30.3 %copy-start.6 = (bf16[128,1792]{1,0:T(8,128)(2,1)S(1)}, bf16[128,1792]{1,0:T(8,128)(2,1)}, u32[]{:S(2)}) copy-start(bf16[128,1792]{1,0:T(8,128)(2,1)} %hidden.3) | copy-start | bytes 1376260
  7.2 49.9 %all-gather.12.cloned.1.call-start = ((), (), s32[]{:S(2)}) async-start(), calls=%async_computation.10 | async-start | bytes 2359296 | tf_op jit(solution)/shard_map/all_gather | solution.py:445
  10.8 21.0 %all-to-all-start.1 = ((bf16[4,128,512]{2,1,0:T(8,128)(2,1)}), bf16[4,128,512]{2,1,0:T(8,128)(2,1)S(1)}, u32[]{:S(2)}, u32[]{:S(2)}) async-start(bf16[4,128,512]{2,1,0:T(8,128)(2,1)} %broadcast_in_dim.307), calls=%async_computation.2 | async-start | bytes 1048576 | tf_op jit(solution)/shard_map/all_to_all | solution.py:413
  31.8 5.8 %collective-permute-start = (bf16[4,128,512]{2,1,0:T(8,128)(2,1)S(1)}, bf16[4,128,512]{2,1,0:T(8,128)(2,1)S(1)}, u32[]{:S(2)}, u32[]{:S(2)}) collective-permute-start(bf16[4,128,512]{2,1,0:T(8,128)(2,1)S(1)} %all-to-all-done.1.mine), channel_id=1, source_target_pairs={{0,1},{1,0},{2,3},{3,2},{4,5},{5,4},{6,7},{7,6},{8,9},{9,8},{10,11... | collective-permute-start | bytes 1572872 | tf_op jit(solution)/shard_map/ppermute | solution.py:417
  40.7 1.0 copy-start.3
  41.7 49.5 %all-to-all-start.2 = ((bf16[4,32,40,128]{3,2,1,0:T(8,128)(2,1)}), bf16[4,32,40,128]{3,2,1,0:T(8,128)(2,1)S(1)}, u32[]{:S(2)}, u32[]{:S(2)}) async-start(bf16[4,32,40,128]{3,2,1,0:T(8,128)(2,1)} %get-tuple-element.209), calls=%async_computation.3 | async-start | bytes 2621440 | tf_op jit(solution)/shard_map/all_to_all | solution.py:413
  57.1 1.6 %copy-start = (bf16[1,256,32,128]{3,2,0,1:T(8,128)(2,1)S(1)}, bf16[1,256,32,128]{3,2,0,1:T(8,128)(2,1)}, u32[]{:S(2)}) copy-start(bf16[1,256,32,128]{3,2,0,1:T(8,128)(2,1)} %all-gather.12.cloned.1.call-done) | copy-start | bytes 6291460
  59.4 45.9 %copy-start.9 = (f32[1,32,256]{2,1,0:T(8,128)S(1)}, f32[1,32,256]{2,1,0:T(8,128)}, u32[]{:S(2)}) copy-start(f32[1,32,256]{2,1,0:T(8,128)} %param.26) | copy-start | bytes 98308
  59.4 45.9 %copy-start.11 = (f32[1,32,256]{2,1,0:T(8,128)S(1)}, f32[1,32,256]{2,1,0:T(8,128)}, u32[]{:S(2)}) copy-start(f32[1,32,256]{2,1,0:T(8,128)} %param.27) | copy-start | bytes 98308
  59.4 10.9 %collective-permute-start.1 = (bf16[44,32,128]{2,1,0:T(8,128)(2,1)S(1)}, bf16[44,32,128]{2,1,0:T(8,128)(2,1)S(1)}, u32[]{:S(2)}, u32[]{:S(2)}) collective-permute-start(bf16[44,32,128]{2,1,0:T(8,128)(2,1)S(1)} %shard_map.151.w0), channel_id=1, source_target_pairs={{0,16},{16,32},{32,48},{48,0},{1,17},{17,33},{33,49},{49,1},{2,18}... | collective-permute-start | bytes 1081352 | tf_op jit(solution)/shard_map/ppermute | solution.py:417
  62.6 16.5 %collective-permute-start.2 = (bf16[44,32,128]{2,1,0:T(8,128)(2,1)S(1)}, bf16[44,32,128]{2,1,0:T(8,128)(2,1)S(1)}, u32[]{:S(2)}, u32[]{:S(2)}) collective-permute-start(bf16[44,32,128]{2,1,0:T(8,128)(2,1)S(1)} %shard_map.151.w0), channel_id=1, source_target_pairs={{0,32},{16,48},{32,0},{48,16},{1,33},{17,49},{33,1},{49,17},{2,34}... | collective-permute-start | bytes 1081352 | tf_op jit(solution)/shard_map/ppermute | solution.py:417
  66.9 14.2 %collective-permute-start.3 = (bf16[44,32,128]{2,1,0:T(8,128)(2,1)S(1)}, bf16[44,32,128]{2,1,0:T(8,128)(2,1)S(1)}, u32[]{:S(2)}, u32[]{:S(2)}) collective-permute-start(bf16[44,32,128]{2,1,0:T(8,128)(2,1)S(1)} %shard_map.151.w0), channel_id=1, source_target_pairs={{0,48},{16,0},{32,16},{48,32},{1,49},{17,1},{33,17},{49,33},{2,50}... | collective-permute-start | bytes 1081352 | tf_op jit(solution)/shard_map/ppermute | solution.py:417
  84.1 1.0 copy-start.1
  85.1 43.1 %copy-start.16 = (s32[8,32]{1,0:T(8,128)S(1)}, s32[8,32]{1,0:T(8,128)}, u32[]{:S(2)}) copy-start(s32[8,32]{1,0:T(8,128)} %param.25) | copy-start | bytes 3076
  85.2 45.2 %collective-permute-start.4 = (f32[4,4,128,128]{3,2,1,0:T(8,128)}, f32[4,4,128,128]{3,2,1,0:T(8,128)}, u32[]{:S(2)}, u32[]{:S(2)}) collective-permute-start(f32[4,4,128,128]{3,2,1,0:T(8,128)} %get-tuple-element.214), channel_id=1, source_target_pairs={{0,1},{1,0},{2,3},{3,2},{4,5},{5,4},{6,7},{7,6},{8,9},{9,8},{10,11... | collective-permute-start | bytes 3145736 | tf_op jit(solution)/shard_map/ppermute | solution.py:417
  92.1 29.6 %all-to-all-start.3 = ((bf16[16,2,40,128]{3,2,1,0:T(8,128)(2,1)}), bf16[16,2,40,128]{3,2,1,0:T(8,128)(2,1)S(1)}, u32[]{:S(2)}, u32[]{:S(2)}) async-start(bf16[16,2,40,128]{3,2,1,0:T(8,128)(2,1)} %bitcast.44), calls=%async_computation.4 | async-start | bytes 655360 | tf_op jit(solution)/shard_map/all_to_all | solution.py:413
  123.1 20.5 %all-to-all-start.4 = ((f32[8,40,128]{2,1,0:T(8,128)}), f32[8,40,128]{2,1,0:T(8,128)S(1)}, u32[]{:S(2)}, u32[]{:S(2)}) async-start(f32[8,40,128]{2,1,0:T(8,128)} %shard_map.149), calls=%async_computation.5 | async-start | bytes 327680 | tf_op jit(solution)/shard_map/all_to_all | solution.py:413
  130.4 1.2 copy-start.2
  132.9 16.6 %copy-start.7 = (bf16[128,512]{1,0:T(8,128)(2,1)S(1)}, bf16[128,512]{1,0:T(8,128)(2,1)}, u32[]{:S(2)}) copy-start(bf16[128,512]{1,0:T(8,128)(2,1)} %param.19) | copy-start | bytes 393220
  132.9 16.5 %copy-start.10 = (f32[1,32,256]{2,1,0:T(8,128)S(1)}, f32[1,32,256]{2,1,0:T(8,128)}, u32[]{:S(2)}) copy-start(f32[1,32,256]{2,1,0:T(8,128)} %param.26) | copy-start | bytes 98308
  132.9 16.5 %copy-start.18 = (s32[8]{0:T(128)S(1)}, s32[8]{0:T(128)}, u32[]{:S(2)}) copy-start(s32[8]{0:T(128)} %param.23) | copy-start | bytes 100
  133.0 16.4 %collective-permute-start.5 = (bf16[4,128,128]{2,1,0:T(8,128)(2,1)S(1)}, bf16[4,128,128]{2,1,0:T(8,128)(2,1)S(1)}, u32[]{:S(2)}, u32[]{:S(2)}) collective-permute-start(bf16[4,128,128]{2,1,0:T(8,128)(2,1)S(1)} %get-tuple-element.216), channel_id=1, source_target_pairs={{0,2},{2,4},{4,6},{6,0},{1,3},{3,5},{5,7},{7,1},{8,10},{10,12},{12... | collective-permute-start | bytes 393224 | tf_op jit(solution)/shard_map/ppermute | solution.py:417
  136.4 13.0 %collective-permute-start.6 = (bf16[4,128,128]{2,1,0:T(8,128)(2,1)S(1)}, bf16[4,128,128]{2,1,0:T(8,128)(2,1)S(1)}, u32[]{:S(2)}, u32[]{:S(2)}) collective-permute-start(bf16[4,128,128]{2,1,0:T(8,128)(2,1)S(1)} %get-tuple-element.217), channel_id=1, source_target_pairs={{0,4},{2,6},{4,0},{6,2},{1,5},{3,7},{5,1},{7,3},{8,12},{10,14},{12... | collective-permute-start | bytes 393224 | tf_op jit(solution)/shard_map/ppermute | solution.py:417
  140.4 9.0 %collective-permute-start.7 = (bf16[4,128,128]{2,1,0:T(8,128)(2,1)S(1)}, bf16[4,128,128]{2,1,0:T(8,128)(2,1)S(1)}, u32[]{:S(2)}, u32[]{:S(2)}) collective-permute-start(bf16[4,128,128]{2,1,0:T(8,128)(2,1)S(1)} %get-tuple-element.218), channel_id=1, source_target_pairs={{0,6},{2,0},{4,2},{6,4},{1,7},{3,1},{5,3},{7,5},{8,14},{10,8},{12,... | collective-permute-start | bytes 393224 | tf_op jit(solution)/shard_map/ppermute | solution.py:417
  145.4 1.2 copy-start.4
  149.7 0.7 copy-start.8
Sparse Core Ops, SparseCore 0:
  10.9 46.1 all-gather.11

commit v4 on v3

--- a/solution.py
+++ b/solution.py
@@ -196,13 +196,13 @@
 i32 = jnp.int32
 
 
-def call(kernel, outs, n_smem, n_vmem, scratch=(), flops=0, byts=0):
+def call(kernel, outs, n_smem, n_vmem, scratch=(), flops=0, byts=0, n_after=0):
     smem = pl.BlockSpec(memory_space=pltpu.SMEM)
     vmem = pl.BlockSpec(memory_space=pltpu.VMEM)
     return pl.pallas_call(
         kernel,
         out_shape=outs,
-        in_specs=[smem] * n_smem + [vmem] * n_vmem,
+        in_specs=[smem] * n_smem + [vmem] * n_vmem + [pl.BlockSpec(memory_space=pl.ANY)] * n_after,
         out_specs=jax.tree.map(lambda _: vmem, outs),
         scratch_shapes=list(scratch),
         compiler_params=pltpu.CompilerParams(vmem_limit_bytes=VMEM_LIMIT),
@@ -298,7 +298,7 @@
     lax.fori_loop(0, out.shape[0], step, 0, unroll=4)
 
 
-def share_kernel(scale, send, state_send, parts, stacked, out, total):
+def share_kernel(scale, send, state_send, parts, stacked, _after, out, total):
     for b in range(2):
         value = parts[0, b].astype(f32)
         for n in range(1, parts.shape[0]):
@@ -326,7 +326,7 @@
     lax.fori_loop(0, WCAP, step, 0, unroll=4)
 
 
-def forward_kernel(info, code, hidden, w0, w1, w2, w3, mine, theirs, weights, total):
+def forward_kernel(info, code, hidden, w0, w1, w2, w3, _after, mine, theirs, weights, total):
     my_core, my_x = info[2], info[3]
     total[...] = jnp.zeros_like(total)
 
@@ -371,7 +371,7 @@
         back[:, r * BS : (r + 1) * BS] = total[r].astype(bf16)
 
 
-def chip_kernel(info, mine, came, own, s1, s2, s3):
+def chip_kernel(info, mine, came, _after, own, s1, s2, s3):
     my_zl = info[4]
     own[...] = mine[my_zl] + came[my_zl]
     for k, out in enumerate((s1, s2, s3)):
@@ -463,18 +463,9 @@
     along_x = all_to_all(partial, "x")
     summed = call(sum_kernel, like(partial.shape[1:], bf16), 0, 1, byts=2 * 1024 * 1024)(along_x)
     along_yz = all_to_all(summed.reshape(NY * NZH, 2, GCAP, BS), ("y", "zh"))
-    shares = call(
-        functools.partial(share_kernel, scale),
-        like((shard_count, 2 * PAIR + MV * stacked.shape[1] // BS, BS), f32),
-        2,
-        2,
-        [pltpu.VMEM((2, GCAP, BS), f32)],
-        byts=1024 * 1024,
-    )(send, state_send, along_yz, stacked)
-    shares = all_to_all(shares, SHARD)
 
     w0 = call(select_kernel, like((WCAP, BS // NX, BS), bf16), 2, 1, byts=1024 * 1024)(info, code, gathered)
-    w1, w2, w3 = (shift(w0, "x", NX, k) for k in (1, 2, 3))
+    w2, w1, w3 = (shift(w0, "x", NX, k) for k in (2, 1, 3))
 
     out_mine, out_theirs, weights = call(
         forward_kernel,
@@ -488,7 +479,8 @@
         [pltpu.VMEM((shard_count * 4, tokens, BS), f32)],
         flops=2 * WCAP * BS**3,
         byts=8 * 1024 * 1024,
-    )(info, code, hidden, w0, w1, w2, w3)
+        n_after=1,
+    )(info, code, hidden, w0, w1, w2, w3, summed)
     came = shift(out_theirs, "core", 2, 1)
     hidden_grad = call(
         backward_kernel,
@@ -501,10 +493,19 @@
     )(info, code, cols, weights)
     part = (4, tokens, BS)
     own, s1, s2, s3 = call(
-        chip_kernel, (like(part, f32),) + (like(part, bf16),) * 3, 1, 2, byts=3 * 1024 * 1024
-    )(info, out_mine, came)
-    r1, r2, r3 = (shift(s, "zl", NZL, k + 1) for k, s in enumerate((s1, s2, s3)))
-    r1, r2, r3, hidden_grad = lax.optimization_barrier((r1, r2, r3, hidden_grad))
+        chip_kernel, (like(part, f32),) + (like(part, bf16),) * 3, 1, 2, byts=3 * 1024 * 1024, n_after=1
+    )(info, out_mine, came, hidden_grad)
+    shares = call(
+        functools.partial(share_kernel, scale),
+        like((shard_count, 2 * PAIR + MV * stacked.shape[1] // BS, BS), f32),
+        2,
+        2,
+        [pltpu.VMEM((2, GCAP, BS), f32)],
+        byts=1024 * 1024,
+        n_after=1,
+    )(send, state_send, along_yz, stacked, s1)
+    shares = all_to_all(shares, SHARD)
+    r2, r1, r3 = (shift(s, "zl", NZL, k) for k, s in ((2, s2), (1, s1), (3, s3)))
     projected = call(project_kernel, like(out_grad.shape, bf16), 0, 4, byts=1024 * 1024)(own, r1, r2, r3)
 
     shape = like((slot_count, share), f32)

time: 158 us -> 158 us (level)
  waiting for transfers between devices: 49.3 us -> 44.3 us
  other arithmetic: 3.42 us -> 5.87 us
  local copies, waits for them, and re-layouts: 11.1 us -> 13.4 us
    all_to_all x4, waiting for transfers between devices: 26 us -> 19.2 us  [all_to_all(): return lax.all_to_all(values, axis, split_axis=0, concat_axis=0, tiled=True)]
    unnamed x35 -> x53, local copies, waits for them, and re-layouts: 6.74 us -> 9.06 us
    ppermute x8, waiting for transfers between devices: 11.9 us -> 13.7 us  [shift(): lax.ppermute(values, axis, [(i, (i + step) % count) for i in range(count)])]
  transfers between devices with their start and end apart: 13 -> 13, of which waited for: 7 -> 8; matrix products, arithmetic and copies ran while one was open for 4% -> 5% of each run, Pallas kernels for 10% -> 6%
where the time goes in v4:
time: 158 us; the launch traced here: 157 us
  starting transfers between devices  60.2 us (38%)
  waiting for transfers between devices  44.3 us (28%)
  between operations  17.6 us (11%)
  Pallas kernels  15.6 us (10%)
  local copies, waits for them, and re-layouts  13.4 us (8%)
  other arithmetic  5.87 us (4%)
    all_to_all x4, starting transfers between devices, all_to_all(): return lax.all_to_all(values, axis, split_axis=0, concat_axis=0, tiled=True)  30.5 us
    ppermute x8, starting transfers between devices, shift(): lax.ppermute(values, axis, [(i, (i + step) % count) for i in range(count)])  29.6 us
    all_to_all x4, waiting for transfers between devices, all_to_all(): return lax.all_to_all(values, axis, split_axis=0, concat_axis=0, tiled=True)  19.2 us
    ppermute x8, waiting for transfers between devices, shift(): lax.ppermute(values, axis, [(i, (i + step) % count) for i in range(count)])  13.7 us
    all_gather x1, waiting for transfers between devices, shards(): gathered = lax.all_gather(quarter, SHARD, axis=0, tiled=True)  11.4 us
    unnamed x53, local copies, waits for them, and re-layouts  9.06 us
    pallas_call x1, Pallas kernels, shards(): call(forward_kernel, (like((NZL, 4, tokens, BS), f32), like((NZL, 4, toke...  3.25 us
  transfers between devices with their start and end apart: 13, of which 8 were waited for; matrix products, arithmetic and copies ran while one was open for 5% of the time, Pallas kernels for 6%

profile of v4, /device:TPU:1, one launch (start us, length us, event | category | flops | bytes accessed | tf_op | source)
XLA Modules:
  0.0 157.2 jit_solution(3100591862359778554)
XLA Ops:
  7.3 1.7 %constant_dynamic-slice_fusion.9 = bf16[1,32,32,128]{3,2,0,1:T(8,128)(2,1)} fusion(bf16[1,32,128,128]{3,2,0,1:T(8,128)(2,1)} %bitcast.130, s32[]{:T(128)S(6)} %select_n.333), kind=kLoop, calls=%fused_computation.174 | loop fusion | bytes 524292 | tf_op jit(solution)/shard_map/dynamic_slice | solution.py:444
  9.0 1.8 %broadcast_in_dim.307 = bf16[4,128,512]{2,1,0:T(8,128)(2,1)} broadcast(bf16[128,512]{1,0:T(8,128)(2,1)} %param.19), dimensions={1,2} | broadcast | bytes 655360 | tf_op jit(solution)/shard_map/broadcast_in_dim | solution.py:442
  10.8 7.8 %all-to-all-start.1 = ((bf16[4,128,512]{2,1,0:T(8,128)(2,1)}), bf16[4,128,512]{2,1,0:T(8,128)(2,1)S(1)}, u32[]{:S(2)}, u32[]{:S(2)}) async-start(bf16[4,128,512]{2,1,0:T(8,128)(2,1)} %broadcast_in_dim.307), calls=%async_computation.2 | async-start | bytes 1048576 | tf_op jit(solution)/shard_map/all_to_all | solution.py:413
  21.0 1.4 convert_reduce_fusion.4
  23.8 7.9 %all-to-all-done.1.mine = bf16[4,128,512]{2,1,0:T(8,128)(2,1)S(1)} async-done(((bf16[4,128,512]{2,1,0:T(8,128)(2,1)}), bf16[4,128,512]{2,1,0:T(8,128)(2,1)S(1)}, u32[]{:S(2)}, u32[]{:S(2)}) %all-to-all-start.1) | async-done | bytes 524320 | tf_op jit(solution)/shard_map/all_to_all | solution.py:413
  31.8 4.3 %collective-permute-start = (bf16[4,128,512]{2,1,0:T(8,128)(2,1)S(1)}, bf16[4,128,512]{2,1,0:T(8,128)(2,1)S(1)}, u32[]{:S(2)}, u32[]{:S(2)}) collective-permute-start(bf16[4,128,512]{2,1,0:T(8,128)(2,1)S(1)} %all-to-all-done.1.mine), channel_id=1, source_target_pairs={{0,1},{1,0},{2,3},{3,2},{4,5},{5,4},{6,7},{7,6},{8,9},{9,8},{10,11... | collective-permute-start | bytes 1572872 | tf_op jit(solution)/shard_map/ppermute | solution.py:417
  36.0 1.3 and_select_fusion.3
  37.5 3.2 %shard_map.147 = (bf16[4,32,40,128]{3,2,1,0:T(8,128)(2,1)}, bf16[32,128,128]{2,1,0:T(8,128)(2,1)S(1)}) custom-call(s32[5]{0:T(128)S(1)} %stack.23.info, s32[44]{0:T(128)S(1)} %select_reduce_fusion.4.code, bf16[128,1792]{1,0:T(8,128)(2,1)S(1)} %copy-done.10, bf16[4,128,512]{2,1,0:T(8,128)(2,1)S(1)} %all-to-all-done.1.mine, ...), custom_call_target="tpu_custom_call" | custom-call | flops 184549376 | bytes 4194304 | tf_op jit(solution)/shard_map/pallas_call | solution.py:454
  41.7 4.0 %all-to-all-start.2 = ((bf16[4,32,40,128]{3,2,1,0:T(8,128)(2,1)}), bf16[4,32,40,128]{3,2,1,0:T(8,128)(2,1)S(1)}, u32[]{:S(2)}, u32[]{:S(2)}) async-start(bf16[4,32,40,128]{3,2,1,0:T(8,128)(2,1)} %get-tuple-element.205), calls=%async_computation.3 | async-start | bytes 2621440 | tf_op jit(solution)/shard_map/all_to_all | solution.py:413
  45.7 11.4 %all-gather.12.cloned.1.call-done = bf16[1,256,32,128]{3,2,0,1:T(8,128)(2,1)} async-done(((bf16[1,32,32,128]{3,2,0,1:T(8,128)(2,1)}), bf16[1,256,32,128]{3,2,0,1:T(8,128)(2,1)}) %all-gather.12.cloned.1.call-update) | async-done | bytes 2097168 | tf_op jit(solution)/shard_map/all_gather | solution.py:445
  57.1 1.6 %copy-done = bf16[1,256,32,128]{3,2,0,1:T(8,128)(2,1)S(1)} copy-done((bf16[1,256,32,128]{3,2,0,1:T(8,128)(2,1)S(1)}, bf16[1,256,32,128]{3,2,0,1:T(8,128)(2,1)}, u32[]{:S(2)}) %copy-start) | copy-done | bytes 2097176
  59.5 3.2 %collective-permute-start.1 = (bf16[44,32,128]{2,1,0:T(8,128)(2,1)S(1)}, bf16[44,32,128]{2,1,0:T(8,128)(2,1)S(1)}, u32[]{:S(2)}, u32[]{:S(2)}) collective-permute-start(bf16[44,32,128]{2,1,0:T(8,128)(2,1)S(1)} %shard_map.149.w0), channel_id=1, source_target_pairs={{0,16},{16,32},{32,48},{48,0},{1,17},{17,33},{33,49},{49,1},{2,18}... | collective-permute-start | bytes 1081352 | tf_op jit(solution)/shard_map/ppermute | solution.py:417
  62.7 4.3 %collective-permute-start.2 = (bf16[44,32,128]{2,1,0:T(8,128)(2,1)S(1)}, bf16[44,32,128]{2,1,0:T(8,128)(2,1)S(1)}, u32[]{:S(2)}, u32[]{:S(2)}) collective-permute-start(bf16[44,32,128]{2,1,0:T(8,128)(2,1)S(1)} %shard_map.149.w0), channel_id=1, source_target_pairs={{0,32},{16,48},{32,0},{48,16},{1,33},{17,49},{33,1},{49,17},{2,34}... | collective-permute-start | bytes 1081352 | tf_op jit(solution)/shard_map/ppermute | solution.py:417
  67.0 3.1 %collective-permute-start.3 = (bf16[44,32,128]{2,1,0:T(8,128)(2,1)S(1)}, bf16[44,32,128]{2,1,0:T(8,128)(2,1)S(1)}, u32[]{:S(2)}, u32[]{:S(2)}) collective-permute-start(bf16[44,32,128]{2,1,0:T(8,128)(2,1)S(1)} %shard_map.149.w0), channel_id=1, source_target_pairs={{0,48},{16,0},{32,16},{48,32},{1,49},{17,1},{33,17},{49,33},{2,50}... | collective-permute-start | bytes 1081352 | tf_op jit(solution)/shard_map/ppermute | solution.py:417
  71.1 8.1 %collective-permute-done.2.w2 = bf16[44,32,128]{2,1,0:T(8,128)(2,1)S(1)} collective-permute-done((bf16[44,32,128]{2,1,0:T(8,128)(2,1)S(1)}, bf16[44,32,128]{2,1,0:T(8,128)(2,1)S(1)}, u32[]{:S(2)}, u32[]{:S(2)}) %collective-permute-start.2) | collective-permute-done | bytes 360480 | tf_op jit(solution)/shard_map/ppermute | solution.py:417
  79.9 1.4 collective-permute-done.3.w3
  82.0 1.0 copy-done.6
  84.0 3.3 %shard_map.150 = (f32[4,4,128,128]{3,2,1,0:T(8,128)S(1)}, f32[4,4,128,128]{3,2,1,0:T(8,128)}, bf16[44,4,32,128]{3,2,1,0:T(8,128)(2,1)S(1)}) custom-call(s32[5]{0:T(128)S(1)} %stack.23.info, s32[44]{0:T(128)S(1)} %select_reduce_fusion.4.code, bf16[128,1792]{1,0:T(8,128)(2,1)S(1)} %copy-done.10, bf16[44,32,128]{2,1,0:T(8,128)(2,1)S(1)} %shard_map.149.w0, ...), custom_call_target="tpu_custom_call" | custom-call | flops 184549376 | bytes 8388608 | tf_op jit(solution)/shard_map/pallas_call | solution.py:470
  87.2 1.0 copy-done.3
  88.2 4.4 %collective-permute-start.4 = (f32[4,4,128,128]{3,2,1,0:T(8,128)}, f32[4,4,128,128]{3,2,1,0:T(8,128)}, u32[]{:S(2)}, u32[]{:S(2)}) collective-permute-start(f32[4,4,128,128]{3,2,1,0:T(8,128)} %get-tuple-element.207), channel_id=1, source_target_pairs={{0,1},{1,0},{2,3},{3,2},{4,5},{5,4},{6,7},{7,6},{8,9},{9,8},{10,11... | collective-permute-start | bytes 3145736 | tf_op jit(solution)/shard_map/ppermute | solution.py:417
  93.5 13.5 %all-to-all-start.3 = ((bf16[16,2,40,128]{3,2,1,0:T(8,128)(2,1)}), bf16[16,2,40,128]{3,2,1,0:T(8,128)(2,1)S(1)}, u32[]{:S(2)}, u32[]{:S(2)}) async-start(bf16[16,2,40,128]{3,2,1,0:T(8,128)(2,1)} %bitcast.44), calls=%async_computation.4 | async-start | bytes 655360 | tf_op jit(solution)/shard_map/all_to_all | solution.py:413
  107.4 1.2 copy-done.2
  108.6 2.2 %shard_map.151._after = bf16[128,1792]{1,0:T(8,128)(2,1)S(1)} custom-call(s32[5]{0:T(128)S(1)} %stack.23.info, s32[44]{0:T(128)S(1)} %select_reduce_fusion.4.code, bf16[32,128,128]{2,1,0:T(8,128)(2,1)S(1)} %copy-done.2, bf16[44,4,32,128]{3,2,1,0:T(8,128)(2,1)S(1)} %get-tuple-element.209.weights), custom_call_target="tpu_custom_call" | custom-call | flops 184549376 | bytes 4194304 | tf_op jit(solution)/shard_map/pallas_call | solution.py:485
  110.9 1.4 shard_map.152
  112.3 11.3 %all-to-all-done.3.parts = bf16[16,2,40,128]{3,2,1,0:T(8,128)(2,1)S(1)} async-done(((bf16[16,2,40,128]{3,2,1,0:T(8,128)(2,1)}), bf16[16,2,40,128]{3,2,1,0:T(8,128)(2,1)S(1)}, u32[]{:S(2)}, u32[]{:S(2)}) %all-to-all-start.3) | async-done | bytes 327712 | tf_op jit(solution)/shard_map/all_to_all | solution.py:413
  123.6 1.4 shard_map.153
  125.0 5.2 %all-to-all-start.4 = ((f32[8,40,128]{2,1,0:T(8,128)}), f32[8,40,128]{2,1,0:T(8,128)S(1)}, u32[]{:S(2)}, u32[]{:S(2)}) async-start(f32[8,40,128]{2,1,0:T(8,128)} %shard_map.153), calls=%async_computation.5 | async-start | bytes 327680 | tf_op jit(solution)/shard_map/all_to_all | solution.py:413
  130.2 3.3 %collective-permute-start.5 = (bf16[4,128,128]{2,1,0:T(8,128)(2,1)S(1)}, bf16[4,128,128]{2,1,0:T(8,128)(2,1)S(1)}, u32[]{:S(2)}, u32[]{:S(2)}) collective-permute-start(bf16[4,128,128]{2,1,0:T(8,128)(2,1)S(1)} %get-tuple-element.210._after), channel_id=1, source_target_pairs={{0,2},{2,4},{4,6},{6,0},{1,3},{3,5},{5,7},{7,1},{8,10},{10,12},{12... | collective-permute-start | bytes 393224 | tf_op jit(solution)/shard_map/ppermute | solution.py:417
  133.5 4.0 %collective-permute-start.6 = (bf16[4,128,128]{2,1,0:T(8,128)(2,1)S(1)}, bf16[4,128,128]{2,1,0:T(8,128)(2,1)S(1)}, u32[]{:S(2)}, u32[]{:S(2)}) collective-permute-start(bf16[4,128,128]{2,1,0:T(8,128)(2,1)S(1)} %get-tuple-element.215), channel_id=1, source_target_pairs={{0,4},{2,6},{4,0},{6,2},{1,5},{3,7},{5,1},{7,3},{8,12},{10,14},{12... | collective-permute-start | bytes 393224 | tf_op jit(solution)/shard_map/ppermute | solution.py:417
  137.5 3.1 %collective-permute-start.7 = (bf16[4,128,128]{2,1,0:T(8,128)(2,1)S(1)}, bf16[4,128,128]{2,1,0:T(8,128)(2,1)S(1)}, u32[]{:S(2)}, u32[]{:S(2)}) collective-permute-start(bf16[4,128,128]{2,1,0:T(8,128)(2,1)S(1)} %get-tuple-element.216), channel_id=1, source_target_pairs={{0,6},{2,0},{4,2},{6,4},{1,7},{3,1},{5,3},{7,5},{8,14},{10,8},{12,... | collective-permute-start | bytes 393224 | tf_op jit(solution)/shard_map/ppermute | solution.py:417
  142.7 3.2 %collective-permute-done.6.r2 = bf16[4,128,128]{2,1,0:T(8,128)(2,1)S(1)} collective-permute-done((bf16[4,128,128]{2,1,0:T(8,128)(2,1)S(1)}, bf16[4,128,128]{2,1,0:T(8,128)(2,1)S(1)}, u32[]{:S(2)}, u32[]{:S(2)}) %collective-permute-start.6) | collective-permute-done | bytes 131104 | tf_op jit(solution)/shard_map/ppermute | solution.py:417
  147.6 1.8 %shard_map.154 = (f32[32,256]{1,0:T(8,128)}, f32[32,256]{1,0:T(8,128)}, f32[32,256]{1,0:T(8,128)}) custom-call(s32[32]{0:T(128)S(1)} %select_reduce_fusion.5.place, f32[32,768]{1,0:T(8,128)S(1)} %pad_maximum_fusion.1.stacked, f32[8,40,128]{2,1,0:T(8,128)S(1)} %all-to-all-done.4.came), custom_call_target="tpu_custom_call" | custom-call | bytes 1048576 | tf_op jit(solution)/shard_map/pallas_call | solution.py:512
  (92 shorter events, 12.1 us)
Async XLA Ops:
  7.2 11.5 %copy-start.16 = (s32[8,32]{1,0:T(8,128)S(1)}, s32[8,32]{1,0:T(8,128)}, u32[]{:S(2)}) copy-start(s32[8,32]{1,0:T(8,128)} %param.24) | copy-start | bytes 3076
  7.2 11.5 %copy-start.17 = (s32[8,32]{1,0:T(8,128)S(1)}, s32[8,32]{1,0:T(8,128)}, u32[]{:S(2)}) copy-start(s32[8,32]{1,0:T(8,128)} %param.21) | copy-start | bytes 3076
  7.2 11.5 %copy-start.25 = (s32[8]{0:T(128)S(1)}, s32[8]{0:T(128)}, u32[]{:S(2)}) copy-start(s32[8]{0:T(128)} %param.23) | copy-start | bytes 100
  7.2 30.3 %copy-start.10 = (bf16[128,1792]{1,0:T(8,128)(2,1)S(1)}, bf16[128,1792]{1,0:T(8,128)(2,1)}, u32[]{:S(2)}) copy-start(bf16[128,1792]{1,0:T(8,128)(2,1)} %hidden.3) | copy-start | bytes 1376260
  7.2 49.9 %all-gather.12.cloned.1.call-start = ((), (), s32[]{:S(2)}) async-start(), calls=%async_computation.10 | async-start | bytes 2359296 | tf_op jit(solution)/shard_map/all_gather | solution.py:445
  10.8 21.0 %all-to-all-start.1 = ((bf16[4,128,512]{2,1,0:T(8,128)(2,1)}), bf16[4,128,512]{2,1,0:T(8,128)(2,1)S(1)}, u32[]{:S(2)}, u32[]{:S(2)}) async-start(bf16[4,128,512]{2,1,0:T(8,128)(2,1)} %broadcast_in_dim.307), calls=%async_computation.2 | async-start | bytes 1048576 | tf_op jit(solution)/shard_map/all_to_all | solution.py:413
  20.5 21.2 %copy-start.18 = (s32[256]{0:T(256)}, s32[256]{0:T(256)S(1)}, u32[]{:S(2)}) copy-start(s32[256]{0:T(256)S(1)} %get-tuple-element.334) | copy-start | bytes 3076
  31.8 5.8 %collective-permute-start = (bf16[4,128,512]{2,1,0:T(8,128)(2,1)S(1)}, bf16[4,128,512]{2,1,0:T(8,128)(2,1)S(1)}, u32[]{:S(2)}, u32[]{:S(2)}) collective-permute-start(bf16[4,128,512]{2,1,0:T(8,128)(2,1)S(1)} %all-to-all-done.1.mine), channel_id=1, source_target_pairs={{0,1},{1,0},{2,3},{3,2},{4,5},{5,4},{6,7},{7,6},{8,9},{9,8},{10,11... | collective-permute-start | bytes 1572872 | tf_op jit(solution)/shard_map/ppermute | solution.py:417
  41.7 28.5 %all-to-all-start.2 = ((bf16[4,32,40,128]{3,2,1,0:T(8,128)(2,1)}), bf16[4,32,40,128]{3,2,1,0:T(8,128)(2,1)S(1)}, u32[]{:S(2)}, u32[]{:S(2)}) async-start(bf16[4,32,40,128]{3,2,1,0:T(8,128)(2,1)} %get-tuple-element.205), calls=%async_computation.3 | async-start | bytes 2621440 | tf_op jit(solution)/shard_map/all_to_all | solution.py:413
  57.1 1.6 %copy-start = (bf16[1,256,32,128]{3,2,0,1:T(8,128)(2,1)S(1)}, bf16[1,256,32,128]{3,2,0,1:T(8,128)(2,1)}, u32[]{:S(2)}) copy-start(bf16[1,256,32,128]{3,2,0,1:T(8,128)(2,1)} %all-gather.12.cloned.1.call-done) | copy-start | bytes 6291460
  59.4 47.6 %copy-start.20 = (s32[8,32]{1,0:T(8,128)S(1)}, s32[8,32]{1,0:T(8,128)}, u32[]{:S(2)}) copy-start(s32[8,32]{1,0:T(8,128)} %get-tuple-element.404) | copy-start | bytes 3076
  59.4 47.8 %copy-start.13 = (f32[1,32,256]{2,1,0:T(8,128)S(1)}, f32[1,32,256]{2,1,0:T(8,128)}, u32[]{:S(2)}) copy-start(f32[1,32,256]{2,1,0:T(8,128)} %param.26) | copy-start | bytes 98308
  59.4 47.8 %copy-start.14 = (f32[1,32,256]{2,1,0:T(8,128)S(1)}, f32[1,32,256]{2,1,0:T(8,128)}, u32[]{:S(2)}) copy-start(f32[1,32,256]{2,1,0:T(8,128)} %param.27) | copy-start | bytes 98308
  59.4 47.8 %copy-start.19 = (s32[256]{0:T(256)S(1)}, s32[256]{0:T(256)}, u32[]{:S(2)}) copy-start(s32[256]{0:T(256)} %copy-done.18) | copy-start | bytes 3076
  59.5 47.8 %copy-start.23 = (s32[256]{0:T(256)S(1)}, s32[256]{0:T(256)}, u32[]{:S(2)}) copy-start(s32[256]{0:T(256)} %get-tuple-element.370) | copy-start | bytes 3076
  59.5 11.6 %collective-permute-start.1 = (bf16[44,32,128]{2,1,0:T(8,128)(2,1)S(1)}, bf16[44,32,128]{2,1,0:T(8,128)(2,1)S(1)}, u32[]{:S(2)}, u32[]{:S(2)}) collective-permute-start(bf16[44,32,128]{2,1,0:T(8,128)(2,1)S(1)} %shard_map.149.w0), channel_id=1, source_target_pairs={{0,16},{16,32},{32,48},{48,0},{1,17},{17,33},{33,49},{49,1},{2,18}... | collective-permute-start | bytes 1081352 | tf_op jit(solution)/shard_map/ppermute | solution.py:417
  62.7 16.4 %collective-permute-start.2 = (bf16[44,32,128]{2,1,0:T(8,128)(2,1)S(1)}, bf16[44,32,128]{2,1,0:T(8,128)(2,1)S(1)}, u32[]{:S(2)}, u32[]{:S(2)}) collective-permute-start(bf16[44,32,128]{2,1,0:T(8,128)(2,1)S(1)} %shard_map.149.w0), channel_id=1, source_target_pairs={{0,32},{16,48},{32,0},{48,16},{1,33},{17,49},{33,1},{49,17},{2,34}... | collective-permute-start | bytes 1081352 | tf_op jit(solution)/shard_map/ppermute | solution.py:417
  67.0 14.3 %collective-permute-start.3 = (bf16[44,32,128]{2,1,0:T(8,128)(2,1)S(1)}, bf16[44,32,128]{2,1,0:T(8,128)(2,1)S(1)}, u32[]{:S(2)}, u32[]{:S(2)}) collective-permute-start(bf16[44,32,128]{2,1,0:T(8,128)(2,1)S(1)} %shard_map.149.w0), channel_id=1, source_target_pairs={{0,48},{16,0},{32,16},{48,32},{1,49},{17,1},{33,17},{49,33},{2,50}... | collective-permute-start | bytes 1081352 | tf_op jit(solution)/shard_map/ppermute | solution.py:417
  88.2 22.6 %collective-permute-start.4 = (f32[4,4,128,128]{3,2,1,0:T(8,128)}, f32[4,4,128,128]{3,2,1,0:T(8,128)}, u32[]{:S(2)}, u32[]{:S(2)}) collective-permute-start(f32[4,4,128,128]{3,2,1,0:T(8,128)} %get-tuple-element.207), channel_id=1, source_target_pairs={{0,1},{1,0},{2,3},{3,2},{4,5},{5,4},{6,7},{7,6},{8,9},{9,8},{10,11... | collective-permute-start | bytes 3145736 | tf_op jit(solution)/shard_map/ppermute | solution.py:417
  93.5 30.2 %all-to-all-start.3 = ((bf16[16,2,40,128]{3,2,1,0:T(8,128)(2,1)}), bf16[16,2,40,128]{3,2,1,0:T(8,128)(2,1)S(1)}, u32[]{:S(2)}, u32[]{:S(2)}) async-start(bf16[16,2,40,128]{3,2,1,0:T(8,128)(2,1)} %bitcast.44), calls=%async_computation.4 | async-start | bytes 655360 | tf_op jit(solution)/shard_map/all_to_all | solution.py:413
  107.4 1.2 copy-start.2
  108.6 2.2 %copy-start.4 = (f32[4,4,128,128]{3,2,1,0:T(8,128)S(1)}, f32[4,4,128,128]{3,2,1,0:T(8,128)}, u32[]{:S(2)}) copy-start(f32[4,4,128,128]{3,2,1,0:T(8,128)} %copy-done.3) | copy-start | bytes 3145732
  110.8 29.8 %copy-start.21 = (s32[8,32]{1,0:T(8,128)S(1)}, s32[8,32]{1,0:T(8,128)}, u32[]{:S(2)}) copy-start(s32[8,32]{1,0:T(8,128)} %param.25) | copy-start | bytes 3076
  110.8 31.8 %copy-start.22 = (s32[256]{0:T(256)S(1)}, s32[256]{0:T(256)}, u32[]{:S(2)}) copy-start(s32[256]{0:T(256)} %get-tuple-element.398) | copy-start | bytes 3076
  110.9 31.8 %copy-start.24 = (pred[256]{0:T(512)(128)(4,1)S(1)}, pred[256]{0:T(512)(128)(4,1)}, u32[]{:S(2)}) copy-start(pred[256]{0:T(512)(128)(4,1)} %get-tuple-element.372) | copy-start | bytes 772
  110.9 38.5 %copy-start.12 = (bf16[128,512]{1,0:T(8,128)(2,1)S(1)}, bf16[128,512]{1,0:T(8,128)(2,1)}, u32[]{:S(2)}) copy-start(bf16[128,512]{1,0:T(8,128)(2,1)} %param.19) | copy-start | bytes 393220
  110.9 38.5 %copy-start.15 = (f32[1,32,256]{2,1,0:T(8,128)S(1)}, f32[1,32,256]{2,1,0:T(8,128)}, u32[]{:S(2)}) copy-start(f32[1,32,256]{2,1,0:T(8,128)} %param.27) | copy-start | bytes 98308
  110.9 38.4 %copy-start.26 = (s32[8]{0:T(128)S(1)}, s32[8]{0:T(128)}, u32[]{:S(2)}) copy-start(s32[8]{0:T(128)} %param.23) | copy-start | bytes 100
  125.0 22.6 %all-to-all-start.4 = ((f32[8,40,128]{2,1,0:T(8,128)}), f32[8,40,128]{2,1,0:T(8,128)S(1)}, u32[]{:S(2)}, u32[]{:S(2)}) async-start(f32[8,40,128]{2,1,0:T(8,128)} %shard_map.153), calls=%async_computation.5 | async-start | bytes 327680 | tf_op jit(solution)/shard_map/all_to_all | solution.py:413
  130.2 12.5 %collective-permute-start.5 = (bf16[4,128,128]{2,1,0:T(8,128)(2,1)S(1)}, bf16[4,128,128]{2,1,0:T(8,128)(2,1)S(1)}, u32[]{:S(2)}, u32[]{:S(2)}) collective-permute-start(bf16[4,128,128]{2,1,0:T(8,128)(2,1)S(1)} %get-tuple-element.210._after), channel_id=1, source_target_pairs={{0,2},{2,4},{4,6},{6,0},{1,3},{3,5},{5,7},{7,1},{8,10},{10,12},{12... | collective-permute-start | bytes 393224 | tf_op jit(solution)/shard_map/ppermute | solution.py:417
  133.5 12.5 %collective-permute-start.6 = (bf16[4,128,128]{2,1,0:T(8,128)(2,1)S(1)}, bf16[4,128,128]{2,1,0:T(8,128)(2,1)S(1)}, u32[]{:S(2)}, u32[]{:S(2)}) collective-permute-start(bf16[4,128,128]{2,1,0:T(8,128)(2,1)S(1)} %get-tuple-element.215), channel_id=1, source_target_pairs={{0,4},{2,6},{4,0},{6,2},{1,5},{3,7},{5,1},{7,3},{8,12},{10,14},{12... | collective-permute-start | bytes 393224 | tf_op jit(solution)/shard_map/ppermute | solution.py:417
  137.5 9.3 %collective-permute-start.7 = (bf16[4,128,128]{2,1,0:T(8,128)(2,1)S(1)}, bf16[4,128,128]{2,1,0:T(8,128)(2,1)S(1)}, u32[]{:S(2)}, u32[]{:S(2)}) collective-permute-start(bf16[4,128,128]{2,1,0:T(8,128)(2,1)S(1)} %get-tuple-element.216), channel_id=1, source_target_pairs={{0,6},{2,0},{4,2},{6,4},{1,7},{3,1},{5,3},{7,5},{8,14},{10,8},{12,... | collective-permute-start | bytes 393224 | tf_op jit(solution)/shard_map/ppermute | solution.py:417
  (7 other events, 6.2 us)
Sparse Core Ops, SparseCore 0:
  10.9 46.1 all-gather.11

commit v5 on v4

--- a/solution.py
+++ b/solution.py
@@ -287,15 +287,25 @@
                 out[x, 4 * y + q] = total[source * GCAP : (source + 1) * GCAP, :].astype(bf16)
 
 
-def sum_kernel(parts, out):
+def sum_kernel(info, parts, keep, send):
+    my_zh = info[5]
+
     def step(i, carry):
-        value = parts[0, i].astype(f32)
-        for n in range(1, parts.shape[0]):
-            value += parts[n, i].astype(f32)
-        out[i] = value.astype(bf16)
+        for out, zh in ((keep, my_zh), (send, 1 - my_zh)):
+            for b in range(2):
+                row = 4 * i + 2 * zh + b
+                value = parts[0, row].astype(f32)
+                for n in range(1, parts.shape[0]):
+                    value += parts[n, row].astype(f32)
+                out[i, b] = value.astype(out.dtype)
         return carry
 
-    lax.fori_loop(0, out.shape[0], step, 0, unroll=4)
+    lax.fori_loop(0, keep.shape[0], step, 0, unroll=2)
+
+
+def pair_kernel(keep, came, out):
+    for i in range(keep.shape[0]):
+        out[i] = (keep[i] + came[i].astype(f32)).astype(bf16)
 
 
 def share_kernel(scale, send, state_send, parts, stacked, _after, out, total):
@@ -317,17 +327,19 @@
                 out[d, at : at + 1, :] = row[:, n * BS : (n + 1) * BS]
 
 
-def select_kernel(info, code, gathered, out):
+def select_kernel(info, code, gathered, _after, out):
     def step(c, carry):
         value = gathered[code[c] & 255]
-        out[c] = jnp.where(c < info[0], value, jnp.zeros_like(value))
+        value = jnp.where(c < info[0], value, jnp.zeros_like(value))
+        for x in range(NX):
+            out[x, c] = value
         return carry
 
     lax.fori_loop(0, WCAP, step, 0, unroll=4)
 
 
-def forward_kernel(info, code, hidden, w0, w1, w2, w3, _after, mine, theirs, weights, total):
-    my_core, my_x = info[2], info[3]
+def forward_kernel(info, code, hidden, quarters, _after, mine, theirs, weights, total):
+    my_core = info[2]
     total[...] = jnp.zeros_like(total)
 
     def step(i, carry):
@@ -335,8 +347,8 @@
         for u in range(UNROLL):
             c = i * UNROLL + u
             word = code[c]
-            for k, part in enumerate((w0, w1, w2, w3)):
-                weights[c, (my_x + NX - k) % NX] = part[c]
+            for x in range(NX):
+                weights[c, x] = quarters[x, c]
             lanes = pl.ds(pl.multiple_of(((word >> 8) & 15) * BS, BS), BS)
             w = weights[c].reshape(BS, BS)
             adds.append((word >> 12, jnp.dot(hidden[:, lanes], w, preferred_element_type=f32)))
@@ -449,7 +461,7 @@
     fits, code, counts, send, state_send, place = make_plan(
         block_row, block_col, live_count, new_owner, new_slot, row_local, me
     )
-    info = jnp.stack(counts + [lax.axis_index("core"), x_index, lax.axis_index("zl")])
+    info = jnp.stack(counts + [lax.axis_index("core"), x_index, lax.axis_index("zl"), lax.axis_index("zh")])
 
     partial, cols = call(
         grad_kernel,
@@ -461,11 +473,16 @@
         byts=4 * 1024 * 1024,
     )(info, code, hidden, mine, other)
     along_x = all_to_all(partial, "x")
-    summed = call(sum_kernel, like(partial.shape[1:], bf16), 0, 1, byts=2 * 1024 * 1024)(along_x)
-    along_yz = all_to_all(summed.reshape(NY * NZH, 2, GCAP, BS), ("y", "zh"))
-
-    w0 = call(select_kernel, like((WCAP, BS // NX, BS), bf16), 2, 1, byts=1024 * 1024)(info, code, gathered)
-    w2, w1, w3 = (shift(w0, "x", NX, k) for k in (2, 1, 3))
+    part = (NY, 2, GCAP, BS)
+    keep, send_zh = call(sum_kernel, (like(part, f32), like(part, bf16)), 1, 1, byts=2 * 1024 * 1024)(info, along_x)
+    came_zh = shift(send_zh, "zh", NZH, 1)
+    summed = call(pair_kernel, like(part, bf16), 0, 2, byts=1024 * 1024)(keep, came_zh)
+    along_y = all_to_all(summed, "y")
+
+    picked = call(select_kernel, like((NX, WCAP, BS // NX, BS), bf16), 2, 1, byts=1024 * 1024, n_after=1)(
+        info, code, gathered, along_x
+    )
+    quarters = all_to_all(picked, "x")
 
     out_mine, out_theirs, weights = call(
         forward_kernel,
@@ -475,12 +492,12 @@
             like((WCAP, NX, BS // NX, BS), bf16),
         ),
         2,
-        5,
+        2,
         [pltpu.VMEM((shard_count * 4, tokens, BS), f32)],
         flops=2 * WCAP * BS**3,
         byts=8 * 1024 * 1024,
         n_after=1,
-    )(info, code, hidden, w0, w1, w2, w3, summed)
+    )(info, code, hidden, quarters, summed)
     came = shift(out_theirs, "core", 2, 1)
     hidden_grad = call(
         backward_kernel,
@@ -503,7 +520,7 @@
         [pltpu.VMEM((2, GCAP, BS), f32)],
         byts=1024 * 1024,
         n_after=1,
-    )(send, state_send, along_yz, stacked, s1)
+    )(send, state_send, along_y, stacked, s1)
     shares = all_to_all(shares, SHARD)
     r2, r1, r3 = (shift(s, "zl", NZL, k) for k, s in ((2, s2), (1, s1), (3, s3)))
     projected = call(project_kernel, like(out_grad.shape, bf16), 0, 4, byts=1024 * 1024)(own, r1, r2, r3)

time: 158 us -> 146 us (0.924)
  waiting for transfers between devices: 44.3 us -> 21.6 us
  blocking collectives: 0 us -> 20.7 us
  starting transfers between devices: 60.2 us -> 55 us
  Pallas kernels: 15.6 us -> 13.1 us
  local copies, waits for them, and re-layouts: 13.4 us -> 11.1 us
    all_to_all x0 -> x1, blocking collectives: none -> 20.7 us  [all_to_all(): return lax.all_to_all(values, axis, split_axis=0, concat_axis=0, tiled=True)]
    all_gather x1, waiting for transfers between devices: 11.4 us -> 0.01 us  [shards(): gathered = lax.all_gather(quarter, SHARD, axis=0, tiled=True)]
    ppermute x8 -> x6, waiting for transfers between devices: 13.7 us -> 7.02 us  [shift(): lax.ppermute(values, axis, [(i, (i + step) % count) for i in range(count)])]
    all_to_all x4, starting transfers between devices: 30.5 us -> 24.2 us  [all_to_all(): return lax.all_to_all(values, axis, split_axis=0, concat_axis=0, tiled=True)]
    all_to_all x4, waiting for transfers between devices: 19.2 us -> 14.5 us  [all_to_all(): return lax.all_to_all(values, axis, split_axis=0, concat_axis=0, tiled=True)]
    unnamed x53 -> x37, local copies, waits for them, and re-layouts: 9.06 us -> 6.71 us
    ppermute x8 -> x6, starting transfers between devices: 29.6 us -> 30.8 us  [shift(): lax.ppermute(values, axis, [(i, (i + step) % count) for i in range(count)])]
  transfers between devices with their start and end apart: 13 -> 11, of which waited for: 8 -> 7; matrix products, arithmetic and copies ran while one was open for 5% -> 6% of each run, Pallas kernels for 6% -> 4%
where the time goes in v5:
time: 146 us; the launch traced here: 145 us
  starting transfers between devices  55 us (38%)
  waiting for transfers between devices  21.6 us (15%)
  blocking collectives  20.7 us (14%)
  between operations  17.7 us (12%)
  Pallas kernels  13.1 us (9%)
  local copies, waits for them, and re-layouts  11.1 us (8%)
  other arithmetic  5.88 us (4%)
    ppermute x6, starting transfers between devices, shift(): lax.ppermute(values, axis, [(i, (i + step) % count) for i in range(count)])  30.8 us
    all_to_all x4, starting transfers between devices, all_to_all(): return lax.all_to_all(values, axis, split_axis=0, concat_axis=0, tiled=True)  24.2 us
    all_to_all x1, blocking collectives, all_to_all(): return lax.all_to_all(values, axis, split_axis=0, concat_axis=0, tiled=True)  20.7 us
    all_to_all x4, waiting for transfers between devices, all_to_all(): return lax.all_to_all(values, axis, split_axis=0, concat_axis=0, tiled=True)  14.5 us
    ppermute x6, waiting for transfers between devices, shift(): lax.ppermute(values, axis, [(i, (i + step) % count) for i in range(count)])  7.02 us
    unnamed x37, local copies, waits for them, and re-layouts  6.71 us
  transfers between devices with their start and end apart: 11, of which 7 were waited for; matrix products, arithmetic and copies ran while one was open for 6% of the time, Pallas kernels for 4%

profile of v5, /device:TPU:1, one launch (start us, length us, event | category | flops | bytes accessed | tf_op | source)
XLA Modules:
  0.0 145.3 jit_solution(14638997014689089819)
XLA Ops:
  7.3 1.7 %constant_dynamic-slice_fusion.9 = bf16[1,32,32,128]{3,2,0,1:T(8,128)(2,1)} fusion(bf16[1,32,128,128]{3,2,0,1:T(8,128)(2,1)} %bitcast.130, s32[]{:T(128)S(6)} %select_n.333), kind=kLoop, calls=%fused_computation.174 | loop fusion | bytes 524292 | tf_op jit(solution)/shard_map/dynamic_slice | solution.py:456
  9.0 1.7 %broadcast_in_dim.307 = bf16[4,128,512]{2,1,0:T(8,128)(2,1)} broadcast(bf16[128,512]{1,0:T(8,128)(2,1)} %param.19), dimensions={1,2} | broadcast | bytes 655360 | tf_op jit(solution)/shard_map/broadcast_in_dim | solution.py:454
  10.8 7.8 %all-to-all-start.1 = ((bf16[4,128,512]{2,1,0:T(8,128)(2,1)}), bf16[4,128,512]{2,1,0:T(8,128)(2,1)S(1)}, u32[]{:S(2)}, u32[]{:S(2)}) async-start(bf16[4,128,512]{2,1,0:T(8,128)(2,1)} %broadcast_in_dim.307), calls=%async_computation.2 | async-start | bytes 1048576 | tf_op jit(solution)/shard_map/all_to_all | solution.py:425
  24.0 7.7 %all-to-all-done.1.mine = bf16[4,128,512]{2,1,0:T(8,128)(2,1)S(1)} async-done(((bf16[4,128,512]{2,1,0:T(8,128)(2,1)}), bf16[4,128,512]{2,1,0:T(8,128)(2,1)S(1)}, u32[]{:S(2)}, u32[]{:S(2)}) %all-to-all-start.1) | async-done | bytes 524320 | tf_op jit(solution)/shard_map/all_to_all | solution.py:425
  31.7 4.3 %collective-permute-start = (bf16[4,128,512]{2,1,0:T(8,128)(2,1)S(1)}, bf16[4,128,512]{2,1,0:T(8,128)(2,1)S(1)}, u32[]{:S(2)}, u32[]{:S(2)}) collective-permute-start(bf16[4,128,512]{2,1,0:T(8,128)(2,1)S(1)} %all-to-all-done.1.mine), channel_id=1, source_target_pairs={{0,1},{1,0},{2,3},{3,2},{4,5},{5,4},{6,7},{7,6},{8,9},{9,8},{10,11... | collective-permute-start | bytes 1572872 | tf_op jit(solution)/shard_map/ppermute | solution.py:429
  36.0 1.2 and_select_fusion.3
  37.5 1.9 %shard_map.147 = (bf16[4,32,40,128]{3,2,1,0:T(8,128)(2,1)S(1)}, bf16[32,128,128]{2,1,0:T(8,128)(2,1)S(1)}) custom-call(s32[6]{0:T(128)S(1)} %stack.27.info, s32[44]{0:T(128)S(1)} %select_reduce_fusion.4.code, bf16[128,1792]{1,0:T(8,128)(2,1)S(1)} %copy-done.7, bf16[4,128,512]{2,1,0:T(8,128)(2,1)S(1)} %all-to-all-done.1.mine, ...), custom_call_target="tpu_custom_call" | custom-call | flops 184549376 | bytes 4194304 | tf_op jit(solution)/shard_map/pallas_call | solution.py:466
  39.4 1.0 copy-done.2
  40.4 20.7 %all_to_all.29.parts._after = bf16[4,32,40,128]{3,2,1,0:T(8,128)(2,1)S(1)} all-to-all(bf16[4,32,40,128]{3,2,1,0:T(8,128)(2,1)S(1)} %get-tuple-element.207), channel_id=1, replica_groups=mesh['y'=8,'x'=4,'zh'=2,'zl'=4,'core'=2] {'x'}, dimensions={0} | all-to-all | bytes 2621440 | tf_op jit(solution)/shard_map/all_to_all | solution.py:425
  61.1 1.6 %copy-done.1 = bf16[1,256,32,128]{3,2,0,1:T(8,128)(2,1)S(1)} copy-done((bf16[1,256,32,128]{3,2,0,1:T(8,128)(2,1)S(1)}, bf16[1,256,32,128]{3,2,0,1:T(8,128)(2,1)}, u32[]{:S(2)}) %copy-start.1) | copy-done | bytes 2097176
  62.7 0.8 shard_map.150
  63.5 1.1 copy-done
  64.6 3.5 %all-to-all-start.4 = ((bf16[4,44,32,128]{3,2,1,0:T(8,128)(2,1)}), bf16[4,44,32,128]{3,2,1,0:T(8,128)(2,1)S(1)}, u32[]{:S(2)}, u32[]{:S(2)}) async-start(bf16[4,44,32,128]{3,2,1,0:T(8,128)(2,1)} %copy-done), calls=%async_computation.5 | async-start | bytes 2883584 | tf_op jit(solution)/shard_map/all_to_all | solution.py:425
  68.9 11.0 %collective-permute-start.1 = (bf16[8,2,40,128]{3,2,1,0:T(8,128)(2,1)S(1)}, bf16[8,2,40,128]{3,2,1,0:T(8,128)(2,1)S(1)}, u32[]{:S(2)}, u32[]{:S(2)}) collective-permute-start(bf16[8,2,40,128]{3,2,1,0:T(8,128)(2,1)S(1)} %get-tuple-element.209), channel_id=1, source_target_pairs={{0,8},{8,0},{1,9},{9,1},{2,10},{10,2},{3,11},{11,3},{4,12},{12,4},... | collective-permute-start | bytes 491528 | tf_op jit(solution)/shard_map/ppermute | solution.py:429
  79.9 2.8 %collective-permute-done.1.came = bf16[8,2,40,128]{3,2,1,0:T(8,128)(2,1)S(1)} collective-permute-done((bf16[8,2,40,128]{3,2,1,0:T(8,128)(2,1)S(1)}, bf16[8,2,40,128]{3,2,1,0:T(8,128)(2,1)S(1)}, u32[]{:S(2)}, u32[]{:S(2)}) %collective-permute-start.1) | collective-permute-done | bytes 163872 | tf_op jit(solution)/shard_map/ppermute | solution.py:429
  83.4 2.1 %all-to-all-done.4.quarters = bf16[4,44,32,128]{3,2,1,0:T(8,128)(2,1)S(1)} async-done(((bf16[4,44,32,128]{3,2,1,0:T(8,128)(2,1)}), bf16[4,44,32,128]{3,2,1,0:T(8,128)(2,1)S(1)}, u32[]{:S(2)}, u32[]{:S(2)}) %all-to-all-start.4) | async-done | bytes 1441824 | tf_op jit(solution)/shard_map/all_to_all | solution.py:425
  85.5 2.8 %shard_map.151 = (f32[4,4,128,128]{3,2,1,0:T(8,128)S(1)}, f32[4,4,128,128]{3,2,1,0:T(8,128)}, bf16[44,4,32,128]{3,2,1,0:T(8,128)(2,1)S(1)}) custom-call(s32[6]{0:T(128)S(1)} %stack.27.info, s32[44]{0:T(128)S(1)} %select_reduce_fusion.4.code, bf16[128,1792]{1,0:T(8,128)(2,1)S(1)} %copy-done.7, bf16[4,44,32,128]{3,2,1,0:T(8,128)(2,1)S(1)} %all-to-all-done.4.quarters, ...), custom_call_target="tpu_custom_call" | custom-call | flops 184549376 | bytes 8388608 | tf_op jit(solution)/shard_map/pallas_call | solution.py:487
  88.3 1.0 copy-done.4
  89.3 5.2 %collective-permute-start.2 = (f32[4,4,128,128]{3,2,1,0:T(8,128)}, f32[4,4,128,128]{3,2,1,0:T(8,128)S(1)}, u32[]{:S(2)}, u32[]{:S(2)}) collective-permute-start(f32[4,4,128,128]{3,2,1,0:T(8,128)} %get-tuple-element.211), channel_id=1, source_target_pairs={{0,1},{1,0},{2,3},{3,2},{4,5},{5,4},{6,7},{7,6},{8,9},{9,8},{10,11... | collective-permute-start | bytes 3145736 | tf_op jit(solution)/shard_map/ppermute | solution.py:429
  94.6 0.9 dynamic-slice_convert_fusion
  95.6 8.0 %all-to-all-start.3 = ((bf16[8,2,40,128]{3,2,1,0:T(8,128)(2,1)}), bf16[8,2,40,128]{3,2,1,0:T(8,128)(2,1)S(1)}, u32[]{:S(2)}, u32[]{:S(2)}) async-start(bf16[8,2,40,128]{3,2,1,0:T(8,128)(2,1)} %shard_map.149._after), calls=%async_computation.4 | async-start | bytes 327680 | tf_op jit(solution)/shard_map/all_to_all | solution.py:425
  103.7 1.2 copy-done.3
  104.9 1.7 %shard_map.152._after = bf16[128,1792]{1,0:T(8,128)(2,1)S(1)} custom-call(s32[6]{0:T(128)S(1)} %stack.27.info, s32[44]{0:T(128)S(1)} %select_reduce_fusion.4.code, bf16[32,128,128]{2,1,0:T(8,128)(2,1)S(1)} %copy-done.3, bf16[44,4,32,128]{3,2,1,0:T(8,128)(2,1)S(1)} %get-tuple-element.213.weights), custom_call_target="tpu_custom_call" | custom-call | flops 184549376 | bytes 4194304 | tf_op jit(solution)/shard_map/pallas_call | solution.py:502
  108.1 4.7 %all-to-all-done.3.parts = bf16[8,2,40,128]{3,2,1,0:T(8,128)(2,1)S(1)} async-done(((bf16[8,2,40,128]{3,2,1,0:T(8,128)(2,1)}), bf16[8,2,40,128]{3,2,1,0:T(8,128)(2,1)S(1)}, u32[]{:S(2)}, u32[]{:S(2)}) %all-to-all-start.3) | async-done | bytes 163872 | tf_op jit(solution)/shard_map/all_to_all | solution.py:425
  112.8 1.4 shard_map.154
  114.2 4.9 %all-to-all-start.5 = ((f32[8,40,128]{2,1,0:T(8,128)}), f32[8,40,128]{2,1,0:T(8,128)S(1)}, u32[]{:S(2)}, u32[]{:S(2)}) async-start(f32[8,40,128]{2,1,0:T(8,128)} %shard_map.154), calls=%async_computation.6 | async-start | bytes 327680 | tf_op jit(solution)/shard_map/all_to_all | solution.py:425
  119.1 3.3 %collective-permute-start.3 = (bf16[4,128,128]{2,1,0:T(8,128)(2,1)S(1)}, bf16[4,128,128]{2,1,0:T(8,128)(2,1)S(1)}, u32[]{:S(2)}, u32[]{:S(2)}) collective-permute-start(bf16[4,128,128]{2,1,0:T(8,128)(2,1)S(1)} %get-tuple-element.214._after), channel_id=1, source_target_pairs={{0,2},{2,4},{4,6},{6,0},{1,3},{3,5},{5,7},{7,1},{8,10},{10,12},{12... | collective-permute-start | bytes 393224 | tf_op jit(solution)/shard_map/ppermute | solution.py:429
  122.4 4.0 %collective-permute-start.4 = (bf16[4,128,128]{2,1,0:T(8,128)(2,1)S(1)}, bf16[4,128,128]{2,1,0:T(8,128)(2,1)S(1)}, u32[]{:S(2)}, u32[]{:S(2)}) collective-permute-start(bf16[4,128,128]{2,1,0:T(8,128)(2,1)S(1)} %get-tuple-element.219), channel_id=1, source_target_pairs={{0,4},{2,6},{4,0},{6,2},{1,5},{3,7},{5,1},{7,3},{8,12},{10,14},{12... | collective-permute-start | bytes 393224 | tf_op jit(solution)/shard_map/ppermute | solution.py:429
  126.4 3.1 %collective-permute-start.5 = (bf16[4,128,128]{2,1,0:T(8,128)(2,1)S(1)}, bf16[4,128,128]{2,1,0:T(8,128)(2,1)S(1)}, u32[]{:S(2)}, u32[]{:S(2)}) collective-permute-start(bf16[4,128,128]{2,1,0:T(8,128)(2,1)S(1)} %get-tuple-element.220), channel_id=1, source_target_pairs={{0,6},{2,0},{4,2},{6,4},{1,7},{3,1},{5,3},{7,5},{8,14},{10,8},{12,... | collective-permute-start | bytes 393224 | tf_op jit(solution)/shard_map/ppermute | solution.py:429
  131.7 3.1 %collective-permute-done.4.r2 = bf16[4,128,128]{2,1,0:T(8,128)(2,1)S(1)} collective-permute-done((bf16[4,128,128]{2,1,0:T(8,128)(2,1)S(1)}, bf16[4,128,128]{2,1,0:T(8,128)(2,1)S(1)}, u32[]{:S(2)}, u32[]{:S(2)}) %collective-permute-start.4) | collective-permute-done | bytes 131104 | tf_op jit(solution)/shard_map/ppermute | solution.py:429
  134.8 0.9 collective-permute-done.5.r3
  136.4 1.8 %shard_map.155 = (f32[32,256]{1,0:T(8,128)}, f32[32,256]{1,0:T(8,128)}, f32[32,256]{1,0:T(8,128)}) custom-call(s32[32]{0:T(128)S(1)} %select_reduce_fusion.5.place, f32[32,768]{1,0:T(8,128)S(1)} %pad_maximum_fusion.1.stacked, f32[8,40,128]{2,1,0:T(8,128)S(1)} %all-to-all-done.5.came), custom_call_target="tpu_custom_call" | custom-call | bytes 1048576 | tf_op jit(solution)/shard_map/pallas_call | solution.py:529
  (74 shorter events, 8.8 us)
Async XLA Ops:
  7.2 11.4 %copy-start.12 = (s32[8,32]{1,0:T(8,128)S(1)}, s32[8,32]{1,0:T(8,128)}, u32[]{:S(2)}) copy-start(s32[8,32]{1,0:T(8,128)} %param.24) | copy-start | bytes 3076
  7.2 11.5 %copy-start.17 = (s32[8]{0:T(128)S(1)}, s32[8]{0:T(128)}, u32[]{:S(2)}) copy-start(s32[8]{0:T(128)} %param.23) | copy-start | bytes 100
  7.2 30.3 %copy-start.7 = (bf16[128,1792]{1,0:T(8,128)(2,1)S(1)}, bf16[128,1792]{1,0:T(8,128)(2,1)}, u32[]{:S(2)}) copy-start(bf16[128,1792]{1,0:T(8,128)(2,1)} %hidden.3) | copy-start | bytes 1376260
  7.2 53.9 %all-gather.12.cloned.1.call-start = ((), (), s32[]{:S(2)}) async-start(), calls=%async_computation.11 | async-start | bytes 2359296 | tf_op jit(solution)/shard_map/all_gather | solution.py:457
  10.8 20.9 %all-to-all-start.1 = ((bf16[4,128,512]{2,1,0:T(8,128)(2,1)}), bf16[4,128,512]{2,1,0:T(8,128)(2,1)S(1)}, u32[]{:S(2)}, u32[]{:S(2)}) async-start(bf16[4,128,512]{2,1,0:T(8,128)(2,1)} %broadcast_in_dim.307), calls=%async_computation.2 | async-start | bytes 1048576 | tf_op jit(solution)/shard_map/all_to_all | solution.py:425
  31.7 5.8 %collective-permute-start = (bf16[4,128,512]{2,1,0:T(8,128)(2,1)S(1)}, bf16[4,128,512]{2,1,0:T(8,128)(2,1)S(1)}, u32[]{:S(2)}, u32[]{:S(2)}) collective-permute-start(bf16[4,128,512]{2,1,0:T(8,128)(2,1)S(1)} %all-to-all-done.1.mine), channel_id=1, source_target_pairs={{0,1},{1,0},{2,3},{3,2},{4,5},{5,4},{6,7},{7,6},{8,9},{9,8},{10,11... | collective-permute-start | bytes 1572872 | tf_op jit(solution)/shard_map/ppermute | solution.py:429
  39.4 1.0 copy-start.2
  61.1 1.6 %copy-start.1 = (bf16[1,256,32,128]{3,2,0,1:T(8,128)(2,1)S(1)}, bf16[1,256,32,128]{3,2,0,1:T(8,128)(2,1)}, u32[]{:S(2)}) copy-start(bf16[1,256,32,128]{3,2,0,1:T(8,128)(2,1)} %all-gather.12.cloned.1.call-done) | copy-start | bytes 6291460
  63.5 1.1 copy-start
  64.6 20.9 %all-to-all-start.4 = ((bf16[4,44,32,128]{3,2,1,0:T(8,128)(2,1)}), bf16[4,44,32,128]{3,2,1,0:T(8,128)(2,1)S(1)}, u32[]{:S(2)}, u32[]{:S(2)}) async-start(bf16[4,44,32,128]{3,2,1,0:T(8,128)(2,1)} %copy-done), calls=%async_computation.5 | async-start | bytes 2883584 | tf_op jit(solution)/shard_map/all_to_all | solution.py:425
  68.2 27.3 %copy-start.10 = (f32[1,32,256]{2,1,0:T(8,128)S(1)}, f32[1,32,256]{2,1,0:T(8,128)}, u32[]{:S(2)}) copy-start(f32[1,32,256]{2,1,0:T(8,128)} %param.26) | copy-start | bytes 98308
  68.2 27.3 %copy-start.11 = (f32[1,32,256]{2,1,0:T(8,128)S(1)}, f32[1,32,256]{2,1,0:T(8,128)}, u32[]{:S(2)}) copy-start(f32[1,32,256]{2,1,0:T(8,128)} %param.27) | copy-start | bytes 98308
  68.9 13.8 %collective-permute-start.1 = (bf16[8,2,40,128]{3,2,1,0:T(8,128)(2,1)S(1)}, bf16[8,2,40,128]{3,2,1,0:T(8,128)(2,1)S(1)}, u32[]{:S(2)}, u32[]{:S(2)}) collective-permute-start(bf16[8,2,40,128]{3,2,1,0:T(8,128)(2,1)S(1)} %get-tuple-element.209), channel_id=1, source_target_pairs={{0,8},{8,0},{1,9},{9,1},{2,10},{10,2},{3,11},{11,3},{4,12},{12,4},... | collective-permute-start | bytes 491528 | tf_op jit(solution)/shard_map/ppermute | solution.py:429
  88.3 1.0 copy-start.4
  89.3 17.4 %collective-permute-start.2 = (f32[4,4,128,128]{3,2,1,0:T(8,128)}, f32[4,4,128,128]{3,2,1,0:T(8,128)S(1)}, u32[]{:S(2)}, u32[]{:S(2)}) collective-permute-start(f32[4,4,128,128]{3,2,1,0:T(8,128)} %get-tuple-element.211), channel_id=1, source_target_pairs={{0,1},{1,0},{2,3},{3,2},{4,5},{5,4},{6,7},{7,6},{8,9},{9,8},{10,11... | collective-permute-start | bytes 3145736 | tf_op jit(solution)/shard_map/ppermute | solution.py:429
  95.6 17.2 %all-to-all-start.3 = ((bf16[8,2,40,128]{3,2,1,0:T(8,128)(2,1)}), bf16[8,2,40,128]{3,2,1,0:T(8,128)(2,1)S(1)}, u32[]{:S(2)}, u32[]{:S(2)}) async-start(bf16[8,2,40,128]{3,2,1,0:T(8,128)(2,1)} %shard_map.149._after), calls=%async_computation.4 | async-start | bytes 327680 | tf_op jit(solution)/shard_map/all_to_all | solution.py:425
  103.7 1.2 copy-start.3
  104.9 2.5 %copy-start.5 = (f32[4,4,128,128]{3,2,1,0:T(8,128)S(1)}, f32[4,4,128,128]{3,2,1,0:T(8,128)}, u32[]{:S(2)}) copy-start(f32[4,4,128,128]{3,2,1,0:T(8,128)} %copy-done.4) | copy-start | bytes 3145732
  106.7 0.8 copy-start.8
  106.7 22.8 %copy-start.14 = (s32[8,32]{1,0:T(8,128)S(1)}, s32[8,32]{1,0:T(8,128)}, u32[]{:S(2)}) copy-start(s32[8,32]{1,0:T(8,128)} %param.25) | copy-start | bytes 3076
  106.7 24.8 %copy-start.15 = (s32[256]{0:T(256)S(1)}, s32[256]{0:T(256)}, u32[]{:S(2)}) copy-start(s32[256]{0:T(256)} %get-tuple-element.402) | copy-start | bytes 3076
  106.7 24.8 %copy-start.16 = (pred[256]{0:T(512)(128)(4,1)S(1)}, pred[256]{0:T(512)(128)(4,1)}, u32[]{:S(2)}) copy-start(pred[256]{0:T(512)(128)(4,1)} %get-tuple-element.376) | copy-start | bytes 772
  107.5 30.8 %copy-start.9 = (bf16[128,512]{1,0:T(8,128)(2,1)S(1)}, bf16[128,512]{1,0:T(8,128)(2,1)}, u32[]{:S(2)}) copy-start(bf16[128,512]{1,0:T(8,128)(2,1)} %param.19) | copy-start | bytes 393220
  107.5 30.8 %copy-start.13 = (s32[8,32]{1,0:T(8,128)S(1)}, s32[8,32]{1,0:T(8,128)}, u32[]{:S(2)}) copy-start(s32[8,32]{1,0:T(8,128)} %param.24) | copy-start | bytes 3076
  107.5 30.8 %copy-start.18 = (s32[8]{0:T(128)S(1)}, s32[8]{0:T(128)}, u32[]{:S(2)}) copy-start(s32[8]{0:T(128)} %param.23) | copy-start | bytes 100
  114.2 22.2 %all-to-all-start.5 = ((f32[8,40,128]{2,1,0:T(8,128)}), f32[8,40,128]{2,1,0:T(8,128)S(1)}, u32[]{:S(2)}, u32[]{:S(2)}) async-start(f32[8,40,128]{2,1,0:T(8,128)} %shard_map.154), calls=%async_computation.6 | async-start | bytes 327680 | tf_op jit(solution)/shard_map/all_to_all | solution.py:425
  119.1 12.6 %collective-permute-start.3 = (bf16[4,128,128]{2,1,0:T(8,128)(2,1)S(1)}, bf16[4,128,128]{2,1,0:T(8,128)(2,1)S(1)}, u32[]{:S(2)}, u32[]{:S(2)}) collective-permute-start(bf16[4,128,128]{2,1,0:T(8,128)(2,1)S(1)} %get-tuple-element.214._after), channel_id=1, source_target_pairs={{0,2},{2,4},{4,6},{6,0},{1,3},{3,5},{5,7},{7,1},{8,10},{10,12},{12... | collective-permute-start | bytes 393224 | tf_op jit(solution)/shard_map/ppermute | solution.py:429
  122.4 12.4 %collective-permute-start.4 = (bf16[4,128,128]{2,1,0:T(8,128)(2,1)S(1)}, bf16[4,128,128]{2,1,0:T(8,128)(2,1)S(1)}, u32[]{:S(2)}, u32[]{:S(2)}) collective-permute-start(bf16[4,128,128]{2,1,0:T(8,128)(2,1)S(1)} %get-tuple-element.219), channel_id=1, source_target_pairs={{0,4},{2,6},{4,0},{6,2},{1,5},{3,7},{5,1},{7,3},{8,12},{10,14},{12... | collective-permute-start | bytes 393224 | tf_op jit(solution)/shard_map/ppermute | solution.py:429
  126.4 9.3 %collective-permute-start.5 = (bf16[4,128,128]{2,1,0:T(8,128)(2,1)S(1)}, bf16[4,128,128]{2,1,0:T(8,128)(2,1)S(1)}, u32[]{:S(2)}, u32[]{:S(2)}) collective-permute-start(bf16[4,128,128]{2,1,0:T(8,128)(2,1)S(1)} %get-tuple-element.220), channel_id=1, source_target_pairs={{0,6},{2,0},{4,2},{6,4},{1,7},{3,1},{5,3},{7,5},{8,14},{10,8},{12,... | collective-permute-start | bytes 393224 | tf_op jit(solution)/shard_map/ppermute | solution.py:429
Sparse Core Ops, SparseCore 0:
  10.9 46.1 all-gather.11

commit v6 on v4

--- a/solution.py
+++ b/solution.py
@@ -190,7 +190,7 @@
 UNROLL = 4
 NX, NY, NZH, NZL = 4, 8, 2, 4
 BS = 128
-VMEM_LIMIT = 14 * 1024 * 1024
+VMEM_LIMIT = 4 * 1024 * 1024
 f32 = jnp.float32
 bf16 = jnp.bfloat16
 i32 = jnp.int32
@@ -298,12 +298,18 @@
     lax.fori_loop(0, out.shape[0], step, 0, unroll=4)
 
 
-def share_kernel(scale, send, state_send, parts, stacked, _after, out, total):
-    for b in range(2):
-        value = parts[0, b].astype(f32)
-        for n in range(1, parts.shape[0]):
-            value += parts[n, b].astype(f32)
-        total[b] = value * scale
+def pair_kernel(info, parts, keep, send):
+    my_zh = info[5]
+    for out, zh in ((keep, my_zh), (send, 1 - my_zh)):
+        for b in range(2):
+            value = parts[0, 2 * zh + b].astype(f32)
+            for n in range(1, parts.shape[0]):
+                value += parts[n, 2 * zh + b].astype(f32)
+            out[b] = value
+
+
+def share_kernel(scale, send, state_send, keep, came, stacked, _after, out, total):
+    total[...] = (keep[...] + came[...]) * scale
     width = stacked.shape[1] // BS
     for d in range(out.shape[0]):
         for p in range(PAIR):
@@ -317,7 +323,7 @@
                 out[d, at : at + 1, :] = row[:, n * BS : (n + 1) * BS]
 
 
-def select_kernel(info, code, gathered, out):
+def select_kernel(info, code, gathered, _after, out):
     def step(c, carry):
         value = gathered[code[c] & 255]
         out[c] = jnp.where(c < info[0], value, jnp.zeros_like(value))
@@ -326,17 +332,23 @@
     lax.fori_loop(0, WCAP, step, 0, unroll=4)
 
 
-def forward_kernel(info, code, hidden, w0, w1, w2, w3, _after, mine, theirs, weights, total):
+def forward_kernel(info, code, hidden, w0, w1, w2, w3, _after, mine, theirs, weights, total, sems):
     my_core, my_x = info[2], info[3]
+    copies = [
+        pltpu.make_async_copy(part, weights.at[:, (my_x + NX - k) % NX], sems.at[k])
+        for k, part in enumerate((w0, w1, w2, w3))
+    ]
+    for copy in copies:
+        copy.start()
     total[...] = jnp.zeros_like(total)
+    for copy in copies:
+        copy.wait()
 
     def step(i, carry):
         adds = []
         for u in range(UNROLL):
             c = i * UNROLL + u
             word = code[c]
-            for k, part in enumerate((w0, w1, w2, w3)):
-                weights[c, (my_x + NX - k) % NX] = part[c]
             lanes = pl.ds(pl.multiple_of(((word >> 8) & 15) * BS, BS), BS)
             w = weights[c].reshape(BS, BS)
             adds.append((word >> 12, jnp.dot(hidden[:, lanes], w, preferred_element_type=f32)))
@@ -449,7 +461,7 @@
     fits, code, counts, send, state_send, place = make_plan(
         block_row, block_col, live_count, new_owner, new_slot, row_local, me
     )
-    info = jnp.stack(counts + [lax.axis_index("core"), x_index, lax.axis_index("zl")])
+    info = jnp.stack(counts + [lax.axis_index("core"), x_index, lax.axis_index("zl"), lax.axis_index("zh")])
 
     partial, cols = call(
         grad_kernel,
@@ -462,10 +474,15 @@
     )(info, code, hidden, mine, other)
     along_x = all_to_all(partial, "x")
     summed = call(sum_kernel, like(partial.shape[1:], bf16), 0, 1, byts=2 * 1024 * 1024)(along_x)
-    along_yz = all_to_all(summed.reshape(NY * NZH, 2, GCAP, BS), ("y", "zh"))
-
-    w0 = call(select_kernel, like((WCAP, BS // NX, BS), bf16), 2, 1, byts=1024 * 1024)(info, code, gathered)
-    w2, w1, w3 = (shift(w0, "x", NX, k) for k in (2, 1, 3))
+    along_y = all_to_all(summed.reshape(NY, 2 * NZH, GCAP, BS), "y")
+    part = (2, GCAP, BS)
+    keep, send_zh = call(pair_kernel, (like(part, f32), like(part, f32)), 1, 1, byts=1024 * 1024)(info, along_y)
+    came_zh = shift(send_zh, "zh", NZH, 1)
+
+    picked = call(select_kernel, like((WCAP, BS // NX, BS), bf16), 2, 1, byts=1024 * 1024, n_after=1)(
+        info, code, gathered, summed
+    )
+    w2, w1, w3 = (shift(picked, "x", NX, k) for k in (2, 1, 3))
 
     out_mine, out_theirs, weights = call(
         forward_kernel,
@@ -475,12 +492,12 @@
             like((WCAP, NX, BS // NX, BS), bf16),
         ),
         2,
-        5,
-        [pltpu.VMEM((shard_count * 4, tokens, BS), f32)],
+        1,
+        [pltpu.VMEM((shard_count * 4, tokens, BS), f32), pltpu.SemaphoreType.DMA((NX,))],
         flops=2 * WCAP * BS**3,
         byts=8 * 1024 * 1024,
-        n_after=1,
-    )(info, code, hidden, w0, w1, w2, w3, summed)
+        n_after=5,
+    )(info, code, hidden, picked, w1, w2, w3, keep)
     came = shift(out_theirs, "core", 2, 1)
     hidden_grad = call(
         backward_kernel,
@@ -491,20 +508,20 @@
         flops=2 * WCAP * BS**3,
         byts=4 * 1024 * 1024,
     )(info, code, cols, weights)
+    packed = call(
+        functools.partial(share_kernel, scale),
+        like((shard_count, 2 * PAIR + MV * stacked.shape[1] // BS, BS), f32),
+        2,
+        3,
+        [pltpu.VMEM((2, GCAP, BS), f32)],
+        byts=1024 * 1024,
+        n_after=1,
+    )(send, state_send, keep, came_zh, stacked, hidden_grad)
+    shares = all_to_all(packed, SHARD)
     part = (4, tokens, BS)
     own, s1, s2, s3 = call(
         chip_kernel, (like(part, f32),) + (like(part, bf16),) * 3, 1, 2, byts=3 * 1024 * 1024, n_after=1
-    )(info, out_mine, came, hidden_grad)
-    shares = call(
-        functools.partial(share_kernel, scale),
-        like((shard_count, 2 * PAIR + MV * stacked.shape[1] // BS, BS), f32),
-        2,
-        2,
-        [pltpu.VMEM((2, GCAP, BS), f32)],
-        byts=1024 * 1024,
-        n_after=1,
-    )(send, state_send, along_yz, stacked, s1)
-    shares = all_to_all(shares, SHARD)
+    )(info, out_mine, came, packed)
     r2, r1, r3 = (shift(s, "zl", NZL, k) for k, s in ((2, s2), (1, s1), (3, s3)))
     projected = call(project_kernel, like(out_grad.shape, bf16), 0, 4, byts=1024 * 1024)(own, r1, r2, r3)
 

time: 158 us -> 147 us (0.930)
  blocking collectives: 0 us -> 21.1 us
  waiting for transfers between devices: 44.3 us -> 23.2 us
  starting transfers between devices: 60.2 us -> 53 us
  other arithmetic: 5.87 us -> 3.35 us
    all_to_all x0 -> x1, blocking collectives: none -> 21.1 us  [all_to_all(): return lax.all_to_all(values, axis, split_axis=0, concat_axis=0, tiled=True)]
    all_to_all x4 -> x3, starting transfers between devices: 30.5 us -> 18.4 us  [all_to_all(): return lax.all_to_all(values, axis, split_axis=0, concat_axis=0, tiled=True)]
    all_gather x1, waiting for transfers between devices: 11.4 us -> 0.01 us  [shards(): gathered = lax.all_gather(quarter, SHARD, axis=0, tiled=True)]
    all_to_all x4 -> x3, waiting for transfers between devices: 19.2 us -> 7.99 us  [all_to_all(): return lax.all_to_all(values, axis, split_axis=0, concat_axis=0, tiled=True)]
    ppermute x8 -> x9, starting transfers between devices: 29.6 us -> 34.6 us  [shift(): lax.ppermute(values, axis, [(i, (i + step) % count) for i in range(count)])]
    ppermute x8 -> x9, waiting for transfers between devices: 13.7 us -> 15.2 us  [shift(): lax.ppermute(values, axis, [(i, (i + step) % count) for i in range(count)])]
    unnamed x53 -> x37, local copies, waits for them, and re-layouts: 9.06 us -> 8 us
  transfers between devices with their start and end apart: 13 -> 13, of which waited for: 8 -> 7; matrix products, arithmetic and copies ran while one was open for 5% -> 4% of each run, Pallas kernels for 6% -> 7%
where the time goes in v6:
time: 147 us; the launch traced here: 146 us
  starting transfers between devices  53 us (36%)
  waiting for transfers between devices  23.2 us (16%)
  blocking collectives  21.1 us (14%)
  between operations  17.6 us (12%)
  Pallas kernels  15.1 us (10%)
  local copies, waits for them, and re-layouts  12.4 us (8%)
  other arithmetic  3.35 us (2%)
    ppermute x9, starting transfers between devices, shift(): lax.ppermute(values, axis, [(i, (i + step) % count) for i in range(count)])  34.6 us
    all_to_all x1, blocking collectives, all_to_all(): return lax.all_to_all(values, axis, split_axis=0, concat_axis=0, tiled=True)  21.1 us
    all_to_all x3, starting transfers between devices, all_to_all(): return lax.all_to_all(values, axis, split_axis=0, concat_axis=0, tiled=True)  18.4 us
    ppermute x9, waiting for transfers between devices, shift(): lax.ppermute(values, axis, [(i, (i + step) % count) for i in range(count)])  15.2 us
    unnamed x37, local copies, waits for them, and re-layouts  8 us
    all_to_all x3, waiting for transfers between devices, all_to_all(): return lax.all_to_all(values, axis, split_axis=0, concat_axis=0, tiled=True)  7.99 us
    pallas_call x1, Pallas kernels, shards(): call(forward_kernel, (like((NZL, 4, tokens, BS), f32), like((NZL, 4, toke...  3.53 us
  transfers between devices with their start and end apart: 13, of which 7 were waited for; matrix products, arithmetic and copies ran while one was open for 4% of the time, Pallas kernels for 7%

profile of v6, /device:TPU:1, one launch (start us, length us, event | category | flops | bytes accessed | tf_op | source)
XLA Modules:
  0.0 145.7 jit_solution(8553598048723123784)
XLA Ops:
  7.2 1.8 %broadcast_in_dim.304 = bf16[4,128,512]{2,1,0:T(8,128)(2,1)} broadcast(bf16[128,512]{1,0:T(8,128)(2,1)} %param.19), dimensions={1,2} | broadcast | bytes 655360 | tf_op jit(solution)/shard_map/broadcast_in_dim | solution.py:454
  9.0 7.8 %all-to-all-start.1 = ((bf16[4,128,512]{2,1,0:T(8,128)(2,1)}), bf16[4,128,512]{2,1,0:T(8,128)(2,1)S(1)}, u32[]{:S(2)}, u32[]{:S(2)}) async-start(bf16[4,128,512]{2,1,0:T(8,128)(2,1)} %broadcast_in_dim.304), calls=%async_computation.2 | async-start | bytes 1048576 | tf_op jit(solution)/shard_map/all_to_all | solution.py:425
  16.8 1.7 %constant_dynamic-slice_fusion.9 = bf16[1,32,32,128]{3,2,0,1:T(8,128)(2,1)} fusion(bf16[1,32,128,128]{3,2,0,1:T(8,128)(2,1)} %bitcast.131, s32[]{:T(128)S(6)} %select_n.333), kind=kLoop, calls=%fused_computation.174 | loop fusion | bytes 524292 | tf_op jit(solution)/shard_map/dynamic_slice | solution.py:456
  22.0 7.9 %all-to-all-done.1.mine = bf16[4,128,512]{2,1,0:T(8,128)(2,1)S(1)} async-done(((bf16[4,128,512]{2,1,0:T(8,128)(2,1)}), bf16[4,128,512]{2,1,0:T(8,128)(2,1)S(1)}, u32[]{:S(2)}, u32[]{:S(2)}) %all-to-all-start.1) | async-done | bytes 524320 | tf_op jit(solution)/shard_map/all_to_all | solution.py:425
  30.0 4.2 %collective-permute-start = (bf16[4,128,512]{2,1,0:T(8,128)(2,1)S(1)}, bf16[4,128,512]{2,1,0:T(8,128)(2,1)S(1)}, u32[]{:S(2)}, u32[]{:S(2)}) collective-permute-start(bf16[4,128,512]{2,1,0:T(8,128)(2,1)S(1)} %all-to-all-done.1.mine), channel_id=1, source_target_pairs={{0,1},{1,0},{2,3},{3,2},{4,5},{5,4},{6,7},{7,6},{8,9},{9,8},{10,11... | collective-permute-start | bytes 1572872 | tf_op jit(solution)/shard_map/ppermute | solution.py:429
  35.7 2.1 %shard_map.147 = (bf16[4,32,40,128]{3,2,1,0:T(8,128)(2,1)S(1)}, bf16[32,128,128]{2,1,0:T(8,128)(2,1)S(1)}) custom-call(s32[6]{0:T(128)S(1)} %stack.27.info, s32[44]{0:T(128)S(1)} %select_reduce_fusion.4.code, bf16[128,1792]{1,0:T(8,128)(2,1)S(1)} %copy-done.8, bf16[4,128,512]{2,1,0:T(8,128)(2,1)S(1)} %all-to-all-done.1.mine, ...), custom_call_target="tpu_custom_call" | custom-call | flops 184549376 | bytes 4194304 | tf_op jit(solution)/shard_map/pallas_call | solution.py:466
  37.8 1.0 copy-done.1
  38.8 21.1 %all_to_all.24.parts = bf16[4,32,40,128]{3,2,1,0:T(8,128)(2,1)S(1)} all-to-all(bf16[4,32,40,128]{3,2,1,0:T(8,128)(2,1)S(1)} %get-tuple-element.207), channel_id=1, replica_groups=mesh['y'=8,'x'=4,'zh'=2,'zl'=4,'core'=2] {'x'}, dimensions={0} | all-to-all | bytes 2621440 | tf_op jit(solution)/shard_map/all_to_all | solution.py:425
  59.9 0.9 shard_map.148._after
  60.8 6.8 %all-to-all-start.3 = ((bf16[8,4,40,128]{3,2,1,0:T(8,128)(2,1)}), bf16[8,4,40,128]{3,2,1,0:T(8,128)(2,1)S(1)}, u32[]{:S(2)}, u32[]{:S(2)}) async-start(bf16[8,4,40,128]{3,2,1,0:T(8,128)(2,1)} %bitcast.45), calls=%async_computation.4 | async-start | bytes 655360 | tf_op jit(solution)/shard_map/all_to_all | solution.py:425
  67.6 1.6 %copy-done = bf16[1,256,32,128]{3,2,0,1:T(8,128)(2,1)S(1)} copy-done((bf16[1,256,32,128]{3,2,0,1:T(8,128)(2,1)S(1)}, bf16[1,256,32,128]{3,2,0,1:T(8,128)(2,1)}, u32[]{:S(2)}) %copy-start) | copy-done | bytes 2097176
  69.9 2.4 %collective-permute-start.2 = (bf16[44,32,128]{2,1,0:T(8,128)(2,1)S(1)}, bf16[44,32,128]{2,1,0:T(8,128)(2,1)S(1)}, u32[]{:S(2)}, u32[]{:S(2)}) collective-permute-start(bf16[44,32,128]{2,1,0:T(8,128)(2,1)S(1)} %shard_map.150.w0), channel_id=1, source_target_pairs={{0,16},{16,32},{32,48},{48,0},{1,17},{17,33},{33,49},{49,1},{2,18}... | collective-permute-start | bytes 1081352 | tf_op jit(solution)/shard_map/ppermute | solution.py:429
  72.4 3.5 %collective-permute-start.3 = (bf16[44,32,128]{2,1,0:T(8,128)(2,1)S(1)}, bf16[44,32,128]{2,1,0:T(8,128)(2,1)S(1)}, u32[]{:S(2)}, u32[]{:S(2)}) collective-permute-start(bf16[44,32,128]{2,1,0:T(8,128)(2,1)S(1)} %shard_map.150.w0), channel_id=1, source_target_pairs={{0,32},{16,48},{32,0},{48,16},{1,33},{17,49},{33,1},{49,17},{2,34}... | collective-permute-start | bytes 1081352 | tf_op jit(solution)/shard_map/ppermute | solution.py:429
  75.9 2.7 %collective-permute-start.4 = (bf16[44,32,128]{2,1,0:T(8,128)(2,1)S(1)}, bf16[44,32,128]{2,1,0:T(8,128)(2,1)S(1)}, u32[]{:S(2)}, u32[]{:S(2)}) collective-permute-start(bf16[44,32,128]{2,1,0:T(8,128)(2,1)S(1)} %shard_map.150.w0), channel_id=1, source_target_pairs={{0,48},{16,0},{32,16},{48,32},{1,49},{17,1},{33,17},{49,33},{2,50}... | collective-permute-start | bytes 1081352 | tf_op jit(solution)/shard_map/ppermute | solution.py:429
  79.2 2.3 %collective-permute-done.2.w1 = bf16[44,32,128]{2,1,0:T(8,128)(2,1)S(1)} collective-permute-done((bf16[44,32,128]{2,1,0:T(8,128)(2,1)S(1)}, bf16[44,32,128]{2,1,0:T(8,128)(2,1)S(1)}, u32[]{:S(2)}, u32[]{:S(2)}) %collective-permute-start.2) | collective-permute-done | bytes 360480 | tf_op jit(solution)/shard_map/ppermute | solution.py:429
  81.5 6.8 %collective-permute-done.3.w2 = bf16[44,32,128]{2,1,0:T(8,128)(2,1)S(1)} collective-permute-done((bf16[44,32,128]{2,1,0:T(8,128)(2,1)S(1)}, bf16[44,32,128]{2,1,0:T(8,128)(2,1)S(1)}, u32[]{:S(2)}, u32[]{:S(2)}) %collective-permute-start.3) | collective-permute-done | bytes 360480 | tf_op jit(solution)/shard_map/ppermute | solution.py:429
  89.1 3.5 %collective-permute-done.4.w3 = bf16[44,32,128]{2,1,0:T(8,128)(2,1)S(1)} collective-permute-done((bf16[44,32,128]{2,1,0:T(8,128)(2,1)S(1)}, bf16[44,32,128]{2,1,0:T(8,128)(2,1)S(1)}, u32[]{:S(2)}, u32[]{:S(2)}) %collective-permute-start.4) | collective-permute-done | bytes 360480 | tf_op jit(solution)/shard_map/ppermute | solution.py:429
  93.3 1.0 copy-done.4
  94.3 1.0 copy-done.6
  95.3 3.5 %shard_map.151 = (f32[4,4,128,128]{3,2,1,0:T(8,128)S(1)}, f32[4,4,128,128]{3,2,1,0:T(8,128)}, bf16[44,4,32,128]{3,2,1,0:T(8,128)(2,1)S(1)}) custom-call(s32[6]{0:T(128)S(1)} %stack.27.info, s32[44]{0:T(128)S(1)} %select_reduce_fusion.4.code, bf16[128,1792]{1,0:T(8,128)(2,1)} %hidden.3, bf16[44,32,128]{2,1,0:T(8,128)(2,1)S(1)} %shard_map.150.w0, ...), custom_call_target="tpu_custom_call" | custom-call | flops 184549376 | bytes 8388608 | tf_op jit(solution)/shard_map/pallas_call | solution.py:487
  98.8 3.7 %collective-permute-start.5 = (f32[4,4,128,128]{3,2,1,0:T(8,128)}, f32[4,4,128,128]{3,2,1,0:T(8,128)}, u32[]{:S(2)}, u32[]{:S(2)}) collective-permute-start(f32[4,4,128,128]{3,2,1,0:T(8,128)} %get-tuple-element.216), channel_id=1, source_target_pairs={{0,1},{1,0},{2,3},{3,2},{4,5},{5,4},{6,7},{7,6},{8,9},{9,8},{10,11... | collective-permute-start | bytes 3145736 | tf_op jit(solution)/shard_map/ppermute | solution.py:429
  103.6 7.8 %collective-permute-start.1 = (f32[2,40,128]{2,1,0:T(8,128)S(1)}, f32[2,40,128]{2,1,0:T(8,128)S(1)}, u32[]{:S(2)}, u32[]{:S(2)}) collective-permute-start(f32[2,40,128]{2,1,0:T(8,128)S(1)} %get-tuple-element.209), channel_id=1, source_target_pairs={{0,8},{8,0},{1,9},{9,1},{2,10},{10,2},{3,11},{11,3},{4,12},{12,4},... | collective-permute-start | bytes 122888 | tf_op jit(solution)/shard_map/ppermute | solution.py:429
  111.5 1.2 copy-done.2
  112.7 2.0 %shard_map.152._after = bf16[128,1792]{1,0:T(8,128)(2,1)S(1)} custom-call(s32[6]{0:T(128)S(1)} %stack.27.info, s32[44]{0:T(128)S(1)} %select_reduce_fusion.4.code, bf16[32,128,128]{2,1,0:T(8,128)(2,1)S(1)} %copy-done.2, bf16[44,4,32,128]{3,2,1,0:T(8,128)(2,1)S(1)} %get-tuple-element.211.weights), custom_call_target="tpu_custom_call" | custom-call | flops 184549376 | bytes 4194304 | tf_op jit(solution)/shard_map/pallas_call | solution.py:502
  115.5 1.4 shard_map.153._after
  116.8 3.8 %all-to-all-start.4 = ((f32[8,40,128]{2,1,0:T(8,128)}), f32[8,40,128]{2,1,0:T(8,128)S(1)}, u32[]{:S(2)}, u32[]{:S(2)}) async-start(f32[8,40,128]{2,1,0:T(8,128)} %shard_map.153._after), calls=%async_computation.5 | async-start | bytes 327680 | tf_op jit(solution)/shard_map/all_to_all | solution.py:425
  120.6 1.3 shard_map.155
  122.0 3.3 %collective-permute-start.6 = (bf16[4,128,128]{2,1,0:T(8,128)(2,1)S(1)}, bf16[4,128,128]{2,1,0:T(8,128)(2,1)S(1)}, u32[]{:S(2)}, u32[]{:S(2)}) collective-permute-start(bf16[4,128,128]{2,1,0:T(8,128)(2,1)S(1)} %get-tuple-element.218), channel_id=1, source_target_pairs={{0,2},{2,4},{4,6},{6,0},{1,3},{3,5},{5,7},{7,1},{8,10},{10,12},{12... | collective-permute-start | bytes 393224 | tf_op jit(solution)/shard_map/ppermute | solution.py:429
  125.3 4.0 %collective-permute-start.7 = (bf16[4,128,128]{2,1,0:T(8,128)(2,1)S(1)}, bf16[4,128,128]{2,1,0:T(8,128)(2,1)S(1)}, u32[]{:S(2)}, u32[]{:S(2)}) collective-permute-start(bf16[4,128,128]{2,1,0:T(8,128)(2,1)S(1)} %get-tuple-element.219), channel_id=1, source_target_pairs={{0,4},{2,6},{4,0},{6,2},{1,5},{3,7},{5,1},{7,3},{8,12},{10,14},{12... | collective-permute-start | bytes 393224 | tf_op jit(solution)/shard_map/ppermute | solution.py:429
  129.3 3.1 %collective-permute-start.8 = (bf16[4,128,128]{2,1,0:T(8,128)(2,1)S(1)}, bf16[4,128,128]{2,1,0:T(8,128)(2,1)S(1)}, u32[]{:S(2)}, u32[]{:S(2)}) collective-permute-start(bf16[4,128,128]{2,1,0:T(8,128)(2,1)S(1)} %get-tuple-element.220), channel_id=1, source_target_pairs={{0,6},{2,0},{4,2},{6,4},{1,7},{3,1},{5,3},{7,5},{8,14},{10,8},{12,... | collective-permute-start | bytes 393224 | tf_op jit(solution)/shard_map/ppermute | solution.py:429
  134.5 1.8 %shard_map.154 = (f32[32,256]{1,0:T(8,128)}, f32[32,256]{1,0:T(8,128)}, f32[32,256]{1,0:T(8,128)}) custom-call(s32[32]{0:T(128)S(1)} %select_reduce_fusion.5.place, f32[32,768]{1,0:T(8,128)S(1)} %pad_maximum_fusion.1.stacked, f32[8,40,128]{2,1,0:T(8,128)S(1)} %all-to-all-done.4.came), custom_call_target="tpu_custom_call" | custom-call | bytes 1048576 | tf_op jit(solution)/shard_map/pallas_call | solution.py:529
  136.3 1.8 %collective-permute-done.8.r3 = bf16[4,128,128]{2,1,0:T(8,128)(2,1)S(1)} collective-permute-done((bf16[4,128,128]{2,1,0:T(8,128)(2,1)S(1)}, bf16[4,128,128]{2,1,0:T(8,128)(2,1)S(1)}, u32[]{:S(2)}, u32[]{:S(2)}) %collective-permute-start.8) | collective-permute-done | bytes 131104 | tf_op jit(solution)/shard_map/ppermute | solution.py:429
  (78 shorter events, 9.4 us)
Async XLA Ops:
  7.2 11.4 %copy-start.14 = (s32[8,32]{1,0:T(8,128)S(1)}, s32[8,32]{1,0:T(8,128)}, u32[]{:S(2)}) copy-start(s32[8,32]{1,0:T(8,128)} %param.24) | copy-start | bytes 3076
  7.2 11.5 %copy-start.15 = (s32[8,32]{1,0:T(8,128)S(1)}, s32[8,32]{1,0:T(8,128)}, u32[]{:S(2)}) copy-start(s32[8,32]{1,0:T(8,128)} %param.21) | copy-start | bytes 3076
  7.2 11.5 %copy-start.18 = (s32[8]{0:T(128)S(1)}, s32[8]{0:T(128)}, u32[]{:S(2)}) copy-start(s32[8]{0:T(128)} %param.23) | copy-start | bytes 100
  7.2 11.7 %copy-start.16 = (s32[8,32]{1,0:T(8,128)S(1)}, s32[8,32]{1,0:T(8,128)}, u32[]{:S(2)}) copy-start(s32[8,32]{1,0:T(8,128)} %param.22) | copy-start | bytes 3076
  7.2 28.5 %copy-start.8 = (bf16[128,1792]{1,0:T(8,128)(2,1)S(1)}, bf16[128,1792]{1,0:T(8,128)(2,1)}, u32[]{:S(2)}) copy-start(bf16[128,1792]{1,0:T(8,128)(2,1)} %hidden.3) | copy-start | bytes 1376260
  9.0 20.9 %all-to-all-start.1 = ((bf16[4,128,512]{2,1,0:T(8,128)(2,1)}), bf16[4,128,512]{2,1,0:T(8,128)(2,1)S(1)}, u32[]{:S(2)}, u32[]{:S(2)}) async-start(bf16[4,128,512]{2,1,0:T(8,128)(2,1)} %broadcast_in_dim.304), calls=%async_computation.2 | async-start | bytes 1048576 | tf_op jit(solution)/shard_map/all_to_all | solution.py:425
  16.8 50.8 %all-gather.12.cloned.1.call-start = ((), (), s32[]{:S(2)}) async-start(), calls=%async_computation.10 | async-start | bytes 2359296 | tf_op jit(solution)/shard_map/all_gather | solution.py:457
  30.0 5.7 %collective-permute-start = (bf16[4,128,512]{2,1,0:T(8,128)(2,1)S(1)}, bf16[4,128,512]{2,1,0:T(8,128)(2,1)S(1)}, u32[]{:S(2)}, u32[]{:S(2)}) collective-permute-start(bf16[4,128,512]{2,1,0:T(8,128)(2,1)S(1)} %all-to-all-done.1.mine), channel_id=1, source_target_pairs={{0,1},{1,0},{2,3},{3,2},{4,5},{5,4},{6,7},{7,6},{8,9},{9,8},{10,11... | collective-permute-start | bytes 1572872 | tf_op jit(solution)/shard_map/ppermute | solution.py:429
  37.8 1.0 copy-start.1
  60.8 17.8 %all-to-all-start.3 = ((bf16[8,4,40,128]{3,2,1,0:T(8,128)(2,1)}), bf16[8,4,40,128]{3,2,1,0:T(8,128)(2,1)S(1)}, u32[]{:S(2)}, u32[]{:S(2)}) async-start(bf16[8,4,40,128]{3,2,1,0:T(8,128)(2,1)} %bitcast.45), calls=%async_computation.4 | async-start | bytes 655360 | tf_op jit(solution)/shard_map/all_to_all | solution.py:425
  67.6 1.6 %copy-start = (bf16[1,256,32,128]{3,2,0,1:T(8,128)(2,1)S(1)}, bf16[1,256,32,128]{3,2,0,1:T(8,128)(2,1)}, u32[]{:S(2)}) copy-start(bf16[1,256,32,128]{3,2,0,1:T(8,128)(2,1)} %all-gather.12.cloned.1.call-done) | copy-start | bytes 6291460
  69.2 34.3 %copy-start.12 = (f32[1,32,256]{2,1,0:T(8,128)S(1)}, f32[1,32,256]{2,1,0:T(8,128)}, u32[]{:S(2)}) copy-start(f32[1,32,256]{2,1,0:T(8,128)} %param.26) | copy-start | bytes 98308
  69.2 34.3 %copy-start.13 = (f32[1,32,256]{2,1,0:T(8,128)S(1)}, f32[1,32,256]{2,1,0:T(8,128)}, u32[]{:S(2)}) copy-start(f32[1,32,256]{2,1,0:T(8,128)} %param.27) | copy-start | bytes 98308
  69.9 11.6 %collective-permute-start.2 = (bf16[44,32,128]{2,1,0:T(8,128)(2,1)S(1)}, bf16[44,32,128]{2,1,0:T(8,128)(2,1)S(1)}, u32[]{:S(2)}, u32[]{:S(2)}) collective-permute-start(bf16[44,32,128]{2,1,0:T(8,128)(2,1)S(1)} %shard_map.150.w0), channel_id=1, source_target_pairs={{0,16},{16,32},{32,48},{48,0},{1,17},{17,33},{33,49},{49,1},{2,18}... | collective-permute-start | bytes 1081352 | tf_op jit(solution)/shard_map/ppermute | solution.py:429
  72.4 16.0 %collective-permute-start.3 = (bf16[44,32,128]{2,1,0:T(8,128)(2,1)S(1)}, bf16[44,32,128]{2,1,0:T(8,128)(2,1)S(1)}, u32[]{:S(2)}, u32[]{:S(2)}) collective-permute-start(bf16[44,32,128]{2,1,0:T(8,128)(2,1)S(1)} %shard_map.150.w0), channel_id=1, source_target_pairs={{0,32},{16,48},{32,0},{48,16},{1,33},{17,49},{33,1},{49,17},{2,34}... | collective-permute-start | bytes 1081352 | tf_op jit(solution)/shard_map/ppermute | solution.py:429
  75.9 16.7 %collective-permute-start.4 = (bf16[44,32,128]{2,1,0:T(8,128)(2,1)S(1)}, bf16[44,32,128]{2,1,0:T(8,128)(2,1)S(1)}, u32[]{:S(2)}, u32[]{:S(2)}) collective-permute-start(bf16[44,32,128]{2,1,0:T(8,128)(2,1)S(1)} %shard_map.150.w0), channel_id=1, source_target_pairs={{0,48},{16,0},{32,16},{48,32},{1,49},{17,1},{33,17},{49,33},{2,50}... | collective-permute-start | bytes 1081352 | tf_op jit(solution)/shard_map/ppermute | solution.py:429
  88.3 0.7 copy-start.3
  92.6 0.7 copy-start.5
  93.3 1.0 copy-start.4
  94.3 1.0 copy-start.6
  98.8 21.8 %collective-permute-start.5 = (f32[4,4,128,128]{3,2,1,0:T(8,128)}, f32[4,4,128,128]{3,2,1,0:T(8,128)}, u32[]{:S(2)}, u32[]{:S(2)}) collective-permute-start(f32[4,4,128,128]{3,2,1,0:T(8,128)} %get-tuple-element.216), channel_id=1, source_target_pairs={{0,1},{1,0},{2,3},{3,2},{4,5},{5,4},{6,7},{7,6},{8,9},{9,8},{10,11... | collective-permute-start | bytes 3145736 | tf_op jit(solution)/shard_map/ppermute | solution.py:429
  103.6 11.1 %collective-permute-start.1 = (f32[2,40,128]{2,1,0:T(8,128)S(1)}, f32[2,40,128]{2,1,0:T(8,128)S(1)}, u32[]{:S(2)}, u32[]{:S(2)}) collective-permute-start(f32[2,40,128]{2,1,0:T(8,128)S(1)} %get-tuple-element.209), channel_id=1, source_target_pairs={{0,8},{8,0},{1,9},{9,1},{2,10},{10,2},{3,11},{11,3},{4,12},{12,4},... | collective-permute-start | bytes 122888 | tf_op jit(solution)/shard_map/ppermute | solution.py:429
  111.5 1.2 copy-start.2
  114.7 0.8 copy-start.10
  114.7 17.7 %copy-start.17 = (s32[8,32]{1,0:T(8,128)S(1)}, s32[8,32]{1,0:T(8,128)}, u32[]{:S(2)}) copy-start(s32[8,32]{1,0:T(8,128)} %param.25) | copy-start | bytes 3076
  114.7 24.1 %copy-start.9 = (bf16[128,1792]{1,0:T(8,128)(2,1)S(1)}, bf16[128,1792]{1,0:T(8,128)(2,1)}, u32[]{:S(2)}) copy-start(bf16[128,1792]{1,0:T(8,128)(2,1)} %hidden.3) | copy-start | bytes 1376260
  114.7 24.1 %copy-start.11 = (bf16[128,512]{1,0:T(8,128)(2,1)S(1)}, bf16[128,512]{1,0:T(8,128)(2,1)}, u32[]{:S(2)}) copy-start(bf16[128,512]{1,0:T(8,128)(2,1)} %param.19) | copy-start | bytes 393220
  116.8 17.6 %all-to-all-start.4 = ((f32[8,40,128]{2,1,0:T(8,128)}), f32[8,40,128]{2,1,0:T(8,128)S(1)}, u32[]{:S(2)}, u32[]{:S(2)}) async-start(f32[8,40,128]{2,1,0:T(8,128)} %shard_map.153._after), calls=%async_computation.5 | async-start | bytes 327680 | tf_op jit(solution)/shard_map/all_to_all | solution.py:425
  122.0 14.3 %collective-permute-start.6 = (bf16[4,128,128]{2,1,0:T(8,128)(2,1)S(1)}, bf16[4,128,128]{2,1,0:T(8,128)(2,1)S(1)}, u32[]{:S(2)}, u32[]{:S(2)}) collective-permute-start(bf16[4,128,128]{2,1,0:T(8,128)(2,1)S(1)} %get-tuple-element.218), channel_id=1, source_target_pairs={{0,2},{2,4},{4,6},{6,0},{1,3},{3,5},{5,7},{7,1},{8,10},{10,12},{12... | collective-permute-start | bytes 393224 | tf_op jit(solution)/shard_map/ppermute | solution.py:429
  125.3 11.0 %collective-permute-start.7 = (bf16[4,128,128]{2,1,0:T(8,128)(2,1)S(1)}, bf16[4,128,128]{2,1,0:T(8,128)(2,1)S(1)}, u32[]{:S(2)}, u32[]{:S(2)}) collective-permute-start(bf16[4,128,128]{2,1,0:T(8,128)(2,1)S(1)} %get-tuple-element.219), channel_id=1, source_target_pairs={{0,4},{2,6},{4,0},{6,2},{1,5},{3,7},{5,1},{7,3},{8,12},{10,14},{12... | collective-permute-start | bytes 393224 | tf_op jit(solution)/shard_map/ppermute | solution.py:429
  129.3 8.8 %collective-permute-start.8 = (bf16[4,128,128]{2,1,0:T(8,128)(2,1)S(1)}, bf16[4,128,128]{2,1,0:T(8,128)(2,1)S(1)}, u32[]{:S(2)}, u32[]{:S(2)}) collective-permute-start(bf16[4,128,128]{2,1,0:T(8,128)(2,1)S(1)} %get-tuple-element.220), channel_id=1, source_target_pairs={{0,6},{2,0},{4,2},{6,4},{1,7},{3,1},{5,3},{7,5},{8,14},{10,8},{12,... | collective-permute-start | bytes 393224 | tf_op jit(solution)/shard_map/ppermute | solution.py:429
Sparse Core Ops, SparseCore 0:
  19.9 43.6 all-gather.11

commit v7 on v6

--- a/solution.py
+++ b/solution.py
@@ -190,7 +190,7 @@
 UNROLL = 4
 NX, NY, NZH, NZL = 4, 8, 2, 4
 BS = 128
-VMEM_LIMIT = 4 * 1024 * 1024
+VMEM_LIMIT = 10 * 1024 * 1024
 f32 = jnp.float32
 bf16 = jnp.bfloat16
 i32 = jnp.int32
@@ -280,36 +280,19 @@
         return carry
 
     lax.fori_loop(0, (info[1] + UNROLL - 1) // UNROLL, step, 0)
-    for x in range(NX):
-        for y in range(NY):
-            for q in range(4):
-                source = 16 * y + 4 * x + q
-                out[x, 4 * y + q] = total[source * GCAP : (source + 1) * GCAP, :].astype(bf16)
-
-
-def sum_kernel(parts, out):
-    def step(i, carry):
-        value = parts[0, i].astype(f32)
-        for n in range(1, parts.shape[0]):
-            value += parts[n, i].astype(f32)
-        out[i] = value.astype(bf16)
+    for row in range(BS):
+        out[row // 2, row % 2] = total[row * GCAP : (row + 1) * GCAP, :].astype(bf16)
+
+
+def share_kernel(scale, send, state_send, parts, stacked, _after, out, total):
+    total[...] = parts[0].astype(f32)
+
+    def step(n, carry):
+        total[...] += parts[n].astype(f32)
         return carry
 
-    lax.fori_loop(0, out.shape[0], step, 0, unroll=4)
-
-
-def pair_kernel(info, parts, keep, send):
-    my_zh = info[5]
-    for out, zh in ((keep, my_zh), (send, 1 - my_zh)):
-        for b in range(2):
-            value = parts[0, 2 * zh + b].astype(f32)
-            for n in range(1, parts.shape[0]):
-                value += parts[n, 2 * zh + b].astype(f32)
-            out[b] = value
-
-
-def share_kernel(scale, send, state_send, keep, came, stacked, _after, out, total):
-    total[...] = (keep[...] + came[...]) * scale
+    lax.fori_loop(1, parts.shape[0], step, 0)
+    total[...] = total[...] * scale
     width = stacked.shape[1] // BS
     for d in range(out.shape[0]):
         for p in range(PAIR):
@@ -332,7 +315,7 @@
     lax.fori_loop(0, WCAP, step, 0, unroll=4)
 
 
-def forward_kernel(info, code, hidden, w0, w1, w2, w3, _after, mine, theirs, weights, total, sems):
+def forward_kernel(info, code, hidden, w0, w1, w2, w3, mine, theirs, weights, total, sems):
     my_core, my_x = info[2], info[3]
     copies = [
         pltpu.make_async_copy(part, weights.at[:, (my_x + NX - k) % NX], sems.at[k])
@@ -465,22 +448,17 @@
 
     partial, cols = call(
         grad_kernel,
-        (like((NX, NY * NZH * 2, GCAP, BS), bf16), like((shard_count * 4, BS, BS), bf16)),
+        (like((NY * NX * NZH, 2, GCAP, BS), bf16), like((shard_count * 4, BS, BS), bf16)),
         2,
         3,
         [pltpu.VMEM((row_local, BS, BS), bf16), pltpu.VMEM((BS * GCAP, BS), f32)],
         flops=2 * WCAP * BS**3,
         byts=4 * 1024 * 1024,
     )(info, code, hidden, mine, other)
-    along_x = all_to_all(partial, "x")
-    summed = call(sum_kernel, like(partial.shape[1:], bf16), 0, 1, byts=2 * 1024 * 1024)(along_x)
-    along_y = all_to_all(summed.reshape(NY, 2 * NZH, GCAP, BS), "y")
-    part = (2, GCAP, BS)
-    keep, send_zh = call(pair_kernel, (like(part, f32), like(part, f32)), 1, 1, byts=1024 * 1024)(info, along_y)
-    came_zh = shift(send_zh, "zh", NZH, 1)
+    along_dp = all_to_all(partial, DP)
 
     picked = call(select_kernel, like((WCAP, BS // NX, BS), bf16), 2, 1, byts=1024 * 1024, n_after=1)(
-        info, code, gathered, summed
+        info, code, gathered, partial
     )
     w2, w1, w3 = (shift(picked, "x", NX, k) for k in (2, 1, 3))
 
@@ -496,8 +474,8 @@
         [pltpu.VMEM((shard_count * 4, tokens, BS), f32), pltpu.SemaphoreType.DMA((NX,))],
         flops=2 * WCAP * BS**3,
         byts=8 * 1024 * 1024,
-        n_after=5,
-    )(info, code, hidden, picked, w1, w2, w3, keep)
+        n_after=4,
+    )(info, code, hidden, picked, w1, w2, w3)
     came = shift(out_theirs, "core", 2, 1)
     hidden_grad = call(
         backward_kernel,
@@ -508,20 +486,20 @@
         flops=2 * WCAP * BS**3,
         byts=4 * 1024 * 1024,
     )(info, code, cols, weights)
+    part = (4, tokens, BS)
+    own, s1, s2, s3 = call(
+        chip_kernel, (like(part, f32),) + (like(part, bf16),) * 3, 1, 2, byts=3 * 1024 * 1024, n_after=1
+    )(info, out_mine, came, hidden_grad)
     packed = call(
         functools.partial(share_kernel, scale),
         like((shard_count, 2 * PAIR + MV * stacked.shape[1] // BS, BS), f32),
         2,
-        3,
+        2,
         [pltpu.VMEM((2, GCAP, BS), f32)],
         byts=1024 * 1024,
         n_after=1,
-    )(send, state_send, keep, came_zh, stacked, hidden_grad)
+    )(send, state_send, along_dp, stacked, s1)
     shares = all_to_all(packed, SHARD)
-    part = (4, tokens, BS)
-    own, s1, s2, s3 = call(
-        chip_kernel, (like(part, f32),) + (like(part, bf16),) * 3, 1, 2, byts=3 * 1024 * 1024, n_after=1
-    )(info, out_mine, came, packed)
     r2, r1, r3 = (shift(s, "zl", NZL, k) for k, s in ((2, s2), (1, s1), (3, s3)))
     projected = call(project_kernel, like(out_grad.shape, bf16), 0, 4, byts=1024 * 1024)(own, r1, r2, r3)
 

time: 147 us -> 145 us (0.986)
  blocking collectives: 21.1 us -> 0 us
  waiting for transfers between devices: 23.2 us -> 37.7 us
  starting transfers between devices: 53 us -> 59.4 us
  local copies, waits for them, and re-layouts: 12.4 us -> 10.6 us
    all_to_all x1 -> x0, blocking collectives: 21.1 us -> none  [all_to_all(): return lax.all_to_all(values, axis, split_axis=0, concat_axis=0, tiled=True)]
    ppermute x9 -> x8, waiting for transfers between devices: 15.2 us -> 28.1 us  [shift(): lax.ppermute(values, axis, [(i, (i + step) % count) for i in range(count)])]
    all_to_all x3, starting transfers between devices: 18.4 us -> 31.2 us  [all_to_all(): return lax.all_to_all(values, axis, split_axis=0, concat_axis=0, tiled=True)]
    ppermute x9 -> x8, starting transfers between devices: 34.6 us -> 28.2 us  [shift(): lax.ppermute(values, axis, [(i, (i + step) % count) for i in range(count)])]
    unnamed x37 -> x43, local copies, waits for them, and re-layouts: 8 us -> 6.27 us
    all_to_all x3, waiting for transfers between devices: 7.99 us -> 9.56 us  [all_to_all(): return lax.all_to_all(values, axis, split_axis=0, concat_axis=0, tiled=True)]
    pallas_call x3 -> x1, Pallas kernels: 3.63 us -> 3.33 us  [shards(): call(grad_kernel, (like((NY * NX * NZH, 2, GCAP, BS), bf16), like((shard_...]
  transfers between devices with their start and end apart: 13 -> 12, of which waited for: 7 -> 6; matrix products, arithmetic and copies ran while one was open for 4% -> 4% of each run, Pallas kernels for 7% -> 8%
where the time goes in v7:
time: 145 us; the launch traced here: 144 us
  starting transfers between devices  59.4 us (41%)
  waiting for transfers between devices  37.7 us (26%)
  between operations  17.8 us (12%)
  Pallas kernels  14.7 us (10%)
  local copies, waits for them, and re-layouts  10.6 us (7%)
  other arithmetic  3.43 us (2%)
    all_to_all x3, starting transfers between devices, all_to_all(): return lax.all_to_all(values, axis, split_axis=0, concat_axis=0, tiled=True)  31.2 us
    ppermute x8, starting transfers between devices, shift(): lax.ppermute(values, axis, [(i, (i + step) % count) for i in range(count)])  28.2 us
    ppermute x8, waiting for transfers between devices, shift(): lax.ppermute(values, axis, [(i, (i + step) % count) for i in range(count)])  28.1 us
    all_to_all x3, waiting for transfers between devices, all_to_all(): return lax.all_to_all(values, axis, split_axis=0, concat_axis=0, tiled=True)  9.56 us
    unnamed x43, local copies, waits for them, and re-layouts  6.27 us
    pallas_call x1, Pallas kernels, shards(): call(grad_kernel, (like((NY * NX * NZH, 2, GCAP, BS), bf16), like((shard_...  3.33 us
    pallas_call x1, Pallas kernels, shards(): call(forward_kernel, (like((NZL, 4, tokens, BS), f32), like((NZL, 4, toke...  3.22 us
  transfers between devices with their start and end apart: 12, of which 6 were waited for; matrix products, arithmetic and copies ran while one was open for 4% of the time, Pallas kernels for 8%

profile of v7, /device:TPU:1, one launch (start us, length us, event | category | flops | bytes accessed | tf_op | source)
XLA Modules:
  0.0 143.9 jit_solution(9353870328061617758)
XLA Ops:
  7.3 1.7 %constant_dynamic-slice_fusion.9 = bf16[1,32,32,128]{3,2,0,1:T(8,128)(2,1)} fusion(bf16[1,32,128,128]{3,2,0,1:T(8,128)(2,1)} %bitcast.130, s32[]{:T(128)S(6)} %select_n.333), kind=kLoop, calls=%fused_computation.174 | loop fusion | bytes 524292 | tf_op jit(solution)/shard_map/dynamic_slice | solution.py:439
  9.0 1.8 %broadcast_in_dim.307 = bf16[4,128,512]{2,1,0:T(8,128)(2,1)} broadcast(bf16[128,512]{1,0:T(8,128)(2,1)} %param.19), dimensions={1,2} | broadcast | bytes 655360 | tf_op jit(solution)/shard_map/broadcast_in_dim | solution.py:437
  10.8 7.8 %all-to-all-start.1 = ((bf16[4,128,512]{2,1,0:T(8,128)(2,1)}), bf16[4,128,512]{2,1,0:T(8,128)(2,1)S(1)}, u32[]{:S(2)}, u32[]{:S(2)}) async-start(bf16[4,128,512]{2,1,0:T(8,128)(2,1)} %broadcast_in_dim.307), calls=%async_computation.2 | async-start | bytes 1048576 | tf_op jit(solution)/shard_map/all_to_all | solution.py:408
  19.9 0.8 convert_reduce_fusion.4
  22.2 9.6 %all-to-all-done.1.mine = bf16[4,128,512]{2,1,0:T(8,128)(2,1)S(1)} async-done(((bf16[4,128,512]{2,1,0:T(8,128)(2,1)}), bf16[4,128,512]{2,1,0:T(8,128)(2,1)S(1)}, u32[]{:S(2)}, u32[]{:S(2)}) %all-to-all-start.1) | async-done | bytes 524320 | tf_op jit(solution)/shard_map/all_to_all | solution.py:408
  31.8 4.2 %collective-permute-start = (bf16[4,128,512]{2,1,0:T(8,128)(2,1)S(1)}, bf16[4,128,512]{2,1,0:T(8,128)(2,1)S(1)}, u32[]{:S(2)}, u32[]{:S(2)}) collective-permute-start(bf16[4,128,512]{2,1,0:T(8,128)(2,1)S(1)} %all-to-all-done.1.mine), channel_id=1, source_target_pairs={{0,1},{1,0},{2,3},{3,2},{4,5},{5,4},{6,7},{7,6},{8,9},{9,8},{10,11... | collective-permute-start | bytes 1572872 | tf_op jit(solution)/shard_map/ppermute | solution.py:412
  36.8 0.8 collective-permute-done.other
  37.6 3.3 %shard_map.147 = (bf16[64,2,40,128]{3,2,1,0:T(8,128)(2,1)}, bf16[32,128,128]{2,1,0:T(8,128)(2,1)S(1)}) custom-call(s32[6]{0:T(128)S(1)} %stack.27.info, s32[44]{0:T(128)S(1)} %select_reduce_fusion.4.code, bf16[128,1792]{1,0:T(8,128)(2,1)S(1)} %copy-done.6, bf16[4,128,512]{2,1,0:T(8,128)(2,1)S(1)} %all-to-all-done.1.mine, ...), custom_call_target="tpu_custom_call" | custom-call | flops 184549376 | bytes 4194304 | tf_op jit(solution)/shard_map/pallas_call | solution.py:449
  40.9 1.0 copy-done.1
  41.9 20.0 %all-to-all-start.2 = ((bf16[64,2,40,128]{3,2,1,0:T(8,128)(2,1)}), bf16[64,2,40,128]{3,2,1,0:T(8,128)(2,1)S(1)}, u32[]{:S(2)}, u32[]{:S(2)}) async-start(bf16[64,2,40,128]{3,2,1,0:T(8,128)(2,1)} %get-tuple-element.205._after), calls=%async_computation.3 | async-start | bytes 2621440 | tf_op jit(solution)/shard_map/all_to_all | solution.py:408
  61.9 1.6 %copy-done = bf16[1,256,32,128]{3,2,0,1:T(8,128)(2,1)S(1)} copy-done((bf16[1,256,32,128]{3,2,0,1:T(8,128)(2,1)S(1)}, bf16[1,256,32,128]{3,2,0,1:T(8,128)(2,1)}, u32[]{:S(2)}) %copy-start) | copy-done | bytes 2097176
  64.2 2.9 %collective-permute-start.1 = (bf16[44,32,128]{2,1,0:T(8,128)(2,1)S(1)}, bf16[44,32,128]{2,1,0:T(8,128)(2,1)S(1)}, u32[]{:S(2)}, u32[]{:S(2)}) collective-permute-start(bf16[44,32,128]{2,1,0:T(8,128)(2,1)S(1)} %shard_map.148.w0), channel_id=1, source_target_pairs={{0,16},{16,32},{32,48},{48,0},{1,17},{17,33},{33,49},{49,1},{2,18}... | collective-permute-start | bytes 1081352 | tf_op jit(solution)/shard_map/ppermute | solution.py:412
  67.1 4.3 %collective-permute-start.2 = (bf16[44,32,128]{2,1,0:T(8,128)(2,1)S(1)}, bf16[44,32,128]{2,1,0:T(8,128)(2,1)S(1)}, u32[]{:S(2)}, u32[]{:S(2)}) collective-permute-start(bf16[44,32,128]{2,1,0:T(8,128)(2,1)S(1)} %shard_map.148.w0), channel_id=1, source_target_pairs={{0,32},{16,48},{32,0},{48,16},{1,33},{17,49},{33,1},{49,17},{2,34}... | collective-permute-start | bytes 1081352 | tf_op jit(solution)/shard_map/ppermute | solution.py:412
  71.5 3.1 %collective-permute-start.3 = (bf16[44,32,128]{2,1,0:T(8,128)(2,1)S(1)}, bf16[44,32,128]{2,1,0:T(8,128)(2,1)S(1)}, u32[]{:S(2)}, u32[]{:S(2)}) collective-permute-start(bf16[44,32,128]{2,1,0:T(8,128)(2,1)S(1)} %shard_map.148.w0), channel_id=1, source_target_pairs={{0,48},{16,0},{32,16},{48,32},{1,49},{17,1},{33,17},{49,33},{2,50}... | collective-permute-start | bytes 1081352 | tf_op jit(solution)/shard_map/ppermute | solution.py:412
  74.6 8.9 %collective-permute-done.1.w1 = bf16[44,32,128]{2,1,0:T(8,128)(2,1)S(1)} collective-permute-done((bf16[44,32,128]{2,1,0:T(8,128)(2,1)S(1)}, bf16[44,32,128]{2,1,0:T(8,128)(2,1)S(1)}, u32[]{:S(2)}, u32[]{:S(2)}) %collective-permute-start.1) | collective-permute-done | bytes 360480 | tf_op jit(solution)/shard_map/ppermute | solution.py:412
  83.4 14.4 %collective-permute-done.2.w2 = bf16[44,32,128]{2,1,0:T(8,128)(2,1)S(1)} collective-permute-done((bf16[44,32,128]{2,1,0:T(8,128)(2,1)S(1)}, bf16[44,32,128]{2,1,0:T(8,128)(2,1)S(1)}, u32[]{:S(2)}, u32[]{:S(2)}) %collective-permute-start.2) | collective-permute-done | bytes 360480 | tf_op jit(solution)/shard_map/ppermute | solution.py:412
  97.9 3.2 %shard_map.149 = (f32[4,4,128,128]{3,2,1,0:T(8,128)S(1)}, f32[4,4,128,128]{3,2,1,0:T(8,128)}, bf16[44,4,32,128]{3,2,1,0:T(8,128)(2,1)S(1)}) custom-call(s32[6]{0:T(128)S(1)} %stack.27.info, s32[44]{0:T(128)S(1)} %select_reduce_fusion.4.code, bf16[128,1792]{1,0:T(8,128)(2,1)S(1)} %copy-done.7, bf16[44,32,128]{2,1,0:T(8,128)(2,1)S(1)} %shard_map.148.w0, ...), custom_call_target="tpu_custom_call" | custom-call | flops 184549376 | bytes 8388608 | tf_op jit(solution)/shard_map/pallas_call | solution.py:465
  101.1 1.0 copy-done.3
  102.1 3.3 %collective-permute-start.4 = (f32[4,4,128,128]{3,2,1,0:T(8,128)}, f32[4,4,128,128]{3,2,1,0:T(8,128)}, u32[]{:S(2)}, u32[]{:S(2)}) collective-permute-start(f32[4,4,128,128]{3,2,1,0:T(8,128)} %get-tuple-element.207), channel_id=1, source_target_pairs={{0,1},{1,0},{2,3},{3,2},{4,5},{5,4},{6,7},{7,6},{8,9},{9,8},{10,11... | collective-permute-start | bytes 3145736 | tf_op jit(solution)/shard_map/ppermute | solution.py:412
  105.5 0.9 dynamic-slice_convert_fusion
  106.7 1.2 copy-done.2
  107.9 2.2 %shard_map.150._after = bf16[128,1792]{1,0:T(8,128)(2,1)S(1)} custom-call(s32[6]{0:T(128)S(1)} %stack.27.info, s32[44]{0:T(128)S(1)} %select_reduce_fusion.4.code, bf16[32,128,128]{2,1,0:T(8,128)(2,1)S(1)} %copy-done.2, bf16[44,4,32,128]{3,2,1,0:T(8,128)(2,1)S(1)} %get-tuple-element.209.weights), custom_call_target="tpu_custom_call" | custom-call | flops 184549376 | bytes 4194304 | tf_op jit(solution)/shard_map/pallas_call | solution.py:480
  110.1 0.7 copy-done.9
  110.9 1.3 shard_map.151
  112.3 2.0 %shard_map.152 = f32[8,40,128]{2,1,0:T(8,128)} custom-call(s32[112]{0:T(128)S(1)} %broadcast_minimum_fusion.send, s32[16]{0:T(128)S(1)} %select_reduce_fusion.6.state_send, bf16[64,2,40,128]{3,2,1,0:T(8,128)(2,1)S(1)} %all-to-all-done.2.parts, f32[32,768]{1,0:T(8,128)S(1)} %pad_maximum_fusion.1.stacked, bf16[4,128,128]{2,1,0:T(8,128)(2,1)S(1)} %get-tuple-element.210._after), custom_call_target="tpu_custom_call" | custom-call | bytes 1048576 | tf_op jit(solution)/shard_map/pallas_call | solution.py:493
  114.3 3.3 %all-to-all-start.3 = ((f32[8,40,128]{2,1,0:T(8,128)}), f32[8,40,128]{2,1,0:T(8,128)S(1)}, u32[]{:S(2)}, u32[]{:S(2)}) async-start(f32[8,40,128]{2,1,0:T(8,128)} %shard_map.152), calls=%async_computation.4 | async-start | bytes 327680 | tf_op jit(solution)/shard_map/all_to_all | solution.py:408
  117.7 3.2 %collective-permute-start.5 = (bf16[4,128,128]{2,1,0:T(8,128)(2,1)S(1)}, bf16[4,128,128]{2,1,0:T(8,128)(2,1)S(1)}, u32[]{:S(2)}, u32[]{:S(2)}) collective-permute-start(bf16[4,128,128]{2,1,0:T(8,128)(2,1)S(1)} %get-tuple-element.210._after), channel_id=1, source_target_pairs={{0,2},{2,4},{4,6},{6,0},{1,3},{3,5},{5,7},{7,1},{8,10},{10,12},{12... | collective-permute-start | bytes 393224 | tf_op jit(solution)/shard_map/ppermute | solution.py:412
  120.9 4.0 %collective-permute-start.6 = (bf16[4,128,128]{2,1,0:T(8,128)(2,1)S(1)}, bf16[4,128,128]{2,1,0:T(8,128)(2,1)S(1)}, u32[]{:S(2)}, u32[]{:S(2)}) collective-permute-start(bf16[4,128,128]{2,1,0:T(8,128)(2,1)S(1)} %get-tuple-element.215), channel_id=1, source_target_pairs={{0,4},{2,6},{4,0},{6,2},{1,5},{3,7},{5,1},{7,3},{8,12},{10,14},{12... | collective-permute-start | bytes 393224 | tf_op jit(solution)/shard_map/ppermute | solution.py:412
  124.9 3.1 %collective-permute-start.7 = (bf16[4,128,128]{2,1,0:T(8,128)(2,1)S(1)}, bf16[4,128,128]{2,1,0:T(8,128)(2,1)S(1)}, u32[]{:S(2)}, u32[]{:S(2)}) collective-permute-start(bf16[4,128,128]{2,1,0:T(8,128)(2,1)S(1)} %get-tuple-element.216), channel_id=1, source_target_pairs={{0,6},{2,0},{4,2},{6,4},{1,7},{3,1},{5,3},{7,5},{8,14},{10,8},{12,... | collective-permute-start | bytes 393224 | tf_op jit(solution)/shard_map/ppermute | solution.py:412
  130.2 3.2 %collective-permute-done.6.r2 = bf16[4,128,128]{2,1,0:T(8,128)(2,1)S(1)} collective-permute-done((bf16[4,128,128]{2,1,0:T(8,128)(2,1)S(1)}, bf16[4,128,128]{2,1,0:T(8,128)(2,1)S(1)}, u32[]{:S(2)}, u32[]{:S(2)}) %collective-permute-start.6) | collective-permute-done | bytes 131104 | tf_op jit(solution)/shard_map/ppermute | solution.py:412
  133.4 0.9 collective-permute-done.7.r3
  134.3 1.8 %shard_map.153 = (f32[32,256]{1,0:T(8,128)}, f32[32,256]{1,0:T(8,128)}, f32[32,256]{1,0:T(8,128)}) custom-call(s32[32]{0:T(128)S(1)} %select_reduce_fusion.5.place, f32[32,768]{1,0:T(8,128)S(1)} %pad_maximum_fusion.1.stacked, f32[8,40,128]{2,1,0:T(8,128)S(1)} %all-to-all-done.3.came), custom_call_target="tpu_custom_call" | custom-call | bytes 1048576 | tf_op jit(solution)/shard_map/pallas_call | solution.py:507
  (79 shorter events, 4.6 us)
Async XLA Ops:
  7.2 11.5 %copy-start.16 = (s32[8,32]{1,0:T(8,128)S(1)}, s32[8,32]{1,0:T(8,128)}, u32[]{:S(2)}) copy-start(s32[8,32]{1,0:T(8,128)} %param.24) | copy-start | bytes 3076
  7.2 11.5 %copy-start.17 = (s32[8,32]{1,0:T(8,128)S(1)}, s32[8,32]{1,0:T(8,128)}, u32[]{:S(2)}) copy-start(s32[8,32]{1,0:T(8,128)} %param.21) | copy-start | bytes 3076
  7.2 11.5 %copy-start.20 = (s32[8]{0:T(128)S(1)}, s32[8]{0:T(128)}, u32[]{:S(2)}) copy-start(s32[8]{0:T(128)} %param.23) | copy-start | bytes 100
  7.2 11.8 %copy-start.18 = (s32[8,32]{1,0:T(8,128)S(1)}, s32[8,32]{1,0:T(8,128)}, u32[]{:S(2)}) copy-start(s32[8,32]{1,0:T(8,128)} %param.22) | copy-start | bytes 3076
  7.2 30.3 %copy-start.6 = (bf16[128,1792]{1,0:T(8,128)(2,1)S(1)}, bf16[128,1792]{1,0:T(8,128)(2,1)}, u32[]{:S(2)}) copy-start(bf16[128,1792]{1,0:T(8,128)(2,1)} %hidden.3) | copy-start | bytes 1376260
  7.2 54.6 %all-gather.12.cloned.1.call-start = ((), (), s32[]{:S(2)}) async-start(), calls=%async_computation.9 | async-start | bytes 2359296 | tf_op jit(solution)/shard_map/all_gather | solution.py:440
  10.8 21.0 %all-to-all-start.1 = ((bf16[4,128,512]{2,1,0:T(8,128)(2,1)}), bf16[4,128,512]{2,1,0:T(8,128)(2,1)S(1)}, u32[]{:S(2)}, u32[]{:S(2)}) async-start(bf16[4,128,512]{2,1,0:T(8,128)(2,1)} %broadcast_in_dim.307), calls=%async_computation.2 | async-start | bytes 1048576 | tf_op jit(solution)/shard_map/all_to_all | solution.py:408
  31.8 5.8 %collective-permute-start = (bf16[4,128,512]{2,1,0:T(8,128)(2,1)S(1)}, bf16[4,128,512]{2,1,0:T(8,128)(2,1)S(1)}, u32[]{:S(2)}, u32[]{:S(2)}) collective-permute-start(bf16[4,128,512]{2,1,0:T(8,128)(2,1)S(1)} %all-to-all-done.1.mine), channel_id=1, source_target_pairs={{0,1},{1,0},{2,3},{3,2},{4,5},{5,4},{6,7},{7,6},{8,9},{9,8},{10,11... | collective-permute-start | bytes 1572872 | tf_op jit(solution)/shard_map/ppermute | solution.py:412
  40.9 1.0 copy-start.1
  41.9 56.0 %copy-start.7 = (bf16[128,1792]{1,0:T(8,128)(2,1)S(1)}, bf16[128,1792]{1,0:T(8,128)(2,1)}, u32[]{:S(2)}) copy-start(bf16[128,1792]{1,0:T(8,128)(2,1)} %hidden.3) | copy-start | bytes 1376260
  41.9 70.5 %all-to-all-start.2 = ((bf16[64,2,40,128]{3,2,1,0:T(8,128)(2,1)}), bf16[64,2,40,128]{3,2,1,0:T(8,128)(2,1)S(1)}, u32[]{:S(2)}, u32[]{:S(2)}) async-start(bf16[64,2,40,128]{3,2,1,0:T(8,128)(2,1)} %get-tuple-element.205._after), calls=%async_computation.3 | async-start | bytes 2621440 | tf_op jit(solution)/shard_map/all_to_all | solution.py:408
  61.9 1.6 %copy-start = (bf16[1,256,32,128]{3,2,0,1:T(8,128)(2,1)S(1)}, bf16[1,256,32,128]{3,2,0,1:T(8,128)(2,1)}, u32[]{:S(2)}) copy-start(bf16[1,256,32,128]{3,2,0,1:T(8,128)(2,1)} %all-gather.12.cloned.1.call-done) | copy-start | bytes 6291460
  63.5 43.1 %copy-start.12 = (f32[1,32,256]{2,1,0:T(8,128)S(1)}, f32[1,32,256]{2,1,0:T(8,128)}, u32[]{:S(2)}) copy-start(f32[1,32,256]{2,1,0:T(8,128)} %param.26) | copy-start | bytes 98308
  63.5 43.1 %copy-start.14 = (f32[1,32,256]{2,1,0:T(8,128)S(1)}, f32[1,32,256]{2,1,0:T(8,128)}, u32[]{:S(2)}) copy-start(f32[1,32,256]{2,1,0:T(8,128)} %param.27) | copy-start | bytes 98308
  64.2 19.2 %collective-permute-start.1 = (bf16[44,32,128]{2,1,0:T(8,128)(2,1)S(1)}, bf16[44,32,128]{2,1,0:T(8,128)(2,1)S(1)}, u32[]{:S(2)}, u32[]{:S(2)}) collective-permute-start(bf16[44,32,128]{2,1,0:T(8,128)(2,1)S(1)} %shard_map.148.w0), channel_id=1, source_target_pairs={{0,16},{16,32},{32,48},{48,0},{1,17},{17,33},{33,49},{49,1},{2,18}... | collective-permute-start | bytes 1081352 | tf_op jit(solution)/shard_map/ppermute | solution.py:412
  67.1 30.7 %collective-permute-start.2 = (bf16[44,32,128]{2,1,0:T(8,128)(2,1)S(1)}, bf16[44,32,128]{2,1,0:T(8,128)(2,1)S(1)}, u32[]{:S(2)}, u32[]{:S(2)}) collective-permute-start(bf16[44,32,128]{2,1,0:T(8,128)(2,1)S(1)} %shard_map.148.w0), channel_id=1, source_target_pairs={{0,32},{16,48},{32,0},{48,16},{1,33},{17,49},{33,1},{49,17},{2,34}... | collective-permute-start | bytes 1081352 | tf_op jit(solution)/shard_map/ppermute | solution.py:412
  71.5 26.4 %collective-permute-start.3 = (bf16[44,32,128]{2,1,0:T(8,128)(2,1)S(1)}, bf16[44,32,128]{2,1,0:T(8,128)(2,1)S(1)}, u32[]{:S(2)}, u32[]{:S(2)}) collective-permute-start(bf16[44,32,128]{2,1,0:T(8,128)(2,1)S(1)} %shard_map.148.w0), channel_id=1, source_target_pairs={{0,48},{16,0},{32,16},{48,32},{1,49},{17,1},{33,17},{49,33},{2,50}... | collective-permute-start | bytes 1081352 | tf_op jit(solution)/shard_map/ppermute | solution.py:412
  101.1 1.0 copy-start.3
  102.1 8.0 %collective-permute-start.4 = (f32[4,4,128,128]{3,2,1,0:T(8,128)}, f32[4,4,128,128]{3,2,1,0:T(8,128)}, u32[]{:S(2)}, u32[]{:S(2)}) collective-permute-start(f32[4,4,128,128]{3,2,1,0:T(8,128)} %get-tuple-element.207), channel_id=1, source_target_pairs={{0,1},{1,0},{2,3},{3,2},{4,5},{5,4},{6,7},{7,6},{8,9},{9,8},{10,11... | collective-permute-start | bytes 3145736 | tf_op jit(solution)/shard_map/ppermute | solution.py:412
  106.7 1.2 copy-start.2
  107.9 3.0 %copy-start.4 = (f32[4,4,128,128]{3,2,1,0:T(8,128)S(1)}, f32[4,4,128,128]{3,2,1,0:T(8,128)}, u32[]{:S(2)}) copy-start(f32[4,4,128,128]{3,2,1,0:T(8,128)} %copy-done.3) | copy-start | bytes 3145732
  110.1 0.8 copy-start.9
  110.9 17.1 %copy-start.19 = (s32[8,32]{1,0:T(8,128)S(1)}, s32[8,32]{1,0:T(8,128)}, u32[]{:S(2)}) copy-start(s32[8,32]{1,0:T(8,128)} %param.25) | copy-start | bytes 3076
  112.3 23.9 %copy-start.8 = (bf16[128,1792]{1,0:T(8,128)(2,1)S(1)}, bf16[128,1792]{1,0:T(8,128)(2,1)}, u32[]{:S(2)}) copy-start(bf16[128,1792]{1,0:T(8,128)(2,1)} %hidden.3) | copy-start | bytes 1376260
  112.3 23.9 %copy-start.10 = (bf16[128,512]{1,0:T(8,128)(2,1)S(1)}, bf16[128,512]{1,0:T(8,128)(2,1)}, u32[]{:S(2)}) copy-start(bf16[128,512]{1,0:T(8,128)(2,1)} %param.19) | copy-start | bytes 393220
  112.3 23.9 %copy-start.13 = (f32[1,32,256]{2,1,0:T(8,128)S(1)}, f32[1,32,256]{2,1,0:T(8,128)}, u32[]{:S(2)}) copy-start(f32[1,32,256]{2,1,0:T(8,128)} %param.26) | copy-start | bytes 98308
  112.3 23.9 %copy-start.15 = (f32[1,32,256]{2,1,0:T(8,128)S(1)}, f32[1,32,256]{2,1,0:T(8,128)}, u32[]{:S(2)}) copy-start(f32[1,32,256]{2,1,0:T(8,128)} %param.27) | copy-start | bytes 98308
  112.3 23.9 %copy-start.21 = (s32[8]{0:T(128)S(1)}, s32[8]{0:T(128)}, u32[]{:S(2)}) copy-start(s32[8]{0:T(128)} %param.23) | copy-start | bytes 100
  114.3 20.0 %all-to-all-start.3 = ((f32[8,40,128]{2,1,0:T(8,128)}), f32[8,40,128]{2,1,0:T(8,128)S(1)}, u32[]{:S(2)}, u32[]{:S(2)}) async-start(f32[8,40,128]{2,1,0:T(8,128)} %shard_map.152), calls=%async_computation.4 | async-start | bytes 327680 | tf_op jit(solution)/shard_map/all_to_all | solution.py:408
  117.7 12.6 %collective-permute-start.5 = (bf16[4,128,128]{2,1,0:T(8,128)(2,1)S(1)}, bf16[4,128,128]{2,1,0:T(8,128)(2,1)S(1)}, u32[]{:S(2)}, u32[]{:S(2)}) collective-permute-start(bf16[4,128,128]{2,1,0:T(8,128)(2,1)S(1)} %get-tuple-element.210._after), channel_id=1, source_target_pairs={{0,2},{2,4},{4,6},{6,0},{1,3},{3,5},{5,7},{7,1},{8,10},{10,12},{12... | collective-permute-start | bytes 393224 | tf_op jit(solution)/shard_map/ppermute | solution.py:412
  120.9 12.5 %collective-permute-start.6 = (bf16[4,128,128]{2,1,0:T(8,128)(2,1)S(1)}, bf16[4,128,128]{2,1,0:T(8,128)(2,1)S(1)}, u32[]{:S(2)}, u32[]{:S(2)}) collective-permute-start(bf16[4,128,128]{2,1,0:T(8,128)(2,1)S(1)} %get-tuple-element.215), channel_id=1, source_target_pairs={{0,4},{2,6},{4,0},{6,2},{1,5},{3,7},{5,1},{7,3},{8,12},{10,14},{12... | collective-permute-start | bytes 393224 | tf_op jit(solution)/shard_map/ppermute | solution.py:412
  124.9 9.3 %collective-permute-start.7 = (bf16[4,128,128]{2,1,0:T(8,128)(2,1)S(1)}, bf16[4,128,128]{2,1,0:T(8,128)(2,1)S(1)}, u32[]{:S(2)}, u32[]{:S(2)}) collective-permute-start(bf16[4,128,128]{2,1,0:T(8,128)(2,1)S(1)} %get-tuple-element.216), channel_id=1, source_target_pairs={{0,6},{2,0},{4,2},{6,4},{1,7},{3,1},{5,3},{7,5},{8,14},{10,8},{12,... | collective-permute-start | bytes 393224 | tf_op jit(solution)/shard_map/ppermute | solution.py:412
  (1 other events, 0.7 us)
Sparse Core Ops, SparseCore 0:
  10.9 46.1 all-gather.11

commit v8 on v3

--- a/solution.py
+++ b/solution.py
@@ -190,19 +190,20 @@
 UNROLL = 4
 NX, NY, NZH, NZL = 4, 8, 2, 4
 BS = 128
-VMEM_LIMIT = 14 * 1024 * 1024
+VMEM_LIMIT = 10 * 1024 * 1024
 f32 = jnp.float32
 bf16 = jnp.bfloat16
 i32 = jnp.int32
 
 
-def call(kernel, outs, n_smem, n_vmem, scratch=(), flops=0, byts=0):
+def call(kernel, outs, n_smem, n_vmem, scratch=(), flops=0, byts=0, n_after=0):
     smem = pl.BlockSpec(memory_space=pltpu.SMEM)
     vmem = pl.BlockSpec(memory_space=pltpu.VMEM)
+    anywhere = pl.BlockSpec(memory_space=pl.ANY)
     return pl.pallas_call(
         kernel,
         out_shape=outs,
-        in_specs=[smem] * n_smem + [vmem] * n_vmem,
+        in_specs=[smem] * n_smem + [vmem] * n_vmem + [anywhere] * n_after,
         out_specs=jax.tree.map(lambda _: vmem, outs),
         scratch_shapes=list(scratch),
         compiler_params=pltpu.CompilerParams(vmem_limit_bytes=VMEM_LIMIT),
@@ -287,7 +288,7 @@
                 out[x, 4 * y + q] = total[source * GCAP : (source + 1) * GCAP, :].astype(bf16)
 
 
-def sum_kernel(parts, out):
+def sum_kernel(parts, _after, out):
     def step(i, carry):
         value = parts[0, i].astype(f32)
         for n in range(1, parts.shape[0]):
@@ -299,11 +300,14 @@
 
 
 def share_kernel(scale, send, state_send, parts, stacked, out, total):
-    for b in range(2):
-        value = parts[0, b].astype(f32)
-        for n in range(1, parts.shape[0]):
-            value += parts[n, b].astype(f32)
-        total[b] = value * scale
+    total[...] = parts[0].astype(f32)
+
+    def step(n, carry):
+        total[...] += parts[n].astype(f32)
+        return carry
+
+    lax.fori_loop(1, parts.shape[0], step, 0)
+    total[...] = total[...] * scale
     width = stacked.shape[1] // BS
     for d in range(out.shape[0]):
         for p in range(PAIR):
@@ -317,7 +321,7 @@
                 out[d, at : at + 1, :] = row[:, n * BS : (n + 1) * BS]
 
 
-def select_kernel(info, code, gathered, out):
+def select_kernel(info, code, gathered, _after, out):
     def step(c, carry):
         value = gathered[code[c] & 255]
         out[c] = jnp.where(c < info[0], value, jnp.zeros_like(value))
@@ -326,17 +330,20 @@
     lax.fori_loop(0, WCAP, step, 0, unroll=4)
 
 
-def forward_kernel(info, code, hidden, w0, w1, w2, w3, mine, theirs, weights, total):
-    my_core, my_x = info[2], info[3]
+def forward_kernel(info, code, hidden, quarters, _after, mine, theirs, weights, total, sems):
+    my_core = info[2]
+    copies = [pltpu.make_async_copy(quarters.at[x], weights.at[:, x], sems.at[x]) for x in range(NX)]
+    for copy in copies:
+        copy.start()
     total[...] = jnp.zeros_like(total)
+    for copy in copies:
+        copy.wait()
 
     def step(i, carry):
         adds = []
         for u in range(UNROLL):
             c = i * UNROLL + u
             word = code[c]
-            for k, part in enumerate((w0, w1, w2, w3)):
-                weights[c, (my_x + NX - k) % NX] = part[c]
             lanes = pl.ds(pl.multiple_of(((word >> 8) & 15) * BS, BS), BS)
             w = weights[c].reshape(BS, BS)
             adds.append((word >> 12, jnp.dot(hidden[:, lanes], w, preferred_element_type=f32)))
@@ -371,7 +378,7 @@
         back[:, r * BS : (r + 1) * BS] = total[r].astype(bf16)
 
 
-def chip_kernel(info, mine, came, own, s1, s2, s3):
+def chip_kernel(info, mine, came, _after, own, s1, s2, s3):
     my_zl = info[4]
     own[...] = mine[my_zl] + came[my_zl]
     for k, out in enumerate((s1, s2, s3)):
@@ -449,7 +456,7 @@
     fits, code, counts, send, state_send, place = make_plan(
         block_row, block_col, live_count, new_owner, new_slot, row_local, me
     )
-    info = jnp.stack(counts + [lax.axis_index("core"), x_index, lax.axis_index("zl")])
+    info = jnp.stack(counts + [lax.axis_index("core"), x_index, lax.axis_index("zl"), lax.axis_index("zh")])
 
     partial, cols = call(
         grad_kernel,
@@ -461,9 +468,14 @@
         byts=4 * 1024 * 1024,
     )(info, code, hidden, mine, other)
     along_x = all_to_all(partial, "x")
-    summed = call(sum_kernel, like(partial.shape[1:], bf16), 0, 1, byts=2 * 1024 * 1024)(along_x)
+    picked = call(select_kernel, like((WCAP, BS // NX, BS), bf16), 2, 1, byts=1024 * 1024, n_after=1)(
+        info, code, gathered, along_x
+    )
+    quarters = lax.all_gather(picked, "x", axis=0)
+
+    summed = call(sum_kernel, like(partial.shape[1:], bf16), 0, 1, byts=2 * 1024 * 1024, n_after=1)(along_x, picked)
     along_yz = all_to_all(summed.reshape(NY * NZH, 2, GCAP, BS), ("y", "zh"))
-    shares = call(
+    packed = call(
         functools.partial(share_kernel, scale),
         like((shard_count, 2 * PAIR + MV * stacked.shape[1] // BS, BS), f32),
         2,
@@ -471,10 +483,7 @@
         [pltpu.VMEM((2, GCAP, BS), f32)],
         byts=1024 * 1024,
     )(send, state_send, along_yz, stacked)
-    shares = all_to_all(shares, SHARD)
-
-    w0 = call(select_kernel, like((WCAP, BS // NX, BS), bf16), 2, 1, byts=1024 * 1024)(info, code, gathered)
-    w1, w2, w3 = (shift(w0, "x", NX, k) for k in (1, 2, 3))
+    shares = all_to_all(packed, SHARD)
 
     out_mine, out_theirs, weights = call(
         forward_kernel,
@@ -484,11 +493,12 @@
             like((WCAP, NX, BS // NX, BS), bf16),
         ),
         2,
-        5,
-        [pltpu.VMEM((shard_count * 4, tokens, BS), f32)],
+        1,
+        [pltpu.VMEM((shard_count * 4, tokens, BS), f32), pltpu.SemaphoreType.DMA((NX,))],
         flops=2 * WCAP * BS**3,
         byts=8 * 1024 * 1024,
-    )(info, code, hidden, w0, w1, w2, w3)
+        n_after=2,
+    )(info, code, hidden, quarters, packed)
     came = shift(out_theirs, "core", 2, 1)
     hidden_grad = call(
         backward_kernel,
@@ -501,10 +511,9 @@
     )(info, code, cols, weights)
     part = (4, tokens, BS)
     own, s1, s2, s3 = call(
-        chip_kernel, (like(part, f32),) + (like(part, bf16),) * 3, 1, 2, byts=3 * 1024 * 1024
-    )(info, out_mine, came)
-    r1, r2, r3 = (shift(s, "zl", NZL, k + 1) for k, s in enumerate((s1, s2, s3)))
-    r1, r2, r3, hidden_grad = lax.optimization_barrier((r1, r2, r3, hidden_grad))
+        chip_kernel, (like(part, f32),) + (like(part, bf16),) * 3, 1, 2, byts=3 * 1024 * 1024, n_after=1
+    )(info, out_mine, came, hidden_grad)
+    r2, r1, r3 = (shift(s, "zl", NZL, k) for k, s in ((2, s2), (1, s1), (3, s3)))
     projected = call(project_kernel, like(out_grad.shape, bf16), 0, 4, byts=1024 * 1024)(own, r1, r2, r3)
 
     shape = like((slot_count, share), f32)

time: 158 us -> 142 us (0.90)
  waiting for transfers between devices: 49.3 us -> 28 us
  blocking collectives: 0 us -> 20.8 us
  starting transfers between devices: 60.4 us -> 47.6 us
  local copies, waits for them, and re-layouts: 11.1 us -> 8.08 us
    all_to_all x0 -> x1, blocking collectives: none -> 20.8 us  [all_to_all(): return lax.all_to_all(values, axis, split_axis=0, concat_axis=0, tiled=True)]
    all_gather x1, waiting for transfers between devices: 11.4 us -> 0.01 us  [shards(): gathered = lax.all_gather(quarter, SHARD, axis=0, tiled=True)]
    ppermute x8 -> x5, starting transfers between devices: 30.5 us -> 19.2 us  [shift(): lax.ppermute(values, axis, [(i, (i + step) % count) for i in range(count)])]
    ppermute x8 -> x5, waiting for transfers between devices: 11.9 us -> 3.03 us  [shift(): lax.ppermute(values, axis, [(i, (i + step) % count) for i in range(count)])]
    unnamed x35 -> x49, local copies, waits for them, and re-layouts: 6.74 us -> 3.71 us
    all_to_all x4 -> x3, waiting for transfers between devices: 26 us -> 23.7 us  [all_to_all(): return lax.all_to_all(values, axis, split_axis=0, concat_axis=0, tiled=True)]
    all_to_all x4 -> x3, starting transfers between devices: 29.9 us -> 28.3 us  [all_to_all(): return lax.all_to_all(values, axis, split_axis=0, concat_axis=0, tiled=True)]
  transfers between devices with their start and end apart: 13 -> 10, of which waited for: 7 -> 6; matrix products, arithmetic and copies ran while one was open for 4% -> 5% of each run, Pallas kernels for 10% -> 7%
where the time goes in v8:
time: 142 us; the launch traced here: 141 us
  starting transfers between devices  47.6 us (34%)
  waiting for transfers between devices  28 us (20%)
  blocking collectives  20.8 us (15%)
  between operations  17.5 us (12%)
  Pallas kernels  14.7 us (10%)
  local copies, waits for them, and re-layouts  8.08 us (6%)
  other arithmetic  4.42 us (3%)
    all_to_all x3, starting transfers between devices, all_to_all(): return lax.all_to_all(values, axis, split_axis=0, concat_axis=0, tiled=True)  28.3 us
    all_to_all x3, waiting for transfers between devices, all_to_all(): return lax.all_to_all(values, axis, split_axis=0, concat_axis=0, tiled=True)  23.7 us
    all_to_all x1, blocking collectives, all_to_all(): return lax.all_to_all(values, axis, split_axis=0, concat_axis=0, tiled=True)  20.8 us
    ppermute x5, starting transfers between devices, shift(): lax.ppermute(values, axis, [(i, (i + step) % count) for i in range(count)])  19.2 us
    unnamed x49, local copies, waits for them, and re-layouts  3.71 us
    pallas_call x1, Pallas kernels, shards(): call(forward_kernel, (like((NZL, 4, tokens, BS), f32), like((NZL, 4, toke...  3.52 us
    ppermute x5, waiting for transfers between devices, shift(): lax.ppermute(values, axis, [(i, (i + step) % count) for i in range(count)])  3.03 us
  transfers between devices with their start and end apart: 10, of which 6 were waited for; matrix products, arithmetic and copies ran while one was open for 5% of the time, Pallas kernels for 7%

profile of v8, /device:TPU:1, one launch (start us, length us, event | category | flops | bytes accessed | tf_op | source)
XLA Modules:
  0.0 141.2 jit_solution(8988431295982470018)
XLA Ops:
  7.3 1.7 %constant_dynamic-slice_fusion.9 = bf16[1,32,32,128]{3,2,0,1:T(8,128)(2,1)} fusion(bf16[1,32,128,128]{3,2,0,1:T(8,128)(2,1)} %bitcast.133, s32[]{:T(128)S(6)} %select_n.333), kind=kLoop, calls=%fused_computation.174 | loop fusion | bytes 524292 | tf_op jit(solution)/shard_map/dynamic_slice | solution.py:451
  9.0 1.8 %broadcast_in_dim.304 = bf16[4,128,512]{2,1,0:T(8,128)(2,1)} broadcast(bf16[128,512]{1,0:T(8,128)(2,1)} %param.19), dimensions={1,2} | broadcast | bytes 655360 | tf_op jit(solution)/shard_map/broadcast_in_dim | solution.py:449
  10.8 7.8 %all-to-all-start.1 = ((bf16[4,128,512]{2,1,0:T(8,128)(2,1)}), bf16[4,128,512]{2,1,0:T(8,128)(2,1)S(1)}, u32[]{:S(2)}, u32[]{:S(2)}) async-start(bf16[4,128,512]{2,1,0:T(8,128)(2,1)} %broadcast_in_dim.304), calls=%async_computation.2 | async-start | bytes 1048576 | tf_op jit(solution)/shard_map/all_to_all | solution.py:420
  19.1 0.5 broadcast_compare_fusion.1
  20.1 0.3 convert_reduce_fusion.3
  20.4 0.7 convert_reduce_fusion.4
  22.5 9.3 %all-to-all-done.1.mine = bf16[4,128,512]{2,1,0:T(8,128)(2,1)S(1)} async-done(((bf16[4,128,512]{2,1,0:T(8,128)(2,1)}), bf16[4,128,512]{2,1,0:T(8,128)(2,1)S(1)}, u32[]{:S(2)}, u32[]{:S(2)}) %all-to-all-start.1) | async-done | bytes 524320 | tf_op jit(solution)/shard_map/all_to_all | solution.py:420
  31.8 4.2 %collective-permute-start = (bf16[4,128,512]{2,1,0:T(8,128)(2,1)S(1)}, bf16[4,128,512]{2,1,0:T(8,128)(2,1)S(1)}, u32[]{:S(2)}, u32[]{:S(2)}) collective-permute-start(bf16[4,128,512]{2,1,0:T(8,128)(2,1)S(1)} %all-to-all-done.1.mine), channel_id=1, source_target_pairs={{0,1},{1,0},{2,3},{3,2},{4,5},{5,4},{6,7},{7,6},{8,9},{9,8},{10,11... | collective-permute-start | bytes 1572872 | tf_op jit(solution)/shard_map/ppermute | solution.py:424
  36.1 1.2 and_select_fusion.3
  37.6 2.1 %shard_map.147 = (bf16[4,32,40,128]{3,2,1,0:T(8,128)(2,1)S(1)}, bf16[32,128,128]{2,1,0:T(8,128)(2,1)S(1)}) custom-call(s32[6]{0:T(128)S(1)} %stack.27.info, s32[44]{0:T(128)S(1)} %select_reduce_fusion.4.code, bf16[128,1792]{1,0:T(8,128)(2,1)S(1)} %copy-done.5, bf16[4,128,512]{2,1,0:T(8,128)(2,1)S(1)} %all-to-all-done.1.mine, ...), custom_call_target="tpu_custom_call" | custom-call | flops 184549376 | bytes 4194304 | tf_op jit(solution)/shard_map/pallas_call | solution.py:461
  39.6 20.8 %all_to_all.24._after.parts = bf16[4,32,40,128]{3,2,1,0:T(8,128)(2,1)S(1)} all-to-all(bf16[4,32,40,128]{3,2,1,0:T(8,128)(2,1)S(1)} %get-tuple-element.205), channel_id=1, replica_groups=mesh['y'=8,'x'=4,'zh'=2,'zl'=4,'core'=2] {'x'}, dimensions={0} | all-to-all | bytes 2621440 | tf_op jit(solution)/shard_map/all_to_all | solution.py:420
  60.4 1.6 %copy-done = bf16[1,256,32,128]{3,2,0,1:T(8,128)(2,1)S(1)} copy-done((bf16[1,256,32,128]{3,2,0,1:T(8,128)(2,1)S(1)}, bf16[1,256,32,128]{3,2,0,1:T(8,128)(2,1)}, u32[]{:S(2)}) %copy-start) | copy-done | bytes 2097176
  62.0 1.5 %shard_map.148._after = bf16[44,32,128]{2,1,0:T(8,128)(2,1)} custom-call(s32[6]{0:T(128)S(1)} %stack.27.info, s32[44]{0:T(128)S(1)} %select_reduce_fusion.4.code, bf16[256,32,128]{2,1,0:T(8,128)(2,1)S(1)} %bitcast.130, bf16[4,32,40,128]{3,2,1,0:T(8,128)(2,1)S(1)} %all_to_all.24._after.parts), custom_call_target="tpu_custom_call" | custom-call | bytes 1048576 | tf_op jit(solution)/shard_map/pallas_call | solution.py:471
  63.5 0.9 dynamic-slice_convert_fusion
  64.4 0.9 shard_map.149
  65.3 16.5 %all-to-all-start.3 = ((bf16[16,2,40,128]{3,2,1,0:T(8,128)(2,1)}), bf16[16,2,40,128]{3,2,1,0:T(8,128)(2,1)S(1)}, u32[]{:S(2)}, u32[]{:S(2)}) async-start(bf16[16,2,40,128]{3,2,1,0:T(8,128)(2,1)} %bitcast.47), calls=%async_computation.4 | async-start | bytes 655360 | tf_op jit(solution)/shard_map/all_to_all | solution.py:420
  82.2 14.4 %all-to-all-done.3.parts = bf16[16,2,40,128]{3,2,1,0:T(8,128)(2,1)S(1)} async-done(((bf16[16,2,40,128]{3,2,1,0:T(8,128)(2,1)}), bf16[16,2,40,128]{3,2,1,0:T(8,128)(2,1)S(1)}, u32[]{:S(2)}, u32[]{:S(2)}) %all-to-all-start.3) | async-done | bytes 327712 | tf_op jit(solution)/shard_map/all_to_all | solution.py:420
  96.7 1.5 %shard_map.150._after = f32[8,40,128]{2,1,0:T(8,128)} custom-call(s32[112]{0:T(128)S(1)} %broadcast_minimum_fusion.send, s32[16]{0:T(128)S(1)} %select_reduce_fusion.6.state_send, bf16[16,2,40,128]{3,2,1,0:T(8,128)(2,1)S(1)} %all-to-all-done.3.parts, f32[32,768]{1,0:T(8,128)S(1)} %pad_maximum_fusion.1.stacked), custom_call_target="tpu_custom_call" | custom-call | bytes 1048576 | tf_op jit(solution)/shard_map/pallas_call | solution.py:478
  98.2 1.2 all-gather.16.cloned.1.call-done
  99.3 1.4 copy-done.1
  100.7 3.5 %shard_map.152 = (f32[4,4,128,128]{3,2,1,0:T(8,128)S(1)}, f32[4,4,128,128]{3,2,1,0:T(8,128)}, bf16[44,4,32,128]{3,2,1,0:T(8,128)(2,1)S(1)}) custom-call(s32[6]{0:T(128)S(1)} %stack.27.info, s32[44]{0:T(128)S(1)} %select_reduce_fusion.4.code, bf16[128,1792]{1,0:T(8,128)(2,1)} %hidden.3, bf16[4,44,32,128]{3,2,1,0:T(8,128)(2,1)S(1)} %bitcast.131, ...), custom_call_target="tpu_custom_call" | custom-call | flops 184549376 | bytes 8388608 | tf_op jit(solution)/shard_map/pallas_call | solution.py:488
  104.2 4.6 %collective-permute-start.1 = (f32[4,4,128,128]{3,2,1,0:T(8,128)}, f32[4,4,128,128]{3,2,1,0:T(8,128)}, u32[]{:S(2)}, u32[]{:S(2)}) collective-permute-start(f32[4,4,128,128]{3,2,1,0:T(8,128)} %get-tuple-element.210), channel_id=1, source_target_pairs={{0,1},{1,0},{2,3},{3,2},{4,5},{5,4},{6,7},{7,6},{8,9},{9,8},{10,11... | collective-permute-start | bytes 3145736 | tf_op jit(solution)/shard_map/ppermute | solution.py:424
  108.8 4.0 %all-to-all-start.4 = ((f32[8,40,128]{2,1,0:T(8,128)}), f32[8,40,128]{2,1,0:T(8,128)}, u32[]{:S(2)}, u32[]{:S(2)}) async-start(f32[8,40,128]{2,1,0:T(8,128)} %shard_map.150._after), calls=%async_computation.5 | async-start | bytes 327680 | tf_op jit(solution)/shard_map/all_to_all | solution.py:420
  112.8 1.9 %shard_map.153._after = bf16[128,1792]{1,0:T(8,128)(2,1)S(1)} custom-call(s32[6]{0:T(128)S(1)} %stack.27.info, s32[44]{0:T(128)S(1)} %select_reduce_fusion.4.code, bf16[32,128,128]{2,1,0:T(8,128)(2,1)S(1)} %get-tuple-element.211.cols, bf16[44,4,32,128]{3,2,1,0:T(8,128)(2,1)S(1)} %get-tuple-element.212.weights), custom_call_target="tpu_custom_call" | custom-call | flops 184549376 | bytes 4194304 | tf_op jit(solution)/shard_map/pallas_call | solution.py:503
  114.9 1.6 %shard_map.154 = (f32[4,128,128]{2,1,0:T(8,128)S(1)}, bf16[4,128,128]{2,1,0:T(8,128)(2,1)S(1)}, bf16[4,128,128]{2,1,0:T(8,128)(2,1)S(1)}, bf16[4,128,128]{2,1,0:T(8,128)(2,1)S(1)}) custom-call(s32[6]{0:T(128)S(1)} %stack.27.info, f32[4,4,128,128]{3,2,1,0:T(8,128)S(1)} %get-tuple-element.209.mine, f32[4,4,128,128]{3,2,1,0:T(8,128)} %collective-permute-done.1.came, ...), custom_call_target="tpu_custom_call" | custom-call | bytes 3145728 | tf_op jit(solution)/shard_map/pallas_call | solution.py:513
  116.5 3.7 %collective-permute-start.2 = (bf16[4,128,128]{2,1,0:T(8,128)(2,1)S(1)}, bf16[4,128,128]{2,1,0:T(8,128)(2,1)S(1)}, u32[]{:S(2)}, u32[]{:S(2)}) collective-permute-start(bf16[4,128,128]{2,1,0:T(8,128)(2,1)S(1)} %get-tuple-element.214), channel_id=1, source_target_pairs={{0,2},{2,4},{4,6},{6,0},{1,3},{3,5},{5,7},{7,1},{8,10},{10,12},{12... | collective-permute-start | bytes 393224 | tf_op jit(solution)/shard_map/ppermute | solution.py:424
  120.2 3.8 %collective-permute-start.3 = (bf16[4,128,128]{2,1,0:T(8,128)(2,1)S(1)}, bf16[4,128,128]{2,1,0:T(8,128)(2,1)S(1)}, u32[]{:S(2)}, u32[]{:S(2)}) collective-permute-start(bf16[4,128,128]{2,1,0:T(8,128)(2,1)S(1)} %get-tuple-element.215), channel_id=1, source_target_pairs={{0,4},{2,6},{4,0},{6,2},{1,5},{3,7},{5,1},{7,3},{8,12},{10,14},{12... | collective-permute-start | bytes 393224 | tf_op jit(solution)/shard_map/ppermute | solution.py:424
  124.0 2.9 %collective-permute-start.4 = (bf16[4,128,128]{2,1,0:T(8,128)(2,1)S(1)}, bf16[4,128,128]{2,1,0:T(8,128)(2,1)S(1)}, u32[]{:S(2)}, u32[]{:S(2)}) collective-permute-start(bf16[4,128,128]{2,1,0:T(8,128)(2,1)S(1)} %get-tuple-element.216), channel_id=1, source_target_pairs={{0,6},{2,0},{4,2},{6,4},{1,7},{3,1},{5,3},{7,5},{8,14},{10,8},{12,... | collective-permute-start | bytes 393224 | tf_op jit(solution)/shard_map/ppermute | solution.py:424
  128.9 1.6 %shard_map.151 = (f32[32,256]{1,0:T(8,128)S(1)}, f32[32,256]{1,0:T(8,128)S(1)}, f32[32,256]{1,0:T(8,128)S(1)}) custom-call(s32[32]{0:T(128)S(1)} %select_reduce_fusion.5.place, f32[32,768]{1,0:T(8,128)S(1)} %copy-done.3, f32[8,40,128]{2,1,0:T(8,128)} %all-to-all-done.4.came), custom_call_target="tpu_custom_call" | custom-call | bytes 1048576 | tf_op jit(solution)/shard_map/pallas_call | solution.py:520
  130.5 0.7 collective-permute-done.3.r2
  131.1 2.2 %collective-permute-done.4.r3 = bf16[4,128,128]{2,1,0:T(8,128)(2,1)S(1)} collective-permute-done((bf16[4,128,128]{2,1,0:T(8,128)(2,1)S(1)}, bf16[4,128,128]{2,1,0:T(8,128)(2,1)S(1)}, u32[]{:S(2)}, u32[]{:S(2)}) %collective-permute-start.4) | collective-permute-done | bytes 131104 | tf_op jit(solution)/shard_map/ppermute | solution.py:424
  133.7 0.6 copy-done.9
  (84 shorter events, 2.5 us)
Async XLA Ops:
  7.2 11.5 %copy-start.14 = (s32[8,32]{1,0:T(8,128)S(1)}, s32[8,32]{1,0:T(8,128)}, u32[]{:S(2)}) copy-start(s32[8,32]{1,0:T(8,128)} %param.24) | copy-start | bytes 3076
  7.2 11.5 %copy-start.15 = (s32[8,32]{1,0:T(8,128)S(1)}, s32[8,32]{1,0:T(8,128)}, u32[]{:S(2)}) copy-start(s32[8,32]{1,0:T(8,128)} %param.21) | copy-start | bytes 3076
  7.2 11.5 %copy-start.20 = (s32[8]{0:T(128)S(1)}, s32[8]{0:T(128)}, u32[]{:S(2)}) copy-start(s32[8]{0:T(128)} %param.23) | copy-start | bytes 100
  7.2 11.8 %copy-start.16 = (s32[8,32]{1,0:T(8,128)S(1)}, s32[8,32]{1,0:T(8,128)}, u32[]{:S(2)}) copy-start(s32[8,32]{1,0:T(8,128)} %param.22) | copy-start | bytes 3076
  7.2 30.3 %copy-start.5 = (bf16[128,1792]{1,0:T(8,128)(2,1)S(1)}, bf16[128,1792]{1,0:T(8,128)(2,1)}, u32[]{:S(2)}) copy-start(bf16[128,1792]{1,0:T(8,128)(2,1)} %hidden.3) | copy-start | bytes 1376260
  7.2 53.2 %all-gather.14.cloned.1.call-start = ((), (), s32[]{:S(2)}) async-start(), calls=%async_computation.10 | async-start | bytes 2359296 | tf_op jit(solution)/shard_map/all_gather | solution.py:452
  10.8 21.0 %all-to-all-start.1 = ((bf16[4,128,512]{2,1,0:T(8,128)(2,1)}), bf16[4,128,512]{2,1,0:T(8,128)(2,1)S(1)}, u32[]{:S(2)}, u32[]{:S(2)}) async-start(bf16[4,128,512]{2,1,0:T(8,128)(2,1)} %broadcast_in_dim.304), calls=%async_computation.2 | async-start | bytes 1048576 | tf_op jit(solution)/shard_map/all_to_all | solution.py:420
  18.6 80.7 %all-gather.16.cloned.1.call-start = ((), (), s32[]{:S(2)}) async-start(), calls=%async_computation.11 | async-start | bytes 1802240 | tf_op jit(solution)/shard_map/all_gather | solution.py:474
  31.8 5.8 %collective-permute-start = (bf16[4,128,512]{2,1,0:T(8,128)(2,1)S(1)}, bf16[4,128,512]{2,1,0:T(8,128)(2,1)S(1)}, u32[]{:S(2)}, u32[]{:S(2)}) collective-permute-start(bf16[4,128,512]{2,1,0:T(8,128)(2,1)S(1)} %all-to-all-done.1.mine), channel_id=1, source_target_pairs={{0,1},{1,0},{2,3},{3,2},{4,5},{5,4},{6,7},{7,6},{8,9},{9,8},{10,11... | collective-permute-start | bytes 1572872 | tf_op jit(solution)/shard_map/ppermute | solution.py:424
  60.4 1.6 %copy-start = (bf16[1,256,32,128]{3,2,0,1:T(8,128)(2,1)S(1)}, bf16[1,256,32,128]{3,2,0,1:T(8,128)(2,1)}, u32[]{:S(2)}) copy-start(bf16[1,256,32,128]{3,2,0,1:T(8,128)(2,1)} %all-gather.14.cloned.1.call-done) | copy-start | bytes 6291460
  63.5 18.6 %copy-start.10 = (f32[1,32,256]{2,1,0:T(8,128)S(1)}, f32[1,32,256]{2,1,0:T(8,128)}, u32[]{:S(2)}) copy-start(f32[1,32,256]{2,1,0:T(8,128)} %param.26) | copy-start | bytes 98308
  63.5 18.6 %copy-start.12 = (f32[1,32,256]{2,1,0:T(8,128)S(1)}, f32[1,32,256]{2,1,0:T(8,128)}, u32[]{:S(2)}) copy-start(f32[1,32,256]{2,1,0:T(8,128)} %param.27) | copy-start | bytes 98308
  65.3 31.3 %all-to-all-start.3 = ((bf16[16,2,40,128]{3,2,1,0:T(8,128)(2,1)}), bf16[16,2,40,128]{3,2,1,0:T(8,128)(2,1)S(1)}, u32[]{:S(2)}, u32[]{:S(2)}) async-start(bf16[16,2,40,128]{3,2,1,0:T(8,128)(2,1)} %bitcast.47), calls=%async_computation.4 | async-start | bytes 655360 | tf_op jit(solution)/shard_map/all_to_all | solution.py:420
  82.1 17.3 %copy-start.2 = (f32[32,768]{1,0:T(8,128)}, f32[32,768]{1,0:T(8,128)S(1)}, u32[]{:S(2)}) copy-start(f32[32,768]{1,0:T(8,128)S(1)} %pad_maximum_fusion.1.stacked) | copy-start | bytes 294916
  99.3 1.4 copy-start.1
  104.2 10.7 %collective-permute-start.1 = (f32[4,4,128,128]{3,2,1,0:T(8,128)}, f32[4,4,128,128]{3,2,1,0:T(8,128)}, u32[]{:S(2)}, u32[]{:S(2)}) collective-permute-start(f32[4,4,128,128]{3,2,1,0:T(8,128)} %get-tuple-element.210), channel_id=1, source_target_pairs={{0,1},{1,0},{2,3},{3,2},{4,5},{5,4},{6,7},{7,6},{8,9},{9,8},{10,11... | collective-permute-start | bytes 3145736 | tf_op jit(solution)/shard_map/ppermute | solution.py:424
  108.8 20.0 %all-to-all-start.4 = ((f32[8,40,128]{2,1,0:T(8,128)}), f32[8,40,128]{2,1,0:T(8,128)}, u32[]{:S(2)}, u32[]{:S(2)}) async-start(f32[8,40,128]{2,1,0:T(8,128)} %shard_map.150._after), calls=%async_computation.5 | async-start | bytes 327680 | tf_op jit(solution)/shard_map/all_to_all | solution.py:420
  114.8 9.2 %copy-start.7 = (bf16[128,1792]{1,0:T(8,128)(2,1)}, bf16[128,1792]{1,0:T(8,128)(2,1)S(1)}, u32[]{:S(2)}) copy-start(bf16[128,1792]{1,0:T(8,128)(2,1)S(1)} %shard_map.153._after) | copy-start | bytes 1376260
  114.8 12.1 %copy-start.17 = (s32[8,32]{1,0:T(8,128)S(1)}, s32[8,32]{1,0:T(8,128)}, u32[]{:S(2)}) copy-start(s32[8,32]{1,0:T(8,128)} %param.25) | copy-start | bytes 3076
  114.8 14.0 %copy-start.18 = (s32[256]{0:T(256)S(1)}, s32[256]{0:T(256)}, u32[]{:S(2)}) copy-start(s32[256]{0:T(256)} %get-tuple-element.398) | copy-start | bytes 3076
  114.8 13.9 %copy-start.19 = (pred[256]{0:T(512)(128)(4,1)S(1)}, pred[256]{0:T(512)(128)(4,1)}, u32[]{:S(2)}) copy-start(pred[256]{0:T(512)(128)(4,1)} %get-tuple-element.372) | copy-start | bytes 772
  114.8 14.1 %copy-start.3 = (f32[32,768]{1,0:T(8,128)S(1)}, f32[32,768]{1,0:T(8,128)}, u32[]{:S(2)}) copy-start(f32[32,768]{1,0:T(8,128)} %copy-done.2) | copy-start | bytes 294916
  114.8 18.6 %copy-start.6 = (bf16[128,1792]{1,0:T(8,128)(2,1)S(1)}, bf16[128,1792]{1,0:T(8,128)(2,1)}, u32[]{:S(2)}) copy-start(bf16[128,1792]{1,0:T(8,128)(2,1)} %hidden.3) | copy-start | bytes 1376260
  114.8 18.6 %copy-start.8 = (bf16[128,512]{1,0:T(8,128)(2,1)S(1)}, bf16[128,512]{1,0:T(8,128)(2,1)}, u32[]{:S(2)}) copy-start(bf16[128,512]{1,0:T(8,128)(2,1)} %param.19) | copy-start | bytes 393220
  114.8 18.6 %copy-start.11 = (f32[1,32,256]{2,1,0:T(8,128)S(1)}, f32[1,32,256]{2,1,0:T(8,128)}, u32[]{:S(2)}) copy-start(f32[1,32,256]{2,1,0:T(8,128)} %param.26) | copy-start | bytes 98308
  114.9 18.6 %copy-start.13 = (f32[1,32,256]{2,1,0:T(8,128)S(1)}, f32[1,32,256]{2,1,0:T(8,128)}, u32[]{:S(2)}) copy-start(f32[1,32,256]{2,1,0:T(8,128)} %param.27) | copy-start | bytes 98308
  114.9 18.6 %copy-start.21 = (s32[8]{0:T(128)S(1)}, s32[8]{0:T(128)}, u32[]{:S(2)}) copy-start(s32[8]{0:T(128)} %param.23) | copy-start | bytes 100
  116.5 14.0 %collective-permute-start.2 = (bf16[4,128,128]{2,1,0:T(8,128)(2,1)S(1)}, bf16[4,128,128]{2,1,0:T(8,128)(2,1)S(1)}, u32[]{:S(2)}, u32[]{:S(2)}) collective-permute-start(bf16[4,128,128]{2,1,0:T(8,128)(2,1)S(1)} %get-tuple-element.214), channel_id=1, source_target_pairs={{0,2},{2,4},{4,6},{6,0},{1,3},{3,5},{5,7},{7,1},{8,10},{10,12},{12... | collective-permute-start | bytes 393224 | tf_op jit(solution)/shard_map/ppermute | solution.py:424
  120.2 10.9 %collective-permute-start.3 = (bf16[4,128,128]{2,1,0:T(8,128)(2,1)S(1)}, bf16[4,128,128]{2,1,0:T(8,128)(2,1)S(1)}, u32[]{:S(2)}, u32[]{:S(2)}) collective-permute-start(bf16[4,128,128]{2,1,0:T(8,128)(2,1)S(1)} %get-tuple-element.215), channel_id=1, source_target_pairs={{0,4},{2,6},{4,0},{6,2},{1,5},{3,7},{5,1},{7,3},{8,12},{10,14},{12... | collective-permute-start | bytes 393224 | tf_op jit(solution)/shard_map/ppermute | solution.py:424
  124.0 9.3 %collective-permute-start.4 = (bf16[4,128,128]{2,1,0:T(8,128)(2,1)S(1)}, bf16[4,128,128]{2,1,0:T(8,128)(2,1)S(1)}, u32[]{:S(2)}, u32[]{:S(2)}) collective-permute-start(bf16[4,128,128]{2,1,0:T(8,128)(2,1)S(1)} %get-tuple-element.216), channel_id=1, source_target_pairs={{0,6},{2,0},{4,2},{6,4},{1,7},{3,1},{5,3},{7,5},{8,14},{10,8},{12,... | collective-permute-start | bytes 393224 | tf_op jit(solution)/shard_map/ppermute | solution.py:424
  133.7 0.7 copy-start.9
  133.7 0.6 copy-start.22
  (2 other events, 1.3 us)
Sparse Core Ops, SparseCore 0:
  10.9 46.3 all-gather.13
  63.6 35.6 all-gather.15

commit v9 on v8

--- a/solution.py
+++ b/solution.py
@@ -288,17 +288,6 @@
                 out[x, 4 * y + q] = total[source * GCAP : (source + 1) * GCAP, :].astype(bf16)
 
 
-def sum_kernel(parts, _after, out):
-    def step(i, carry):
-        value = parts[0, i].astype(f32)
-        for n in range(1, parts.shape[0]):
-            value += parts[n, i].astype(f32)
-        out[i] = value.astype(bf16)
-        return carry
-
-    lax.fori_loop(0, out.shape[0], step, 0, unroll=4)
-
-
 def share_kernel(scale, send, state_send, parts, stacked, out, total):
     total[...] = parts[0].astype(f32)
 
@@ -321,13 +310,21 @@
                 out[d, at : at + 1, :] = row[:, n * BS : (n + 1) * BS]
 
 
-def select_kernel(info, code, gathered, _after, out):
-    def step(c, carry):
+def select_sum_kernel(info, code, gathered, parts, picked, summed):
+    def select(c, carry):
         value = gathered[code[c] & 255]
-        out[c] = jnp.where(c < info[0], value, jnp.zeros_like(value))
+        picked[c] = jnp.where(c < info[0], value, jnp.zeros_like(value))
         return carry
 
-    lax.fori_loop(0, WCAP, step, 0, unroll=4)
+    def add(i, carry):
+        value = parts[0, i].astype(f32)
+        for n in range(1, parts.shape[0]):
+            value += parts[n, i].astype(f32)
+        summed[i] = value.astype(bf16)
+        return carry
+
+    lax.fori_loop(0, WCAP, select, 0, unroll=4)
+    lax.fori_loop(0, summed.shape[0], add, 0, unroll=4)
 
 
 def forward_kernel(info, code, hidden, quarters, _after, mine, theirs, weights, total, sems):
@@ -378,7 +375,7 @@
         back[:, r * BS : (r + 1) * BS] = total[r].astype(bf16)
 
 
-def chip_kernel(info, mine, came, _after, own, s1, s2, s3):
+def chip_kernel(info, mine, came, own, s1, s2, s3):
     my_zl = info[4]
     own[...] = mine[my_zl] + came[my_zl]
     for k, out in enumerate((s1, s2, s3)):
@@ -386,13 +383,13 @@
         out[...] = (mine[zl] + came[zl]).astype(bf16)
 
 
-def project_kernel(own, r1, r2, r3, out):
+def project_kernel(own, r1, r2, r3, _after, out):
     for sub in range(4):
         value = own[sub] + r1[sub].astype(f32) + r2[sub].astype(f32) + r3[sub].astype(f32)
         out[:, sub * BS : (sub + 1) * BS] = value.astype(bf16)
 
 
-def adam_kernel(place, stacked, came, new_w, new_m, new_v, rows, grad):
+def adam_kernel(place, stacked, came, _after, new_w, new_m, new_v, rows, grad):
     slots, share = new_w.shape
     places = came.shape[0] * PAIR
     width = stacked.shape[1] // BS
@@ -446,10 +443,11 @@
     share = first_moment.shape[2]
     scale = 1.0 / math.sqrt(tokens * lax.axis_size(DP))
 
-    mine = all_to_all(jnp.broadcast_to(out_grad[None], (NZL,) + out_grad.shape), "zl")
+    quarter = lax.dynamic_slice_in_dim(block_weight[0], x_index * (BS // NX), BS // NX, 1)
+    quarter, sent = lax.optimization_barrier((quarter, out_grad))
+    gathered = lax.all_gather(quarter, SHARD, axis=0, tiled=True)
+    mine = all_to_all(jnp.broadcast_to(sent[None], (NZL,) + out_grad.shape), "zl")
     other = shift(mine, "core", 2, 1)
-    quarter = lax.dynamic_slice_in_dim(block_weight[0], x_index * (BS // NX), BS // NX, 1)
-    gathered = lax.all_gather(quarter, SHARD, axis=0, tiled=True)
     weight_share = lax.dynamic_slice_in_dim(block_weight[0], dp_index * 2, 2, 1).reshape(slot_count, share)
     stacked = jnp.concatenate([weight_share.astype(f32), first_moment[0], second_moment[0]], axis=1)
 
@@ -468,12 +466,14 @@
         byts=4 * 1024 * 1024,
     )(info, code, hidden, mine, other)
     along_x = all_to_all(partial, "x")
-    picked = call(select_kernel, like((WCAP, BS // NX, BS), bf16), 2, 1, byts=1024 * 1024, n_after=1)(
-        info, code, gathered, along_x
-    )
+    picked, summed = call(
+        select_sum_kernel,
+        (like((WCAP, BS // NX, BS), bf16), like(partial.shape[1:], bf16)),
+        2,
+        2,
+        byts=4 * 1024 * 1024,
+    )(info, code, gathered, along_x)
     quarters = lax.all_gather(picked, "x", axis=0)
-
-    summed = call(sum_kernel, like(partial.shape[1:], bf16), 0, 1, byts=2 * 1024 * 1024, n_after=1)(along_x, picked)
     along_yz = all_to_all(summed.reshape(NY * NZH, 2, GCAP, BS), ("y", "zh"))
     packed = call(
         functools.partial(share_kernel, scale),
@@ -511,10 +511,12 @@
     )(info, code, cols, weights)
     part = (4, tokens, BS)
     own, s1, s2, s3 = call(
-        chip_kernel, (like(part, f32),) + (like(part, bf16),) * 3, 1, 2, byts=3 * 1024 * 1024, n_after=1
-    )(info, out_mine, came, hidden_grad)
+        chip_kernel, (like(part, f32),) + (like(part, bf16),) * 3, 1, 2, byts=3 * 1024 * 1024
+    )(info, out_mine, came)
     r2, r1, r3 = (shift(s, "zl", NZL, k) for k, s in ((2, s2), (1, s1), (3, s3)))
-    projected = call(project_kernel, like(out_grad.shape, bf16), 0, 4, byts=1024 * 1024)(own, r1, r2, r3)
+    projected = call(project_kernel, like(out_grad.shape, bf16), 0, 4, byts=1024 * 1024, n_after=1)(
+        own, r1, r2, r3, hidden_grad
+    )
 
     shape = like((slot_count, share), f32)
     new_weight, new_first, new_second = call(
@@ -524,7 +526,8 @@
         2,
         [pltpu.VMEM((slot_count, 3 * share), f32), pltpu.VMEM((slot_count, share), f32)],
         byts=1024 * 1024,
-    )(place, stacked, shares)
+        n_after=1,
+    )(place, stacked, shares, hidden_grad)
     result = (projected, hidden_grad, new_weight[None], new_first[None], new_second[None])
     return lax.cond(
         fits,

time: 142 us -> 143 us (level)
  local copies, waits for them, and re-layouts: 8.08 us -> 11.1 us
    ppermute x5, waiting for transfers between devices: 3.03 us -> 1.04 us  [shift(): lax.ppermute(values, axis, [(i, (i + step) % count) for i in range(count)])]
    unnamed x49, local copies, waits for them, and re-layouts: 3.71 us -> 5.51 us
  transfers between devices with their start and end apart: 10 -> 10, of which waited for: 6 -> 5; matrix products, arithmetic and copies ran while one was open for 5% -> 6% of each run, Pallas kernels for 7% -> 6%
where the time goes in v9:
time: 143 us
  starting transfers between devices  47.1 us (33%)
  waiting for transfers between devices  26.7 us (19%)
  blocking collectives  20.9 us (15%)
  between operations  17.6 us (12%)
  Pallas kernels  14 us (10%)
  local copies, waits for them, and re-layouts  11.1 us (8%)
  other arithmetic  5.16 us (4%)
    all_to_all x3, starting transfers between devices, all_to_all(): return lax.all_to_all(values, axis, split_axis=0, concat_axis=0, tiled=True)  28.7 us
    all_to_all x3, waiting for transfers between devices, all_to_all(): return lax.all_to_all(values, axis, split_axis=0, concat_axis=0, tiled=True)  23.7 us
    all_to_all x1, blocking collectives, all_to_all(): return lax.all_to_all(values, axis, split_axis=0, concat_axis=0, tiled=True)  20.9 us
    ppermute x5, starting transfers between devices, shift(): lax.ppermute(values, axis, [(i, (i + step) % count) for i in range(count)])  18.3 us
    unnamed x49, local copies, waits for them, and re-layouts  5.51 us
    pallas_call x1, Pallas kernels, shards(): call(forward_kernel, (like((NZL, 4, tokens, BS), f32), like((NZL, 4, toke...  3.03 us
  transfers between devices with their start and end apart: 10, of which 5 were waited for; matrix products, arithmetic and copies ran while one was open for 6% of the time, Pallas kernels for 6%

profile of v9, /device:TPU:1, one launch (start us, length us, event | category | flops | bytes accessed | tf_op | source)
XLA Modules:
  0.0 142.7 jit_solution(5568886429072070247)
XLA Ops:
  7.3 1.7 %dynamic-slice_bitcast_fusion.1 = bf16[32,32,128]{2,1,0:T(8,128)(2,1)} fusion(bf16[1,32,128,128]{3,2,1,0:T(8,128)(2,1)} %param.20, s32[]{:T(128)S(6)} %select_n.333), kind=kLoop, calls=%fused_computation.122 | loop fusion | bytes 524292 | tf_op jit(solution)/shard_map/dynamic_slice | solution.py:446
  9.0 1.7 %broadcast_in_dim.304 = bf16[4,128,512]{2,1,0:T(8,128)(2,1)} broadcast(bf16[128,512]{1,0:T(8,128)(2,1)} %param.19), dimensions={1,2} | broadcast | bytes 655360 | tf_op jit(solution)/shard_map/broadcast_in_dim | solution.py:449
  10.8 7.8 %all-to-all-start.1 = ((bf16[4,128,512]{2,1,0:T(8,128)(2,1)}), bf16[4,128,512]{2,1,0:T(8,128)(2,1)S(1)}, u32[]{:S(2)}, u32[]{:S(2)}) async-start(bf16[4,128,512]{2,1,0:T(8,128)(2,1)} %broadcast_in_dim.304), calls=%async_computation.2 | async-start | bytes 1048576 | tf_op jit(solution)/shard_map/all_to_all | solution.py:417
  20.3 0.7 convert_reduce_fusion.4
  22.5 9.2 %all-to-all-done.1.mine = bf16[4,128,512]{2,1,0:T(8,128)(2,1)S(1)} async-done(((bf16[4,128,512]{2,1,0:T(8,128)(2,1)}), bf16[4,128,512]{2,1,0:T(8,128)(2,1)S(1)}, u32[]{:S(2)}, u32[]{:S(2)}) %all-to-all-start.1) | async-done | bytes 524320 | tf_op jit(solution)/shard_map/all_to_all | solution.py:417
  31.7 4.3 %collective-permute-start = (bf16[4,128,512]{2,1,0:T(8,128)(2,1)S(1)}, bf16[4,128,512]{2,1,0:T(8,128)(2,1)S(1)}, u32[]{:S(2)}, u32[]{:S(2)}) collective-permute-start(bf16[4,128,512]{2,1,0:T(8,128)(2,1)S(1)} %all-to-all-done.1.mine), channel_id=1, source_target_pairs={{0,1},{1,0},{2,3},{3,2},{4,5},{5,4},{6,7},{7,6},{8,9},{9,8},{10,11... | collective-permute-start | bytes 1572872 | tf_op jit(solution)/shard_map/ppermute | solution.py:421
  36.0 1.2 and_select_fusion.3
  37.5 2.1 %shard_map.147 = (bf16[4,32,40,128]{3,2,1,0:T(8,128)(2,1)S(1)}, bf16[32,128,128]{2,1,0:T(8,128)(2,1)S(1)}) custom-call(s32[6]{0:T(128)S(1)} %stack.27.info, s32[44]{0:T(128)S(1)} %select_reduce_fusion.4.code, bf16[128,1792]{1,0:T(8,128)(2,1)S(1)} %copy-done.9, bf16[4,128,512]{2,1,0:T(8,128)(2,1)S(1)} %all-to-all-done.1.mine, ...), custom_call_target="tpu_custom_call" | custom-call | flops 184549376 | bytes 4194304 | tf_op jit(solution)/shard_map/pallas_call | solution.py:459
  39.6 1.0 copy-done.2
  40.6 20.9 %all_to_all.24.parts = bf16[4,32,40,128]{3,2,1,0:T(8,128)(2,1)S(1)} all-to-all(bf16[4,32,40,128]{3,2,1,0:T(8,128)(2,1)S(1)} %get-tuple-element.211), channel_id=1, replica_groups=mesh['y'=8,'x'=4,'zh'=2,'zl'=4,'core'=2] {'x'}, dimensions={0} | all-to-all | bytes 2621440 | tf_op jit(solution)/shard_map/all_to_all | solution.py:417
  61.5 1.6 %copy-done = bf16[256,32,128]{2,1,0:T(8,128)(2,1)S(1)} copy-done((bf16[256,32,128]{2,1,0:T(8,128)(2,1)S(1)}, bf16[256,32,128]{2,1,0:T(8,128)(2,1)}, u32[]{:S(2)}) %copy-start) | copy-done | bytes 2097176
  63.0 1.8 %shard_map.148 = (bf16[44,32,128]{2,1,0:T(8,128)(2,1)}, bf16[32,40,128]{2,1,0:T(8,128)(2,1)}) custom-call(s32[6]{0:T(128)S(1)} %stack.27.info, s32[44]{0:T(128)S(1)} %select_reduce_fusion.4.code, bf16[256,32,128]{2,1,0:T(8,128)(2,1)S(1)} %copy-done, bf16[4,32,40,128]{3,2,1,0:T(8,128)(2,1)S(1)} %all_to_all.24.parts), custom_call_target="tpu_custom_call" | custom-call | bytes 4194304 | tf_op jit(solution)/shard_map/pallas_call | solution.py:469
  64.8 0.9 dynamic-slice_convert_fusion
  65.7 16.5 %all-to-all-start.3 = ((bf16[16,2,40,128]{3,2,1,0:T(8,128)(2,1)}), bf16[16,2,40,128]{3,2,1,0:T(8,128)(2,1)S(1)}, u32[]{:S(2)}, u32[]{:S(2)}) async-start(bf16[16,2,40,128]{3,2,1,0:T(8,128)(2,1)} %bitcast.46), calls=%async_computation.4 | async-start | bytes 655360 | tf_op jit(solution)/shard_map/all_to_all | solution.py:417
  82.6 14.4 %all-to-all-done.3.parts = bf16[16,2,40,128]{3,2,1,0:T(8,128)(2,1)S(1)} async-done(((bf16[16,2,40,128]{3,2,1,0:T(8,128)(2,1)}), bf16[16,2,40,128]{3,2,1,0:T(8,128)(2,1)S(1)}, u32[]{:S(2)}, u32[]{:S(2)}) %all-to-all-start.3) | async-done | bytes 327712 | tf_op jit(solution)/shard_map/all_to_all | solution.py:417
  97.0 1.5 %shard_map.149._after = f32[8,40,128]{2,1,0:T(8,128)} custom-call(s32[112]{0:T(128)S(1)} %broadcast_minimum_fusion.send, s32[16]{0:T(128)S(1)} %select_reduce_fusion.6.state_send, bf16[16,2,40,128]{3,2,1,0:T(8,128)(2,1)S(1)} %all-to-all-done.3.parts, f32[32,768]{1,0:T(8,128)S(1)} %pad_maximum_fusion.1.stacked), custom_call_target="tpu_custom_call" | custom-call | bytes 1048576 | tf_op jit(solution)/shard_map/pallas_call | solution.py:478
  98.5 2.0 %all-gather.15.cloned.1.call-done = bf16[176,32,128]{2,1,0:T(8,128)(2,1)} async-done(((bf16[44,32,128]{2,1,0:T(8,128)(2,1)}), bf16[176,32,128]{2,1,0:T(8,128)(2,1)}) %all-gather.15.cloned.1.call-update) | async-done | bytes 1441808 | tf_op jit(solution)/shard_map/all_gather | solution.py:476
  100.5 1.4 copy-done.1
  101.9 3.0 %shard_map.150 = (f32[4,4,128,128]{3,2,1,0:T(8,128)S(1)}, f32[4,4,128,128]{3,2,1,0:T(8,128)}, bf16[44,4,32,128]{3,2,1,0:T(8,128)(2,1)S(1)}) custom-call(s32[6]{0:T(128)S(1)} %stack.27.info, s32[44]{0:T(128)S(1)} %select_reduce_fusion.4.code, bf16[128,1792]{1,0:T(8,128)(2,1)S(1)} %copy-done.9, bf16[4,44,32,128]{3,2,1,0:T(8,128)(2,1)S(1)} %bitcast.130, ...), custom_call_target="tpu_custom_call" | custom-call | flops 184549376 | bytes 8388608 | tf_op jit(solution)/shard_map/pallas_call | solution.py:488
  104.9 3.6 %collective-permute-start.1 = (f32[4,4,128,128]{3,2,1,0:T(8,128)}, f32[4,4,128,128]{3,2,1,0:T(8,128)S(1)}, u32[]{:S(2)}, u32[]{:S(2)}) collective-permute-start(f32[4,4,128,128]{3,2,1,0:T(8,128)} %get-tuple-element.220), channel_id=1, source_target_pairs={{0,1},{1,0},{2,3},{3,2},{4,5},{5,4},{6,7},{7,6},{8,9},{9,8},{10,11... | collective-permute-start | bytes 3145736 | tf_op jit(solution)/shard_map/ppermute | solution.py:421
  108.5 4.5 %all-to-all-start.4 = ((f32[8,40,128]{2,1,0:T(8,128)}), f32[8,40,128]{2,1,0:T(8,128)}, u32[]{:S(2)}, u32[]{:S(2)}) async-start(f32[8,40,128]{2,1,0:T(8,128)} %shard_map.149._after), calls=%async_computation.5 | async-start | bytes 327680 | tf_op jit(solution)/shard_map/all_to_all | solution.py:417
  113.0 1.3 eq.214
  116.2 1.3 shard_map.153
  117.6 0.7 copy-done.6
  118.3 3.4 %collective-permute-start.2 = (bf16[4,128,128]{2,1,0:T(8,128)(2,1)}, bf16[4,128,128]{2,1,0:T(8,128)(2,1)S(1)}, u32[]{:S(2)}, u32[]{:S(2)}) collective-permute-start(bf16[4,128,128]{2,1,0:T(8,128)(2,1)} %get-tuple-element.222), channel_id=1, source_target_pairs={{0,2},{2,4},{4,6},{6,0},{1,3},{3,5},{5,7},{7,1},{8,10},{10,12},{12... | collective-permute-start | bytes 393224 | tf_op jit(solution)/shard_map/ppermute | solution.py:421
  121.7 4.0 %collective-permute-start.3 = (bf16[4,128,128]{2,1,0:T(8,128)(2,1)}, bf16[4,128,128]{2,1,0:T(8,128)(2,1)S(1)}, u32[]{:S(2)}, u32[]{:S(2)}) collective-permute-start(bf16[4,128,128]{2,1,0:T(8,128)(2,1)} %get-tuple-element.223), channel_id=1, source_target_pairs={{0,4},{2,6},{4,0},{6,2},{1,5},{3,7},{5,1},{7,3},{8,12},{10,14},{12... | collective-permute-start | bytes 393224 | tf_op jit(solution)/shard_map/ppermute | solution.py:421
  125.7 3.1 %collective-permute-start.4 = (bf16[4,128,128]{2,1,0:T(8,128)(2,1)}, bf16[4,128,128]{2,1,0:T(8,128)(2,1)S(1)}, u32[]{:S(2)}, u32[]{:S(2)}) collective-permute-start(bf16[4,128,128]{2,1,0:T(8,128)(2,1)} %get-tuple-element.224), channel_id=1, source_target_pairs={{0,6},{2,0},{4,2},{6,4},{1,7},{3,1},{5,3},{7,5},{8,14},{10,8},{12,... | collective-permute-start | bytes 393224 | tf_op jit(solution)/shard_map/ppermute | solution.py:421
  128.8 0.8 select_reduce_fusion.5.place
  129.7 2.0 %shard_map.151._after = bf16[128,1792]{1,0:T(8,128)(2,1)S(1)} custom-call(s32[6]{0:T(128)S(1)} %stack.27.info, s32[44]{0:T(128)S(1)} %select_reduce_fusion.4.code, bf16[32,128,128]{2,1,0:T(8,128)(2,1)S(1)} %copy-done.3, bf16[44,4,32,128]{3,2,1,0:T(8,128)(2,1)S(1)} %get-tuple-element.215.weights), custom_call_target="tpu_custom_call" | custom-call | flops 184549376 | bytes 4194304 | tf_op jit(solution)/shard_map/pallas_call | solution.py:503
  131.7 2.2 %shard_map.152 = (f32[32,256]{1,0:T(8,128)}, f32[32,256]{1,0:T(8,128)}, f32[32,256]{1,0:T(8,128)}) custom-call(s32[32]{0:T(128)S(1)} %select_reduce_fusion.5.place, f32[32,768]{1,0:T(8,128)S(1)} %copy-done.5, f32[8,40,128]{2,1,0:T(8,128)} %all-to-all-done.4.came, bf16[128,1792]{1,0:T(8,128)(2,1)S(1)} %shard_map.151._after), custom_call_target="tpu_custom_call" | custom-call | bytes 1048576 | tf_op jit(solution)/shard_map/pallas_call | solution.py:522
  133.8 0.8 collective-permute-done.4.r3
  135.1 0.7 copy-done.11
  (83 shorter events, 3.1 us)
Async XLA Ops:
  7.2 11.4 %copy-start.18 = (s32[8,32]{1,0:T(8,128)S(1)}, s32[8,32]{1,0:T(8,128)}, u32[]{:S(2)}) copy-start(s32[8,32]{1,0:T(8,128)} %param.24) | copy-start | bytes 3076
  7.2 11.5 %copy-start.19 = (s32[8,32]{1,0:T(8,128)S(1)}, s32[8,32]{1,0:T(8,128)}, u32[]{:S(2)}) copy-start(s32[8,32]{1,0:T(8,128)} %param.21) | copy-start | bytes 3076
  7.2 11.5 %copy-start.23 = (s32[8]{0:T(128)S(1)}, s32[8]{0:T(128)}, u32[]{:S(2)}) copy-start(s32[8]{0:T(128)} %param.23) | copy-start | bytes 100
  7.2 11.7 %copy-start.20 = (s32[8,32]{1,0:T(8,128)S(1)}, s32[8,32]{1,0:T(8,128)}, u32[]{:S(2)}) copy-start(s32[8,32]{1,0:T(8,128)} %param.22) | copy-start | bytes 3076
  7.2 30.3 %copy-start.9 = (bf16[128,1792]{1,0:T(8,128)(2,1)S(1)}, bf16[128,1792]{1,0:T(8,128)(2,1)}, u32[]{:S(2)}) copy-start(bf16[128,1792]{1,0:T(8,128)(2,1)} %hidden.3) | copy-start | bytes 1376260
  7.2 54.2 %all-gather.13.cloned.1.call-start = ((), (), s32[]{:S(2)}) async-start(), calls=%async_computation.10 | async-start | bytes 2359296 | tf_op jit(solution)/shard_map/all_gather | solution.py:448
  10.8 20.9 %all-to-all-start.1 = ((bf16[4,128,512]{2,1,0:T(8,128)(2,1)}), bf16[4,128,512]{2,1,0:T(8,128)(2,1)S(1)}, u32[]{:S(2)}, u32[]{:S(2)}) async-start(bf16[4,128,512]{2,1,0:T(8,128)(2,1)} %broadcast_in_dim.304), calls=%async_computation.2 | async-start | bytes 1048576 | tf_op jit(solution)/shard_map/all_to_all | solution.py:417
  18.6 82.0 %all-gather.15.cloned.1.call-start = ((), (), s32[]{:S(2)}) async-start(), calls=%async_computation.11 | async-start | bytes 1802240 | tf_op jit(solution)/shard_map/all_gather | solution.py:476
  31.7 5.8 %collective-permute-start = (bf16[4,128,512]{2,1,0:T(8,128)(2,1)S(1)}, bf16[4,128,512]{2,1,0:T(8,128)(2,1)S(1)}, u32[]{:S(2)}, u32[]{:S(2)}) collective-permute-start(bf16[4,128,512]{2,1,0:T(8,128)(2,1)S(1)} %all-to-all-done.1.mine), channel_id=1, source_target_pairs={{0,1},{1,0},{2,3},{3,2},{4,5},{5,4},{6,7},{7,6},{8,9},{9,8},{10,11... | collective-permute-start | bytes 1572872 | tf_op jit(solution)/shard_map/ppermute | solution.py:421
  39.6 1.0 copy-start.2
  61.5 1.6 %copy-start = (bf16[256,32,128]{2,1,0:T(8,128)(2,1)S(1)}, bf16[256,32,128]{2,1,0:T(8,128)(2,1)}, u32[]{:S(2)}) copy-start(bf16[256,32,128]{2,1,0:T(8,128)(2,1)} %all-gather.13.cloned.1.call-done.gathered) | copy-start | bytes 6291460
  63.0 19.4 %copy-start.14 = (f32[1,32,256]{2,1,0:T(8,128)S(1)}, f32[1,32,256]{2,1,0:T(8,128)}, u32[]{:S(2)}) copy-start(f32[1,32,256]{2,1,0:T(8,128)} %param.26) | copy-start | bytes 98308
  63.0 19.4 %copy-start.16 = (f32[1,32,256]{2,1,0:T(8,128)S(1)}, f32[1,32,256]{2,1,0:T(8,128)}, u32[]{:S(2)}) copy-start(f32[1,32,256]{2,1,0:T(8,128)} %param.27) | copy-start | bytes 98308
  65.7 31.3 %all-to-all-start.3 = ((bf16[16,2,40,128]{3,2,1,0:T(8,128)(2,1)}), bf16[16,2,40,128]{3,2,1,0:T(8,128)(2,1)S(1)}, u32[]{:S(2)}, u32[]{:S(2)}) async-start(bf16[16,2,40,128]{3,2,1,0:T(8,128)(2,1)} %bitcast.46), calls=%async_computation.4 | async-start | bytes 655360 | tf_op jit(solution)/shard_map/all_to_all | solution.py:417
  82.4 18.1 %copy-start.4 = (f32[32,768]{1,0:T(8,128)}, f32[32,768]{1,0:T(8,128)S(1)}, u32[]{:S(2)}) copy-start(f32[32,768]{1,0:T(8,128)S(1)} %pad_maximum_fusion.1.stacked) | copy-start | bytes 294916
  100.5 1.4 copy-start.1
  104.9 11.3 %collective-permute-start.1 = (f32[4,4,128,128]{3,2,1,0:T(8,128)}, f32[4,4,128,128]{3,2,1,0:T(8,128)S(1)}, u32[]{:S(2)}, u32[]{:S(2)}) collective-permute-start(f32[4,4,128,128]{3,2,1,0:T(8,128)} %get-tuple-element.220), channel_id=1, source_target_pairs={{0,1},{1,0},{2,3},{3,2},{4,5},{5,4},{6,7},{7,6},{8,9},{9,8},{10,11... | collective-permute-start | bytes 3145736 | tf_op jit(solution)/shard_map/ppermute | solution.py:421
  108.5 23.1 %all-to-all-start.4 = ((f32[8,40,128]{2,1,0:T(8,128)}), f32[8,40,128]{2,1,0:T(8,128)}, u32[]{:S(2)}, u32[]{:S(2)}) async-start(f32[8,40,128]{2,1,0:T(8,128)} %shard_map.149._after), calls=%async_computation.5 | async-start | bytes 327680 | tf_op jit(solution)/shard_map/all_to_all | solution.py:417
  116.2 12.6 %copy-start.22 = (s32[256]{0:T(256)S(1)}, s32[256]{0:T(256)}, u32[]{:S(2)}) copy-start(s32[256]{0:T(256)} %eq.214) | copy-start | bytes 3076
  116.2 13.4 %copy-start.3 = (bf16[32,128,128]{2,1,0:T(8,128)(2,1)S(1)}, bf16[32,128,128]{2,1,0:T(8,128)(2,1)}, u32[]{:S(2)}) copy-start(bf16[32,128,128]{2,1,0:T(8,128)(2,1)} %copy-done.2) | copy-start | bytes 3145732
  118.3 13.4 %copy-start.5 = (f32[32,768]{1,0:T(8,128)S(1)}, f32[32,768]{1,0:T(8,128)}, u32[]{:S(2)}) copy-start(f32[32,768]{1,0:T(8,128)} %copy-done.4) | copy-start | bytes 294916
  118.3 16.4 %copy-start.7 = (f32[4,128,128]{2,1,0:T(8,128)S(1)}, f32[4,128,128]{2,1,0:T(8,128)}, u32[]{:S(2)}) copy-start(f32[4,128,128]{2,1,0:T(8,128)} %copy-done.6) | copy-start | bytes 786436
  118.3 15.6 %collective-permute-start.2 = (bf16[4,128,128]{2,1,0:T(8,128)(2,1)}, bf16[4,128,128]{2,1,0:T(8,128)(2,1)S(1)}, u32[]{:S(2)}, u32[]{:S(2)}) collective-permute-start(bf16[4,128,128]{2,1,0:T(8,128)(2,1)} %get-tuple-element.222), channel_id=1, source_target_pairs={{0,2},{2,4},{4,6},{6,0},{1,3},{3,5},{5,7},{7,1},{8,10},{10,12},{12... | collective-permute-start | bytes 393224 | tf_op jit(solution)/shard_map/ppermute | solution.py:421
  121.7 12.2 %collective-permute-start.3 = (bf16[4,128,128]{2,1,0:T(8,128)(2,1)}, bf16[4,128,128]{2,1,0:T(8,128)(2,1)S(1)}, u32[]{:S(2)}, u32[]{:S(2)}) collective-permute-start(bf16[4,128,128]{2,1,0:T(8,128)(2,1)} %get-tuple-element.223), channel_id=1, source_target_pairs={{0,4},{2,6},{4,0},{6,2},{1,5},{3,7},{5,1},{7,3},{8,12},{10,14},{12... | collective-permute-start | bytes 393224 | tf_op jit(solution)/shard_map/ppermute | solution.py:421
  125.7 9.0 %collective-permute-start.4 = (bf16[4,128,128]{2,1,0:T(8,128)(2,1)}, bf16[4,128,128]{2,1,0:T(8,128)(2,1)S(1)}, u32[]{:S(2)}, u32[]{:S(2)}) collective-permute-start(bf16[4,128,128]{2,1,0:T(8,128)(2,1)} %get-tuple-element.224), channel_id=1, source_target_pairs={{0,6},{2,0},{4,2},{6,4},{1,7},{3,1},{5,3},{7,5},{8,14},{10,8},{12,... | collective-permute-start | bytes 393224 | tf_op jit(solution)/shard_map/ppermute | solution.py:421
  129.6 5.2 %copy-start.10 = (bf16[128,1792]{1,0:T(8,128)(2,1)S(1)}, bf16[128,1792]{1,0:T(8,128)(2,1)}, u32[]{:S(2)}) copy-start(bf16[128,1792]{1,0:T(8,128)(2,1)} %hidden.3) | copy-start | bytes 1376260
  129.6 5.2 %copy-start.12 = (bf16[128,512]{1,0:T(8,128)(2,1)S(1)}, bf16[128,512]{1,0:T(8,128)(2,1)}, u32[]{:S(2)}) copy-start(bf16[128,512]{1,0:T(8,128)(2,1)} %param.19) | copy-start | bytes 393220
  129.6 5.2 %copy-start.15 = (f32[1,32,256]{2,1,0:T(8,128)S(1)}, f32[1,32,256]{2,1,0:T(8,128)}, u32[]{:S(2)}) copy-start(f32[1,32,256]{2,1,0:T(8,128)} %param.26) | copy-start | bytes 98308
  129.6 5.2 %copy-start.17 = (f32[1,32,256]{2,1,0:T(8,128)S(1)}, f32[1,32,256]{2,1,0:T(8,128)}, u32[]{:S(2)}) copy-start(f32[1,32,256]{2,1,0:T(8,128)} %param.27) | copy-start | bytes 98308
  129.7 5.2 %copy-start.21 = (s32[8,32]{1,0:T(8,128)S(1)}, s32[8,32]{1,0:T(8,128)}, u32[]{:S(2)}) copy-start(s32[8,32]{1,0:T(8,128)} %param.25) | copy-start | bytes 3076
  129.7 5.2 %copy-start.24 = (s32[8]{0:T(128)S(1)}, s32[8]{0:T(128)}, u32[]{:S(2)}) copy-start(s32[8]{0:T(128)} %param.23) | copy-start | bytes 100
  135.1 0.8 copy-start.13
  (2 other events, 1.5 us)
Sparse Core Ops, SparseCore 0:
  10.9 46.0 all-gather.12
  65.0 35.5 all-gather.14

commit v10 on v9

--- a/solution.py
+++ b/solution.py
@@ -260,6 +260,17 @@
     return fits, code, counts, send, state_send, place
 
 
+def prepare_kernel(blocks, out_grad, quarter, sent, sems):
+    rows = quarter.shape[1]
+    first = pl.multiple_of(lax.axis_index("x") * rows, rows)
+    copies = [pltpu.make_async_copy(blocks.at[0, :, pl.ds(first, rows)], quarter, sems.at[NZL])]
+    copies += [pltpu.make_async_copy(out_grad, sent.at[n], sems.at[n]) for n in range(NZL)]
+    for copy in copies:
+        copy.start()
+    for copy in copies:
+        copy.wait()
+
+
 def grad_kernel(info, code, hidden, mine, other, out, cols, hidden_t, total):
     my_core = info[2]
     for zl in range(NZL):
@@ -352,7 +363,7 @@
     for zl in range(NZL):
         for sub in range(4):
             mine[zl, sub] = total[(2 * zl + my_core) * 4 + sub]
-            theirs[zl, sub] = total[(2 * zl + 1 - my_core) * 4 + sub]
+            theirs[zl, sub] = total[(2 * zl + 1 - my_core) * 4 + sub].astype(bf16)
 
 
 def backward_kernel(info, code, cols, weights, back, total):
@@ -377,10 +388,10 @@
 
 def chip_kernel(info, mine, came, own, s1, s2, s3):
     my_zl = info[4]
-    own[...] = mine[my_zl] + came[my_zl]
+    own[...] = mine[my_zl] + came[my_zl].astype(f32)
     for k, out in enumerate((s1, s2, s3)):
         zl = (my_zl + k + 1) % NZL
-        out[...] = (mine[zl] + came[zl]).astype(bf16)
+        out[...] = (mine[zl] + came[zl].astype(f32)).astype(bf16)
 
 
 def project_kernel(own, r1, r2, r3, _after, out):
@@ -443,10 +454,16 @@
     share = first_moment.shape[2]
     scale = 1.0 / math.sqrt(tokens * lax.axis_size(DP))
 
-    quarter = lax.dynamic_slice_in_dim(block_weight[0], x_index * (BS // NX), BS // NX, 1)
-    quarter, sent = lax.optimization_barrier((quarter, out_grad))
+    anywhere = pl.BlockSpec(memory_space=pl.ANY)
+    quarter, sent = pl.pallas_call(
+        prepare_kernel,
+        out_shape=(like((slot_count, BS // NX, BS), bf16), like((NZL,) + out_grad.shape, bf16)),
+        in_specs=[anywhere] * 2,
+        out_specs=(anywhere, anywhere),
+        scratch_shapes=[pltpu.SemaphoreType.DMA((NZL + 1,))],
+    )(block_weight, out_grad)
     gathered = lax.all_gather(quarter, SHARD, axis=0, tiled=True)
-    mine = all_to_all(jnp.broadcast_to(sent[None], (NZL,) + out_grad.shape), "zl")
+    mine = all_to_all(sent, "zl")
     other = shift(mine, "core", 2, 1)
     weight_share = lax.dynamic_slice_in_dim(block_weight[0], dp_index * 2, 2, 1).reshape(slot_count, share)
     stacked = jnp.concatenate([weight_share.astype(f32), first_moment[0], second_moment[0]], axis=1)
@@ -489,7 +506,7 @@
         forward_kernel,
         (
             like((NZL, 4, tokens, BS), f32),
-            like((NZL, 4, tokens, BS), f32),
+            like((NZL, 4, tokens, BS), bf16),
             like((WCAP, NX, BS // NX, BS), bf16),
         ),
         2,

time: 143 us -> 165 us (1.15)
  Pallas kernels: 14 us -> 40.3 us
  local copies, waits for them, and re-layouts: 11.1 us -> 6.49 us
    pallas_call x0 -> x1, Pallas kernels: none -> 25 us  [shards(): pl.pallas_call(prepare_kernel, out_shape=(like((slot_count, BS // NX, BS)...]
    broadcast_in_dim x1 -> x0, local copies, waits for them, and re-layouts: 1.75 us -> none  [shards(): jnp.broadcast_to(sent[None], (NZL,) + out_grad.shape)]
    dynamic_slice x1 -> x0, local copies, waits for them, and re-layouts: 1.74 us -> none  [shards(): lax.dynamic_slice_in_dim(block_weight[0], x_index * (BS // NX), BS // NX, 1)]
    unnamed x49 -> x35, local copies, waits for them, and re-layouts: 5.51 us -> 4.37 us
  transfers between devices with their start and end apart: 10 -> 10, of which waited for: 5 -> 5; matrix products, arithmetic and copies ran while one was open for 6% -> 4% of each run, Pallas kernels for 6% -> 6%
where the time goes in v10:
time: 165 us; the launch traced here: 164 us
  starting transfers between devices  47.2 us (29%)
  Pallas kernels  40.3 us (24%)
  waiting for transfers between devices  26.1 us (16%)
  blocking collectives  20.8 us (13%)
  between operations  17.5 us (11%)
  local copies, waits for them, and re-layouts  6.49 us (4%)
  other arithmetic  5.17 us (3%)
    all_to_all x3, starting transfers between devices, all_to_all(): return lax.all_to_all(values, axis, split_axis=0, concat_axis=0, tiled=True)  28.9 us
    pallas_call x1, Pallas kernels, shards(): pl.pallas_call(prepare_kernel, out_shape=(like((slot_count, BS // NX, BS)...  25 us
    all_to_all x3, waiting for transfers between devices, all_to_all(): return lax.all_to_all(values, axis, split_axis=0, concat_axis=0, tiled=True)  23.7 us
    all_to_all x1, blocking collectives, all_to_all(): return lax.all_to_all(values, axis, split_axis=0, concat_axis=0, tiled=True)  20.8 us
    ppermute x5, starting transfers between devices, shift(): lax.ppermute(values, axis, [(i, (i + step) % count) for i in range(count)])  18.3 us
    unnamed x35, local copies, waits for them, and re-layouts  4.37 us
    pallas_call x1, Pallas kernels, shards(): call(forward_kernel, (like((NZL, 4, tokens, BS), f32), like((NZL, 4, toke...  3.32 us
  transfers between devices with their start and end apart: 10, of which 5 were waited for; matrix products, arithmetic and copies ran while one was open for 4% of the time, Pallas kernels for 6%

profile of v10, /device:TPU:1, one launch (start us, length us, event | category | flops | bytes accessed | tf_op | source)
XLA Modules:
  0.0 163.7 jit_solution(15336163075500496530)
XLA Ops:
  7.3 25.0 %shard_map.147 = (bf16[32,32,128]{2,1,0:T(8,128)(2,1)}, bf16[4,128,512]{2,1,0:T(8,128)(2,1)}) custom-call(bf16[1,32,128,128]{3,2,1,0:T(8,128)(2,1)} %blocks.1, bf16[128,512]{1,0:T(8,128)(2,1)} %out_grad.1), custom_call_target="tpu_custom_call" | custom-call | tf_op jit(solution)/shard_map/pallas_call | solution.py:458
  32.3 7.8 %all-to-all-start.1 = ((bf16[4,128,512]{2,1,0:T(8,128)(2,1)}), bf16[4,128,512]{2,1,0:T(8,128)(2,1)S(1)}, u32[]{:S(2)}, u32[]{:S(2)}) async-start(bf16[4,128,512]{2,1,0:T(8,128)(2,1)} %get-tuple-element.210), calls=%async_computation.2 | async-start | bytes 1048576 | tf_op jit(solution)/shard_map/all_to_all | solution.py:428
  40.5 0.5 broadcast_compare_fusion.1
  41.1 0.3 convert_reduce_fusion.1
  41.6 0.3 convert_reduce_fusion.3
  41.9 0.7 convert_reduce_fusion.4
  44.0 9.2 %all-to-all-done.1.mine = bf16[4,128,512]{2,1,0:T(8,128)(2,1)S(1)} async-done(((bf16[4,128,512]{2,1,0:T(8,128)(2,1)}), bf16[4,128,512]{2,1,0:T(8,128)(2,1)S(1)}, u32[]{:S(2)}, u32[]{:S(2)}) %all-to-all-start.1) | async-done | bytes 524320 | tf_op jit(solution)/shard_map/all_to_all | solution.py:428
  53.2 4.3 %collective-permute-start = (bf16[4,128,512]{2,1,0:T(8,128)(2,1)S(1)}, bf16[4,128,512]{2,1,0:T(8,128)(2,1)S(1)}, u32[]{:S(2)}, u32[]{:S(2)}) collective-permute-start(bf16[4,128,512]{2,1,0:T(8,128)(2,1)S(1)} %all-to-all-done.1.mine), channel_id=1, source_target_pairs={{0,1},{1,0},{2,3},{3,2},{4,5},{5,4},{6,7},{7,6},{8,9},{9,8},{10,11... | collective-permute-start | bytes 1572872 | tf_op jit(solution)/shard_map/ppermute | solution.py:432
  57.5 1.2 and_select_fusion.3
  59.0 1.9 %shard_map.148 = (bf16[4,32,40,128]{3,2,1,0:T(8,128)(2,1)S(1)}, bf16[32,128,128]{2,1,0:T(8,128)(2,1)S(1)}) custom-call(s32[6]{0:T(128)S(1)} %stack.27.info, s32[44]{0:T(128)S(1)} %select_reduce_fusion.4.code, bf16[128,1792]{1,0:T(8,128)(2,1)S(1)} %copy-done.7, bf16[4,128,512]{2,1,0:T(8,128)(2,1)S(1)} %all-to-all-done.1.mine, ...), custom_call_target="tpu_custom_call" | custom-call | flops 184549376 | bytes 4194304 | tf_op jit(solution)/shard_map/pallas_call | solution.py:476
  61.0 20.8 %all_to_all.24.parts = bf16[4,32,40,128]{3,2,1,0:T(8,128)(2,1)S(1)} all-to-all(bf16[4,32,40,128]{3,2,1,0:T(8,128)(2,1)S(1)} %get-tuple-element.211), channel_id=1, replica_groups=mesh['y'=8,'x'=4,'zh'=2,'zl'=4,'core'=2] {'x'}, dimensions={0} | all-to-all | bytes 2621440 | tf_op jit(solution)/shard_map/all_to_all | solution.py:428
  81.8 1.6 copy-done
  83.4 1.8 %shard_map.149 = (bf16[44,32,128]{2,1,0:T(8,128)(2,1)}, bf16[32,40,128]{2,1,0:T(8,128)(2,1)}) custom-call(s32[6]{0:T(128)S(1)} %stack.27.info, s32[44]{0:T(128)S(1)} %select_reduce_fusion.4.code, bf16[256,32,128]{2,1,0:T(8,128)(2,1)S(1)} %copy-done, bf16[4,32,40,128]{3,2,1,0:T(8,128)(2,1)S(1)} %all_to_all.24.parts), custom_call_target="tpu_custom_call" | custom-call | bytes 4194304 | tf_op jit(solution)/shard_map/pallas_call | solution.py:486
  85.2 0.9 dynamic-slice_convert_fusion
  86.0 16.5 %all-to-all-start.3 = ((bf16[16,2,40,128]{3,2,1,0:T(8,128)(2,1)}), bf16[16,2,40,128]{3,2,1,0:T(8,128)(2,1)S(1)}, u32[]{:S(2)}, u32[]{:S(2)}) async-start(bf16[16,2,40,128]{3,2,1,0:T(8,128)(2,1)} %bitcast.45), calls=%async_computation.4 | async-start | bytes 655360 | tf_op jit(solution)/shard_map/all_to_all | solution.py:428
  102.9 14.5 %all-to-all-done.3.parts = bf16[16,2,40,128]{3,2,1,0:T(8,128)(2,1)S(1)} async-done(((bf16[16,2,40,128]{3,2,1,0:T(8,128)(2,1)}), bf16[16,2,40,128]{3,2,1,0:T(8,128)(2,1)S(1)}, u32[]{:S(2)}, u32[]{:S(2)}) %all-to-all-start.3) | async-done | bytes 327712 | tf_op jit(solution)/shard_map/all_to_all | solution.py:428
  117.4 1.5 shard_map.150._after
  118.9 2.1 %all-gather.15.cloned.1.call-done = bf16[176,32,128]{2,1,0:T(8,128)(2,1)} async-done(((bf16[44,32,128]{2,1,0:T(8,128)(2,1)}), bf16[176,32,128]{2,1,0:T(8,128)(2,1)}) %all-gather.15.cloned.1.call-update) | async-done | bytes 1441808 | tf_op jit(solution)/shard_map/all_gather | solution.py:493
  121.0 1.4 copy-done.1
  122.3 3.3 %shard_map.151 = (f32[4,4,128,128]{3,2,1,0:T(8,128)S(1)}, bf16[4,4,128,128]{3,2,1,0:T(8,128)(2,1)}, bf16[44,4,32,128]{3,2,1,0:T(8,128)(2,1)S(1)}) custom-call(s32[6]{0:T(128)S(1)} %stack.27.info, s32[44]{0:T(128)S(1)} %select_reduce_fusion.4.code, bf16[128,1792]{1,0:T(8,128)(2,1)} %hidden.3, bf16[4,44,32,128]{3,2,1,0:T(8,128)(2,1)S(1)} %bitcast.128, ...), custom_call_target="tpu_custom_call" | custom-call | flops 184549376 | bytes 8388608 | tf_op jit(solution)/shard_map/pallas_call | solution.py:505
  125.6 3.5 %collective-permute-start.1 = (bf16[4,4,128,128]{3,2,1,0:T(8,128)(2,1)}, bf16[4,4,128,128]{3,2,1,0:T(8,128)(2,1)}, u32[]{:S(2)}, u32[]{:S(2)}) collective-permute-start(bf16[4,4,128,128]{3,2,1,0:T(8,128)(2,1)} %get-tuple-element.220), channel_id=1, source_target_pairs={{0,1},{1,0},{2,3},{3,2},{4,5},{5,4},{6,7},{7,6},{8,9},{9,8},{10,11... | collective-permute-start | bytes 1572872 | tf_op jit(solution)/shard_map/ppermute | solution.py:432
  129.1 4.5 %all-to-all-start.4 = ((f32[8,40,128]{2,1,0:T(8,128)}), f32[8,40,128]{2,1,0:T(8,128)}, u32[]{:S(2)}, u32[]{:S(2)}) async-start(f32[8,40,128]{2,1,0:T(8,128)} %shard_map.150._after), calls=%async_computation.5 | async-start | bytes 327680 | tf_op jit(solution)/shard_map/all_to_all | solution.py:428
  133.7 1.3 eq.214
  136.9 1.9 %shard_map.154 = (f32[4,128,128]{2,1,0:T(8,128)S(1)}, bf16[4,128,128]{2,1,0:T(8,128)(2,1)}, bf16[4,128,128]{2,1,0:T(8,128)(2,1)}, bf16[4,128,128]{2,1,0:T(8,128)(2,1)}) custom-call(s32[6]{0:T(128)S(1)} %stack.27.info, f32[4,4,128,128]{3,2,1,0:T(8,128)S(1)} %get-tuple-element.219.mine, bf16[4,4,128,128]{3,2,1,0:T(8,128)(2,1)} %collective-permute-done.1.came), custom_call_target="tpu_custom_call" | custom-call | bytes 3145728 | tf_op jit(solution)/shard_map/pallas_call | solution.py:530
  138.8 0.7 copy-done.4
  139.5 3.4 %collective-permute-start.2 = (bf16[4,128,128]{2,1,0:T(8,128)(2,1)}, bf16[4,128,128]{2,1,0:T(8,128)(2,1)S(1)}, u32[]{:S(2)}, u32[]{:S(2)}) collective-permute-start(bf16[4,128,128]{2,1,0:T(8,128)(2,1)} %get-tuple-element.222), channel_id=1, source_target_pairs={{0,2},{2,4},{4,6},{6,0},{1,3},{3,5},{5,7},{7,1},{8,10},{10,12},{12... | collective-permute-start | bytes 393224 | tf_op jit(solution)/shard_map/ppermute | solution.py:432
  142.9 4.0 %collective-permute-start.3 = (bf16[4,128,128]{2,1,0:T(8,128)(2,1)}, bf16[4,128,128]{2,1,0:T(8,128)(2,1)S(1)}, u32[]{:S(2)}, u32[]{:S(2)}) collective-permute-start(bf16[4,128,128]{2,1,0:T(8,128)(2,1)} %get-tuple-element.223), channel_id=1, source_target_pairs={{0,4},{2,6},{4,0},{6,2},{1,5},{3,7},{5,1},{7,3},{8,12},{10,14},{12... | collective-permute-start | bytes 393224 | tf_op jit(solution)/shard_map/ppermute | solution.py:432
  146.9 3.1 %collective-permute-start.4 = (bf16[4,128,128]{2,1,0:T(8,128)(2,1)}, bf16[4,128,128]{2,1,0:T(8,128)(2,1)S(1)}, u32[]{:S(2)}, u32[]{:S(2)}) collective-permute-start(bf16[4,128,128]{2,1,0:T(8,128)(2,1)} %get-tuple-element.224), channel_id=1, source_target_pairs={{0,6},{2,0},{4,2},{6,4},{1,7},{3,1},{5,3},{7,5},{8,14},{10,8},{12,... | collective-permute-start | bytes 393224 | tf_op jit(solution)/shard_map/ppermute | solution.py:432
  150.0 0.8 select_reduce_fusion.5.place
  150.8 2.7 %shard_map.152._after = bf16[128,1792]{1,0:T(8,128)(2,1)} custom-call(s32[6]{0:T(128)S(1)} %stack.27.info, s32[44]{0:T(128)S(1)} %select_reduce_fusion.4.code, bf16[32,128,128]{2,1,0:T(8,128)(2,1)S(1)} %get-tuple-element.213.cols, bf16[44,4,32,128]{3,2,1,0:T(8,128)(2,1)S(1)} %get-tuple-element.215.weights), custom_call_target="tpu_custom_call" | custom-call | flops 184549376 | bytes 4194304 | tf_op jit(solution)/shard_map/pallas_call | solution.py:520
  153.6 2.2 %shard_map.153 = (f32[32,256]{1,0:T(8,128)}, f32[32,256]{1,0:T(8,128)}, f32[32,256]{1,0:T(8,128)}) custom-call(s32[32]{0:T(128)S(1)} %select_reduce_fusion.5.place, f32[32,768]{1,0:T(8,128)S(1)} %copy-done.3, f32[8,40,128]{2,1,0:T(8,128)} %all-to-all-done.4.came, bf16[128,1792]{1,0:T(8,128)(2,1)} %shard_map.152._after), custom_call_target="tpu_custom_call" | custom-call | bytes 1048576 | tf_op jit(solution)/shard_map/pallas_call | solution.py:539
  156.3 0.6 copy-done.9
  (68 shorter events, 2.1 us)
Async XLA Ops:
  7.2 33.0 %copy-start.14 = (s32[8,32]{1,0:T(8,128)S(1)}, s32[8,32]{1,0:T(8,128)}, u32[]{:S(2)}) copy-start(s32[8,32]{1,0:T(8,128)} %param.24) | copy-start | bytes 3076
  7.2 33.0 %copy-start.15 = (s32[8,32]{1,0:T(8,128)S(1)}, s32[8,32]{1,0:T(8,128)}, u32[]{:S(2)}) copy-start(s32[8,32]{1,0:T(8,128)} %param.21) | copy-start | bytes 3076
  7.2 33.0 %copy-start.18 = (s32[8]{0:T(128)S(1)}, s32[8]{0:T(128)}, u32[]{:S(2)}) copy-start(s32[8]{0:T(128)} %param.23) | copy-start | bytes 100
  7.2 33.3 %copy-start.16 = (s32[8,32]{1,0:T(8,128)S(1)}, s32[8,32]{1,0:T(8,128)}, u32[]{:S(2)}) copy-start(s32[8,32]{1,0:T(8,128)} %param.22) | copy-start | bytes 3076
  7.2 51.8 %copy-start.7 = (bf16[128,1792]{1,0:T(8,128)(2,1)S(1)}, bf16[128,1792]{1,0:T(8,128)(2,1)}, u32[]{:S(2)}) copy-start(bf16[128,1792]{1,0:T(8,128)(2,1)} %hidden.3) | copy-start | bytes 1376260
  7.2 74.5 %all-gather.13.cloned.1.call-start = ((), (), s32[]{:S(2)}) async-start(), calls=%async_computation.10 | async-start | bytes 2359296 | tf_op jit(solution)/shard_map/all_gather | solution.py:465
  32.3 21.0 %all-to-all-start.1 = ((bf16[4,128,512]{2,1,0:T(8,128)(2,1)}), bf16[4,128,512]{2,1,0:T(8,128)(2,1)S(1)}, u32[]{:S(2)}, u32[]{:S(2)}) async-start(bf16[4,128,512]{2,1,0:T(8,128)(2,1)} %get-tuple-element.210), calls=%async_computation.2 | async-start | bytes 1048576 | tf_op jit(solution)/shard_map/all_to_all | solution.py:428
  40.1 80.8 %all-gather.15.cloned.1.call-start = ((), (), s32[]{:S(2)}) async-start(), calls=%async_computation.11 | async-start | bytes 1802240 | tf_op jit(solution)/shard_map/all_gather | solution.py:493
  53.2 5.8 %collective-permute-start = (bf16[4,128,512]{2,1,0:T(8,128)(2,1)S(1)}, bf16[4,128,512]{2,1,0:T(8,128)(2,1)S(1)}, u32[]{:S(2)}, u32[]{:S(2)}) collective-permute-start(bf16[4,128,512]{2,1,0:T(8,128)(2,1)S(1)} %all-to-all-done.1.mine), channel_id=1, source_target_pairs={{0,1},{1,0},{2,3},{3,2},{4,5},{5,4},{6,7},{7,6},{8,9},{9,8},{10,11... | collective-permute-start | bytes 1572872 | tf_op jit(solution)/shard_map/ppermute | solution.py:432
  81.8 1.6 copy-start
  83.4 19.4 %copy-start.10 = (f32[1,32,256]{2,1,0:T(8,128)S(1)}, f32[1,32,256]{2,1,0:T(8,128)}, u32[]{:S(2)}) copy-start(f32[1,32,256]{2,1,0:T(8,128)} %param.26) | copy-start | bytes 98308
  83.4 19.4 %copy-start.12 = (f32[1,32,256]{2,1,0:T(8,128)S(1)}, f32[1,32,256]{2,1,0:T(8,128)}, u32[]{:S(2)}) copy-start(f32[1,32,256]{2,1,0:T(8,128)} %param.27) | copy-start | bytes 98308
  86.0 31.3 %all-to-all-start.3 = ((bf16[16,2,40,128]{3,2,1,0:T(8,128)(2,1)}), bf16[16,2,40,128]{3,2,1,0:T(8,128)(2,1)S(1)}, u32[]{:S(2)}, u32[]{:S(2)}) async-start(bf16[16,2,40,128]{3,2,1,0:T(8,128)(2,1)} %bitcast.45), calls=%async_computation.4 | async-start | bytes 655360 | tf_op jit(solution)/shard_map/all_to_all | solution.py:428
  102.8 18.2 %copy-start.2 = (f32[32,768]{1,0:T(8,128)}, f32[32,768]{1,0:T(8,128)S(1)}, u32[]{:S(2)}) copy-start(f32[32,768]{1,0:T(8,128)S(1)} %pad_maximum_fusion.1.stacked) | copy-start | bytes 294916
  121.0 1.4 copy-start.1
  125.6 11.3 %collective-permute-start.1 = (bf16[4,4,128,128]{3,2,1,0:T(8,128)(2,1)}, bf16[4,4,128,128]{3,2,1,0:T(8,128)(2,1)}, u32[]{:S(2)}, u32[]{:S(2)}) collective-permute-start(bf16[4,4,128,128]{3,2,1,0:T(8,128)(2,1)} %get-tuple-element.220), channel_id=1, source_target_pairs={{0,1},{1,0},{2,3},{3,2},{4,5},{5,4},{6,7},{7,6},{8,9},{9,8},{10,11... | collective-permute-start | bytes 1572872 | tf_op jit(solution)/shard_map/ppermute | solution.py:432
  129.1 24.4 %all-to-all-start.4 = ((f32[8,40,128]{2,1,0:T(8,128)}), f32[8,40,128]{2,1,0:T(8,128)}, u32[]{:S(2)}, u32[]{:S(2)}) async-start(f32[8,40,128]{2,1,0:T(8,128)} %shard_map.150._after), calls=%async_computation.5 | async-start | bytes 327680 | tf_op jit(solution)/shard_map/all_to_all | solution.py:428
  138.8 0.7 copy-start.4
  139.5 14.1 %copy-start.3 = (f32[32,768]{1,0:T(8,128)S(1)}, f32[32,768]{1,0:T(8,128)}, u32[]{:S(2)}) copy-start(f32[32,768]{1,0:T(8,128)} %copy-done.2) | copy-start | bytes 294916
  139.5 16.4 %copy-start.5 = (f32[4,128,128]{2,1,0:T(8,128)S(1)}, f32[4,128,128]{2,1,0:T(8,128)}, u32[]{:S(2)}) copy-start(f32[4,128,128]{2,1,0:T(8,128)} %copy-done.4) | copy-start | bytes 786436
  139.5 16.3 %collective-permute-start.2 = (bf16[4,128,128]{2,1,0:T(8,128)(2,1)}, bf16[4,128,128]{2,1,0:T(8,128)(2,1)S(1)}, u32[]{:S(2)}, u32[]{:S(2)}) collective-permute-start(bf16[4,128,128]{2,1,0:T(8,128)(2,1)} %get-tuple-element.222), channel_id=1, source_target_pairs={{0,2},{2,4},{4,6},{6,0},{1,3},{3,5},{5,7},{7,1},{8,10},{10,12},{12... | collective-permute-start | bytes 393224 | tf_op jit(solution)/shard_map/ppermute | solution.py:432
  142.9 12.8 %collective-permute-start.3 = (bf16[4,128,128]{2,1,0:T(8,128)(2,1)}, bf16[4,128,128]{2,1,0:T(8,128)(2,1)S(1)}, u32[]{:S(2)}, u32[]{:S(2)}) collective-permute-start(bf16[4,128,128]{2,1,0:T(8,128)(2,1)} %get-tuple-element.223), channel_id=1, source_target_pairs={{0,4},{2,6},{4,0},{6,2},{1,5},{3,7},{5,1},{7,3},{8,12},{10,14},{12... | collective-permute-start | bytes 393224 | tf_op jit(solution)/shard_map/ppermute | solution.py:432
  146.9 9.0 %collective-permute-start.4 = (bf16[4,128,128]{2,1,0:T(8,128)(2,1)}, bf16[4,128,128]{2,1,0:T(8,128)(2,1)S(1)}, u32[]{:S(2)}, u32[]{:S(2)}) collective-permute-start(bf16[4,128,128]{2,1,0:T(8,128)(2,1)} %get-tuple-element.224), channel_id=1, source_target_pairs={{0,6},{2,0},{4,2},{6,4},{1,7},{3,1},{5,3},{7,5},{8,14},{10,8},{12,... | collective-permute-start | bytes 393224 | tf_op jit(solution)/shard_map/ppermute | solution.py:432
  150.8 5.2 %copy-start.8 = (bf16[128,512]{1,0:T(8,128)(2,1)S(1)}, bf16[128,512]{1,0:T(8,128)(2,1)}, u32[]{:S(2)}) copy-start(bf16[128,512]{1,0:T(8,128)(2,1)} %out_grad.1) | copy-start | bytes 393220
  150.8 5.2 %copy-start.17 = (s32[8,32]{1,0:T(8,128)S(1)}, s32[8,32]{1,0:T(8,128)}, u32[]{:S(2)}) copy-start(s32[8,32]{1,0:T(8,128)} %param.25) | copy-start | bytes 3076
  150.8 5.2 %copy-start.19 = (s32[8]{0:T(128)S(1)}, s32[8]{0:T(128)}, u32[]{:S(2)}) copy-start(s32[8]{0:T(128)} %param.23) | copy-start | bytes 100
  156.2 0.7 copy-start.9
Sparse Core Ops, SparseCore 0:
  32.4 46.1 all-gather.12
  85.3 35.6 all-gather.14

commit v11 on v9

--- a/solution.py
+++ b/solution.py
@@ -257,7 +257,7 @@
     landing = 1 + row_shard * PAIR + jnp.minimum(pos, PAIR - 1) + shard_count * PAIR * state_row
     lands = (owner == me)[None, :] & (slot[None, :] == jnp.arange(slot_count)[:, None])
     place = jnp.sum(jnp.where(lands, landing[None, :], 0), axis=1)
-    return fits, code, counts, send, state_send, place
+    return fits.astype(i32).reshape(1), code, counts, send, state_send, place
 
 
 def grad_kernel(info, code, hidden, mine, other, out, cols, hidden_t, total):
@@ -288,7 +288,7 @@
                 out[x, 4 * y + q] = total[source * GCAP : (source + 1) * GCAP, :].astype(bf16)
 
 
-def share_kernel(scale, send, state_send, parts, stacked, out, total):
+def share_kernel(scale, send, state_send, parts, stacked, _after, _after2, out, total):
     total[...] = parts[0].astype(f32)
 
     def step(n, carry):
@@ -482,7 +482,8 @@
         2,
         [pltpu.VMEM((2, GCAP, BS), f32)],
         byts=1024 * 1024,
-    )(send, state_send, along_yz, stacked)
+        n_after=2,
+    )(send, state_send, along_yz, stacked, place, fits)
     shares = all_to_all(packed, SHARD)
 
     out_mine, out_theirs, weights = call(
@@ -530,7 +531,7 @@
     )(place, stacked, shares, hidden_grad)
     result = (projected, hidden_grad, new_weight[None], new_first[None], new_second[None])
     return lax.cond(
-        fits,
+        fits[0] > 0,
         lambda: result,
         lambda: general(
             hidden,

time: 143 us -> 141 us (0.986)
  waiting for transfers between devices: 26.7 us -> 24.3 us
  other arithmetic: 5.16 us -> 3.34 us
    unnamed x49, local copies, waits for them, and re-layouts: 5.51 us -> 7.6 us
  transfers between devices with their start and end apart: 10 -> 10, of which waited for: 5 -> 4; matrix products, arithmetic and copies ran while one was open for 6% -> 4% of each run, Pallas kernels for 6% -> 7%
where the time goes in v11:
time: 141 us
  starting transfers between devices  47.3 us (34%)
  waiting for transfers between devices  24.3 us (17%)
  blocking collectives  21.5 us (15%)
  between operations  17.5 us (12%)
  Pallas kernels  14.4 us (10%)
  local copies, waits for them, and re-layouts  12 us (9%)
  other arithmetic  3.34 us (2%)
    all_to_all x3, starting transfers between devices, all_to_all(): return lax.all_to_all(values, axis, split_axis=0, concat_axis=0, tiled=True)  29.3 us
    all_to_all x3, waiting for transfers between devices, all_to_all(): return lax.all_to_all(values, axis, split_axis=0, concat_axis=0, tiled=True)  22.3 us
    all_to_all x1, blocking collectives, all_to_all(): return lax.all_to_all(values, axis, split_axis=0, concat_axis=0, tiled=True)  21.5 us
    ppermute x5, starting transfers between devices, shift(): lax.ppermute(values, axis, [(i, (i + step) % count) for i in range(count)])  18 us
    unnamed x49, local copies, waits for them, and re-layouts  7.6 us
    pallas_call x1, Pallas kernels, shards(): call(forward_kernel, (like((NZL, 4, tokens, BS), f32), like((NZL, 4, toke...  3.22 us
  transfers between devices with their start and end apart: 10, of which 4 were waited for; matrix products, arithmetic and copies ran while one was open for 4% of the time, Pallas kernels for 7%

profile of v11, /device:TPU:1, one launch (start us, length us, event | category | flops | bytes accessed | tf_op | source)
XLA Modules:
  0.0 140.6 jit_solution(11171778285994353917)
XLA Ops:
  7.3 1.7 %dynamic-slice_bitcast_fusion.1 = bf16[32,32,128]{2,1,0:T(8,128)(2,1)} fusion(bf16[1,32,128,128]{3,2,1,0:T(8,128)(2,1)} %param.20, s32[]{:T(128)S(6)} %select_n.333), kind=kLoop, calls=%fused_computation.122 | loop fusion | bytes 524292 | tf_op jit(solution)/shard_map/dynamic_slice | solution.py:446
  9.0 1.7 %broadcast_in_dim.304 = bf16[4,128,512]{2,1,0:T(8,128)(2,1)} broadcast(bf16[128,512]{1,0:T(8,128)(2,1)} %param.19), dimensions={1,2} | broadcast | bytes 655360 | tf_op jit(solution)/shard_map/broadcast_in_dim | solution.py:449
  10.8 7.8 %all-to-all-start.1 = ((bf16[4,128,512]{2,1,0:T(8,128)(2,1)}), bf16[4,128,512]{2,1,0:T(8,128)(2,1)S(1)}, u32[]{:S(2)}, u32[]{:S(2)}) async-start(bf16[4,128,512]{2,1,0:T(8,128)(2,1)} %broadcast_in_dim.304), calls=%async_computation.2 | async-start | bytes 1048576 | tf_op jit(solution)/shard_map/all_to_all | solution.py:417
  19.8 0.7 convert_reduce_fusion.4
  21.9 9.8 %all-to-all-done.1.mine = bf16[4,128,512]{2,1,0:T(8,128)(2,1)S(1)} async-done(((bf16[4,128,512]{2,1,0:T(8,128)(2,1)}), bf16[4,128,512]{2,1,0:T(8,128)(2,1)S(1)}, u32[]{:S(2)}, u32[]{:S(2)}) %all-to-all-start.1) | async-done | bytes 524320 | tf_op jit(solution)/shard_map/all_to_all | solution.py:417
  31.7 4.3 %collective-permute-start = (bf16[4,128,512]{2,1,0:T(8,128)(2,1)S(1)}, bf16[4,128,512]{2,1,0:T(8,128)(2,1)S(1)}, u32[]{:S(2)}, u32[]{:S(2)}) collective-permute-start(bf16[4,128,512]{2,1,0:T(8,128)(2,1)S(1)} %all-to-all-done.1.mine), channel_id=1, source_target_pairs={{0,1},{1,0},{2,3},{3,2},{4,5},{5,4},{6,7},{7,6},{8,9},{9,8},{10,11... | collective-permute-start | bytes 1572872 | tf_op jit(solution)/shard_map/ppermute | solution.py:421
  36.0 0.6 and_select_fusion.3
  36.8 0.8 collective-permute-done.other
  37.5 2.1 %shard_map.147 = (bf16[4,32,40,128]{3,2,1,0:T(8,128)(2,1)S(1)}, bf16[32,128,128]{2,1,0:T(8,128)(2,1)S(1)}) custom-call(s32[6]{0:T(128)S(1)} %stack.27.info, s32[44]{0:T(128)S(1)} %select_reduce_fusion.4.code, bf16[128,1792]{1,0:T(8,128)(2,1)S(1)} %copy-done.9, bf16[4,128,512]{2,1,0:T(8,128)(2,1)S(1)} %all-to-all-done.1.mine, ...), custom_call_target="tpu_custom_call" | custom-call | flops 184549376 | bytes 4194304 | tf_op jit(solution)/shard_map/pallas_call | solution.py:459
  39.6 1.0 copy-done.2
  40.6 21.5 %all_to_all.24.parts = bf16[4,32,40,128]{3,2,1,0:T(8,128)(2,1)S(1)} all-to-all(bf16[4,32,40,128]{3,2,1,0:T(8,128)(2,1)S(1)} %get-tuple-element.211), channel_id=1, replica_groups=mesh['y'=8,'x'=4,'zh'=2,'zl'=4,'core'=2] {'x'}, dimensions={0} | all-to-all | bytes 2621440 | tf_op jit(solution)/shard_map/all_to_all | solution.py:417
  62.1 1.6 %copy-done = bf16[256,32,128]{2,1,0:T(8,128)(2,1)S(1)} copy-done((bf16[256,32,128]{2,1,0:T(8,128)(2,1)S(1)}, bf16[256,32,128]{2,1,0:T(8,128)(2,1)}, u32[]{:S(2)}) %copy-start) | copy-done | bytes 2097176
  63.7 1.8 %shard_map.148 = (bf16[44,32,128]{2,1,0:T(8,128)(2,1)}, bf16[32,40,128]{2,1,0:T(8,128)(2,1)}) custom-call(s32[6]{0:T(128)S(1)} %stack.27.info, s32[44]{0:T(128)S(1)} %select_reduce_fusion.4.code, bf16[256,32,128]{2,1,0:T(8,128)(2,1)S(1)} %copy-done, bf16[4,32,40,128]{3,2,1,0:T(8,128)(2,1)S(1)} %all_to_all.24.parts), custom_call_target="tpu_custom_call" | custom-call | bytes 4194304 | tf_op jit(solution)/shard_map/pallas_call | solution.py:469
  65.6 0.9 dynamic-slice_convert_fusion
  66.5 16.5 %all-to-all-start.3 = ((bf16[16,2,40,128]{3,2,1,0:T(8,128)(2,1)}), bf16[16,2,40,128]{3,2,1,0:T(8,128)(2,1)S(1)}, u32[]{:S(2)}, u32[]{:S(2)}) async-start(bf16[16,2,40,128]{3,2,1,0:T(8,128)(2,1)} %bitcast.46), calls=%async_computation.4 | async-start | bytes 655360 | tf_op jit(solution)/shard_map/all_to_all | solution.py:417
  85.3 12.5 %all-to-all-done.3.parts = bf16[16,2,40,128]{3,2,1,0:T(8,128)(2,1)S(1)} async-done(((bf16[16,2,40,128]{3,2,1,0:T(8,128)(2,1)}), bf16[16,2,40,128]{3,2,1,0:T(8,128)(2,1)S(1)}, u32[]{:S(2)}, u32[]{:S(2)}) %all-to-all-start.3) | async-done | bytes 327712 | tf_op jit(solution)/shard_map/all_to_all | solution.py:417
  97.8 1.5 %shard_map.149._after = f32[8,40,128]{2,1,0:T(8,128)} custom-call(s32[112]{0:T(128)S(1)} %broadcast_minimum_fusion.send, s32[16]{0:T(128)S(1)} %select_reduce_fusion.6.state_send, bf16[16,2,40,128]{3,2,1,0:T(8,128)(2,1)S(1)} %all-to-all-done.3.parts, f32[32,768]{1,0:T(8,128)S(1)} %pad_maximum_fusion.1.stacked, s32[32]{0:T(128)S(1)} %select_reduce_fusion.5._after.place, ...), custom_call_target="tpu_custom_call" | custom-call | bytes 1048576 | tf_op jit(solution)/shard_map/pallas_call | solution.py:478
  99.3 1.2 all-gather.15.cloned.1.call-done
  100.6 1.4 copy-done.1
  101.9 3.2 %shard_map.150 = (f32[4,4,128,128]{3,2,1,0:T(8,128)S(1)}, f32[4,4,128,128]{3,2,1,0:T(8,128)}, bf16[44,4,32,128]{3,2,1,0:T(8,128)(2,1)S(1)}) custom-call(s32[6]{0:T(128)S(1)} %stack.27.info, s32[44]{0:T(128)S(1)} %select_reduce_fusion.4.code, bf16[128,1792]{1,0:T(8,128)(2,1)S(1)} %copy-done.9, bf16[4,44,32,128]{3,2,1,0:T(8,128)(2,1)S(1)} %bitcast.131, ...), custom_call_target="tpu_custom_call" | custom-call | flops 184549376 | bytes 8388608 | tf_op jit(solution)/shard_map/pallas_call | solution.py:489
  105.2 3.3 %collective-permute-start.1 = (f32[4,4,128,128]{3,2,1,0:T(8,128)}, f32[4,4,128,128]{3,2,1,0:T(8,128)S(1)}, u32[]{:S(2)}, u32[]{:S(2)}) collective-permute-start(f32[4,4,128,128]{3,2,1,0:T(8,128)} %get-tuple-element.220), channel_id=1, source_target_pairs={{0,1},{1,0},{2,3},{3,2},{4,5},{5,4},{6,7},{7,6},{8,9},{9,8},{10,11... | collective-permute-start | bytes 3145736 | tf_op jit(solution)/shard_map/ppermute | solution.py:421
  108.5 5.0 %all-to-all-start.4 = ((f32[8,40,128]{2,1,0:T(8,128)}), f32[8,40,128]{2,1,0:T(8,128)}, u32[]{:S(2)}, u32[]{:S(2)}) async-start(f32[8,40,128]{2,1,0:T(8,128)} %shard_map.149._after), calls=%async_computation.5 | async-start | bytes 327680 | tf_op jit(solution)/shard_map/all_to_all | solution.py:417
  113.5 1.3 shard_map.153
  114.9 0.7 copy-done.6
  115.6 3.3 %collective-permute-start.2 = (bf16[4,128,128]{2,1,0:T(8,128)(2,1)}, bf16[4,128,128]{2,1,0:T(8,128)(2,1)S(1)}, u32[]{:S(2)}, u32[]{:S(2)}) collective-permute-start(bf16[4,128,128]{2,1,0:T(8,128)(2,1)} %get-tuple-element.222), channel_id=1, source_target_pairs={{0,2},{2,4},{4,6},{6,0},{1,3},{3,5},{5,7},{7,1},{8,10},{10,12},{12... | collective-permute-start | bytes 393224 | tf_op jit(solution)/shard_map/ppermute | solution.py:421
  118.9 4.0 %collective-permute-start.3 = (bf16[4,128,128]{2,1,0:T(8,128)(2,1)}, bf16[4,128,128]{2,1,0:T(8,128)(2,1)S(1)}, u32[]{:S(2)}, u32[]{:S(2)}) collective-permute-start(bf16[4,128,128]{2,1,0:T(8,128)(2,1)} %get-tuple-element.223), channel_id=1, source_target_pairs={{0,4},{2,6},{4,0},{6,2},{1,5},{3,7},{5,1},{7,3},{8,12},{10,14},{12... | collective-permute-start | bytes 393224 | tf_op jit(solution)/shard_map/ppermute | solution.py:421
  122.9 3.1 %collective-permute-start.4 = (bf16[4,128,128]{2,1,0:T(8,128)(2,1)}, bf16[4,128,128]{2,1,0:T(8,128)(2,1)S(1)}, u32[]{:S(2)}, u32[]{:S(2)}) collective-permute-start(bf16[4,128,128]{2,1,0:T(8,128)(2,1)} %get-tuple-element.224), channel_id=1, source_target_pairs={{0,6},{2,0},{4,2},{6,4},{1,7},{3,1},{5,3},{7,5},{8,14},{10,8},{12,... | collective-permute-start | bytes 393224 | tf_op jit(solution)/shard_map/ppermute | solution.py:421
  126.0 1.2 copy-done.3
  127.2 2.2 %shard_map.151._after = bf16[128,1792]{1,0:T(8,128)(2,1)S(1)} custom-call(s32[6]{0:T(128)S(1)} %stack.27.info, s32[44]{0:T(128)S(1)} %select_reduce_fusion.4.code, bf16[32,128,128]{2,1,0:T(8,128)(2,1)S(1)} %copy-done.3, bf16[44,4,32,128]{3,2,1,0:T(8,128)(2,1)S(1)} %get-tuple-element.215.weights), custom_call_target="tpu_custom_call" | custom-call | flops 184549376 | bytes 4194304 | tf_op jit(solution)/shard_map/pallas_call | solution.py:504
  129.5 0.9 copy-done.5
  130.3 2.2 %shard_map.152 = (f32[32,256]{1,0:T(8,128)}, f32[32,256]{1,0:T(8,128)}, f32[32,256]{1,0:T(8,128)}) custom-call(s32[32]{0:T(128)S(1)} %select_reduce_fusion.5._after.place, f32[32,768]{1,0:T(8,128)S(1)} %copy-done.5, f32[8,40,128]{2,1,0:T(8,128)} %all-to-all-done.4.came, bf16[128,1792]{1,0:T(8,128)(2,1)S(1)} %shard_map.151._after), custom_call_target="tpu_custom_call" | custom-call | bytes 1048576 | tf_op jit(solution)/shard_map/pallas_call | solution.py:523
  132.9 0.7 copy-done.11
  (83 shorter events, 2.6 us)
Async XLA Ops:
  7.2 11.4 %copy-start.18 = (s32[8,32]{1,0:T(8,128)S(1)}, s32[8,32]{1,0:T(8,128)}, u32[]{:S(2)}) copy-start(s32[8,32]{1,0:T(8,128)} %param.24) | copy-start | bytes 3076
  7.2 11.5 %copy-start.19 = (s32[8,32]{1,0:T(8,128)S(1)}, s32[8,32]{1,0:T(8,128)}, u32[]{:S(2)}) copy-start(s32[8,32]{1,0:T(8,128)} %param.21) | copy-start | bytes 3076
  7.2 11.5 %copy-start.23 = (s32[8]{0:T(128)S(1)}, s32[8]{0:T(128)}, u32[]{:S(2)}) copy-start(s32[8]{0:T(128)} %param.23) | copy-start | bytes 100
  7.2 11.7 %copy-start.20 = (s32[8,32]{1,0:T(8,128)S(1)}, s32[8,32]{1,0:T(8,128)}, u32[]{:S(2)}) copy-start(s32[8,32]{1,0:T(8,128)} %param.22) | copy-start | bytes 3076
  7.2 30.3 %copy-start.9 = (bf16[128,1792]{1,0:T(8,128)(2,1)S(1)}, bf16[128,1792]{1,0:T(8,128)(2,1)}, u32[]{:S(2)}) copy-start(bf16[128,1792]{1,0:T(8,128)(2,1)} %hidden.3) | copy-start | bytes 1376260
  7.2 54.9 %all-gather.13.cloned.1.call-start = ((), (), s32[]{:S(2)}) async-start(), calls=%async_computation.10 | async-start | bytes 2359296 | tf_op jit(solution)/shard_map/all_gather | solution.py:448
  10.8 20.9 %all-to-all-start.1 = ((bf16[4,128,512]{2,1,0:T(8,128)(2,1)}), bf16[4,128,512]{2,1,0:T(8,128)(2,1)S(1)}, u32[]{:S(2)}, u32[]{:S(2)}) async-start(bf16[4,128,512]{2,1,0:T(8,128)(2,1)} %broadcast_in_dim.304), calls=%async_computation.2 | async-start | bytes 1048576 | tf_op jit(solution)/shard_map/all_to_all | solution.py:417
  18.6 82.0 %all-gather.15.cloned.1.call-start = ((), (), s32[]{:S(2)}) async-start(), calls=%async_computation.11 | async-start | bytes 1802240 | tf_op jit(solution)/shard_map/all_gather | solution.py:476
  31.7 5.8 %collective-permute-start = (bf16[4,128,512]{2,1,0:T(8,128)(2,1)S(1)}, bf16[4,128,512]{2,1,0:T(8,128)(2,1)S(1)}, u32[]{:S(2)}, u32[]{:S(2)}) collective-permute-start(bf16[4,128,512]{2,1,0:T(8,128)(2,1)S(1)} %all-to-all-done.1.mine), channel_id=1, source_target_pairs={{0,1},{1,0},{2,3},{3,2},{4,5},{5,4},{6,7},{7,6},{8,9},{9,8},{10,11... | collective-permute-start | bytes 1572872 | tf_op jit(solution)/shard_map/ppermute | solution.py:421
  39.6 1.0 copy-start.2
  62.1 1.6 %copy-start = (bf16[256,32,128]{2,1,0:T(8,128)(2,1)S(1)}, bf16[256,32,128]{2,1,0:T(8,128)(2,1)}, u32[]{:S(2)}) copy-start(bf16[256,32,128]{2,1,0:T(8,128)(2,1)} %all-gather.13.cloned.1.call-done.gathered) | copy-start | bytes 6291460
  63.7 19.3 %copy-start.21 = (s32[8,32]{1,0:T(8,128)S(1)}, s32[8,32]{1,0:T(8,128)}, u32[]{:S(2)}) copy-start(s32[8,32]{1,0:T(8,128)} %param.25) | copy-start | bytes 3076
  63.7 21.4 %copy-start.14 = (f32[1,32,256]{2,1,0:T(8,128)S(1)}, f32[1,32,256]{2,1,0:T(8,128)}, u32[]{:S(2)}) copy-start(f32[1,32,256]{2,1,0:T(8,128)} %param.26) | copy-start | bytes 98308
  63.7 21.4 %copy-start.16 = (f32[1,32,256]{2,1,0:T(8,128)S(1)}, f32[1,32,256]{2,1,0:T(8,128)}, u32[]{:S(2)}) copy-start(f32[1,32,256]{2,1,0:T(8,128)} %param.27) | copy-start | bytes 98308
  66.5 31.4 %all-to-all-start.3 = ((bf16[16,2,40,128]{3,2,1,0:T(8,128)(2,1)}), bf16[16,2,40,128]{3,2,1,0:T(8,128)(2,1)S(1)}, u32[]{:S(2)}, u32[]{:S(2)}) async-start(bf16[16,2,40,128]{3,2,1,0:T(8,128)(2,1)} %bitcast.46), calls=%async_computation.4 | async-start | bytes 655360 | tf_op jit(solution)/shard_map/all_to_all | solution.py:417
  85.2 15.4 %copy-start.4 = (f32[32,768]{1,0:T(8,128)}, f32[32,768]{1,0:T(8,128)S(1)}, u32[]{:S(2)}) copy-start(f32[32,768]{1,0:T(8,128)S(1)} %pad_maximum_fusion.1.stacked) | copy-start | bytes 294916
  100.6 1.4 copy-start.1
  105.2 8.4 %collective-permute-start.1 = (f32[4,4,128,128]{3,2,1,0:T(8,128)}, f32[4,4,128,128]{3,2,1,0:T(8,128)S(1)}, u32[]{:S(2)}, u32[]{:S(2)}) collective-permute-start(f32[4,4,128,128]{3,2,1,0:T(8,128)} %get-tuple-element.220), channel_id=1, source_target_pairs={{0,1},{1,0},{2,3},{3,2},{4,5},{5,4},{6,7},{7,6},{8,9},{9,8},{10,11... | collective-permute-start | bytes 3145736 | tf_op jit(solution)/shard_map/ppermute | solution.py:421
  108.5 20.9 %all-to-all-start.4 = ((f32[8,40,128]{2,1,0:T(8,128)}), f32[8,40,128]{2,1,0:T(8,128)}, u32[]{:S(2)}, u32[]{:S(2)}) async-start(f32[8,40,128]{2,1,0:T(8,128)} %shard_map.149._after), calls=%async_computation.5 | async-start | bytes 327680 | tf_op jit(solution)/shard_map/all_to_all | solution.py:417
  115.6 16.9 %collective-permute-start.2 = (bf16[4,128,128]{2,1,0:T(8,128)(2,1)}, bf16[4,128,128]{2,1,0:T(8,128)(2,1)S(1)}, u32[]{:S(2)}, u32[]{:S(2)}) collective-permute-start(bf16[4,128,128]{2,1,0:T(8,128)(2,1)} %get-tuple-element.222), channel_id=1, source_target_pairs={{0,2},{2,4},{4,6},{6,0},{1,3},{3,5},{5,7},{7,1},{8,10},{10,12},{12... | collective-permute-start | bytes 393224 | tf_op jit(solution)/shard_map/ppermute | solution.py:421
  118.9 13.6 %collective-permute-start.3 = (bf16[4,128,128]{2,1,0:T(8,128)(2,1)}, bf16[4,128,128]{2,1,0:T(8,128)(2,1)S(1)}, u32[]{:S(2)}, u32[]{:S(2)}) collective-permute-start(bf16[4,128,128]{2,1,0:T(8,128)(2,1)} %get-tuple-element.223), channel_id=1, source_target_pairs={{0,4},{2,6},{4,0},{6,2},{1,5},{3,7},{5,1},{7,3},{8,12},{10,14},{12... | collective-permute-start | bytes 393224 | tf_op jit(solution)/shard_map/ppermute | solution.py:421
  122.9 9.7 %collective-permute-start.4 = (bf16[4,128,128]{2,1,0:T(8,128)(2,1)}, bf16[4,128,128]{2,1,0:T(8,128)(2,1)S(1)}, u32[]{:S(2)}, u32[]{:S(2)}) collective-permute-start(bf16[4,128,128]{2,1,0:T(8,128)(2,1)} %get-tuple-element.224), channel_id=1, source_target_pairs={{0,6},{2,0},{4,2},{6,4},{1,7},{3,1},{5,3},{7,5},{8,14},{10,8},{12,... | collective-permute-start | bytes 393224 | tf_op jit(solution)/shard_map/ppermute | solution.py:421
  126.0 1.2 copy-start.3
  127.2 5.3 %copy-start.7 = (f32[4,128,128]{2,1,0:T(8,128)S(1)}, f32[4,128,128]{2,1,0:T(8,128)}, u32[]{:S(2)}) copy-start(f32[4,128,128]{2,1,0:T(8,128)} %copy-done.6) | copy-start | bytes 786436
  127.2 5.4 %copy-start.10 = (bf16[128,1792]{1,0:T(8,128)(2,1)S(1)}, bf16[128,1792]{1,0:T(8,128)(2,1)}, u32[]{:S(2)}) copy-start(bf16[128,1792]{1,0:T(8,128)(2,1)} %hidden.3) | copy-start | bytes 1376260
  127.2 5.4 %copy-start.12 = (bf16[128,512]{1,0:T(8,128)(2,1)S(1)}, bf16[128,512]{1,0:T(8,128)(2,1)}, u32[]{:S(2)}) copy-start(bf16[128,512]{1,0:T(8,128)(2,1)} %param.19) | copy-start | bytes 393220
  127.2 5.4 %copy-start.15 = (f32[1,32,256]{2,1,0:T(8,128)S(1)}, f32[1,32,256]{2,1,0:T(8,128)}, u32[]{:S(2)}) copy-start(f32[1,32,256]{2,1,0:T(8,128)} %param.26) | copy-start | bytes 98308
  127.2 5.4 %copy-start.17 = (f32[1,32,256]{2,1,0:T(8,128)S(1)}, f32[1,32,256]{2,1,0:T(8,128)}, u32[]{:S(2)}) copy-start(f32[1,32,256]{2,1,0:T(8,128)} %param.27) | copy-start | bytes 98308
  127.2 5.4 %copy-start.22 = (s32[8,32]{1,0:T(8,128)S(1)}, s32[8,32]{1,0:T(8,128)}, u32[]{:S(2)}) copy-start(s32[8,32]{1,0:T(8,128)} %param.25) | copy-start | bytes 3076
  127.2 5.4 %copy-start.24 = (s32[8]{0:T(128)S(1)}, s32[8]{0:T(128)}, u32[]{:S(2)}) copy-start(s32[8]{0:T(128)} %param.23) | copy-start | bytes 100
  129.5 0.9 copy-start.5
  132.9 0.8 copy-start.13
  (2 other events, 1.5 us)
Sparse Core Ops, SparseCore 0:
  10.9 46.2 all-gather.12
  65.6 34.9 all-gather.14

commit v12 on v11

--- a/solution.py
+++ b/solution.py
@@ -260,6 +260,11 @@
     return fits.astype(i32).reshape(1), code, counts, send, state_send, place
 
 
+def repeat_kernel(value, out):
+    for n in range(out.shape[0]):
+        out[n] = value[...]
+
+
 def grad_kernel(info, code, hidden, mine, other, out, cols, hidden_t, total):
     my_core = info[2]
     for zl in range(NZL):
@@ -327,14 +332,13 @@
     lax.fori_loop(0, summed.shape[0], add, 0, unroll=4)
 
 
-def forward_kernel(info, code, hidden, quarters, _after, mine, theirs, weights, total, sems):
+def whole_block(quarters, c):
+    return jnp.concatenate([quarters[x, c] for x in range(NX)], axis=0)
+
+
+def forward_kernel(info, code, hidden, quarters, _after, mine, theirs, total):
     my_core = info[2]
-    copies = [pltpu.make_async_copy(quarters.at[x], weights.at[:, x], sems.at[x]) for x in range(NX)]
-    for copy in copies:
-        copy.start()
     total[...] = jnp.zeros_like(total)
-    for copy in copies:
-        copy.wait()
 
     def step(i, carry):
         adds = []
@@ -342,7 +346,7 @@
             c = i * UNROLL + u
             word = code[c]
             lanes = pl.ds(pl.multiple_of(((word >> 8) & 15) * BS, BS), BS)
-            w = weights[c].reshape(BS, BS)
+            w = whole_block(quarters, c)
             adds.append((word >> 12, jnp.dot(hidden[:, lanes], w, preferred_element_type=f32)))
         for col, value in adds:
             total[col] += value
@@ -355,7 +359,7 @@
             theirs[zl, sub] = total[(2 * zl + 1 - my_core) * 4 + sub]
 
 
-def backward_kernel(info, code, cols, weights, back, total):
+def backward_kernel(info, code, cols, quarters, back, total):
     total[...] = jnp.zeros_like(total)
 
     def step(i, carry):
@@ -363,7 +367,7 @@
         for u in range(UNROLL):
             c = i * UNROLL + u
             word = code[c]
-            w = weights[c].reshape(BS, BS)
+            w = whole_block(quarters, c)
             value = lax.dot_general(cols[word >> 12], w, (((1,), (1,)), ((), ())), preferred_element_type=f32)
             adds.append(((word >> 8) & 15, value))
         for r, value in adds:
@@ -446,7 +450,7 @@
     quarter = lax.dynamic_slice_in_dim(block_weight[0], x_index * (BS // NX), BS // NX, 1)
     quarter, sent = lax.optimization_barrier((quarter, out_grad))
     gathered = lax.all_gather(quarter, SHARD, axis=0, tiled=True)
-    mine = all_to_all(jnp.broadcast_to(sent[None], (NZL,) + out_grad.shape), "zl")
+    mine = all_to_all(call(repeat_kernel, like((NZL,) + out_grad.shape, bf16), 0, 1, byts=1024 * 1024)(sent), "zl")
     other = shift(mine, "core", 2, 1)
     weight_share = lax.dynamic_slice_in_dim(block_weight[0], dp_index * 2, 2, 1).reshape(slot_count, share)
     stacked = jnp.concatenate([weight_share.astype(f32), first_moment[0], second_moment[0]], axis=1)
@@ -486,19 +490,18 @@
     )(send, state_send, along_yz, stacked, place, fits)
     shares = all_to_all(packed, SHARD)
 
-    out_mine, out_theirs, weights = call(
+    out_mine, out_theirs = call(
         forward_kernel,
         (
             like((NZL, 4, tokens, BS), f32),
             like((NZL, 4, tokens, BS), f32),
-            like((WCAP, NX, BS // NX, BS), bf16),
         ),
         2,
-        1,
-        [pltpu.VMEM((shard_count * 4, tokens, BS), f32), pltpu.SemaphoreType.DMA((NX,))],
+        2,
+        [pltpu.VMEM((shard_count * 4, tokens, BS), f32)],
         flops=2 * WCAP * BS**3,
         byts=8 * 1024 * 1024,
-        n_after=2,
+        n_after=1,
     )(info, code, hidden, quarters, packed)
     came = shift(out_theirs, "core", 2, 1)
     hidden_grad = call(
@@ -509,7 +512,7 @@
         [pltpu.VMEM((row_local, tokens, BS), f32)],
         flops=2 * WCAP * BS**3,
         byts=4 * 1024 * 1024,
-    )(info, code, cols, weights)
+    )(info, code, cols, quarters)
     part = (4, tokens, BS)
     own, s1, s2, s3 = call(
         chip_kernel, (like(part, f32),) + (like(part, bf16),) * 3, 1, 2, byts=3 * 1024 * 1024
@@ -528,7 +531,7 @@
         [pltpu.VMEM((slot_count, 3 * share), f32), pltpu.VMEM((slot_count, share), f32)],
         byts=1024 * 1024,
         n_after=1,
-    )(place, stacked, shares, hidden_grad)
+    )(place, stacked, shares, projected)
     result = (projected, hidden_grad, new_weight[None], new_first[None], new_second[None])
     return lax.cond(
         fits[0] > 0,

time: 141 us -> 142 us (level)
  local copies, waits for them, and re-layouts: 12 us -> 9.18 us
  waiting for transfers between devices: 24.3 us -> 26.5 us
  Pallas kernels: 14.4 us -> 16 us
    ppermute x5, waiting for transfers between devices: 0.76 us -> 3.13 us  [shift(): lax.ppermute(values, axis, [(i, (i + step) % count) for i in range(count)])]
    broadcast_in_dim x1 -> x0, local copies, waits for them, and re-layouts: 1.75 us -> none  [shards(): jnp.broadcast_to(sent[None], (NZL,) + out_grad.shape)]
    pallas_call x0 -> x1, Pallas kernels: none -> 1.74 us  [shards(): call(repeat_kernel, like((NZL,) + out_grad.shape, bf16), 0, 1, byts=1024...]
    unnamed x49 -> x51, local copies, waits for them, and re-layouts: 7.6 us -> 6.57 us
  transfers between devices with their start and end apart: 10 -> 10, of which waited for: 4 -> 6; matrix products, arithmetic and copies ran while one was open for 4% -> 3% of each run, Pallas kernels for 7% -> 6%
where the time goes in v12:
time: 142 us; the launch traced here: 141 us
  starting transfers between devices  46.8 us (33%)
  waiting for transfers between devices  26.5 us (19%)
  blocking collectives  21.4 us (15%)
  between operations  17.7 us (12%)
  Pallas kernels  16 us (11%)
  local copies, waits for them, and re-layouts  9.18 us (6%)
  other arithmetic  3.42 us (2%)
    all_to_all x3, starting transfers between devices, all_to_all(): return lax.all_to_all(values, axis, split_axis=0, concat_axis=0, tiled=True)  28.3 us
    all_to_all x3, waiting for transfers between devices, all_to_all(): return lax.all_to_all(values, axis, split_axis=0, concat_axis=0, tiled=True)  22.1 us
    all_to_all x1, blocking collectives, all_to_all(): return lax.all_to_all(values, axis, split_axis=0, concat_axis=0, tiled=True)  21.4 us
    ppermute x5, starting transfers between devices, shift(): lax.ppermute(values, axis, [(i, (i + step) % count) for i in range(count)])  18.4 us
    unnamed x51, local copies, waits for them, and re-layouts  6.57 us
    ppermute x5, waiting for transfers between devices, shift(): lax.ppermute(values, axis, [(i, (i + step) % count) for i in range(count)])  3.13 us
    pallas_call x1, Pallas kernels, shards(): call(forward_kernel, (like((NZL, 4, tokens, BS), f32), like((NZL, 4, toke...  3.08 us
  transfers between devices with their start and end apart: 10, of which 6 were waited for; matrix products, arithmetic and copies ran while one was open for 3% of the time, Pallas kernels for 6%

profile of v12, /device:TPU:1, one launch (start us, length us, event | category | flops | bytes accessed | tf_op | source)
XLA Modules:
  0.0 141.2 jit_solution(8683466709872076179)
XLA Ops:
  7.3 1.7 %dynamic-slice_bitcast_fusion.1 = bf16[32,32,128]{2,1,0:T(8,128)(2,1)} fusion(bf16[1,32,128,128]{3,2,1,0:T(8,128)(2,1)} %param.20, s32[]{:T(128)S(6)} %select_n.333), kind=kLoop, calls=%fused_computation.122 | loop fusion | bytes 524292 | tf_op jit(solution)/shard_map/dynamic_slice | solution.py:450
  9.0 1.7 %shard_map.147 = bf16[4,128,512]{2,1,0:T(8,128)(2,1)} custom-call(bf16[128,512]{1,0:T(8,128)(2,1)} %value), custom_call_target="tpu_custom_call" | custom-call | bytes 1048576 | tf_op jit(solution)/shard_map/pallas_call | solution.py:453
  10.8 7.8 %all-to-all-start.1 = ((bf16[4,128,512]{2,1,0:T(8,128)(2,1)}), bf16[4,128,512]{2,1,0:T(8,128)(2,1)S(1)}, u32[]{:S(2)}, u32[]{:S(2)}) async-start(bf16[4,128,512]{2,1,0:T(8,128)(2,1)} %shard_map.147), calls=%async_computation.2 | async-start | bytes 1048576 | tf_op jit(solution)/shard_map/all_to_all | solution.py:421
  19.8 0.8 convert_reduce_fusion.4
  22.1 9.6 %all-to-all-done.1.mine = bf16[4,128,512]{2,1,0:T(8,128)(2,1)S(1)} async-done(((bf16[4,128,512]{2,1,0:T(8,128)(2,1)}), bf16[4,128,512]{2,1,0:T(8,128)(2,1)S(1)}, u32[]{:S(2)}, u32[]{:S(2)}) %all-to-all-start.1) | async-done | bytes 524320 | tf_op jit(solution)/shard_map/all_to_all | solution.py:421
  31.7 4.3 %collective-permute-start = (bf16[4,128,512]{2,1,0:T(8,128)(2,1)S(1)}, bf16[4,128,512]{2,1,0:T(8,128)(2,1)S(1)}, u32[]{:S(2)}, u32[]{:S(2)}) collective-permute-start(bf16[4,128,512]{2,1,0:T(8,128)(2,1)S(1)} %all-to-all-done.1.mine), channel_id=1, source_target_pairs={{0,1},{1,0},{2,3},{3,2},{4,5},{5,4},{6,7},{7,6},{8,9},{9,8},{10,11... | collective-permute-start | bytes 1572872 | tf_op jit(solution)/shard_map/ppermute | solution.py:425
  36.0 0.6 and_select_fusion.3
  36.7 0.8 collective-permute-done.other
  37.5 2.1 %shard_map.148 = (bf16[4,32,40,128]{3,2,1,0:T(8,128)(2,1)S(1)}, bf16[32,128,128]{2,1,0:T(8,128)(2,1)S(1)}) custom-call(s32[6]{0:T(128)S(1)} %stack.27.info, s32[44]{0:T(128)S(1)} %select_reduce_fusion.4.code, bf16[128,1792]{1,0:T(8,128)(2,1)S(1)} %copy-done.10, bf16[4,128,512]{2,1,0:T(8,128)(2,1)S(1)} %all-to-all-done.1.mine, ...), custom_call_target="tpu_custom_call" | custom-call | flops 184549376 | bytes 4194304 | tf_op jit(solution)/shard_map/pallas_call | solution.py:463
  39.6 1.0 copy-done.3
  40.6 21.4 %all_to_all.24.parts = bf16[4,32,40,128]{3,2,1,0:T(8,128)(2,1)S(1)} all-to-all(bf16[4,32,40,128]{3,2,1,0:T(8,128)(2,1)S(1)} %get-tuple-element.210), channel_id=1, replica_groups=mesh['y'=8,'x'=4,'zh'=2,'zl'=4,'core'=2] {'x'}, dimensions={0} | all-to-all | bytes 2621440 | tf_op jit(solution)/shard_map/all_to_all | solution.py:421
  61.9 1.6 %copy-done.2 = bf16[256,32,128]{2,1,0:T(8,128)(2,1)S(1)} copy-done((bf16[256,32,128]{2,1,0:T(8,128)(2,1)S(1)}, bf16[256,32,128]{2,1,0:T(8,128)(2,1)}, u32[]{:S(2)}) %copy-start.2) | copy-done | bytes 2097176
  63.5 1.8 %shard_map.149 = (bf16[44,32,128]{2,1,0:T(8,128)(2,1)}, bf16[32,40,128]{2,1,0:T(8,128)(2,1)}) custom-call(s32[6]{0:T(128)S(1)} %stack.27.info, s32[44]{0:T(128)S(1)} %select_reduce_fusion.4.code, bf16[256,32,128]{2,1,0:T(8,128)(2,1)S(1)} %copy-done.2, bf16[4,32,40,128]{3,2,1,0:T(8,128)(2,1)S(1)} %all_to_all.24.parts), custom_call_target="tpu_custom_call" | custom-call | bytes 4194304 | tf_op jit(solution)/shard_map/pallas_call | solution.py:473
  65.4 0.9 dynamic-slice_convert_fusion
  66.3 16.5 %all-to-all-start.3 = ((bf16[16,2,40,128]{3,2,1,0:T(8,128)(2,1)}), bf16[16,2,40,128]{3,2,1,0:T(8,128)(2,1)S(1)}, u32[]{:S(2)}, u32[]{:S(2)}) async-start(bf16[16,2,40,128]{3,2,1,0:T(8,128)(2,1)} %bitcast.46), calls=%async_computation.4 | async-start | bytes 655360 | tf_op jit(solution)/shard_map/all_to_all | solution.py:421
  85.3 12.5 %all-to-all-done.3.parts = bf16[16,2,40,128]{3,2,1,0:T(8,128)(2,1)S(1)} async-done(((bf16[16,2,40,128]{3,2,1,0:T(8,128)(2,1)}), bf16[16,2,40,128]{3,2,1,0:T(8,128)(2,1)S(1)}, u32[]{:S(2)}, u32[]{:S(2)}) %all-to-all-start.3) | async-done | bytes 327712 | tf_op jit(solution)/shard_map/all_to_all | solution.py:421
  97.8 1.5 %shard_map.150._after = f32[8,40,128]{2,1,0:T(8,128)} custom-call(s32[112]{0:T(128)S(1)} %broadcast_minimum_fusion.send, s32[16]{0:T(128)S(1)} %select_reduce_fusion.6.state_send, bf16[16,2,40,128]{3,2,1,0:T(8,128)(2,1)S(1)} %all-to-all-done.3.parts, f32[32,768]{1,0:T(8,128)S(1)} %pad_maximum_fusion.1.stacked, s32[32]{0:T(128)S(1)} %select_reduce_fusion.5._after.place, ...), custom_call_target="tpu_custom_call" | custom-call | bytes 1048576 | tf_op jit(solution)/shard_map/pallas_call | solution.py:482
  99.3 1.3 all-gather.15.cloned.1.call-done
  100.6 1.4 copy-done
  101.9 3.1 %shard_map.151 = (f32[4,4,128,128]{3,2,1,0:T(8,128)S(1)}, f32[4,4,128,128]{3,2,1,0:T(8,128)}) custom-call(s32[6]{0:T(128)S(1)} %stack.27.info, s32[44]{0:T(128)S(1)} %select_reduce_fusion.4.code, bf16[128,1792]{1,0:T(8,128)(2,1)S(1)} %copy-done.10, bf16[4,44,32,128]{3,2,1,0:T(8,128)(2,1)S(1)} %bitcast.131, f32[8,40,128]{2,1,0:T(8,128)} %shard_map.150._after), custom_call_target="tpu_custom_call" | custom-call | flops 184549376 | bytes 8388608 | tf_op jit(solution)/shard_map/pallas_call | solution.py:493
  105.0 3.8 %collective-permute-start.1 = (f32[4,4,128,128]{3,2,1,0:T(8,128)}, f32[4,4,128,128]{3,2,1,0:T(8,128)S(1)}, u32[]{:S(2)}, u32[]{:S(2)}) collective-permute-start(f32[4,4,128,128]{3,2,1,0:T(8,128)} %get-tuple-element.214), channel_id=1, source_target_pairs={{0,1},{1,0},{2,3},{3,2},{4,5},{5,4},{6,7},{7,6},{8,9},{9,8},{10,11... | collective-permute-start | bytes 3145736 | tf_op jit(solution)/shard_map/ppermute | solution.py:425
  108.8 4.0 %all-to-all-start.4 = ((f32[8,40,128]{2,1,0:T(8,128)}), f32[8,40,128]{2,1,0:T(8,128)}, u32[]{:S(2)}, u32[]{:S(2)}) async-start(f32[8,40,128]{2,1,0:T(8,128)} %shard_map.150._after), calls=%async_computation.5 | async-start | bytes 327680 | tf_op jit(solution)/shard_map/all_to_all | solution.py:421
  112.8 1.4 shard_map.152
  114.2 0.7 copy-done.7
  114.9 3.3 %collective-permute-start.2 = (bf16[4,128,128]{2,1,0:T(8,128)(2,1)}, bf16[4,128,128]{2,1,0:T(8,128)(2,1)S(1)}, u32[]{:S(2)}, u32[]{:S(2)}) collective-permute-start(bf16[4,128,128]{2,1,0:T(8,128)(2,1)} %get-tuple-element.216), channel_id=1, source_target_pairs={{0,2},{2,4},{4,6},{6,0},{1,3},{3,5},{5,7},{7,1},{8,10},{10,12},{12... | collective-permute-start | bytes 393224 | tf_op jit(solution)/shard_map/ppermute | solution.py:425
  118.2 4.0 %collective-permute-start.3 = (bf16[4,128,128]{2,1,0:T(8,128)(2,1)}, bf16[4,128,128]{2,1,0:T(8,128)(2,1)S(1)}, u32[]{:S(2)}, u32[]{:S(2)}) collective-permute-start(bf16[4,128,128]{2,1,0:T(8,128)(2,1)} %get-tuple-element.217), channel_id=1, source_target_pairs={{0,4},{2,6},{4,0},{6,2},{1,5},{3,7},{5,1},{7,3},{8,12},{10,14},{12... | collective-permute-start | bytes 393224 | tf_op jit(solution)/shard_map/ppermute | solution.py:425
  122.2 3.1 %collective-permute-start.4 = (bf16[4,128,128]{2,1,0:T(8,128)(2,1)}, bf16[4,128,128]{2,1,0:T(8,128)(2,1)S(1)}, u32[]{:S(2)}, u32[]{:S(2)}) collective-permute-start(bf16[4,128,128]{2,1,0:T(8,128)(2,1)} %get-tuple-element.218), channel_id=1, source_target_pairs={{0,6},{2,0},{4,2},{6,4},{1,7},{3,1},{5,3},{7,5},{8,14},{10,8},{12,... | collective-permute-start | bytes 393224 | tf_op jit(solution)/shard_map/ppermute | solution.py:425
  125.3 1.2 copy-done.4
  126.5 2.2 %shard_map.153._after = bf16[128,1792]{1,0:T(8,128)(2,1)S(1)} custom-call(s32[6]{0:T(128)S(1)} %stack.27.info, s32[44]{0:T(128)S(1)} %select_reduce_fusion.4.code, bf16[32,128,128]{2,1,0:T(8,128)(2,1)S(1)} %copy-done.4, bf16[4,44,32,128]{3,2,1,0:T(8,128)(2,1)S(1)} %bitcast.132), custom_call_target="tpu_custom_call" | custom-call | flops 184549376 | bytes 4194304 | tf_op jit(solution)/shard_map/pallas_call | solution.py:507
  129.3 1.8 %collective-permute-done.4.r3 = bf16[4,128,128]{2,1,0:T(8,128)(2,1)S(1)} collective-permute-done((bf16[4,128,128]{2,1,0:T(8,128)(2,1)}, bf16[4,128,128]{2,1,0:T(8,128)(2,1)S(1)}, u32[]{:S(2)}, u32[]{:S(2)}) %collective-permute-start.4) | collective-permute-done | bytes 131104 | tf_op jit(solution)/shard_map/ppermute | solution.py:425
  131.3 2.2 %shard_map.155 = (f32[32,256]{1,0:T(8,128)}, f32[32,256]{1,0:T(8,128)}, f32[32,256]{1,0:T(8,128)}) custom-call(s32[32]{0:T(128)S(1)} %select_reduce_fusion.5._after.place, f32[32,768]{1,0:T(8,128)S(1)} %copy-done.6, f32[8,40,128]{2,1,0:T(8,128)} %all-to-all-done.4.came, bf16[128,512]{1,0:T(8,128)(2,1)S(1)} %shard_map.154._after), custom_call_target="tpu_custom_call" | custom-call | bytes 1048576 | tf_op jit(solution)/shard_map/pallas_call | solution.py:526
  133.7 0.6 copy-done.14
  (85 shorter events, 3.1 us)
Async XLA Ops:
  7.2 11.4 %copy-start.19 = (s32[8,32]{1,0:T(8,128)S(1)}, s32[8,32]{1,0:T(8,128)}, u32[]{:S(2)}) copy-start(s32[8,32]{1,0:T(8,128)} %param.24) | copy-start | bytes 3076
  7.2 11.5 %copy-start.20 = (s32[8,32]{1,0:T(8,128)S(1)}, s32[8,32]{1,0:T(8,128)}, u32[]{:S(2)}) copy-start(s32[8,32]{1,0:T(8,128)} %param.21) | copy-start | bytes 3076
  7.2 11.5 %copy-start.24 = (s32[8]{0:T(128)S(1)}, s32[8]{0:T(128)}, u32[]{:S(2)}) copy-start(s32[8]{0:T(128)} %param.23) | copy-start | bytes 100
  7.2 11.7 %copy-start.21 = (s32[8,32]{1,0:T(8,128)S(1)}, s32[8,32]{1,0:T(8,128)}, u32[]{:S(2)}) copy-start(s32[8,32]{1,0:T(8,128)} %param.22) | copy-start | bytes 3076
  7.2 30.3 %copy-start.10 = (bf16[128,1792]{1,0:T(8,128)(2,1)S(1)}, bf16[128,1792]{1,0:T(8,128)(2,1)}, u32[]{:S(2)}) copy-start(bf16[128,1792]{1,0:T(8,128)(2,1)} %hidden.3) | copy-start | bytes 1376260
  7.2 54.7 %all-gather.13.cloned.1.call-start = ((), (), s32[]{:S(2)}) async-start(), calls=%async_computation.10 | async-start | bytes 2359296 | tf_op jit(solution)/shard_map/all_gather | solution.py:452
  10.8 20.9 %all-to-all-start.1 = ((bf16[4,128,512]{2,1,0:T(8,128)(2,1)}), bf16[4,128,512]{2,1,0:T(8,128)(2,1)S(1)}, u32[]{:S(2)}, u32[]{:S(2)}) async-start(bf16[4,128,512]{2,1,0:T(8,128)(2,1)} %shard_map.147), calls=%async_computation.2 | async-start | bytes 1048576 | tf_op jit(solution)/shard_map/all_to_all | solution.py:421
  18.6 82.0 %all-gather.15.cloned.1.call-start = ((), (), s32[]{:S(2)}) async-start(), calls=%async_computation.11 | async-start | bytes 1802240 | tf_op jit(solution)/shard_map/all_gather | solution.py:480
  31.7 5.8 %collective-permute-start = (bf16[4,128,512]{2,1,0:T(8,128)(2,1)S(1)}, bf16[4,128,512]{2,1,0:T(8,128)(2,1)S(1)}, u32[]{:S(2)}, u32[]{:S(2)}) collective-permute-start(bf16[4,128,512]{2,1,0:T(8,128)(2,1)S(1)} %all-to-all-done.1.mine), channel_id=1, source_target_pairs={{0,1},{1,0},{2,3},{3,2},{4,5},{5,4},{6,7},{7,6},{8,9},{9,8},{10,11... | collective-permute-start | bytes 1572872 | tf_op jit(solution)/shard_map/ppermute | solution.py:425
  61.9 1.6 %copy-start.2 = (bf16[256,32,128]{2,1,0:T(8,128)(2,1)S(1)}, bf16[256,32,128]{2,1,0:T(8,128)(2,1)}, u32[]{:S(2)}) copy-start(bf16[256,32,128]{2,1,0:T(8,128)(2,1)} %all-gather.13.cloned.1.call-done.gathered) | copy-start | bytes 6291460
  63.5 19.4 %copy-start.22 = (s32[8,32]{1,0:T(8,128)S(1)}, s32[8,32]{1,0:T(8,128)}, u32[]{:S(2)}) copy-start(s32[8,32]{1,0:T(8,128)} %param.25) | copy-start | bytes 3076
  63.5 21.6 %copy-start.15 = (f32[1,32,256]{2,1,0:T(8,128)S(1)}, f32[1,32,256]{2,1,0:T(8,128)}, u32[]{:S(2)}) copy-start(f32[1,32,256]{2,1,0:T(8,128)} %param.26) | copy-start | bytes 98308
  63.5 21.6 %copy-start.17 = (f32[1,32,256]{2,1,0:T(8,128)S(1)}, f32[1,32,256]{2,1,0:T(8,128)}, u32[]{:S(2)}) copy-start(f32[1,32,256]{2,1,0:T(8,128)} %param.27) | copy-start | bytes 98308
  66.3 31.5 %all-to-all-start.3 = ((bf16[16,2,40,128]{3,2,1,0:T(8,128)(2,1)}), bf16[16,2,40,128]{3,2,1,0:T(8,128)(2,1)S(1)}, u32[]{:S(2)}, u32[]{:S(2)}) async-start(bf16[16,2,40,128]{3,2,1,0:T(8,128)(2,1)} %bitcast.46), calls=%async_computation.4 | async-start | bytes 655360 | tf_op jit(solution)/shard_map/all_to_all | solution.py:421
  85.1 15.4 %copy-start.5 = (f32[32,768]{1,0:T(8,128)}, f32[32,768]{1,0:T(8,128)S(1)}, u32[]{:S(2)}) copy-start(f32[32,768]{1,0:T(8,128)S(1)} %pad_maximum_fusion.1.stacked) | copy-start | bytes 294916
  100.6 1.4 copy-start
  101.9 23.3 %copy-start.1 = (bf16[176,32,128]{2,1,0:T(8,128)(2,1)S(1)}, bf16[176,32,128]{2,1,0:T(8,128)(2,1)}, u32[]{:S(2)}) copy-start(bf16[176,32,128]{2,1,0:T(8,128)(2,1)} %all-gather.15.cloned.1.call-done) | copy-start | bytes 4325380
  105.0 7.8 %collective-permute-start.1 = (f32[4,4,128,128]{3,2,1,0:T(8,128)}, f32[4,4,128,128]{3,2,1,0:T(8,128)S(1)}, u32[]{:S(2)}, u32[]{:S(2)}) collective-permute-start(f32[4,4,128,128]{3,2,1,0:T(8,128)} %get-tuple-element.214), channel_id=1, source_target_pairs={{0,1},{1,0},{2,3},{3,2},{4,5},{5,4},{6,7},{7,6},{8,9},{9,8},{10,11... | collective-permute-start | bytes 3145736 | tf_op jit(solution)/shard_map/ppermute | solution.py:425
  108.8 22.5 %all-to-all-start.4 = ((f32[8,40,128]{2,1,0:T(8,128)}), f32[8,40,128]{2,1,0:T(8,128)}, u32[]{:S(2)}, u32[]{:S(2)}) async-start(f32[8,40,128]{2,1,0:T(8,128)} %shard_map.150._after), calls=%async_computation.5 | async-start | bytes 327680 | tf_op jit(solution)/shard_map/all_to_all | solution.py:421
  114.9 13.9 %collective-permute-start.2 = (bf16[4,128,128]{2,1,0:T(8,128)(2,1)}, bf16[4,128,128]{2,1,0:T(8,128)(2,1)S(1)}, u32[]{:S(2)}, u32[]{:S(2)}) collective-permute-start(bf16[4,128,128]{2,1,0:T(8,128)(2,1)} %get-tuple-element.216), channel_id=1, source_target_pairs={{0,2},{2,4},{4,6},{6,0},{1,3},{3,5},{5,7},{7,1},{8,10},{10,12},{12... | collective-permute-start | bytes 393224 | tf_op jit(solution)/shard_map/ppermute | solution.py:425
  118.2 11.2 %collective-permute-start.3 = (bf16[4,128,128]{2,1,0:T(8,128)(2,1)}, bf16[4,128,128]{2,1,0:T(8,128)(2,1)S(1)}, u32[]{:S(2)}, u32[]{:S(2)}) collective-permute-start(bf16[4,128,128]{2,1,0:T(8,128)(2,1)} %get-tuple-element.217), channel_id=1, source_target_pairs={{0,4},{2,6},{4,0},{6,2},{1,5},{3,7},{5,1},{7,3},{8,12},{10,14},{12... | collective-permute-start | bytes 393224 | tf_op jit(solution)/shard_map/ppermute | solution.py:425
  122.2 9.0 %collective-permute-start.4 = (bf16[4,128,128]{2,1,0:T(8,128)(2,1)}, bf16[4,128,128]{2,1,0:T(8,128)(2,1)S(1)}, u32[]{:S(2)}, u32[]{:S(2)}) collective-permute-start(bf16[4,128,128]{2,1,0:T(8,128)(2,1)} %get-tuple-element.218), channel_id=1, source_target_pairs={{0,6},{2,0},{4,2},{6,4},{1,7},{3,1},{5,3},{7,5},{8,14},{10,8},{12,... | collective-permute-start | bytes 393224 | tf_op jit(solution)/shard_map/ppermute | solution.py:425
  125.3 1.2 copy-start.4
  126.5 4.7 %copy-start.8 = (f32[4,128,128]{2,1,0:T(8,128)S(1)}, f32[4,128,128]{2,1,0:T(8,128)}, u32[]{:S(2)}) copy-start(f32[4,128,128]{2,1,0:T(8,128)} %copy-done.7) | copy-start | bytes 786436
  126.5 4.8 %copy-start.6 = (f32[32,768]{1,0:T(8,128)S(1)}, f32[32,768]{1,0:T(8,128)}, u32[]{:S(2)}) copy-start(f32[32,768]{1,0:T(8,128)} %copy-done.5) | copy-start | bytes 294916
  126.5 6.9 %copy-start.11 = (bf16[128,1792]{1,0:T(8,128)(2,1)S(1)}, bf16[128,1792]{1,0:T(8,128)(2,1)}, u32[]{:S(2)}) copy-start(bf16[128,1792]{1,0:T(8,128)(2,1)} %hidden.3) | copy-start | bytes 1376260
  126.5 6.9 %copy-start.13 = (bf16[128,512]{1,0:T(8,128)(2,1)S(1)}, bf16[128,512]{1,0:T(8,128)(2,1)}, u32[]{:S(2)}) copy-start(bf16[128,512]{1,0:T(8,128)(2,1)} %value) | copy-start | bytes 393220
  126.5 6.9 %copy-start.16 = (f32[1,32,256]{2,1,0:T(8,128)S(1)}, f32[1,32,256]{2,1,0:T(8,128)}, u32[]{:S(2)}) copy-start(f32[1,32,256]{2,1,0:T(8,128)} %param.26) | copy-start | bytes 98308
  126.5 6.9 %copy-start.18 = (f32[1,32,256]{2,1,0:T(8,128)S(1)}, f32[1,32,256]{2,1,0:T(8,128)}, u32[]{:S(2)}) copy-start(f32[1,32,256]{2,1,0:T(8,128)} %param.27) | copy-start | bytes 98308
  126.5 6.9 %copy-start.23 = (s32[8,32]{1,0:T(8,128)S(1)}, s32[8,32]{1,0:T(8,128)}, u32[]{:S(2)}) copy-start(s32[8,32]{1,0:T(8,128)} %param.25) | copy-start | bytes 3076
  126.5 6.9 %copy-start.25 = (s32[8]{0:T(128)S(1)}, s32[8]{0:T(128)}, u32[]{:S(2)}) copy-start(s32[8]{0:T(128)} %param.23) | copy-start | bytes 100
  128.8 2.4 %copy-start.12 = (bf16[128,1792]{1,0:T(8,128)(2,1)}, bf16[128,1792]{1,0:T(8,128)(2,1)S(1)}, u32[]{:S(2)}) copy-start(bf16[128,1792]{1,0:T(8,128)(2,1)S(1)} %shard_map.153._after) | copy-start | bytes 1376260
  (3 other events, 2.3 us)
Sparse Core Ops, SparseCore 0:
  10.9 46.3 all-gather.12
  65.5 35.0 all-gather.14

commit v13 on v11

--- a/solution.py
+++ b/solution.py
@@ -260,6 +260,11 @@
     return fits.astype(i32).reshape(1), code, counts, send, state_send, place
 
 
+def repeat_kernel(value, out):
+    for n in range(out.shape[0]):
+        out[n] = value[...]
+
+
 def grad_kernel(info, code, hidden, mine, other, out, cols, hidden_t, total):
     my_core = info[2]
     for zl in range(NZL):
@@ -288,15 +293,8 @@
                 out[x, 4 * y + q] = total[source * GCAP : (source + 1) * GCAP, :].astype(bf16)
 
 
-def share_kernel(scale, send, state_send, parts, stacked, _after, _after2, out, total):
-    total[...] = parts[0].astype(f32)
-
-    def step(n, carry):
-        total[...] += parts[n].astype(f32)
-        return carry
-
-    lax.fori_loop(1, parts.shape[0], step, 0)
-    total[...] = total[...] * scale
+def share_kernel(scale, send, state_send, keep, came, stacked, _after, _after2, out, total):
+    total[...] = (keep[...] + came[...]) * scale
     width = stacked.shape[1] // BS
     for d in range(out.shape[0]):
         for p in range(PAIR):
@@ -310,26 +308,42 @@
                 out[d, at : at + 1, :] = row[:, n * BS : (n + 1) * BS]
 
 
-def select_sum_kernel(info, code, gathered, parts, picked, summed):
+def select_kernel(info, code, gathered, _after, picked):
     def select(c, carry):
         value = gathered[code[c] & 255]
         picked[c] = jnp.where(c < info[0], value, jnp.zeros_like(value))
         return carry
 
-    def add(i, carry):
+    lax.fori_loop(0, WCAP, select, 0, unroll=4)
+
+
+def sum_kernel(parts, out):
+    def step(i, carry):
         value = parts[0, i].astype(f32)
         for n in range(1, parts.shape[0]):
             value += parts[n, i].astype(f32)
-        summed[i] = value.astype(bf16)
+        out[i] = value.astype(bf16)
         return carry
 
-    lax.fori_loop(0, WCAP, select, 0, unroll=4)
-    lax.fori_loop(0, summed.shape[0], add, 0, unroll=4)
-
-
-def forward_kernel(info, code, hidden, quarters, _after, mine, theirs, weights, total, sems):
-    my_core = info[2]
-    copies = [pltpu.make_async_copy(quarters.at[x], weights.at[:, x], sems.at[x]) for x in range(NX)]
+    lax.fori_loop(0, out.shape[0], step, 0, unroll=4)
+
+
+def pair_kernel(info, parts, keep, send):
+    my_zh = info[5]
+    for out, zh in ((keep, my_zh), (send, 1 - my_zh)):
+        for b in range(2):
+            value = parts[0, 2 * zh + b].astype(f32)
+            for n in range(1, parts.shape[0]):
+                value += parts[n, 2 * zh + b].astype(f32)
+            out[b] = value
+
+
+def forward_kernel(info, code, hidden, w0, w1, w2, w3, _after, mine, theirs, weights, total, sems):
+    my_core, my_x = info[2], info[3]
+    copies = [
+        pltpu.make_async_copy(part, weights.at[:, (my_x + NX - k) % NX], sems.at[k])
+        for k, part in enumerate((w0, w1, w2, w3))
+    ]
     for copy in copies:
         copy.start()
     total[...] = jnp.zeros_like(total)
@@ -446,7 +460,7 @@
     quarter = lax.dynamic_slice_in_dim(block_weight[0], x_index * (BS // NX), BS // NX, 1)
     quarter, sent = lax.optimization_barrier((quarter, out_grad))
     gathered = lax.all_gather(quarter, SHARD, axis=0, tiled=True)
-    mine = all_to_all(jnp.broadcast_to(sent[None], (NZL,) + out_grad.shape), "zl")
+    mine = all_to_all(call(repeat_kernel, like((NZL,) + out_grad.shape, bf16), 0, 1, byts=1024 * 1024)(sent), "zl")
     other = shift(mine, "core", 2, 1)
     weight_share = lax.dynamic_slice_in_dim(block_weight[0], dp_index * 2, 2, 1).reshape(slot_count, share)
     stacked = jnp.concatenate([weight_share.astype(f32), first_moment[0], second_moment[0]], axis=1)
@@ -466,24 +480,25 @@
         byts=4 * 1024 * 1024,
     )(info, code, hidden, mine, other)
     along_x = all_to_all(partial, "x")
-    picked, summed = call(
-        select_sum_kernel,
-        (like((WCAP, BS // NX, BS), bf16), like(partial.shape[1:], bf16)),
-        2,
-        2,
-        byts=4 * 1024 * 1024,
-    )(info, code, gathered, along_x)
-    quarters = lax.all_gather(picked, "x", axis=0)
-    along_yz = all_to_all(summed.reshape(NY * NZH, 2, GCAP, BS), ("y", "zh"))
+    summed = call(sum_kernel, like(partial.shape[1:], bf16), 0, 1, byts=2 * 1024 * 1024)(along_x)
+    along_y = all_to_all(summed.reshape(NY, 2 * NZH, GCAP, BS), "y")
+    half = like((2, GCAP, BS), f32)
+    keep, send_zh = call(pair_kernel, (half, half), 1, 1, byts=1024 * 1024)(info, along_y)
+    came_zh = shift(send_zh, "zh", NZH, 1)
+
+    picked = call(select_kernel, like((WCAP, BS // NX, BS), bf16), 2, 1, byts=1024 * 1024, n_after=1)(
+        info, code, gathered, summed
+    )
+    w2, w1, w3 = (shift(picked, "x", NX, k) for k in (2, 1, 3))
     packed = call(
         functools.partial(share_kernel, scale),
         like((shard_count, 2 * PAIR + MV * stacked.shape[1] // BS, BS), f32),
         2,
-        2,
+        3,
         [pltpu.VMEM((2, GCAP, BS), f32)],
         byts=1024 * 1024,
         n_after=2,
-    )(send, state_send, along_yz, stacked, place, fits)
+    )(send, state_send, keep, came_zh, stacked, place, fits)
     shares = all_to_all(packed, SHARD)
 
     out_mine, out_theirs, weights = call(
@@ -498,8 +513,8 @@
         [pltpu.VMEM((shard_count * 4, tokens, BS), f32), pltpu.SemaphoreType.DMA((NX,))],
         flops=2 * WCAP * BS**3,
         byts=8 * 1024 * 1024,
-        n_after=2,
-    )(info, code, hidden, quarters, packed)
+        n_after=5,
+    )(info, code, hidden, picked, w1, w2, w3, packed)
     came = shift(out_theirs, "core", 2, 1)
     hidden_grad = call(
         backward_kernel,

time: 141 us -> 138 us (0.979)
  blocking collectives: 21.5 us -> 0 us
  starting transfers between devices: 47.3 us -> 56.6 us
  waiting for transfers between devices: 24.3 us -> 29.8 us
  Pallas kernels: 14.4 us -> 18.6 us
    all_to_all x1 -> x0, blocking collectives: 21.5 us -> none  [all_to_all(): return lax.all_to_all(values, axis, split_axis=0, concat_axis=0, tiled=True)]
    ppermute x5 -> x9, starting transfers between devices: 18 us -> 34.5 us  [shift(): lax.ppermute(values, axis, [(i, (i + step) % count) for i in range(count)])]
    all_to_all x3 -> x4, starting transfers between devices: 29.3 us -> 22.1 us  [all_to_all(): return lax.all_to_all(values, axis, split_axis=0, concat_axis=0, tiled=True)]
    all_to_all x3 -> x4, waiting for transfers between devices: 22.3 us -> 26 us  [all_to_all(): return lax.all_to_all(values, axis, split_axis=0, concat_axis=0, tiled=True)]
    ppermute x5 -> x9, waiting for transfers between devices: 0.76 us -> 3.04 us  [shift(): lax.ppermute(values, axis, [(i, (i + step) % count) for i in range(count)])]
    pallas_call x1 -> x4, Pallas kernels: 1.76 us -> 3.98 us  [the longest x1 1.73 us: shards(): call(repeat_kernel, like((NZL,) + out_grad.shape, bf16), 0, 1, byts=1024...]
    broadcast_in_dim x1 -> x0, local copies, waits for them, and re-layouts: 1.75 us -> none  [shards(): jnp.broadcast_to(sent[None], (NZL,) + out_grad.shape)]
    unnamed x49 -> x37, local copies, waits for them, and re-layouts: 7.6 us -> 8 us
  transfers between devices with their start and end apart: 10 -> 14, of which waited for: 4 -> 5; matrix products, arithmetic and copies ran while one was open for 4% -> 3% of each run, Pallas kernels for 7% -> 9%
where the time goes in v13:
time: 138 us; the launch traced here: 137 us
  starting transfers between devices  56.6 us (41%)
  waiting for transfers between devices  29.8 us (22%)
  Pallas kernels  18.6 us (13%)
  between operations  17.5 us (13%)
  local copies, waits for them, and re-layouts  10.6 us (8%)
  other arithmetic  3.35 us (2%)
    ppermute x9, starting transfers between devices, shift(): lax.ppermute(values, axis, [(i, (i + step) % count) for i in range(count)])  34.5 us
    all_to_all x4, waiting for transfers between devices, all_to_all(): return lax.all_to_all(values, axis, split_axis=0, concat_axis=0, tiled=True)  26 us
    all_to_all x4, starting transfers between devices, all_to_all(): return lax.all_to_all(values, axis, split_axis=0, concat_axis=0, tiled=True)  22.1 us
    unnamed x37, local copies, waits for them, and re-layouts  8 us
    pallas_call x1, Pallas kernels, shards(): call(forward_kernel, (like((NZL, 4, tokens, BS), f32), like((NZL, 4, toke...  3.53 us
    pallas_call x1, Pallas kernels, shards(): call(grad_kernel, (like((NX, NY * NZH * 2, GCAP, BS), bf16), like((shard_...  3.18 us
    ppermute x9, waiting for transfers between devices, shift(): lax.ppermute(values, axis, [(i, (i + step) % count) for i in range(count)])  3.04 us
  transfers between devices with their start and end apart: 14, of which 5 were waited for; matrix products, arithmetic and copies ran while one was open for 3% of the time, Pallas kernels for 9%

profile of v13, /device:TPU:1, one launch (start us, length us, event | category | flops | bytes accessed | tf_op | source)
XLA Modules:
  0.0 136.6 jit_solution(17872093534203960588)
XLA Ops:
  7.2 1.7 %dynamic-slice_bitcast_fusion.1 = bf16[32,32,128]{2,1,0:T(8,128)(2,1)} fusion(bf16[1,32,128,128]{3,2,1,0:T(8,128)(2,1)} %param.20, s32[]{:T(128)S(6)} %select_n.333), kind=kLoop, calls=%fused_computation.122 | loop fusion | bytes 524292 | tf_op jit(solution)/shard_map/dynamic_slice | solution.py:460
  9.0 1.7 %shard_map.147 = bf16[4,128,512]{2,1,0:T(8,128)(2,1)} custom-call(bf16[128,512]{1,0:T(8,128)(2,1)} %value), custom_call_target="tpu_custom_call" | custom-call | bytes 1048576 | tf_op jit(solution)/shard_map/pallas_call | solution.py:463
  10.7 7.8 %all-to-all-start.1 = ((bf16[4,128,512]{2,1,0:T(8,128)(2,1)}), bf16[4,128,512]{2,1,0:T(8,128)(2,1)S(1)}, u32[]{:S(2)}, u32[]{:S(2)}) async-start(bf16[4,128,512]{2,1,0:T(8,128)(2,1)} %shard_map.147), calls=%async_computation.2 | async-start | bytes 1048576 | tf_op jit(solution)/shard_map/all_to_all | solution.py:431
  22.7 8.9 %all-to-all-done.1.mine = bf16[4,128,512]{2,1,0:T(8,128)(2,1)S(1)} async-done(((bf16[4,128,512]{2,1,0:T(8,128)(2,1)}), bf16[4,128,512]{2,1,0:T(8,128)(2,1)S(1)}, u32[]{:S(2)}, u32[]{:S(2)}) %all-to-all-start.1) | async-done | bytes 524320 | tf_op jit(solution)/shard_map/all_to_all | solution.py:431
  31.6 4.2 %collective-permute-start = (bf16[4,128,512]{2,1,0:T(8,128)(2,1)S(1)}, bf16[4,128,512]{2,1,0:T(8,128)(2,1)S(1)}, u32[]{:S(2)}, u32[]{:S(2)}) collective-permute-start(bf16[4,128,512]{2,1,0:T(8,128)(2,1)S(1)} %all-to-all-done.1.mine), channel_id=1, source_target_pairs={{0,1},{1,0},{2,3},{3,2},{4,5},{5,4},{6,7},{7,6},{8,9},{9,8},{10,11... | collective-permute-start | bytes 1572872 | tf_op jit(solution)/shard_map/ppermute | solution.py:435
  37.4 3.2 %shard_map.148 = (bf16[4,32,40,128]{3,2,1,0:T(8,128)(2,1)}, bf16[32,128,128]{2,1,0:T(8,128)(2,1)S(1)}) custom-call(s32[6]{0:T(128)S(1)} %stack.27.info, s32[44]{0:T(128)S(1)} %select_reduce_fusion.4.code, bf16[128,1792]{1,0:T(8,128)(2,1)S(1)} %copy-done.8, bf16[4,128,512]{2,1,0:T(8,128)(2,1)S(1)} %all-to-all-done.1.mine, ...), custom_call_target="tpu_custom_call" | custom-call | flops 184549376 | bytes 4194304 | tf_op jit(solution)/shard_map/pallas_call | solution.py:473
  40.6 1.0 copy-done.1
  41.5 4.1 %all-to-all-start.2 = ((bf16[4,32,40,128]{3,2,1,0:T(8,128)(2,1)}), bf16[4,32,40,128]{3,2,1,0:T(8,128)(2,1)S(1)}, u32[]{:S(2)}, u32[]{:S(2)}) async-start(bf16[4,32,40,128]{3,2,1,0:T(8,128)(2,1)} %get-tuple-element.210), calls=%async_computation.3 | async-start | bytes 2621440 | tf_op jit(solution)/shard_map/all_to_all | solution.py:431
  45.9 17.1 %all-to-all-done.2.parts = bf16[4,32,40,128]{3,2,1,0:T(8,128)(2,1)S(1)} async-done(((bf16[4,32,40,128]{3,2,1,0:T(8,128)(2,1)}), bf16[4,32,40,128]{3,2,1,0:T(8,128)(2,1)S(1)}, u32[]{:S(2)}, u32[]{:S(2)}) %all-to-all-start.2) | async-done | bytes 1310752 | tf_op jit(solution)/shard_map/all_to_all | solution.py:431
  63.0 0.9 shard_map.149._after
  63.9 6.8 %all-to-all-start.3 = ((bf16[8,4,40,128]{3,2,1,0:T(8,128)(2,1)}), bf16[8,4,40,128]{3,2,1,0:T(8,128)(2,1)S(1)}, u32[]{:S(2)}, u32[]{:S(2)}) async-start(bf16[8,4,40,128]{3,2,1,0:T(8,128)(2,1)} %bitcast.46), calls=%async_computation.4 | async-start | bytes 655360 | tf_op jit(solution)/shard_map/all_to_all | solution.py:431
  70.8 0.9 dynamic-slice_convert_fusion
  71.8 1.6 %copy-done = bf16[256,32,128]{2,1,0:T(8,128)(2,1)S(1)} copy-done((bf16[256,32,128]{2,1,0:T(8,128)(2,1)S(1)}, bf16[256,32,128]{2,1,0:T(8,128)(2,1)}, u32[]{:S(2)}) %copy-start) | copy-done | bytes 2097176
  74.1 2.3 %collective-permute-start.2 = (bf16[44,32,128]{2,1,0:T(8,128)(2,1)S(1)}, bf16[44,32,128]{2,1,0:T(8,128)(2,1)S(1)}, u32[]{:S(2)}, u32[]{:S(2)}) collective-permute-start(bf16[44,32,128]{2,1,0:T(8,128)(2,1)S(1)} %shard_map.152.w0), channel_id=1, source_target_pairs={{0,16},{16,32},{32,48},{48,0},{1,17},{17,33},{33,49},{49,1},{2,18}... | collective-permute-start | bytes 1081352 | tf_op jit(solution)/shard_map/ppermute | solution.py:435
  76.4 3.6 %collective-permute-start.3 = (bf16[44,32,128]{2,1,0:T(8,128)(2,1)S(1)}, bf16[44,32,128]{2,1,0:T(8,128)(2,1)S(1)}, u32[]{:S(2)}, u32[]{:S(2)}) collective-permute-start(bf16[44,32,128]{2,1,0:T(8,128)(2,1)S(1)} %shard_map.152.w0), channel_id=1, source_target_pairs={{0,32},{16,48},{32,0},{48,16},{1,33},{17,49},{33,1},{49,17},{2,34}... | collective-permute-start | bytes 1081352 | tf_op jit(solution)/shard_map/ppermute | solution.py:435
  80.0 2.6 %collective-permute-start.4 = (bf16[44,32,128]{2,1,0:T(8,128)(2,1)S(1)}, bf16[44,32,128]{2,1,0:T(8,128)(2,1)S(1)}, u32[]{:S(2)}, u32[]{:S(2)}) collective-permute-start(bf16[44,32,128]{2,1,0:T(8,128)(2,1)S(1)} %shard_map.152.w0), channel_id=1, source_target_pairs={{0,48},{16,0},{32,16},{48,32},{1,49},{17,1},{33,17},{49,33},{2,50}... | collective-permute-start | bytes 1081352 | tf_op jit(solution)/shard_map/ppermute | solution.py:435
  83.4 8.0 %collective-permute-start.1 = (f32[2,40,128]{2,1,0:T(8,128)S(1)}, f32[2,40,128]{2,1,0:T(8,128)S(1)}, u32[]{:S(2)}, u32[]{:S(2)}) collective-permute-start(f32[2,40,128]{2,1,0:T(8,128)S(1)} %get-tuple-element.212), channel_id=1, source_target_pairs={{0,8},{8,0},{1,9},{9,1},{2,10},{10,2},{3,11},{11,3},{4,12},{12,4},... | collective-permute-start | bytes 122888 | tf_op jit(solution)/shard_map/ppermute | solution.py:435
  93.3 1.4 shard_map.151._after
  95.4 1.4 %collective-permute-done.4.w3 = bf16[44,32,128]{2,1,0:T(8,128)(2,1)S(1)} collective-permute-done((bf16[44,32,128]{2,1,0:T(8,128)(2,1)S(1)}, bf16[44,32,128]{2,1,0:T(8,128)(2,1)S(1)}, u32[]{:S(2)}, u32[]{:S(2)}) %collective-permute-start.4) | collective-permute-done | bytes 360480 | tf_op jit(solution)/shard_map/ppermute | solution.py:435
  97.5 1.0 copy-done.4
  98.5 1.0 copy-done.6
  99.5 3.5 %shard_map.153 = (f32[4,4,128,128]{3,2,1,0:T(8,128)S(1)}, f32[4,4,128,128]{3,2,1,0:T(8,128)}, bf16[44,4,32,128]{3,2,1,0:T(8,128)(2,1)S(1)}) custom-call(s32[6]{0:T(128)S(1)} %stack.27.info, s32[44]{0:T(128)S(1)} %select_reduce_fusion.4.code, bf16[128,1792]{1,0:T(8,128)(2,1)} %hidden.3, bf16[44,32,128]{2,1,0:T(8,128)(2,1)S(1)} %shard_map.152.w0, ...), custom_call_target="tpu_custom_call" | custom-call | flops 184549376 | bytes 8388608 | tf_op jit(solution)/shard_map/pallas_call | solution.py:504
  103.0 3.5 %collective-permute-start.5 = (f32[4,4,128,128]{3,2,1,0:T(8,128)}, f32[4,4,128,128]{3,2,1,0:T(8,128)}, u32[]{:S(2)}, u32[]{:S(2)}) collective-permute-start(f32[4,4,128,128]{3,2,1,0:T(8,128)} %get-tuple-element.220), channel_id=1, source_target_pairs={{0,1},{1,0},{2,3},{3,2},{4,5},{5,4},{6,7},{7,6},{8,9},{9,8},{10,11... | collective-permute-start | bytes 3145736 | tf_op jit(solution)/shard_map/ppermute | solution.py:435
  106.5 3.3 %all-to-all-start.4 = ((f32[8,40,128]{2,1,0:T(8,128)}), f32[8,40,128]{2,1,0:T(8,128)S(1)}, u32[]{:S(2)}, u32[]{:S(2)}) async-start(f32[8,40,128]{2,1,0:T(8,128)} %shard_map.151._after), calls=%async_computation.5 | async-start | bytes 327680 | tf_op jit(solution)/shard_map/all_to_all | solution.py:431
  109.8 2.1 %shard_map.156 = (f32[4,128,128]{2,1,0:T(8,128)S(1)}, bf16[4,128,128]{2,1,0:T(8,128)(2,1)}, bf16[4,128,128]{2,1,0:T(8,128)(2,1)}, bf16[4,128,128]{2,1,0:T(8,128)(2,1)S(1)}) custom-call(s32[6]{0:T(128)S(1)} %stack.27.info, f32[4,4,128,128]{3,2,1,0:T(8,128)S(1)} %get-tuple-element.219.mine, f32[4,4,128,128]{3,2,1,0:T(8,128)} %collective-permute-done.5.came), custom_call_target="tpu_custom_call" | custom-call | bytes 3145728 | tf_op jit(solution)/shard_map/pallas_call | solution.py:529
  112.0 3.2 %collective-permute-start.6 = (bf16[4,128,128]{2,1,0:T(8,128)(2,1)}, bf16[4,128,128]{2,1,0:T(8,128)(2,1)S(1)}, u32[]{:S(2)}, u32[]{:S(2)}) collective-permute-start(bf16[4,128,128]{2,1,0:T(8,128)(2,1)} %get-tuple-element.222), channel_id=1, source_target_pairs={{0,2},{2,4},{4,6},{6,0},{1,3},{3,5},{5,7},{7,1},{8,10},{10,12},{12... | collective-permute-start | bytes 393224 | tf_op jit(solution)/shard_map/ppermute | solution.py:435
  115.2 4.0 %collective-permute-start.7 = (bf16[4,128,128]{2,1,0:T(8,128)(2,1)}, bf16[4,128,128]{2,1,0:T(8,128)(2,1)S(1)}, u32[]{:S(2)}, u32[]{:S(2)}) collective-permute-start(bf16[4,128,128]{2,1,0:T(8,128)(2,1)} %get-tuple-element.223), channel_id=1, source_target_pairs={{0,4},{2,6},{4,0},{6,2},{1,5},{3,7},{5,1},{7,3},{8,12},{10,14},{12... | collective-permute-start | bytes 393224 | tf_op jit(solution)/shard_map/ppermute | solution.py:435
  119.2 3.1 %collective-permute-start.8 = (bf16[4,128,128]{2,1,0:T(8,128)(2,1)S(1)}, bf16[4,128,128]{2,1,0:T(8,128)(2,1)S(1)}, u32[]{:S(2)}, u32[]{:S(2)}) collective-permute-start(bf16[4,128,128]{2,1,0:T(8,128)(2,1)S(1)} %get-tuple-element.224), channel_id=1, source_target_pairs={{0,6},{2,0},{4,2},{6,4},{1,7},{3,1},{5,3},{7,5},{8,14},{10,8},{12,... | collective-permute-start | bytes 393224 | tf_op jit(solution)/shard_map/ppermute | solution.py:435
  122.3 1.2 copy-done.2
  123.5 2.0 %shard_map.154._after = bf16[128,1792]{1,0:T(8,128)(2,1)S(1)} custom-call(s32[6]{0:T(128)S(1)} %stack.27.info, s32[44]{0:T(128)S(1)} %select_reduce_fusion.4.code, bf16[32,128,128]{2,1,0:T(8,128)(2,1)S(1)} %copy-done.2, bf16[44,4,32,128]{3,2,1,0:T(8,128)(2,1)S(1)} %get-tuple-element.215.weights), custom_call_target="tpu_custom_call" | custom-call | flops 184549376 | bytes 4194304 | tf_op jit(solution)/shard_map/pallas_call | solution.py:519
  125.5 1.8 %shard_map.155 = (f32[32,256]{1,0:T(8,128)}, f32[32,256]{1,0:T(8,128)}, f32[32,256]{1,0:T(8,128)}) custom-call(s32[32]{0:T(128)S(1)} %select_reduce_fusion.5._after.place, f32[32,768]{1,0:T(8,128)S(1)} %pad_maximum_fusion.1.stacked, f32[8,40,128]{2,1,0:T(8,128)S(1)} %all-to-all-done.4.came, bf16[128,1792]{1,0:T(8,128)(2,1)S(1)} %shard_map.154._after), custom_call_target="tpu_custom_call" | custom-call | bytes 1048576 | tf_op jit(solution)/shard_map/pallas_call | solution.py:538
  127.3 0.9 collective-permute-done.8.r3
  (79 shorter events, 9.2 us)
Async XLA Ops:
  7.2 12.1 %copy-start.14 = (s32[8,32]{1,0:T(8,128)S(1)}, s32[8,32]{1,0:T(8,128)}, u32[]{:S(2)}) copy-start(s32[8,32]{1,0:T(8,128)} %param.21) | copy-start | bytes 3076
  7.2 12.1 %copy-start.18 = (s32[8]{0:T(128)S(1)}, s32[8]{0:T(128)}, u32[]{:S(2)}) copy-start(s32[8]{0:T(128)} %param.23) | copy-start | bytes 100
  7.2 12.1 %copy-start.13 = (s32[8,32]{1,0:T(8,128)S(1)}, s32[8,32]{1,0:T(8,128)}, u32[]{:S(2)}) copy-start(s32[8,32]{1,0:T(8,128)} %param.24) | copy-start | bytes 3076
  7.2 12.4 %copy-start.15 = (s32[8,32]{1,0:T(8,128)S(1)}, s32[8,32]{1,0:T(8,128)}, u32[]{:S(2)}) copy-start(s32[8,32]{1,0:T(8,128)} %param.22) | copy-start | bytes 3076
  7.2 30.2 %copy-start.8 = (bf16[128,1792]{1,0:T(8,128)(2,1)S(1)}, bf16[128,1792]{1,0:T(8,128)(2,1)}, u32[]{:S(2)}) copy-start(bf16[128,1792]{1,0:T(8,128)(2,1)} %hidden.3) | copy-start | bytes 1376260
  10.7 20.9 %all-to-all-start.1 = ((bf16[4,128,512]{2,1,0:T(8,128)(2,1)}), bf16[4,128,512]{2,1,0:T(8,128)(2,1)S(1)}, u32[]{:S(2)}, u32[]{:S(2)}) async-start(bf16[4,128,512]{2,1,0:T(8,128)(2,1)} %shard_map.147), calls=%async_computation.2 | async-start | bytes 1048576 | tf_op jit(solution)/shard_map/all_to_all | solution.py:431
  18.5 53.3 %all-gather.11.cloned.1.call-start = ((), (), s32[]{:S(2)}) async-start(), calls=%async_computation.10 | async-start | bytes 2359296 | tf_op jit(solution)/shard_map/all_gather | solution.py:462
  21.3 24.4 %copy-start.16 = (s32[8,32]{1,0:T(8,128)S(1)}, s32[8,32]{1,0:T(8,128)}, u32[]{:S(2)}) copy-start(s32[8,32]{1,0:T(8,128)} %param.25) | copy-start | bytes 3076
  31.6 5.7 %collective-permute-start = (bf16[4,128,512]{2,1,0:T(8,128)(2,1)S(1)}, bf16[4,128,512]{2,1,0:T(8,128)(2,1)S(1)}, u32[]{:S(2)}, u32[]{:S(2)}) collective-permute-start(bf16[4,128,512]{2,1,0:T(8,128)(2,1)S(1)} %all-to-all-done.1.mine), channel_id=1, source_target_pairs={{0,1},{1,0},{2,3},{3,2},{4,5},{5,4},{6,7},{7,6},{8,9},{9,8},{10,11... | collective-permute-start | bytes 1572872 | tf_op jit(solution)/shard_map/ppermute | solution.py:435
  40.6 1.0 copy-start.1
  41.5 30.1 %copy-start.11 = (f32[1,32,256]{2,1,0:T(8,128)S(1)}, f32[1,32,256]{2,1,0:T(8,128)}, u32[]{:S(2)}) copy-start(f32[1,32,256]{2,1,0:T(8,128)} %param.26) | copy-start | bytes 98308
  41.5 30.1 %copy-start.12 = (f32[1,32,256]{2,1,0:T(8,128)S(1)}, f32[1,32,256]{2,1,0:T(8,128)}, u32[]{:S(2)}) copy-start(f32[1,32,256]{2,1,0:T(8,128)} %param.27) | copy-start | bytes 98308
  41.5 21.5 %all-to-all-start.2 = ((bf16[4,32,40,128]{3,2,1,0:T(8,128)(2,1)}), bf16[4,32,40,128]{3,2,1,0:T(8,128)(2,1)S(1)}, u32[]{:S(2)}, u32[]{:S(2)}) async-start(bf16[4,32,40,128]{3,2,1,0:T(8,128)(2,1)} %get-tuple-element.210), calls=%async_computation.3 | async-start | bytes 2621440 | tf_op jit(solution)/shard_map/all_to_all | solution.py:431
  63.9 18.8 %all-to-all-start.3 = ((bf16[8,4,40,128]{3,2,1,0:T(8,128)(2,1)}), bf16[8,4,40,128]{3,2,1,0:T(8,128)(2,1)S(1)}, u32[]{:S(2)}, u32[]{:S(2)}) async-start(bf16[8,4,40,128]{3,2,1,0:T(8,128)(2,1)} %bitcast.46), calls=%async_computation.4 | async-start | bytes 655360 | tf_op jit(solution)/shard_map/all_to_all | solution.py:431
  71.8 1.6 %copy-start = (bf16[256,32,128]{2,1,0:T(8,128)(2,1)S(1)}, bf16[256,32,128]{2,1,0:T(8,128)(2,1)}, u32[]{:S(2)}) copy-start(bf16[256,32,128]{2,1,0:T(8,128)(2,1)} %all-gather.11.cloned.1.call-done.gathered) | copy-start | bytes 6291460
  74.1 20.5 %collective-permute-start.2 = (bf16[44,32,128]{2,1,0:T(8,128)(2,1)S(1)}, bf16[44,32,128]{2,1,0:T(8,128)(2,1)S(1)}, u32[]{:S(2)}, u32[]{:S(2)}) collective-permute-start(bf16[44,32,128]{2,1,0:T(8,128)(2,1)S(1)} %shard_map.152.w0), channel_id=1, source_target_pairs={{0,16},{16,32},{32,48},{48,0},{1,17},{17,33},{33,49},{49,1},{2,18}... | collective-permute-start | bytes 1081352 | tf_op jit(solution)/shard_map/ppermute | solution.py:435
  76.4 18.2 %collective-permute-start.3 = (bf16[44,32,128]{2,1,0:T(8,128)(2,1)S(1)}, bf16[44,32,128]{2,1,0:T(8,128)(2,1)S(1)}, u32[]{:S(2)}, u32[]{:S(2)}) collective-permute-start(bf16[44,32,128]{2,1,0:T(8,128)(2,1)S(1)} %shard_map.152.w0), channel_id=1, source_target_pairs={{0,32},{16,48},{32,0},{48,16},{1,33},{17,49},{33,1},{49,17},{2,34}... | collective-permute-start | bytes 1081352 | tf_op jit(solution)/shard_map/ppermute | solution.py:435
  80.0 16.7 %collective-permute-start.4 = (bf16[44,32,128]{2,1,0:T(8,128)(2,1)S(1)}, bf16[44,32,128]{2,1,0:T(8,128)(2,1)S(1)}, u32[]{:S(2)}, u32[]{:S(2)}) collective-permute-start(bf16[44,32,128]{2,1,0:T(8,128)(2,1)S(1)} %shard_map.152.w0), channel_id=1, source_target_pairs={{0,48},{16,0},{32,16},{48,32},{1,49},{17,1},{33,17},{49,33},{2,50}... | collective-permute-start | bytes 1081352 | tf_op jit(solution)/shard_map/ppermute | solution.py:435
  83.4 9.9 %collective-permute-start.1 = (f32[2,40,128]{2,1,0:T(8,128)S(1)}, f32[2,40,128]{2,1,0:T(8,128)S(1)}, u32[]{:S(2)}, u32[]{:S(2)}) collective-permute-start(f32[2,40,128]{2,1,0:T(8,128)S(1)} %get-tuple-element.212), channel_id=1, source_target_pairs={{0,8},{8,0},{1,9},{9,1},{2,10},{10,2},{3,11},{11,3},{4,12},{12,4},... | collective-permute-start | bytes 122888 | tf_op jit(solution)/shard_map/ppermute | solution.py:435
  94.7 0.7 copy-start.3
  96.8 0.7 copy-start.5
  97.5 1.0 copy-start.4
  98.5 1.0 copy-start.6
  103.0 6.8 %collective-permute-start.5 = (f32[4,4,128,128]{3,2,1,0:T(8,128)}, f32[4,4,128,128]{3,2,1,0:T(8,128)}, u32[]{:S(2)}, u32[]{:S(2)}) collective-permute-start(f32[4,4,128,128]{3,2,1,0:T(8,128)} %get-tuple-element.220), channel_id=1, source_target_pairs={{0,1},{1,0},{2,3},{3,2},{4,5},{5,4},{6,7},{7,6},{8,9},{9,8},{10,11... | collective-permute-start | bytes 3145736 | tf_op jit(solution)/shard_map/ppermute | solution.py:435
  106.5 19.0 %all-to-all-start.4 = ((f32[8,40,128]{2,1,0:T(8,128)}), f32[8,40,128]{2,1,0:T(8,128)S(1)}, u32[]{:S(2)}, u32[]{:S(2)}) async-start(f32[8,40,128]{2,1,0:T(8,128)} %shard_map.151._after), calls=%async_computation.5 | async-start | bytes 327680 | tf_op jit(solution)/shard_map/all_to_all | solution.py:431
  112.0 15.3 %collective-permute-start.6 = (bf16[4,128,128]{2,1,0:T(8,128)(2,1)}, bf16[4,128,128]{2,1,0:T(8,128)(2,1)S(1)}, u32[]{:S(2)}, u32[]{:S(2)}) collective-permute-start(bf16[4,128,128]{2,1,0:T(8,128)(2,1)} %get-tuple-element.222), channel_id=1, source_target_pairs={{0,2},{2,4},{4,6},{6,0},{1,3},{3,5},{5,7},{7,1},{8,10},{10,12},{12... | collective-permute-start | bytes 393224 | tf_op jit(solution)/shard_map/ppermute | solution.py:435
  115.2 12.1 %collective-permute-start.7 = (bf16[4,128,128]{2,1,0:T(8,128)(2,1)}, bf16[4,128,128]{2,1,0:T(8,128)(2,1)S(1)}, u32[]{:S(2)}, u32[]{:S(2)}) collective-permute-start(bf16[4,128,128]{2,1,0:T(8,128)(2,1)} %get-tuple-element.223), channel_id=1, source_target_pairs={{0,4},{2,6},{4,0},{6,2},{1,5},{3,7},{5,1},{7,3},{8,12},{10,14},{12... | collective-permute-start | bytes 393224 | tf_op jit(solution)/shard_map/ppermute | solution.py:435
  119.2 9.0 %collective-permute-start.8 = (bf16[4,128,128]{2,1,0:T(8,128)(2,1)S(1)}, bf16[4,128,128]{2,1,0:T(8,128)(2,1)S(1)}, u32[]{:S(2)}, u32[]{:S(2)}) collective-permute-start(bf16[4,128,128]{2,1,0:T(8,128)(2,1)S(1)} %get-tuple-element.224), channel_id=1, source_target_pairs={{0,6},{2,0},{4,2},{6,4},{1,7},{3,1},{5,3},{7,5},{8,14},{10,8},{12,... | collective-permute-start | bytes 393224 | tf_op jit(solution)/shard_map/ppermute | solution.py:435
  122.3 1.2 copy-start.2
  123.5 5.4 %copy-start.9 = (bf16[128,1792]{1,0:T(8,128)(2,1)S(1)}, bf16[128,1792]{1,0:T(8,128)(2,1)}, u32[]{:S(2)}) copy-start(bf16[128,1792]{1,0:T(8,128)(2,1)} %hidden.3) | copy-start | bytes 1376260
  123.5 5.4 %copy-start.19 = (s32[8]{0:T(128)S(1)}, s32[8]{0:T(128)}, u32[]{:S(2)}) copy-start(s32[8]{0:T(128)} %param.23) | copy-start | bytes 100
  128.9 0.8 copy-start.10
Sparse Core Ops, SparseCore 0:
  21.6 43.6 all-gather.10

commit v14 on v13

--- a/solution.py
+++ b/solution.py
@@ -190,13 +190,14 @@
 UNROLL = 4
 NX, NY, NZH, NZL = 4, 8, 2, 4
 BS = 128
-VMEM_LIMIT = 10 * 1024 * 1024
+VMEM_LIMIT = 8 * 1024 * 1024
+SMALL = 3 * 1024 * 1024
 f32 = jnp.float32
 bf16 = jnp.bfloat16
 i32 = jnp.int32
 
 
-def call(kernel, outs, n_smem, n_vmem, scratch=(), flops=0, byts=0, n_after=0):
+def call(kernel, outs, n_smem, n_vmem, scratch=(), flops=0, byts=0, n_after=0, limit=VMEM_LIMIT):
     smem = pl.BlockSpec(memory_space=pltpu.SMEM)
     vmem = pl.BlockSpec(memory_space=pltpu.VMEM)
     anywhere = pl.BlockSpec(memory_space=pl.ANY)
@@ -206,7 +207,7 @@
         in_specs=[smem] * n_smem + [vmem] * n_vmem + [anywhere] * n_after,
         out_specs=jax.tree.map(lambda _: vmem, outs),
         scratch_shapes=list(scratch),
-        compiler_params=pltpu.CompilerParams(vmem_limit_bytes=VMEM_LIMIT),
+        compiler_params=pltpu.CompilerParams(vmem_limit_bytes=limit),
         cost_estimate=pl.CostEstimate(flops=flops, bytes_accessed=byts, transcendentals=0),
     )
 
@@ -317,7 +318,7 @@
     lax.fori_loop(0, WCAP, select, 0, unroll=4)
 
 
-def sum_kernel(parts, out):
+def sum_kernel(parts, _after, out):
     def step(i, carry):
         value = parts[0, i].astype(f32)
         for n in range(1, parts.shape[0]):
@@ -480,10 +481,12 @@
         byts=4 * 1024 * 1024,
     )(info, code, hidden, mine, other)
     along_x = all_to_all(partial, "x")
-    summed = call(sum_kernel, like(partial.shape[1:], bf16), 0, 1, byts=2 * 1024 * 1024)(along_x)
+    summed = call(sum_kernel, like(partial.shape[1:], bf16), 0, 1, byts=2 * 1024 * 1024, n_after=1, limit=SMALL)(
+        along_x, stacked
+    )
     along_y = all_to_all(summed.reshape(NY, 2 * NZH, GCAP, BS), "y")
     half = like((2, GCAP, BS), f32)
-    keep, send_zh = call(pair_kernel, (half, half), 1, 1, byts=1024 * 1024)(info, along_y)
+    keep, send_zh = call(pair_kernel, (half, half), 1, 1, byts=1024 * 1024, limit=SMALL)(info, along_y)
     came_zh = shift(send_zh, "zh", NZH, 1)
 
     picked = call(select_kernel, like((WCAP, BS // NX, BS), bf16), 2, 1, byts=1024 * 1024, n_after=1)(
@@ -498,6 +501,7 @@
         [pltpu.VMEM((2, GCAP, BS), f32)],
         byts=1024 * 1024,
         n_after=2,
+        limit=SMALL,
     )(send, state_send, keep, came_zh, stacked, place, fits)
     shares = all_to_all(packed, SHARD)
 

time: 138 us -> 137 us (level)
    unnamed x37 -> x41, local copies, waits for them, and re-layouts: 8 us -> 8.41 us
where the time goes in v14:
time: 137 us; the launch traced here: 136 us
  starting transfers between devices  56.9 us (42%)
  waiting for transfers between devices  28.8 us (21%)
  Pallas kernels  17.8 us (13%)
  between operations  17.7 us (13%)
  local copies, waits for them, and re-layouts  11 us (8%)
  other arithmetic  3.43 us (3%)
    ppermute x9, starting transfers between devices, shift(): lax.ppermute(values, axis, [(i, (i + step) % count) for i in range(count)])  34.5 us
    all_to_all x4, waiting for transfers between devices, all_to_all(): return lax.all_to_all(values, axis, split_axis=0, concat_axis=0, tiled=True)  25.1 us
    all_to_all x4, starting transfers between devices, all_to_all(): return lax.all_to_all(values, axis, split_axis=0, concat_axis=0, tiled=True)  22.4 us
    unnamed x41, local copies, waits for them, and re-layouts  8.41 us
    pallas_call x1, Pallas kernels, shards(): call(forward_kernel, (like((NZL, 4, tokens, BS), f32), like((NZL, 4, toke...  3.54 us
    ppermute x9, waiting for transfers between devices, shift(): lax.ppermute(values, axis, [(i, (i + step) % count) for i in range(count)])  3 us
    pallas_call x1, Pallas kernels, shards(): call(grad_kernel, (like((NX, NY * NZH * 2, GCAP, BS), bf16), like((shard_...  2.99 us
    pallas_call x1, Pallas kernels, shards(): call(backward_kernel, like(hidden.shape, bf16), 2, 2, [pltpu.VMEM((row_lo...  2.75 us
  transfers between devices with their start and end apart: 14, of which 5 were waited for; matrix products, arithmetic and copies ran while one was open for 3% of the time, Pallas kernels for 9%

profile of v14, /device:TPU:1, one launch (start us, length us, event | category | flops | bytes accessed | tf_op | source)
XLA Modules:
  0.0 135.9 jit_solution(10005963442426248549)
XLA Ops:
  7.2 1.7 %dynamic-slice_bitcast_fusion.1 = bf16[32,32,128]{2,1,0:T(8,128)(2,1)} fusion(bf16[1,32,128,128]{3,2,1,0:T(8,128)(2,1)} %param.20, s32[]{:T(128)S(6)} %select_n.333), kind=kLoop, calls=%fused_computation.122 | loop fusion | bytes 524292 | tf_op jit(solution)/shard_map/dynamic_slice | solution.py:461
  9.0 1.7 %shard_map.147 = bf16[4,128,512]{2,1,0:T(8,128)(2,1)} custom-call(bf16[128,512]{1,0:T(8,128)(2,1)} %value), custom_call_target="tpu_custom_call" | custom-call | bytes 1048576 | tf_op jit(solution)/shard_map/pallas_call | solution.py:464
  10.7 7.8 %all-to-all-start.1 = ((bf16[4,128,512]{2,1,0:T(8,128)(2,1)}), bf16[4,128,512]{2,1,0:T(8,128)(2,1)S(1)}, u32[]{:S(2)}, u32[]{:S(2)}) async-start(bf16[4,128,512]{2,1,0:T(8,128)(2,1)} %shard_map.147), calls=%async_computation.2 | async-start | bytes 1048576 | tf_op jit(solution)/shard_map/all_to_all | solution.py:432
  22.8 8.8 %all-to-all-done.1.mine = bf16[4,128,512]{2,1,0:T(8,128)(2,1)S(1)} async-done(((bf16[4,128,512]{2,1,0:T(8,128)(2,1)}), bf16[4,128,512]{2,1,0:T(8,128)(2,1)S(1)}, u32[]{:S(2)}, u32[]{:S(2)}) %all-to-all-start.1) | async-done | bytes 524320 | tf_op jit(solution)/shard_map/all_to_all | solution.py:432
  31.6 4.2 %collective-permute-start = (bf16[4,128,512]{2,1,0:T(8,128)(2,1)S(1)}, bf16[4,128,512]{2,1,0:T(8,128)(2,1)S(1)}, u32[]{:S(2)}, u32[]{:S(2)}) collective-permute-start(bf16[4,128,512]{2,1,0:T(8,128)(2,1)S(1)} %all-to-all-done.1.mine), channel_id=1, source_target_pairs={{0,1},{1,0},{2,3},{3,2},{4,5},{5,4},{6,7},{7,6},{8,9},{9,8},{10,11... | collective-permute-start | bytes 1572872 | tf_op jit(solution)/shard_map/ppermute | solution.py:436
  37.4 3.0 %shard_map.148 = (bf16[4,32,40,128]{3,2,1,0:T(8,128)(2,1)}, bf16[32,128,128]{2,1,0:T(8,128)(2,1)S(1)}) custom-call(s32[6]{0:T(128)S(1)} %stack.27.info, s32[44]{0:T(128)S(1)} %select_reduce_fusion.4.code, bf16[128,1792]{1,0:T(8,128)(2,1)S(1)} %copy-done.8, bf16[4,128,512]{2,1,0:T(8,128)(2,1)S(1)} %all-to-all-done.1.mine, ...), custom_call_target="tpu_custom_call" | custom-call | flops 184549376 | bytes 4194304 | tf_op jit(solution)/shard_map/pallas_call | solution.py:474
  40.4 1.0 copy-done.3
  41.4 4.1 %all-to-all-start.2 = ((bf16[4,32,40,128]{3,2,1,0:T(8,128)(2,1)}), bf16[4,32,40,128]{3,2,1,0:T(8,128)(2,1)S(1)}, u32[]{:S(2)}, u32[]{:S(2)}) async-start(bf16[4,32,40,128]{3,2,1,0:T(8,128)(2,1)} %get-tuple-element.210), calls=%async_computation.3 | async-start | bytes 2621440 | tf_op jit(solution)/shard_map/all_to_all | solution.py:432
  45.5 0.9 dynamic-slice_convert_fusion
  46.4 16.2 %all-to-all-done.2.parts = bf16[4,32,40,128]{3,2,1,0:T(8,128)(2,1)S(1)} async-done(((bf16[4,32,40,128]{3,2,1,0:T(8,128)(2,1)}), bf16[4,32,40,128]{3,2,1,0:T(8,128)(2,1)S(1)}, u32[]{:S(2)}, u32[]{:S(2)}) %all-to-all-start.2) | async-done | bytes 1310752 | tf_op jit(solution)/shard_map/all_to_all | solution.py:432
  62.6 0.9 shard_map.149._after
  63.5 6.8 %all-to-all-start.3 = ((bf16[8,4,40,128]{3,2,1,0:T(8,128)(2,1)}), bf16[8,4,40,128]{3,2,1,0:T(8,128)(2,1)S(1)}, u32[]{:S(2)}, u32[]{:S(2)}) async-start(bf16[8,4,40,128]{3,2,1,0:T(8,128)(2,1)} %bitcast.46), calls=%async_computation.4 | async-start | bytes 655360 | tf_op jit(solution)/shard_map/all_to_all | solution.py:432
  70.7 1.6 %copy-done = bf16[256,32,128]{2,1,0:T(8,128)(2,1)S(1)} copy-done((bf16[256,32,128]{2,1,0:T(8,128)(2,1)S(1)}, bf16[256,32,128]{2,1,0:T(8,128)(2,1)}, u32[]{:S(2)}) %copy-start) | copy-done | bytes 2097176
  73.0 2.3 %collective-permute-start.2 = (bf16[44,32,128]{2,1,0:T(8,128)(2,1)S(1)}, bf16[44,32,128]{2,1,0:T(8,128)(2,1)S(1)}, u32[]{:S(2)}, u32[]{:S(2)}) collective-permute-start(bf16[44,32,128]{2,1,0:T(8,128)(2,1)S(1)} %shard_map.152.w0), channel_id=1, source_target_pairs={{0,16},{16,32},{32,48},{48,0},{1,17},{17,33},{33,49},{49,1},{2,18}... | collective-permute-start | bytes 1081352 | tf_op jit(solution)/shard_map/ppermute | solution.py:436
  75.3 3.6 %collective-permute-start.3 = (bf16[44,32,128]{2,1,0:T(8,128)(2,1)S(1)}, bf16[44,32,128]{2,1,0:T(8,128)(2,1)S(1)}, u32[]{:S(2)}, u32[]{:S(2)}) collective-permute-start(bf16[44,32,128]{2,1,0:T(8,128)(2,1)S(1)} %shard_map.152.w0), channel_id=1, source_target_pairs={{0,32},{16,48},{32,0},{48,16},{1,33},{17,49},{33,1},{49,17},{2,34}... | collective-permute-start | bytes 1081352 | tf_op jit(solution)/shard_map/ppermute | solution.py:436
  78.9 2.6 %collective-permute-start.4 = (bf16[44,32,128]{2,1,0:T(8,128)(2,1)S(1)}, bf16[44,32,128]{2,1,0:T(8,128)(2,1)S(1)}, u32[]{:S(2)}, u32[]{:S(2)}) collective-permute-start(bf16[44,32,128]{2,1,0:T(8,128)(2,1)S(1)} %shard_map.152.w0), channel_id=1, source_target_pairs={{0,48},{16,0},{32,16},{48,32},{1,49},{17,1},{33,17},{49,33},{2,50}... | collective-permute-start | bytes 1081352 | tf_op jit(solution)/shard_map/ppermute | solution.py:436
  82.3 7.9 %collective-permute-start.1 = (f32[2,40,128]{2,1,0:T(8,128)S(1)}, f32[2,40,128]{2,1,0:T(8,128)S(1)}, u32[]{:S(2)}, u32[]{:S(2)}) collective-permute-start(f32[2,40,128]{2,1,0:T(8,128)S(1)} %get-tuple-element.212), channel_id=1, source_target_pairs={{0,8},{8,0},{1,9},{9,1},{2,10},{10,2},{3,11},{11,3},{4,12},{12,4},... | collective-permute-start | bytes 122888 | tf_op jit(solution)/shard_map/ppermute | solution.py:436
  92.3 1.4 %shard_map.151._after = f32[8,40,128]{2,1,0:T(8,128)} custom-call(s32[112]{0:T(128)S(1)} %broadcast_minimum_fusion.send, s32[16]{0:T(128)S(1)} %select_reduce_fusion.6.state_send, f32[2,40,128]{2,1,0:T(8,128)S(1)} %get-tuple-element.211.keep, f32[2,40,128]{2,1,0:T(8,128)S(1)} %collective-permute-done.1.came, f32[32,768]{1,0:T(8,128)S(1)} %pad_maximum_fusion.1._after.stacked, ...), custom_call_target="tpu_custom_call" | custom-call | bytes 1048576 | tf_op jit(solution)/shard_map/pallas_call | solution.py:496
  93.7 2.0 %collective-permute-done.4.w3 = bf16[44,32,128]{2,1,0:T(8,128)(2,1)S(1)} collective-permute-done((bf16[44,32,128]{2,1,0:T(8,128)(2,1)S(1)}, bf16[44,32,128]{2,1,0:T(8,128)(2,1)S(1)}, u32[]{:S(2)}, u32[]{:S(2)}) %collective-permute-start.4) | collective-permute-done | bytes 360480 | tf_op jit(solution)/shard_map/ppermute | solution.py:436
  96.4 1.0 copy-done.6
  97.4 3.5 %shard_map.153 = (f32[4,4,128,128]{3,2,1,0:T(8,128)S(1)}, f32[4,4,128,128]{3,2,1,0:T(8,128)}, bf16[44,4,32,128]{3,2,1,0:T(8,128)(2,1)S(1)}) custom-call(s32[6]{0:T(128)S(1)} %stack.27.info, s32[44]{0:T(128)S(1)} %select_reduce_fusion.4.code, bf16[128,1792]{1,0:T(8,128)(2,1)} %hidden.3, bf16[44,32,128]{2,1,0:T(8,128)(2,1)S(1)} %shard_map.152.w0, ...), custom_call_target="tpu_custom_call" | custom-call | flops 184549376 | bytes 8388608 | tf_op jit(solution)/shard_map/pallas_call | solution.py:508
  101.0 1.0 copy-done.1
  101.9 3.4 %collective-permute-start.5 = (f32[4,4,128,128]{3,2,1,0:T(8,128)}, f32[4,4,128,128]{3,2,1,0:T(8,128)S(1)}, u32[]{:S(2)}, u32[]{:S(2)}) collective-permute-start(f32[4,4,128,128]{3,2,1,0:T(8,128)} %get-tuple-element.220), channel_id=1, source_target_pairs={{0,1},{1,0},{2,3},{3,2},{4,5},{5,4},{6,7},{7,6},{8,9},{9,8},{10,11... | collective-permute-start | bytes 3145736 | tf_op jit(solution)/shard_map/ppermute | solution.py:436
  105.4 3.6 %all-to-all-start.4 = ((f32[8,40,128]{2,1,0:T(8,128)}), f32[8,40,128]{2,1,0:T(8,128)S(1)}, u32[]{:S(2)}, u32[]{:S(2)}) async-start(f32[8,40,128]{2,1,0:T(8,128)} %shard_map.151._after), calls=%async_computation.5 | async-start | bytes 327680 | tf_op jit(solution)/shard_map/all_to_all | solution.py:432
  109.1 1.2 copy-done.2
  110.3 1.3 shard_map.156
  111.6 3.3 %collective-permute-start.6 = (bf16[4,128,128]{2,1,0:T(8,128)(2,1)}, bf16[4,128,128]{2,1,0:T(8,128)(2,1)S(1)}, u32[]{:S(2)}, u32[]{:S(2)}) collective-permute-start(bf16[4,128,128]{2,1,0:T(8,128)(2,1)} %get-tuple-element.222), channel_id=1, source_target_pairs={{0,2},{2,4},{4,6},{6,0},{1,3},{3,5},{5,7},{7,1},{8,10},{10,12},{12... | collective-permute-start | bytes 393224 | tf_op jit(solution)/shard_map/ppermute | solution.py:436
  114.9 4.0 %collective-permute-start.7 = (bf16[4,128,128]{2,1,0:T(8,128)(2,1)S(1)}, bf16[4,128,128]{2,1,0:T(8,128)(2,1)S(1)}, u32[]{:S(2)}, u32[]{:S(2)}) collective-permute-start(bf16[4,128,128]{2,1,0:T(8,128)(2,1)S(1)} %get-tuple-element.223), channel_id=1, source_target_pairs={{0,4},{2,6},{4,0},{6,2},{1,5},{3,7},{5,1},{7,3},{8,12},{10,14},{12... | collective-permute-start | bytes 393224 | tf_op jit(solution)/shard_map/ppermute | solution.py:436
  118.9 3.1 %collective-permute-start.8 = (bf16[4,128,128]{2,1,0:T(8,128)(2,1)S(1)}, bf16[4,128,128]{2,1,0:T(8,128)(2,1)S(1)}, u32[]{:S(2)}, u32[]{:S(2)}) collective-permute-start(bf16[4,128,128]{2,1,0:T(8,128)(2,1)S(1)} %get-tuple-element.224), channel_id=1, source_target_pairs={{0,6},{2,0},{4,2},{6,4},{1,7},{3,1},{5,3},{7,5},{8,14},{10,8},{12,... | collective-permute-start | bytes 393224 | tf_op jit(solution)/shard_map/ppermute | solution.py:436
  122.0 1.2 copy-done.4
  123.2 2.7 %shard_map.154._after = bf16[128,1792]{1,0:T(8,128)(2,1)} custom-call(s32[6]{0:T(128)S(1)} %stack.27.info, s32[44]{0:T(128)S(1)} %select_reduce_fusion.4.code, bf16[32,128,128]{2,1,0:T(8,128)(2,1)S(1)} %copy-done.4, bf16[44,4,32,128]{3,2,1,0:T(8,128)(2,1)S(1)} %get-tuple-element.215.weights), custom_call_target="tpu_custom_call" | custom-call | flops 184549376 | bytes 4194304 | tf_op jit(solution)/shard_map/pallas_call | solution.py:523
  126.0 1.8 %shard_map.155 = (f32[32,256]{1,0:T(8,128)}, f32[32,256]{1,0:T(8,128)}, f32[32,256]{1,0:T(8,128)}) custom-call(s32[32]{0:T(128)S(1)} %select_reduce_fusion.5._after.place, f32[32,768]{1,0:T(8,128)S(1)} %pad_maximum_fusion.1._after.stacked, f32[8,40,128]{2,1,0:T(8,128)S(1)} %all-to-all-done.4.came, bf16[128,1792]{1,0:T(8,128)(2,1)} %shard_map.154._after), custom_call_target="tpu_custom_call" | custom-call | bytes 1048576 | tf_op jit(solution)/shard_map/pallas_call | solution.py:542
  (83 shorter events, 8.3 us)
Async XLA Ops:
  7.2 12.1 %copy-start.14 = (s32[8,32]{1,0:T(8,128)S(1)}, s32[8,32]{1,0:T(8,128)}, u32[]{:S(2)}) copy-start(s32[8,32]{1,0:T(8,128)} %param.24) | copy-start | bytes 3076
  7.2 12.2 %copy-start.15 = (s32[8,32]{1,0:T(8,128)S(1)}, s32[8,32]{1,0:T(8,128)}, u32[]{:S(2)}) copy-start(s32[8,32]{1,0:T(8,128)} %param.21) | copy-start | bytes 3076
  7.2 12.2 %copy-start.19 = (s32[8]{0:T(128)S(1)}, s32[8]{0:T(128)}, u32[]{:S(2)}) copy-start(s32[8]{0:T(128)} %param.23) | copy-start | bytes 100
  7.2 12.4 %copy-start.16 = (s32[8,32]{1,0:T(8,128)S(1)}, s32[8,32]{1,0:T(8,128)}, u32[]{:S(2)}) copy-start(s32[8,32]{1,0:T(8,128)} %param.22) | copy-start | bytes 3076
  7.2 30.2 %copy-start.8 = (bf16[128,1792]{1,0:T(8,128)(2,1)S(1)}, bf16[128,1792]{1,0:T(8,128)(2,1)}, u32[]{:S(2)}) copy-start(bf16[128,1792]{1,0:T(8,128)(2,1)} %hidden.3) | copy-start | bytes 1376260
  10.7 20.9 %all-to-all-start.1 = ((bf16[4,128,512]{2,1,0:T(8,128)(2,1)}), bf16[4,128,512]{2,1,0:T(8,128)(2,1)S(1)}, u32[]{:S(2)}, u32[]{:S(2)}) async-start(bf16[4,128,512]{2,1,0:T(8,128)(2,1)} %shard_map.147), calls=%async_computation.2 | async-start | bytes 1048576 | tf_op jit(solution)/shard_map/all_to_all | solution.py:432
  18.5 52.2 %all-gather.11.cloned.1.call-start = ((), (), s32[]{:S(2)}) async-start(), calls=%async_computation.10 | async-start | bytes 2359296 | tf_op jit(solution)/shard_map/all_gather | solution.py:463
  31.6 5.7 %collective-permute-start = (bf16[4,128,512]{2,1,0:T(8,128)(2,1)S(1)}, bf16[4,128,512]{2,1,0:T(8,128)(2,1)S(1)}, u32[]{:S(2)}, u32[]{:S(2)}) collective-permute-start(bf16[4,128,512]{2,1,0:T(8,128)(2,1)S(1)} %all-to-all-done.1.mine), channel_id=1, source_target_pairs={{0,1},{1,0},{2,3},{3,2},{4,5},{5,4},{6,7},{7,6},{8,9},{9,8},{10,11... | collective-permute-start | bytes 1572872 | tf_op jit(solution)/shard_map/ppermute | solution.py:436
  36.6 9.7 %copy-start.12 = (f32[1,32,256]{2,1,0:T(8,128)S(1)}, f32[1,32,256]{2,1,0:T(8,128)}, u32[]{:S(2)}) copy-start(f32[1,32,256]{2,1,0:T(8,128)} %param.26) | copy-start | bytes 98308
  36.6 9.7 %copy-start.13 = (f32[1,32,256]{2,1,0:T(8,128)S(1)}, f32[1,32,256]{2,1,0:T(8,128)}, u32[]{:S(2)}) copy-start(f32[1,32,256]{2,1,0:T(8,128)} %param.27) | copy-start | bytes 98308
  40.4 1.0 copy-start.3
  41.3 29.0 %copy-start.17 = (s32[8,32]{1,0:T(8,128)S(1)}, s32[8,32]{1,0:T(8,128)}, u32[]{:S(2)}) copy-start(s32[8,32]{1,0:T(8,128)} %param.25) | copy-start | bytes 3076
  41.4 21.3 %all-to-all-start.2 = ((bf16[4,32,40,128]{3,2,1,0:T(8,128)(2,1)}), bf16[4,32,40,128]{3,2,1,0:T(8,128)(2,1)S(1)}, u32[]{:S(2)}, u32[]{:S(2)}) async-start(bf16[4,32,40,128]{3,2,1,0:T(8,128)(2,1)} %get-tuple-element.210), calls=%async_computation.3 | async-start | bytes 2621440 | tf_op jit(solution)/shard_map/all_to_all | solution.py:432
  63.5 18.1 %all-to-all-start.3 = ((bf16[8,4,40,128]{3,2,1,0:T(8,128)(2,1)}), bf16[8,4,40,128]{3,2,1,0:T(8,128)(2,1)S(1)}, u32[]{:S(2)}, u32[]{:S(2)}) async-start(bf16[8,4,40,128]{3,2,1,0:T(8,128)(2,1)} %bitcast.46), calls=%async_computation.4 | async-start | bytes 655360 | tf_op jit(solution)/shard_map/all_to_all | solution.py:432
  70.7 1.6 %copy-start = (bf16[256,32,128]{2,1,0:T(8,128)(2,1)S(1)}, bf16[256,32,128]{2,1,0:T(8,128)(2,1)}, u32[]{:S(2)}) copy-start(bf16[256,32,128]{2,1,0:T(8,128)(2,1)} %all-gather.11.cloned.1.call-done.gathered) | copy-start | bytes 6291460
  73.0 20.7 %collective-permute-start.2 = (bf16[44,32,128]{2,1,0:T(8,128)(2,1)S(1)}, bf16[44,32,128]{2,1,0:T(8,128)(2,1)S(1)}, u32[]{:S(2)}, u32[]{:S(2)}) collective-permute-start(bf16[44,32,128]{2,1,0:T(8,128)(2,1)S(1)} %shard_map.152.w0), channel_id=1, source_target_pairs={{0,16},{16,32},{32,48},{48,0},{1,17},{17,33},{33,49},{49,1},{2,18}... | collective-permute-start | bytes 1081352 | tf_op jit(solution)/shard_map/ppermute | solution.py:436
  75.3 18.4 %collective-permute-start.3 = (bf16[44,32,128]{2,1,0:T(8,128)(2,1)S(1)}, bf16[44,32,128]{2,1,0:T(8,128)(2,1)S(1)}, u32[]{:S(2)}, u32[]{:S(2)}) collective-permute-start(bf16[44,32,128]{2,1,0:T(8,128)(2,1)S(1)} %shard_map.152.w0), channel_id=1, source_target_pairs={{0,32},{16,48},{32,0},{48,16},{1,33},{17,49},{33,1},{49,17},{2,34}... | collective-permute-start | bytes 1081352 | tf_op jit(solution)/shard_map/ppermute | solution.py:436
  78.9 16.7 %collective-permute-start.4 = (bf16[44,32,128]{2,1,0:T(8,128)(2,1)S(1)}, bf16[44,32,128]{2,1,0:T(8,128)(2,1)S(1)}, u32[]{:S(2)}, u32[]{:S(2)}) collective-permute-start(bf16[44,32,128]{2,1,0:T(8,128)(2,1)S(1)} %shard_map.152.w0), channel_id=1, source_target_pairs={{0,48},{16,0},{32,16},{48,32},{1,49},{17,1},{33,17},{49,33},{2,50}... | collective-permute-start | bytes 1081352 | tf_op jit(solution)/shard_map/ppermute | solution.py:436
  82.3 10.1 %collective-permute-start.1 = (f32[2,40,128]{2,1,0:T(8,128)S(1)}, f32[2,40,128]{2,1,0:T(8,128)S(1)}, u32[]{:S(2)}, u32[]{:S(2)}) collective-permute-start(f32[2,40,128]{2,1,0:T(8,128)S(1)} %get-tuple-element.212), channel_id=1, source_target_pairs={{0,8},{8,0},{1,9},{9,1},{2,10},{10,2},{3,11},{11,3},{4,12},{12,4},... | collective-permute-start | bytes 122888 | tf_op jit(solution)/shard_map/ppermute | solution.py:436
  96.4 1.0 copy-start.6
  100.9 1.0 copy-start.1
  101.9 7.1 %collective-permute-start.5 = (f32[4,4,128,128]{3,2,1,0:T(8,128)}, f32[4,4,128,128]{3,2,1,0:T(8,128)S(1)}, u32[]{:S(2)}, u32[]{:S(2)}) collective-permute-start(f32[4,4,128,128]{3,2,1,0:T(8,128)} %get-tuple-element.220), channel_id=1, source_target_pairs={{0,1},{1,0},{2,3},{3,2},{4,5},{5,4},{6,7},{7,6},{8,9},{9,8},{10,11... | collective-permute-start | bytes 3145736 | tf_op jit(solution)/shard_map/ppermute | solution.py:436
  105.4 20.5 %all-to-all-start.4 = ((f32[8,40,128]{2,1,0:T(8,128)}), f32[8,40,128]{2,1,0:T(8,128)S(1)}, u32[]{:S(2)}, u32[]{:S(2)}) async-start(f32[8,40,128]{2,1,0:T(8,128)} %shard_map.151._after), calls=%async_computation.5 | async-start | bytes 327680 | tf_op jit(solution)/shard_map/all_to_all | solution.py:432
  109.0 1.2 copy-start.2
  111.6 16.2 %collective-permute-start.6 = (bf16[4,128,128]{2,1,0:T(8,128)(2,1)}, bf16[4,128,128]{2,1,0:T(8,128)(2,1)S(1)}, u32[]{:S(2)}, u32[]{:S(2)}) collective-permute-start(bf16[4,128,128]{2,1,0:T(8,128)(2,1)} %get-tuple-element.222), channel_id=1, source_target_pairs={{0,2},{2,4},{4,6},{6,0},{1,3},{3,5},{5,7},{7,1},{8,10},{10,12},{12... | collective-permute-start | bytes 393224 | tf_op jit(solution)/shard_map/ppermute | solution.py:436
  114.9 12.9 %collective-permute-start.7 = (bf16[4,128,128]{2,1,0:T(8,128)(2,1)S(1)}, bf16[4,128,128]{2,1,0:T(8,128)(2,1)S(1)}, u32[]{:S(2)}, u32[]{:S(2)}) collective-permute-start(bf16[4,128,128]{2,1,0:T(8,128)(2,1)S(1)} %get-tuple-element.223), channel_id=1, source_target_pairs={{0,4},{2,6},{4,0},{6,2},{1,5},{3,7},{5,1},{7,3},{8,12},{10,14},{12... | collective-permute-start | bytes 393224 | tf_op jit(solution)/shard_map/ppermute | solution.py:436
  118.9 9.2 %collective-permute-start.8 = (bf16[4,128,128]{2,1,0:T(8,128)(2,1)S(1)}, bf16[4,128,128]{2,1,0:T(8,128)(2,1)S(1)}, u32[]{:S(2)}, u32[]{:S(2)}) collective-permute-start(bf16[4,128,128]{2,1,0:T(8,128)(2,1)S(1)} %get-tuple-element.224), channel_id=1, source_target_pairs={{0,6},{2,0},{4,2},{6,4},{1,7},{3,1},{5,3},{7,5},{8,14},{10,8},{12,... | collective-permute-start | bytes 393224 | tf_op jit(solution)/shard_map/ppermute | solution.py:436
  122.0 1.2 copy-start.4
  123.2 4.9 %copy-start.9 = (bf16[128,1792]{1,0:T(8,128)(2,1)S(1)}, bf16[128,1792]{1,0:T(8,128)(2,1)}, u32[]{:S(2)}) copy-start(bf16[128,1792]{1,0:T(8,128)(2,1)} %hidden.3) | copy-start | bytes 1376260
  123.2 4.9 %copy-start.10 = (bf16[128,512]{1,0:T(8,128)(2,1)S(1)}, bf16[128,512]{1,0:T(8,128)(2,1)}, u32[]{:S(2)}) copy-start(bf16[128,512]{1,0:T(8,128)(2,1)} %value) | copy-start | bytes 393220
  123.2 4.9 %copy-start.18 = (s32[8,32]{1,0:T(8,128)S(1)}, s32[8,32]{1,0:T(8,128)}, u32[]{:S(2)}) copy-start(s32[8,32]{1,0:T(8,128)} %param.25) | copy-start | bytes 3076
  123.2 4.9 %copy-start.20 = (s32[8]{0:T(128)S(1)}, s32[8]{0:T(128)}, u32[]{:S(2)}) copy-start(s32[8]{0:T(128)} %param.23) | copy-start | bytes 100
  (2 other events, 1.4 us)
Sparse Core Ops, SparseCore 0:
  21.6 43.6 all-gather.10

commit v15 on v14

--- a/solution.py
+++ b/solution.py
@@ -318,7 +318,7 @@
     lax.fori_loop(0, WCAP, select, 0, unroll=4)
 
 
-def sum_kernel(parts, _after, out):
+def sum_kernel(parts, _after, _after2, out):
     def step(i, carry):
         value = parts[0, i].astype(f32)
         for n in range(1, parts.shape[0]):
@@ -481,18 +481,19 @@
         byts=4 * 1024 * 1024,
     )(info, code, hidden, mine, other)
     along_x = all_to_all(partial, "x")
-    summed = call(sum_kernel, like(partial.shape[1:], bf16), 0, 1, byts=2 * 1024 * 1024, n_after=1, limit=SMALL)(
-        along_x, stacked
+    picked = call(select_kernel, like((WCAP, BS // NX, BS), bf16), 2, 1, byts=1024 * 1024, n_after=1)(
+        info, code, gathered, partial
+    )
+    summed = call(sum_kernel, like(partial.shape[1:], bf16), 0, 1, byts=2 * 1024 * 1024, n_after=2, limit=SMALL)(
+        along_x, stacked, picked
     )
     along_y = all_to_all(summed.reshape(NY, 2 * NZH, GCAP, BS), "y")
     half = like((2, GCAP, BS), f32)
     keep, send_zh = call(pair_kernel, (half, half), 1, 1, byts=1024 * 1024, limit=SMALL)(info, along_y)
     came_zh = shift(send_zh, "zh", NZH, 1)
 
-    picked = call(select_kernel, like((WCAP, BS // NX, BS), bf16), 2, 1, byts=1024 * 1024, n_after=1)(
-        info, code, gathered, summed
-    )
-    w2, w1, w3 = (shift(picked, "x", NX, k) for k in (2, 1, 3))
+    ready, _ = lax.optimization_barrier((picked, summed))
+    w2, w1, w3 = (shift(ready, "x", NX, k) for k in (2, 1, 3))
     packed = call(
         functools.partial(share_kernel, scale),
         like((shard_count, 2 * PAIR + MV * stacked.shape[1] // BS, BS), f32),

time: 137 us -> 142 us (1.036)
  starting transfers between devices: 56.9 us -> 62.1 us
  waiting for transfers between devices: 28.8 us -> 27.1 us
    all_gather x1, waiting for transfers between devices: 0.02 us -> 10.5 us  [shards(): gathered = lax.all_gather(quarter, SHARD, axis=0, tiled=True)]
    all_to_all x4, waiting for transfers between devices: 25.1 us -> 15.4 us  [all_to_all(): return lax.all_to_all(values, axis, split_axis=0, concat_axis=0, tiled=True)]
    ppermute x9, starting transfers between devices: 34.5 us -> 40.1 us  [shift(): lax.ppermute(values, axis, [(i, (i + step) % count) for i in range(count)])]
    ppermute x9, waiting for transfers between devices: 3 us -> 1.1 us  [shift(): lax.ppermute(values, axis, [(i, (i + step) % count) for i in range(count)])]
    unnamed x41 -> x43, local copies, waits for them, and re-layouts: 8.41 us -> 9.63 us
  transfers between devices with their start and end apart: 14 -> 14, of which waited for: 5 -> 6; matrix products, arithmetic and copies ran while one was open for 3% -> 3% of each run, Pallas kernels for 9% -> 10%
where the time goes in v15:
time: 142 us; the launch traced here: 141 us
  starting transfers between devices  62.1 us (44%)
  waiting for transfers between devices  27.1 us (19%)
  Pallas kernels  18.6 us (13%)
  between operations  17.5 us (12%)
  local copies, waits for them, and re-layouts  12.2 us (9%)
  other arithmetic  3.37 us (2%)
    ppermute x9, starting transfers between devices, shift(): lax.ppermute(values, axis, [(i, (i + step) % count) for i in range(count)])  40.1 us
    all_to_all x4, starting transfers between devices, all_to_all(): return lax.all_to_all(values, axis, split_axis=0, concat_axis=0, tiled=True)  22 us
    all_to_all x4, waiting for transfers between devices, all_to_all(): return lax.all_to_all(values, axis, split_axis=0, concat_axis=0, tiled=True)  15.4 us
    all_gather x1, waiting for transfers between devices, shards(): gathered = lax.all_gather(quarter, SHARD, axis=0, tiled=True)  10.5 us
    unnamed x43, local copies, waits for them, and re-layouts  9.63 us
    pallas_call x1, Pallas kernels, shards(): call(forward_kernel, (like((NZL, 4, tokens, BS), f32), like((NZL, 4, toke...  3.54 us
    pallas_call x1, Pallas kernels, shards(): call(grad_kernel, (like((NX, NY * NZH * 2, GCAP, BS), bf16), like((shard_...  3.17 us
  transfers between devices with their start and end apart: 14, of which 6 were waited for; matrix products, arithmetic and copies ran while one was open for 3% of the time, Pallas kernels for 10%

profile of v15, /device:TPU:1, one launch (start us, length us, event | category | flops | bytes accessed | tf_op | source)
XLA Modules:
  0.0 141.3 jit_solution(16278932725720497252)
XLA Ops:
  7.3 1.7 %dynamic-slice_bitcast_fusion.1 = bf16[32,32,128]{2,1,0:T(8,128)(2,1)} fusion(bf16[1,32,128,128]{3,2,1,0:T(8,128)(2,1)} %param.20, s32[]{:T(128)S(6)} %select_n.333), kind=kLoop, calls=%fused_computation.122 | loop fusion | bytes 524292 | tf_op jit(solution)/shard_map/dynamic_slice | solution.py:461
  9.0 1.7 %shard_map.147 = bf16[4,128,512]{2,1,0:T(8,128)(2,1)} custom-call(bf16[128,512]{1,0:T(8,128)(2,1)} %value), custom_call_target="tpu_custom_call" | custom-call | bytes 1048576 | tf_op jit(solution)/shard_map/pallas_call | solution.py:464
  10.8 7.8 %all-to-all-start.1 = ((bf16[4,128,512]{2,1,0:T(8,128)(2,1)}), bf16[4,128,512]{2,1,0:T(8,128)(2,1)S(1)}, u32[]{:S(2)}, u32[]{:S(2)}) async-start(bf16[4,128,512]{2,1,0:T(8,128)(2,1)} %shard_map.147), calls=%async_computation.2 | async-start | bytes 1048576 | tf_op jit(solution)/shard_map/all_to_all | solution.py:432
  22.0 9.7 %all-to-all-done.1.mine = bf16[4,128,512]{2,1,0:T(8,128)(2,1)S(1)} async-done(((bf16[4,128,512]{2,1,0:T(8,128)(2,1)}), bf16[4,128,512]{2,1,0:T(8,128)(2,1)S(1)}, u32[]{:S(2)}, u32[]{:S(2)}) %all-to-all-start.1) | async-done | bytes 524320 | tf_op jit(solution)/shard_map/all_to_all | solution.py:432
  31.7 4.3 %collective-permute-start = (bf16[4,128,512]{2,1,0:T(8,128)(2,1)S(1)}, bf16[4,128,512]{2,1,0:T(8,128)(2,1)S(1)}, u32[]{:S(2)}, u32[]{:S(2)}) collective-permute-start(bf16[4,128,512]{2,1,0:T(8,128)(2,1)S(1)} %all-to-all-done.1.mine), channel_id=1, source_target_pairs={{0,1},{1,0},{2,3},{3,2},{4,5},{5,4},{6,7},{7,6},{8,9},{9,8},{10,11... | collective-permute-start | bytes 1572872 | tf_op jit(solution)/shard_map/ppermute | solution.py:436
  37.5 3.2 %shard_map.148 = (bf16[4,32,40,128]{3,2,1,0:T(8,128)(2,1)}, bf16[32,128,128]{2,1,0:T(8,128)(2,1)S(1)}) custom-call(s32[6]{0:T(128)S(1)} %stack.27.info, s32[44]{0:T(128)S(1)} %select_reduce_fusion.4.code, bf16[128,1792]{1,0:T(8,128)(2,1)S(1)} %copy-done.10, bf16[4,128,512]{2,1,0:T(8,128)(2,1)S(1)} %all-to-all-done.1.mine, ...), custom_call_target="tpu_custom_call" | custom-call | flops 184549376 | bytes 4194304 | tf_op jit(solution)/shard_map/pallas_call | solution.py:474
  40.7 1.0 copy-done.1
  41.6 4.0 %all-to-all-start.2 = ((bf16[4,32,40,128]{3,2,1,0:T(8,128)(2,1)}), bf16[4,32,40,128]{3,2,1,0:T(8,128)(2,1)S(1)}, u32[]{:S(2)}, u32[]{:S(2)}) async-start(bf16[4,32,40,128]{3,2,1,0:T(8,128)(2,1)} %get-tuple-element.211._after), calls=%async_computation.3 | async-start | bytes 2621440 | tf_op jit(solution)/shard_map/all_to_all | solution.py:432
  46.6 10.5 %all-gather.11.cloned.1.call-done.gathered = bf16[256,32,128]{2,1,0:T(8,128)(2,1)} async-done(((bf16[32,32,128]{2,1,0:T(8,128)(2,1)}), bf16[256,32,128]{2,1,0:T(8,128)(2,1)}) %all-gather.11.cloned.1.call-update) | async-done | bytes 2097168 | tf_op jit(solution)/shard_map/all_gather | solution.py:463
  57.1 1.6 %copy-done = bf16[256,32,128]{2,1,0:T(8,128)(2,1)S(1)} copy-done((bf16[256,32,128]{2,1,0:T(8,128)(2,1)S(1)}, bf16[256,32,128]{2,1,0:T(8,128)(2,1)}, u32[]{:S(2)}) %copy-start) | copy-done | bytes 2097176
  59.4 3.5 %all-to-all-done.2.parts = bf16[4,32,40,128]{3,2,1,0:T(8,128)(2,1)S(1)} async-done(((bf16[4,32,40,128]{3,2,1,0:T(8,128)(2,1)}), bf16[4,32,40,128]{3,2,1,0:T(8,128)(2,1)S(1)}, u32[]{:S(2)}, u32[]{:S(2)}) %all-to-all-start.2) | async-done | bytes 1310752 | tf_op jit(solution)/shard_map/all_to_all | solution.py:432
  63.0 0.9 shard_map.150
  63.9 6.9 %all-to-all-start.3 = ((bf16[8,4,40,128]{3,2,1,0:T(8,128)(2,1)}), bf16[8,4,40,128]{3,2,1,0:T(8,128)(2,1)S(1)}, u32[]{:S(2)}, u32[]{:S(2)}) async-start(bf16[8,4,40,128]{3,2,1,0:T(8,128)(2,1)} %bitcast.46), calls=%async_computation.4 | async-start | bytes 655360 | tf_op jit(solution)/shard_map/all_to_all | solution.py:432
  71.1 2.2 %collective-permute-start.2 = (bf16[44,32,128]{2,1,0:T(8,128)(2,1)S(1)}, bf16[44,32,128]{2,1,0:T(8,128)(2,1)S(1)}, u32[]{:S(2)}, u32[]{:S(2)}) collective-permute-start(bf16[44,32,128]{2,1,0:T(8,128)(2,1)S(1)} %shard_map.149._after2.w0), channel_id=1, source_target_pairs={{0,16},{16,32},{32,48},{48,0},{1,17},{17,33},{33,49},{49,1},{2,18}... | collective-permute-start | bytes 1081352 | tf_op jit(solution)/shard_map/ppermute | solution.py:436
  73.3 3.7 %collective-permute-start.3 = (bf16[44,32,128]{2,1,0:T(8,128)(2,1)S(1)}, bf16[44,32,128]{2,1,0:T(8,128)(2,1)S(1)}, u32[]{:S(2)}, u32[]{:S(2)}) collective-permute-start(bf16[44,32,128]{2,1,0:T(8,128)(2,1)S(1)} %shard_map.149._after2.w0), channel_id=1, source_target_pairs={{0,32},{16,48},{32,0},{48,16},{1,33},{17,49},{33,1},{49,17},{2,34}... | collective-permute-start | bytes 1081352 | tf_op jit(solution)/shard_map/ppermute | solution.py:436
  77.0 2.5 %collective-permute-start.4 = (bf16[44,32,128]{2,1,0:T(8,128)(2,1)S(1)}, bf16[44,32,128]{2,1,0:T(8,128)(2,1)S(1)}, u32[]{:S(2)}, u32[]{:S(2)}) collective-permute-start(bf16[44,32,128]{2,1,0:T(8,128)(2,1)S(1)} %shard_map.149._after2.w0), channel_id=1, source_target_pairs={{0,48},{16,0},{32,16},{48,32},{1,49},{17,1},{33,17},{49,33},{2,50}... | collective-permute-start | bytes 1081352 | tf_op jit(solution)/shard_map/ppermute | solution.py:436
  79.6 2.2 %all-to-all-done.3.parts = bf16[8,4,40,128]{3,2,1,0:T(8,128)(2,1)S(1)} async-done(((bf16[8,4,40,128]{3,2,1,0:T(8,128)(2,1)}), bf16[8,4,40,128]{3,2,1,0:T(8,128)(2,1)S(1)}, u32[]{:S(2)}, u32[]{:S(2)}) %all-to-all-start.3) | async-done | bytes 327712 | tf_op jit(solution)/shard_map/all_to_all | solution.py:432
  82.5 11.7 %collective-permute-start.1 = (f32[2,40,128]{2,1,0:T(8,128)S(1)}, f32[2,40,128]{2,1,0:T(8,128)S(1)}, u32[]{:S(2)}, u32[]{:S(2)}) collective-permute-start(f32[2,40,128]{2,1,0:T(8,128)S(1)} %get-tuple-element.214), channel_id=1, source_target_pairs={{0,8},{8,0},{1,9},{9,1},{2,10},{10,2},{3,11},{11,3},{4,12},{12,4},... | collective-permute-start | bytes 122888 | tf_op jit(solution)/shard_map/ppermute | solution.py:436
  96.1 1.4 shard_map.152._after
  99.7 1.0 copy-done.4
  100.7 1.0 copy-done.6
  101.7 1.0 copy-done.8
  102.7 3.5 %shard_map.153 = (f32[4,4,128,128]{3,2,1,0:T(8,128)S(1)}, f32[4,4,128,128]{3,2,1,0:T(8,128)}, bf16[44,4,32,128]{3,2,1,0:T(8,128)(2,1)S(1)}) custom-call(s32[6]{0:T(128)S(1)} %stack.27.info, s32[44]{0:T(128)S(1)} %select_reduce_fusion.4.code, bf16[128,1792]{1,0:T(8,128)(2,1)} %hidden.3, bf16[44,32,128]{2,1,0:T(8,128)(2,1)S(1)} %shard_map.149._after2.w0, ...), custom_call_target="tpu_custom_call" | custom-call | flops 184549376 | bytes 8388608 | tf_op jit(solution)/shard_map/pallas_call | solution.py:509
  106.2 5.4 %collective-permute-start.5 = (f32[4,4,128,128]{3,2,1,0:T(8,128)}, f32[4,4,128,128]{3,2,1,0:T(8,128)}, u32[]{:S(2)}, u32[]{:S(2)}) collective-permute-start(f32[4,4,128,128]{3,2,1,0:T(8,128)} %get-tuple-element.222), channel_id=1, source_target_pairs={{0,1},{1,0},{2,3},{3,2},{4,5},{5,4},{6,7},{7,6},{8,9},{9,8},{10,11... | collective-permute-start | bytes 3145736 | tf_op jit(solution)/shard_map/ppermute | solution.py:436
  111.6 3.3 %all-to-all-start.4 = ((f32[8,40,128]{2,1,0:T(8,128)}), f32[8,40,128]{2,1,0:T(8,128)S(1)}, u32[]{:S(2)}, u32[]{:S(2)}) async-start(f32[8,40,128]{2,1,0:T(8,128)} %shard_map.152._after), calls=%async_computation.5 | async-start | bytes 327680 | tf_op jit(solution)/shard_map/all_to_all | solution.py:432
  114.9 2.0 %shard_map.156 = (f32[4,128,128]{2,1,0:T(8,128)S(1)}, bf16[4,128,128]{2,1,0:T(8,128)(2,1)}, bf16[4,128,128]{2,1,0:T(8,128)(2,1)S(1)}, bf16[4,128,128]{2,1,0:T(8,128)(2,1)S(1)}) custom-call(s32[6]{0:T(128)S(1)} %stack.27.info, f32[4,4,128,128]{3,2,1,0:T(8,128)S(1)} %get-tuple-element.221.mine, f32[4,4,128,128]{3,2,1,0:T(8,128)} %collective-permute-done.5.came), custom_call_target="tpu_custom_call" | custom-call | bytes 3145728 | tf_op jit(solution)/shard_map/pallas_call | solution.py:534
  116.9 3.2 %collective-permute-start.6 = (bf16[4,128,128]{2,1,0:T(8,128)(2,1)}, bf16[4,128,128]{2,1,0:T(8,128)(2,1)S(1)}, u32[]{:S(2)}, u32[]{:S(2)}) collective-permute-start(bf16[4,128,128]{2,1,0:T(8,128)(2,1)} %get-tuple-element.224), channel_id=1, source_target_pairs={{0,2},{2,4},{4,6},{6,0},{1,3},{3,5},{5,7},{7,1},{8,10},{10,12},{12... | collective-permute-start | bytes 393224 | tf_op jit(solution)/shard_map/ppermute | solution.py:436
  120.2 4.0 %collective-permute-start.7 = (bf16[4,128,128]{2,1,0:T(8,128)(2,1)S(1)}, bf16[4,128,128]{2,1,0:T(8,128)(2,1)S(1)}, u32[]{:S(2)}, u32[]{:S(2)}) collective-permute-start(bf16[4,128,128]{2,1,0:T(8,128)(2,1)S(1)} %get-tuple-element.225), channel_id=1, source_target_pairs={{0,4},{2,6},{4,0},{6,2},{1,5},{3,7},{5,1},{7,3},{8,12},{10,14},{12... | collective-permute-start | bytes 393224 | tf_op jit(solution)/shard_map/ppermute | solution.py:436
  124.2 3.1 %collective-permute-start.8 = (bf16[4,128,128]{2,1,0:T(8,128)(2,1)S(1)}, bf16[4,128,128]{2,1,0:T(8,128)(2,1)S(1)}, u32[]{:S(2)}, u32[]{:S(2)}) collective-permute-start(bf16[4,128,128]{2,1,0:T(8,128)(2,1)S(1)} %get-tuple-element.226), channel_id=1, source_target_pairs={{0,6},{2,0},{4,2},{6,4},{1,7},{3,1},{5,3},{7,5},{8,14},{10,8},{12,... | collective-permute-start | bytes 393224 | tf_op jit(solution)/shard_map/ppermute | solution.py:436
  127.3 1.2 copy-done.2
  128.5 2.7 %shard_map.154._after = bf16[128,1792]{1,0:T(8,128)(2,1)} custom-call(s32[6]{0:T(128)S(1)} %stack.27.info, s32[44]{0:T(128)S(1)} %select_reduce_fusion.4.code, bf16[32,128,128]{2,1,0:T(8,128)(2,1)S(1)} %copy-done.2, bf16[44,4,32,128]{3,2,1,0:T(8,128)(2,1)S(1)} %get-tuple-element.217.weights), custom_call_target="tpu_custom_call" | custom-call | flops 184549376 | bytes 4194304 | tf_op jit(solution)/shard_map/pallas_call | solution.py:524
  131.3 1.8 %shard_map.155 = (f32[32,256]{1,0:T(8,128)}, f32[32,256]{1,0:T(8,128)}, f32[32,256]{1,0:T(8,128)}) custom-call(s32[32]{0:T(128)S(1)} %select_reduce_fusion.5._after.place, f32[32,768]{1,0:T(8,128)S(1)} %pad_maximum_fusion.1._after.stacked, f32[8,40,128]{2,1,0:T(8,128)S(1)} %all-to-all-done.4.came, bf16[128,1792]{1,0:T(8,128)(2,1)} %shard_map.154._after), custom_call_target="tpu_custom_call" | custom-call | bytes 1048576 | tf_op jit(solution)/shard_map/pallas_call | solution.py:543
  (85 shorter events, 9.9 us)
Async XLA Ops:
  7.2 11.4 %copy-start.16 = (s32[8,32]{1,0:T(8,128)S(1)}, s32[8,32]{1,0:T(8,128)}, u32[]{:S(2)}) copy-start(s32[8,32]{1,0:T(8,128)} %param.24) | copy-start | bytes 3076
  7.2 11.5 %copy-start.17 = (s32[8,32]{1,0:T(8,128)S(1)}, s32[8,32]{1,0:T(8,128)}, u32[]{:S(2)}) copy-start(s32[8,32]{1,0:T(8,128)} %param.21) | copy-start | bytes 3076
  7.2 11.5 %copy-start.21 = (s32[8]{0:T(128)S(1)}, s32[8]{0:T(128)}, u32[]{:S(2)}) copy-start(s32[8]{0:T(128)} %param.23) | copy-start | bytes 100
  7.2 11.7 %copy-start.18 = (s32[8,32]{1,0:T(8,128)S(1)}, s32[8,32]{1,0:T(8,128)}, u32[]{:S(2)}) copy-start(s32[8,32]{1,0:T(8,128)} %param.22) | copy-start | bytes 3076
  7.2 30.3 %copy-start.10 = (bf16[128,1792]{1,0:T(8,128)(2,1)S(1)}, bf16[128,1792]{1,0:T(8,128)(2,1)}, u32[]{:S(2)}) copy-start(bf16[128,1792]{1,0:T(8,128)(2,1)} %hidden.3) | copy-start | bytes 1376260
  7.2 49.9 %all-gather.11.cloned.1.call-start = ((), (), s32[]{:S(2)}) async-start(), calls=%async_computation.10 | async-start | bytes 2359296 | tf_op jit(solution)/shard_map/all_gather | solution.py:463
  10.8 20.9 %all-to-all-start.1 = ((bf16[4,128,512]{2,1,0:T(8,128)(2,1)}), bf16[4,128,512]{2,1,0:T(8,128)(2,1)S(1)}, u32[]{:S(2)}, u32[]{:S(2)}) async-start(bf16[4,128,512]{2,1,0:T(8,128)(2,1)} %shard_map.147), calls=%async_computation.2 | async-start | bytes 1048576 | tf_op jit(solution)/shard_map/all_to_all | solution.py:432
  31.7 5.8 %collective-permute-start = (bf16[4,128,512]{2,1,0:T(8,128)(2,1)S(1)}, bf16[4,128,512]{2,1,0:T(8,128)(2,1)S(1)}, u32[]{:S(2)}, u32[]{:S(2)}) collective-permute-start(bf16[4,128,512]{2,1,0:T(8,128)(2,1)S(1)} %all-to-all-done.1.mine), channel_id=1, source_target_pairs={{0,1},{1,0},{2,3},{3,2},{4,5},{5,4},{6,7},{7,6},{8,9},{9,8},{10,11... | collective-permute-start | bytes 1572872 | tf_op jit(solution)/shard_map/ppermute | solution.py:436
  36.7 9.8 %copy-start.14 = (f32[1,32,256]{2,1,0:T(8,128)S(1)}, f32[1,32,256]{2,1,0:T(8,128)}, u32[]{:S(2)}) copy-start(f32[1,32,256]{2,1,0:T(8,128)} %param.26) | copy-start | bytes 98308
  36.7 9.8 %copy-start.15 = (f32[1,32,256]{2,1,0:T(8,128)S(1)}, f32[1,32,256]{2,1,0:T(8,128)}, u32[]{:S(2)}) copy-start(f32[1,32,256]{2,1,0:T(8,128)} %param.27) | copy-start | bytes 98308
  40.7 1.0 copy-start.1
  41.6 21.4 %all-to-all-start.2 = ((bf16[4,32,40,128]{3,2,1,0:T(8,128)(2,1)}), bf16[4,32,40,128]{3,2,1,0:T(8,128)(2,1)S(1)}, u32[]{:S(2)}, u32[]{:S(2)}) async-start(bf16[4,32,40,128]{3,2,1,0:T(8,128)(2,1)} %get-tuple-element.211._after), calls=%async_computation.3 | async-start | bytes 2621440 | tf_op jit(solution)/shard_map/all_to_all | solution.py:432
  57.1 1.6 %copy-start = (bf16[256,32,128]{2,1,0:T(8,128)(2,1)S(1)}, bf16[256,32,128]{2,1,0:T(8,128)(2,1)}, u32[]{:S(2)}) copy-start(bf16[256,32,128]{2,1,0:T(8,128)(2,1)} %all-gather.11.cloned.1.call-done.gathered) | copy-start | bytes 6291460
  59.4 11.3 %copy-start.19 = (s32[8,32]{1,0:T(8,128)S(1)}, s32[8,32]{1,0:T(8,128)}, u32[]{:S(2)}) copy-start(s32[8,32]{1,0:T(8,128)} %param.25) | copy-start | bytes 3076
  63.9 17.9 %all-to-all-start.3 = ((bf16[8,4,40,128]{3,2,1,0:T(8,128)(2,1)}), bf16[8,4,40,128]{3,2,1,0:T(8,128)(2,1)S(1)}, u32[]{:S(2)}, u32[]{:S(2)}) async-start(bf16[8,4,40,128]{3,2,1,0:T(8,128)(2,1)} %bitcast.46), calls=%async_computation.4 | async-start | bytes 655360 | tf_op jit(solution)/shard_map/all_to_all | solution.py:432
  71.1 26.4 %collective-permute-start.2 = (bf16[44,32,128]{2,1,0:T(8,128)(2,1)S(1)}, bf16[44,32,128]{2,1,0:T(8,128)(2,1)S(1)}, u32[]{:S(2)}, u32[]{:S(2)}) collective-permute-start(bf16[44,32,128]{2,1,0:T(8,128)(2,1)S(1)} %shard_map.149._after2.w0), channel_id=1, source_target_pairs={{0,16},{16,32},{32,48},{48,0},{1,17},{17,33},{33,49},{49,1},{2,18}... | collective-permute-start | bytes 1081352 | tf_op jit(solution)/shard_map/ppermute | solution.py:436
  73.3 25.0 %collective-permute-start.3 = (bf16[44,32,128]{2,1,0:T(8,128)(2,1)S(1)}, bf16[44,32,128]{2,1,0:T(8,128)(2,1)S(1)}, u32[]{:S(2)}, u32[]{:S(2)}) collective-permute-start(bf16[44,32,128]{2,1,0:T(8,128)(2,1)S(1)} %shard_map.149._after2.w0), channel_id=1, source_target_pairs={{0,32},{16,48},{32,0},{48,16},{1,33},{17,49},{33,1},{49,17},{2,34}... | collective-permute-start | bytes 1081352 | tf_op jit(solution)/shard_map/ppermute | solution.py:436
  77.0 22.0 %collective-permute-start.4 = (bf16[44,32,128]{2,1,0:T(8,128)(2,1)S(1)}, bf16[44,32,128]{2,1,0:T(8,128)(2,1)S(1)}, u32[]{:S(2)}, u32[]{:S(2)}) collective-permute-start(bf16[44,32,128]{2,1,0:T(8,128)(2,1)S(1)} %shard_map.149._after2.w0), channel_id=1, source_target_pairs={{0,48},{16,0},{32,16},{48,32},{1,49},{17,1},{33,17},{49,33},{2,50}... | collective-permute-start | bytes 1081352 | tf_op jit(solution)/shard_map/ppermute | solution.py:436
  82.5 13.7 %collective-permute-start.1 = (f32[2,40,128]{2,1,0:T(8,128)S(1)}, f32[2,40,128]{2,1,0:T(8,128)S(1)}, u32[]{:S(2)}, u32[]{:S(2)}) collective-permute-start(f32[2,40,128]{2,1,0:T(8,128)S(1)} %get-tuple-element.214), channel_id=1, source_target_pairs={{0,8},{8,0},{1,9},{9,1},{2,10},{10,2},{3,11},{11,3},{4,12},{12,4},... | collective-permute-start | bytes 122888 | tf_op jit(solution)/shard_map/ppermute | solution.py:436
  97.5 0.7 copy-start.3
  99.7 1.0 copy-start.4
  100.7 1.0 copy-start.6
  101.7 1.0 copy-start.8
  106.2 8.7 %collective-permute-start.5 = (f32[4,4,128,128]{3,2,1,0:T(8,128)}, f32[4,4,128,128]{3,2,1,0:T(8,128)}, u32[]{:S(2)}, u32[]{:S(2)}) collective-permute-start(f32[4,4,128,128]{3,2,1,0:T(8,128)} %get-tuple-element.222), channel_id=1, source_target_pairs={{0,1},{1,0},{2,3},{3,2},{4,5},{5,4},{6,7},{7,6},{8,9},{9,8},{10,11... | collective-permute-start | bytes 3145736 | tf_op jit(solution)/shard_map/ppermute | solution.py:436
  111.6 19.7 %all-to-all-start.4 = ((f32[8,40,128]{2,1,0:T(8,128)}), f32[8,40,128]{2,1,0:T(8,128)S(1)}, u32[]{:S(2)}, u32[]{:S(2)}) async-start(f32[8,40,128]{2,1,0:T(8,128)} %shard_map.152._after), calls=%async_computation.5 | async-start | bytes 327680 | tf_op jit(solution)/shard_map/all_to_all | solution.py:432
  116.9 16.1 %collective-permute-start.6 = (bf16[4,128,128]{2,1,0:T(8,128)(2,1)}, bf16[4,128,128]{2,1,0:T(8,128)(2,1)S(1)}, u32[]{:S(2)}, u32[]{:S(2)}) collective-permute-start(bf16[4,128,128]{2,1,0:T(8,128)(2,1)} %get-tuple-element.224), channel_id=1, source_target_pairs={{0,2},{2,4},{4,6},{6,0},{1,3},{3,5},{5,7},{7,1},{8,10},{10,12},{12... | collective-permute-start | bytes 393224 | tf_op jit(solution)/shard_map/ppermute | solution.py:436
  120.2 12.9 %collective-permute-start.7 = (bf16[4,128,128]{2,1,0:T(8,128)(2,1)S(1)}, bf16[4,128,128]{2,1,0:T(8,128)(2,1)S(1)}, u32[]{:S(2)}, u32[]{:S(2)}) collective-permute-start(bf16[4,128,128]{2,1,0:T(8,128)(2,1)S(1)} %get-tuple-element.225), channel_id=1, source_target_pairs={{0,4},{2,6},{4,0},{6,2},{1,5},{3,7},{5,1},{7,3},{8,12},{10,14},{12... | collective-permute-start | bytes 393224 | tf_op jit(solution)/shard_map/ppermute | solution.py:436
  124.2 9.2 %collective-permute-start.8 = (bf16[4,128,128]{2,1,0:T(8,128)(2,1)S(1)}, bf16[4,128,128]{2,1,0:T(8,128)(2,1)S(1)}, u32[]{:S(2)}, u32[]{:S(2)}) collective-permute-start(bf16[4,128,128]{2,1,0:T(8,128)(2,1)S(1)} %get-tuple-element.226), channel_id=1, source_target_pairs={{0,6},{2,0},{4,2},{6,4},{1,7},{3,1},{5,3},{7,5},{8,14},{10,8},{12,... | collective-permute-start | bytes 393224 | tf_op jit(solution)/shard_map/ppermute | solution.py:436
  127.3 1.2 copy-start.2
  128.5 5.0 %copy-start.11 = (bf16[128,1792]{1,0:T(8,128)(2,1)S(1)}, bf16[128,1792]{1,0:T(8,128)(2,1)}, u32[]{:S(2)}) copy-start(bf16[128,1792]{1,0:T(8,128)(2,1)} %hidden.3) | copy-start | bytes 1376260
  128.5 5.0 %copy-start.12 = (bf16[128,512]{1,0:T(8,128)(2,1)S(1)}, bf16[128,512]{1,0:T(8,128)(2,1)}, u32[]{:S(2)}) copy-start(bf16[128,512]{1,0:T(8,128)(2,1)} %value) | copy-start | bytes 393220
  128.5 5.0 %copy-start.22 = (s32[8]{0:T(128)S(1)}, s32[8]{0:T(128)}, u32[]{:S(2)}) copy-start(s32[8]{0:T(128)} %param.23) | copy-start | bytes 100
  (3 other events, 2.1 us)
Sparse Core Ops, SparseCore 0:
  10.9 46.1 all-gather.10
